TPU v7x, 32 devices: a whole 2x2x4 slice. The times are simulated.
32 devices in a mesh: dp: 8 (over y, x, core), seq: 4 (over z).
Axes of the slice: x: 2, y: 2, z: 4, core: 2. Of those that a mesh axis runs over, the one named last changes fastest.
Arguments:
- inputs: bfloat16 [16, 2048, 768], P('dp', 'seq'), may hold values from -6 to 6
- cotangent: bfloat16 [16, 2048, 768], P('dp', 'seq'), may hold values from -6 to 6
- rand_blocks: int32 [16, 12, 32, 3], P('dp', None, 'seq'), may hold values from 0 to 31
- global_blocks: int32 [16, 2], P('dp'), may hold values from 0 to 31
- w_query: bfloat16 [768, 768], P(('dp', 'seq')), may hold values from -0.21875 to 0.21875
- b_query: bfloat16 [768], P(('dp', 'seq')), may hold values from -3 to 3
- w_key: bfloat16 [768, 768], P(('dp', 'seq')), may hold values from -0.21875 to 0.21875
- w_value: bfloat16 [768, 768], P(('dp', 'seq')), may hold values from -0.21875 to 0.21875
- b_value: bfloat16 [768], P(('dp', 'seq')), may hold values from -3 to 3
- w_out: bfloat16 [768, 768], P(('dp', 'seq')), may hold values from -1.25 to 1.25
- b_out: bfloat16 [768], P(('dp', 'seq')), may hold values from -3 to 3
- gain_one: bfloat16 [768], P(('dp', 'seq')), may hold values from 0.5 to 1.5
- shift_one: bfloat16 [768], P(('dp', 'seq')), may hold values from -3 to 3
- w_up: bfloat16 [768, 3072], P(('dp', 'seq')), may hold values from -0.21875 to 0.21875
- b_up: bfloat16 [3072], P(('dp', 'seq')), may hold values from -3 to 3
- w_down: bfloat16 [3072, 768], P(('dp', 'seq')), may hold values from -0.109375 to 0.109375
- b_down: bfloat16 [768], P(('dp', 'seq')), may hold values from -3 to 3
- gain_two: bfloat16 [768], P(('dp', 'seq')), may hold values from 0.5 to 1.5
- shift_two: bfloat16 [768], P(('dp', 'seq')), may hold values from -3 to 3
Outputs:
- output: bfloat16 [16, 2048, 768], P('dp', 'seq')
- grad_inputs: bfloat16 [16, 2048, 768], P('dp', 'seq')
- grad_w_query: float32 [768, 768], P(('dp', 'seq'))
- grad_b_query: float32 [768], P(('dp', 'seq'))
- grad_w_key: float32 [768, 768], P(('dp', 'seq'))
- grad_w_value: float32 [768, 768], P(('dp', 'seq'))
- grad_b_value: float32 [768], P(('dp', 'seq'))
- grad_w_out: float32 [768, 768], P(('dp', 'seq'))
- grad_b_out: float32 [768], P(('dp', 'seq'))
- grad_gain_one: float32 [768], P(('dp', 'seq'))
- grad_shift_one: float32 [768], P(('dp', 'seq'))
- grad_w_up: float32 [768, 3072], P(('dp', 'seq'))
- grad_b_up: float32 [3072], P(('dp', 'seq'))
- grad_w_down: float32 [3072, 768], P(('dp', 'seq'))
- grad_b_down: float32 [768], P(('dp', 'seq'))
- grad_gain_two: float32 [768], P(('dp', 'seq'))
- grad_shift_two: float32 [768], P(('dp', 'seq'))
Inputs may be any that keep to these rules, and one draw needn't show every extreme that they name: `rand_blocks`: block numbers of one sequence. `global_blocks`: block numbers of one sequence, possibly equal.
All inputs are finite; a program needn't handle non-finite values.
Results may differ from a plain program's by a relative error of at most 0.015.
Values may be sent and summed in bfloat16 or wider, within the bound.
No kernel may reach another device: no remote copies, remote signals or barrier semaphores. Data moves between devices by JAX's collectives and lax.ppermute only.
A program may use at most 384 MiB of HBM per device.

v0:
```python
from functools import partial

import jax
import jax.numpy as jnp
from jax import lax
from jax.sharding import PartitionSpec as P

HEADS = 12
HEAD = 64
BLOCK = 64
MICRO = 2


EPS = 1e-06
NEG = -1e30


def layer_norm(summed, gain, shift):
    center = summed - jnp.mean(summed, -1, keepdims=True)
    spread = jnp.mean(center * center, -1, keepdims=True)
    return center * lax.rsqrt(spread + EPS) * gain + shift


def project(rows_in, weight):
    return jnp.einsum("std,de->ste", rows_in, weight, preferred_element_type=jnp.float32)


def project_back(grad_rows, weight):
    return jnp.einsum("ste,de->std", grad_rows, weight, preferred_element_type=jnp.float32)


def weight_grad(rows_in, grad_rows):
    return jnp.einsum("std,ste->de", rows_in, grad_rows, preferred_element_type=jnp.float32)


def token_sum(grad_rows):
    return jnp.sum(grad_rows.astype(jnp.float32), axis=(0, 1))


def block_masks(rand_blocks, global_blocks):
    local_blocks = rand_blocks.shape[2]
    total_blocks = local_blocks * lax.axis_size("seq")
    query_blocks = lax.axis_index("seq") * local_blocks + jnp.arange(local_blocks, dtype=jnp.int32)
    key_blocks = jnp.arange(total_blocks, dtype=jnp.int32)
    nearby = jnp.abs(query_blocks[:, None] - key_blocks[None, :]) <= 1
    glob_col = jnp.any(key_blocks[None, :, None] == global_blocks[:, None, :], axis=2)
    glob_row = jnp.any(query_blocks[None, :, None] == global_blocks[:, None, :], axis=2)
    base = nearby[None] | glob_col[:, None, :] | glob_row[:, :, None]
    rand_hit = jnp.any(rand_blocks[..., None] == key_blocks, axis=3)
    return base[:, None] | rand_hit


def masked_scores(query_part, key_whole, allowed):
    query_len = query_part.shape[0]
    key_len = key_whole.shape[0]
    q_heads = query_part.reshape(query_len, HEADS, HEAD)
    k_heads = key_whole.reshape(key_len, HEADS, HEAD)
    scores = jnp.einsum(
        "qhe,khe->hqk", q_heads, k_heads, preferred_element_type=jnp.float32
    ) * HEAD ** (-0.5)
    scores = scores.reshape(HEADS, query_len // BLOCK, BLOCK, key_len // BLOCK, BLOCK)
    scores = jnp.where(allowed[:, :, None, :, None], scores, NEG)
    return scores.reshape(HEADS, query_len, key_len)


def attend(member):
    query_part, key_whole, value_whole, allowed = member
    scores = masked_scores(query_part, key_whole, allowed)
    highest_score = jnp.max(scores, -1, keepdims=True)
    weights_exp = jnp.exp(scores - highest_score)
    totals = jnp.sum(weights_exp, -1, keepdims=True)
    prob = (weights_exp / totals).astype(jnp.bfloat16)
    v_heads = value_whole.reshape(value_whole.shape[0], HEADS, HEAD)
    attended = jnp.einsum("hqk,khe->qhe", prob, v_heads, preferred_element_type=jnp.float32)
    attended = attended.reshape(query_part.shape[0], -1).astype(jnp.bfloat16)
    return (attended, (highest_score + jnp.log(totals))[..., 0])


def attend_back(member):
    query_part, key_whole, value_whole, allowed, log_total, grad_out = member
    query_len = query_part.shape[0]
    key_len = key_whole.shape[0]
    scores = masked_scores(query_part, key_whole, allowed)
    prob = jnp.exp(scores - log_total[..., None])
    q_heads = query_part.reshape(query_len, HEADS, HEAD)
    k_heads = key_whole.reshape(key_len, HEADS, HEAD)
    v_heads = value_whole.reshape(key_len, HEADS, HEAD)
    grad_heads = grad_out.reshape(query_len, HEADS, HEAD)
    grad_prob = jnp.einsum("qhe,khe->hqk", grad_heads, v_heads, preferred_element_type=jnp.float32)
    inner = jnp.sum(prob * grad_prob, -1, keepdims=True)
    grad_scores = (prob * (grad_prob - inner)).astype(jnp.bfloat16)
    factor = HEAD ** (-0.5)
    grad_q = jnp.einsum("hqk,khe->qhe", grad_scores, k_heads, preferred_element_type=jnp.float32)
    grad_k = jnp.einsum("hqk,qhe->khe", grad_scores, q_heads, preferred_element_type=jnp.float32)
    grad_v = jnp.einsum(
        "hqk,qhe->khe", prob.astype(jnp.bfloat16), grad_heads, preferred_element_type=jnp.float32
    )
    return (
        grad_q.reshape(query_len, -1) * factor,
        grad_k.reshape(key_len, -1) * factor,
        grad_v.reshape(key_len, -1),
    )


def forward(weights, tokens, masks):
    (
        w_query,
        b_query,
        w_key,
        w_value,
        b_value,
        w_out,
        b_out,
        gain_one,
        shift_one,
        w_up,
        b_up,
        w_down,
        b_down,
        gain_two,
        shift_two,
    ) = weights
    queries = (project(tokens, w_query) + b_query.astype(jnp.float32)).astype(jnp.bfloat16)
    keys_local = project(tokens, w_key).astype(jnp.bfloat16)
    values_local = (project(tokens, w_value) + b_value.astype(jnp.float32)).astype(jnp.bfloat16)
    keys_whole, values_whole = (
        lax.all_gather(keys_local, "seq", axis=1, tiled=True),
        lax.all_gather(values_local, "seq", axis=1, tiled=True),
    )
    attended, log_total = lax.map(attend, (queries, keys_whole, values_whole, masks))
    branch = project(attended, w_out) + b_out.astype(jnp.float32)
    first_sum = tokens.astype(jnp.float32) + branch
    normed = layer_norm(first_sum, gain_one.astype(jnp.float32), shift_one.astype(jnp.float32))
    normed_low = normed.astype(jnp.bfloat16)
    hidden_pre = project(normed_low, w_up) + b_up.astype(jnp.float32)
    hidden = jax.nn.gelu(hidden_pre, approximate=False).astype(jnp.bfloat16)
    second_sum = normed + (project(hidden, w_down) + b_down.astype(jnp.float32))
    output = layer_norm(second_sum, gain_two.astype(jnp.float32), shift_two.astype(jnp.float32))
    return (
        queries,
        keys_whole,
        values_whole,
        log_total,
        attended,
        first_sum,
        normed_low,
        hidden_pre,
        hidden,
        second_sum,
        output.astype(jnp.bfloat16),
    )


def backward(weights, state, tokens, masks, cotangent):
    (
        w_query,
        b_query,
        w_key,
        w_value,
        b_value,
        w_out,
        b_out,
        gain_one,
        shift_one,
        w_up,
        b_up,
        w_down,
        b_down,
        gain_two,
        shift_two,
    ) = weights
    (
        queries,
        keys_whole,
        values_whole,
        log_total,
        attended,
        first_sum,
        normed_low,
        hidden_pre,
        hidden,
        second_sum,
        output,
    ) = state
    unused, norm_two_back = jax.vjp(
        layer_norm, second_sum, gain_two.astype(jnp.float32), shift_two.astype(jnp.float32)
    )
    grad_second, grad_gain_two, grad_shift_two = norm_two_back(cotangent.astype(jnp.float32))
    grad_down = grad_second.astype(jnp.bfloat16)
    grad_b_down = token_sum(grad_down)
    grad_w_down = weight_grad(hidden, grad_down)
    grad_hidden = project_back(grad_down, w_down)
    unused, gelu_back = jax.vjp(partial(jax.nn.gelu, approximate=False), hidden_pre)
    grad_pre = gelu_back(grad_hidden)[0].astype(jnp.bfloat16)
    grad_b_up = token_sum(grad_pre)
    grad_w_up = weight_grad(normed_low, grad_pre)
    grad_normed = grad_second + project_back(grad_pre, w_up)
    unused, norm_one_back = jax.vjp(
        layer_norm, first_sum, gain_one.astype(jnp.float32), shift_one.astype(jnp.float32)
    )
    grad_first, grad_gain_one, grad_shift_one = norm_one_back(grad_normed)
    grad_branch = grad_first.astype(jnp.bfloat16)
    grad_b_out = token_sum(grad_branch)
    grad_w_out = weight_grad(attended, grad_branch)
    grad_attended = project_back(grad_branch, w_out).astype(jnp.bfloat16)
    grad_q, grad_k_whole, grad_v_whole = lax.map(
        attend_back, (queries, keys_whole, values_whole, masks, log_total, grad_attended)
    )
    grad_k, grad_v = (
        lax.psum_scatter(
            grad_k_whole.astype(jnp.bfloat16), "seq", scatter_dimension=1, tiled=True
        ).astype(jnp.float32),
        lax.psum_scatter(
            grad_v_whole.astype(jnp.bfloat16), "seq", scatter_dimension=1, tiled=True
        ).astype(jnp.float32),
    )
    grad_queries = grad_q.astype(jnp.bfloat16)
    grad_keys = grad_k.astype(jnp.bfloat16)
    grad_values = grad_v.astype(jnp.bfloat16)
    grad_tokens = (
        grad_first
        + project_back(grad_queries, w_query)
        + project_back(grad_keys, w_key)
        + project_back(grad_values, w_value)
    )
    grads = (
        weight_grad(tokens, grad_queries),
        token_sum(grad_queries),
        weight_grad(tokens, grad_keys),
        weight_grad(tokens, grad_values),
        token_sum(grad_values),
        grad_w_out,
        grad_b_out,
        grad_gain_one,
        grad_shift_one,
        grad_w_up,
        grad_b_up,
        grad_w_down,
        grad_b_down,
        grad_gain_two,
        grad_shift_two,
    )
    return (grad_tokens.astype(jnp.bfloat16), grads)


def shards(
    inputs,
    cotangent,
    rand_blocks,
    global_blocks,
    w_query,
    b_query,
    w_key,
    w_value,
    b_value,
    w_out,
    b_out,
    gain_one,
    shift_one,
    w_up,
    b_up,
    w_down,
    b_down,
    gain_two,
    shift_two,
):

    def gather_weights():
        return (
            lax.all_gather(w_query, ("dp", "seq"), axis=0, tiled=True),
            lax.all_gather(b_query, ("dp", "seq"), axis=0, tiled=True),
            lax.all_gather(w_key, ("dp", "seq"), axis=0, tiled=True),
            lax.all_gather(w_value, ("dp", "seq"), axis=0, tiled=True),
            lax.all_gather(b_value, ("dp", "seq"), axis=0, tiled=True),
            lax.all_gather(w_out, ("dp", "seq"), axis=0, tiled=True),
            lax.all_gather(b_out, ("dp", "seq"), axis=0, tiled=True),
            lax.all_gather(gain_one, ("dp", "seq"), axis=0, tiled=True),
            lax.all_gather(shift_one, ("dp", "seq"), axis=0, tiled=True),
            lax.all_gather(w_up, ("dp", "seq"), axis=0, tiled=True),
            lax.all_gather(b_up, ("dp", "seq"), axis=0, tiled=True),
            lax.all_gather(w_down, ("dp", "seq"), axis=0, tiled=True),
            lax.all_gather(b_down, ("dp", "seq"), axis=0, tiled=True),
            lax.all_gather(gain_two, ("dp", "seq"), axis=0, tiled=True),
            lax.all_gather(shift_two, ("dp", "seq"), axis=0, tiled=True),
        )

    masks = block_masks(rand_blocks, global_blocks)
    per_batch = inputs.shape[0] // MICRO
    outputs = []
    for micro_index in range(MICRO):
        lower = micro_index * per_batch
        weights = gather_weights()
        state = forward(
            weights, inputs[lower : lower + per_batch], masks[lower : lower + per_batch]
        )
        outputs.append(state[10])
    grads_in = []
    totals = None
    for micro_index in range(MICRO):
        lower = micro_index * per_batch
        weights = gather_weights()
        state = forward(
            weights, inputs[lower : lower + per_batch], masks[lower : lower + per_batch]
        )
        grad_tokens, grads = backward(
            weights,
            state,
            inputs[lower : lower + per_batch],
            masks[lower : lower + per_batch],
            cotangent[lower : lower + per_batch],
        )
        grads_in.append(grad_tokens)
        if totals is None:
            totals = grads
        else:
            totals = tuple((before + after for before, after in zip(totals, grads)))
    owned = (
        lax.psum_scatter(totals[0], ("dp", "seq"), scatter_dimension=0, tiled=True),
        lax.psum_scatter(totals[1], ("dp", "seq"), scatter_dimension=0, tiled=True),
        lax.psum_scatter(totals[2], ("dp", "seq"), scatter_dimension=0, tiled=True),
        lax.psum_scatter(totals[3], ("dp", "seq"), scatter_dimension=0, tiled=True),
        lax.psum_scatter(totals[4], ("dp", "seq"), scatter_dimension=0, tiled=True),
        lax.psum_scatter(totals[5], ("dp", "seq"), scatter_dimension=0, tiled=True),
        lax.psum_scatter(totals[6], ("dp", "seq"), scatter_dimension=0, tiled=True),
        lax.psum_scatter(totals[7], ("dp", "seq"), scatter_dimension=0, tiled=True),
        lax.psum_scatter(totals[8], ("dp", "seq"), scatter_dimension=0, tiled=True),
        lax.psum_scatter(totals[9], ("dp", "seq"), scatter_dimension=0, tiled=True),
        lax.psum_scatter(totals[10], ("dp", "seq"), scatter_dimension=0, tiled=True),
        lax.psum_scatter(totals[11], ("dp", "seq"), scatter_dimension=0, tiled=True),
        lax.psum_scatter(totals[12], ("dp", "seq"), scatter_dimension=0, tiled=True),
        lax.psum_scatter(totals[13], ("dp", "seq"), scatter_dimension=0, tiled=True),
        lax.psum_scatter(totals[14], ("dp", "seq"), scatter_dimension=0, tiled=True),
    )
    return (
        jnp.concatenate(outputs, 0),
        jnp.concatenate(grads_in, 0),
        owned[0],
        owned[1],
        owned[2],
        owned[3],
        owned[4],
        owned[5],
        owned[6],
        owned[7],
        owned[8],
        owned[9],
        owned[10],
        owned[11],
        owned[12],
        owned[13],
        owned[14],
    )


def solution(mesh):
    placed = (
        P("dp", "seq", None),
        P("dp", "seq", None),
        P("dp", None, "seq", None),
        P("dp", None),
        P(("dp", "seq"), None),
        P(("dp", "seq")),
        P(("dp", "seq"), None),
        P(("dp", "seq"), None),
        P(("dp", "seq")),
        P(("dp", "seq"), None),
        P(("dp", "seq")),
        P(("dp", "seq")),
        P(("dp", "seq")),
        P(("dp", "seq"), None),
        P(("dp", "seq")),
        P(("dp", "seq"), None),
        P(("dp", "seq")),
        P(("dp", "seq")),
        P(("dp", "seq")),
    )
    return jax.shard_map(
        shards,
        mesh=mesh,
        in_specs=placed,
        out_specs=(
            P("dp", "seq", None),
            P("dp", "seq", None),
            P(("dp", "seq"), None),
            P(("dp", "seq")),
            P(("dp", "seq"), None),
            P(("dp", "seq"), None),
            P(("dp", "seq")),
            P(("dp", "seq"), None),
            P(("dp", "seq")),
            P(("dp", "seq")),
            P(("dp", "seq")),
            P(("dp", "seq"), None),
            P(("dp", "seq")),
            P(("dp", "seq"), None),
            P(("dp", "seq")),
            P(("dp", "seq")),
            P(("dp", "seq")),
        ),
        check_vma=False,
    )
```

profile of v0, /device:TPU:0, one launch (start us, length us, event | category | flops | bytes accessed | tf_op | source)
XLA Modules:
  0.0 1663.2 jit_solution(2780767223505059402)
XLA Ops:
  9.6 58.2 %all-gather.19.cloned.1.call-done = bf16[768,768]{1,0:T(8,128)(2,1)} async-done(((bf16[24,768]{1,0:T(8,128)(2,1)}), bf16[768,768]{1,0:T(8,128)(2,1)}) %all-gather.19.cloned.1.call-update) | async-done | bytes 1179664 | tf_op jit(solution)/shard_map/all_gather | solution.py:272
  73.2 39.7 %all-reduce.19 = (bf16[768]{0:T(1024)(128)(2,1)S(1)}, bf16[768]{0:T(1024)(128)(2,1)S(1)}, bf16[768]{0:T(1024)(128)(2,1)S(1)}, bf16[768]{0:T(1024)(128)(2,1)S(1)}...) all-reduce(bf16[768]{0:T(1024)(128)(2,1)S(1)} %dynamic-update-slice, ...), channel_id=1, replica_groups=mesh['dp'=8,'seq'=4] {'dp','seq'}, use_global_device_ids=true, to_apply=%add | all-reduce | flops 9216 | bytes 36864
  147.6 66.9 %broadcast_in_dim.232 = pred[12,512,2048]{2,1,0:T(32,128)(4,1)} reshape(pred[12,8,64,32,64]{4,3,2,1,0:T(32,128)(4,1)} %broadcast_in_dim.231) | data formatting | bytes 25165824 | tf_op jit(solution)/shard_map/while/body/eval_jaxpr/jit(_where)/broadcast_in_dim | solution.py:62
  224.3 66.9 %broadcast_in_dim.236 = pred[12,512,2048]{2,1,0:T(32,128)(4,1)} reshape(pred[12,8,64,32,64]{4,3,2,1,0:T(32,128)(4,1)} %broadcast_in_dim.235) | data formatting | bytes 25165824 | tf_op jit(solution)/shard_map/while/body/eval_jaxpr/jit(_where)/broadcast_in_dim | solution.py:62
  300.9 24.4 %fusion.119 = (f32[12,512]{1,0:T(8,128)S(1)}, f32[12,512,2048]{2,1,0:T(8,128)}) fusion(pred[12,512,2048]{2,1,0:T(32,128)(4,1)} %broadcast_in_dim.236, bf16[512,12,64]{0,2,1:T(8,128)(2,1)} %bitcast.247, bf16[2048,12,64]{0,2,1:T(8,128)(2,1)S(1)} %bitcast.231), kind=kOutput, calls=%fused_computation.232 | convolution fusion | flops 1648355328 | bytes 66871296 | tf_op jit(solution)/shard_map/while/body/eval_jaxpr/qhe,khe->hqk/dot_general | solution.py:58
  373.8 53.9 %all-gather.29.cloned.1.call-done = bf16[2048,768]{1,0:T(8,128)(2,1)} async-done(((bf16[512,768]{1,0:T(8,128)(2,1)}), bf16[2048,768]{1,0:T(8,128)(2,1)}) %all-gather.29.cloned.1.call-update) | async-done | bytes 3145744 | tf_op jit(solution)/shard_map/all_gather | solution.py:127
  431.3 24.7 %fusion.117 = (f32[12,512]{1,0:T(8,128)S(1)}, f32[12,512,2048]{2,1,0:T(8,128)}) fusion(pred[12,512,2048]{2,1,0:T(32,128)(4,1)} %broadcast_in_dim.232, bf16[512,12,64]{0,2,1:T(8,128)(2,1)} %bitcast.249, bf16[2048,12,64]{0,2,1:T(8,128)(2,1)S(1)} %bitcast.233), kind=kOutput, calls=%fused_computation.230 | convolution fusion | flops 1648355328 | bytes 66871296 | tf_op jit(solution)/shard_map/while/body/eval_jaxpr/qhe,khe->hqk/dot_general | solution.py:58
  456.0 19.9 %fusion = f32[12,512]{1,0:T(8,128)S(1)} fusion(f32[12,512,2048]{2,1,0:T(8,128)} %get-tuple-element.294, f32[12,512]{1,0:T(8,128)S(1)} %get-tuple-element.293), kind=kLoop, calls=%fused_computation.12 | loop fusion | flops 25159680 | bytes 50380800 | tf_op jit(solution)/shard_map/while/body/eval_jaxpr/reduce_sum | solution.py:71
  494.7 20.2 %fusion.41 = bf16[12,64,512]{2,1,0:T(8,128)(2,1)S(1)} fusion(bf16[2048,12,64]{0,2,1:T(8,128)(2,1)S(1)} %bitcast.241, f32[12,512,2048]{2,1,0:T(8,128)} %get-tuple-element.294, f32[12,512]{1,0:T(8,128)S(1)} %fusion, f32[12,512]{1,0:T(8,128)S(1)} %get-tuple-element.293), kind=kOutput, calls=%fused_computation.137 | convolution fusion | flops 1648754688 | bytes 54312960 | tf_op jit(solution)/shard_map/while/body/eval_jaxpr/hqk,khe->qhe/dot_general | solution.py:74
  516.3 40.2 %all-gather.23.cloned.1.call-done = bf16[768,3072]{1,0:T(8,128)(2,1)} async-done(((bf16[24,3072]{1,0:T(8,128)(2,1)}), bf16[768,3072]{1,0:T(8,128)(2,1)}) %all-gather.23.cloned.1.call-update) | async-done | bytes 4718608 | tf_op jit(solution)/shard_map/all_gather | solution.py:279
  564.1 35.0 %multiply_convert_fusion.5 = (bf16[512,3072]{1,0:T(8,128)(2,1)}, f32[512,3072]{1,0:T(8,128)}, bf16[512,3072]{1,0:T(8,128)(2,1)}, f32[512,3072]{1,0:T(8,128)}, f32[512,3072]{1,0:T(8,128)}) fusion(f32[3072]{0:T(1024)S(1)} %copy-done.79, f32[512,3072]{1,0:T(8,128)S(1)} %fusion.109, bf16[768,3072]{1,0:T(8,128)(2,1)S(1)} %copy-done.90, ...), kind=kOutput, calls=%fused_computation.45 | convolution fusion | flops 2625503232 | bytes 37771264 | tf_op jit(solution)/shard_map/std,de->ste/dot_general | solution.py:25
  599.0 22.5 %all-gather.25.cloned.1.call-done = bf16[3072,768]{1,0:T(8,128)(2,1)} async-done(((bf16[96,768]{1,0:T(8,128)(2,1)}), bf16[3072,768]{1,0:T(8,128)(2,1)}) %all-gather.25.cloned.1.call-update) | async-done | bytes 4718608 | tf_op jit(solution)/shard_map/all_gather | solution.py:281
  669.5 20.3 %fusion.24 = bf16[12,64,2048]{2,1,0:T(8,128)(2,1)} fusion(bf16[512,12,64]{0,2,1:T(8,128)(2,1)S(1)} %bitcast.243, f32[12,512,2048]{2,1,0:T(8,128)} %get-tuple-element.294, f32[12,512]{1,0:T(8,128)S(1)} %log_add_fusion.1), kind=kOutput, calls=%fused_computation.62 | convolution fusion | flops 1637351424 | bytes 54288384 | tf_op jit(solution)/shard_map/while/body/eval_jaxpr/hqk,qhe->khe/dot_general | solution.py:95
  695.6 20.2 %fusion.27 = bf16[12,64,2048]{2,1,0:T(8,128)(2,1)} fusion(bf16[512,12,64]{0,2,1:T(8,128)(2,1)S(1)} %bitcast.245, f32[12,512,2048]{2,1,0:T(8,128)} %get-tuple-element.298, f32[12,512]{1,0:T(8,128)S(1)} %log_add_fusion), kind=kOutput, calls=%fused_computation.63 | convolution fusion | flops 1637351424 | bytes 54288384 | tf_op jit(solution)/shard_map/while/body/eval_jaxpr/hqk,qhe->khe/dot_general | solution.py:95
  717.8 32.6 %multiply_reduce_fusion.1 = (f32[12,512]{1,0:T(8,128)S(1)}, f32[12,512,2048]{2,1,0:T(8,128)}) fusion(f32[12,512,2048]{2,1,0:T(8,128)} %get-tuple-element.294, f32[12,512]{1,0:T(8,128)S(1)} %log_add_fusion.1, bf16[512,12,64]{0,2,1:T(8,128)(2,1)} %bitcast.244, bf16[2048,12,64]{0,2,1:T(8,128)(2,1)S(1)} %bitcast.242), kind=kOutput, calls=%fused_computation.4 | convolution fusion | flops 1648355328 | bytes 104644608 | tf_op jit(solution)/shard_map/while/body/eval_jaxpr/qhe,khe->hqk/dot_general | solution.py:89
  750.4 41.4 %multiply_convert_fusion.1 = bf16[12,512,2048]{2,1,0:T(8,128)(2,1)} fusion(f32[12,512,2048]{2,1,0:T(8,128)} %get-tuple-element.310, f32[12,512,2048]{2,1,0:T(8,128)} %get-tuple-element.294, f32[12,512]{1,0:T(8,128)S(1)} %get-tuple-element.309, f32[12,512]{1,0:T(8,128)S(1)} %log_add_fusion.1), kind=kLoop, calls=%fused_computation.3 | loop fusion | flops 50331648 | bytes 125878272 | tf_op jit(solution)/shard_map/while/body/eval_jaxpr/convert_element_type | solution.py:91
  808.0 32.4 %multiply_reduce_fusion = (f32[12,512]{1,0:T(8,128)S(1)}, f32[12,512,2048]{2,1,0:T(8,128)}) fusion(f32[12,512,2048]{2,1,0:T(8,128)} %get-tuple-element.298, f32[12,512]{1,0:T(8,128)S(1)} %log_add_fusion, bf16[512,12,64]{0,2,1:T(8,128)(2,1)} %bitcast.246, bf16[2048,12,64]{0,2,1:T(8,128)(2,1)S(1)} %bitcast.240), kind=kOutput, calls=%fused_computation.1 | convolution fusion | flops 1648355328 | bytes 104644608 | tf_op jit(solution)/shard_map/while/body/eval_jaxpr/qhe,khe->hqk/dot_general | solution.py:89
  840.4 40.9 %multiply_convert_fusion = bf16[12,512,2048]{2,1,0:T(8,128)(2,1)} fusion(f32[12,512,2048]{2,1,0:T(8,128)} %get-tuple-element.308, f32[12,512,2048]{2,1,0:T(8,128)} %get-tuple-element.298, f32[12,512]{1,0:T(8,128)S(1)} %get-tuple-element.307, f32[12,512]{1,0:T(8,128)S(1)} %log_add_fusion), kind=kLoop, calls=%fused_computation | loop fusion | flops 50331648 | bytes 125878272 | tf_op jit(solution)/shard_map/while/body/eval_jaxpr/convert_element_type | solution.py:91
  990.1 41.7 %all-reduce.18 = (f32[768]{0:T(1024)S(1)}, f32[768]{0:T(1024)S(1)}, f32[768]{0:T(1024)S(1)}, f32[768]{0:T(1024)S(1)}, f32[768]{0:T(1024)S(1)}, /*index=5*/f32[30...) all-reduce(f32[768]{0:T(1024)S(1)} %add.443, ...), channel_id=11, replica_groups=mesh['dp'=8,'seq'=4] {'dp','seq'}, use_global_device_ids=true, to_apply=%region_32.33.clone | all-reduce | flops 9216 | bytes 73728
  1059.9 104.5 %reduce-scatter.31.cloned.1.call-done = f32[24,768]{1,0:T(8,128)} async-done(((f32[768,768]{1,0:T(8,128)}), f32[24,768]{1,0:T(8,128)}) %reduce-scatter.31.cloned.1.call-update) | async-done | bytes 73744
  1164.4 103.9 %reduce-scatter.35.cloned.1.call-done = f32[24,768]{1,0:T(8,128)} async-done(((f32[768,768]{1,0:T(8,128)}), f32[24,768]{1,0:T(8,128)}) %reduce-scatter.35.cloned.1.call-update) | async-done | bytes 73744
  1268.3 104.6 %reduce-scatter.33.cloned.1.call-done = f32[24,768]{1,0:T(8,128)} async-done(((f32[768,768]{1,0:T(8,128)}), f32[24,768]{1,0:T(8,128)}) %reduce-scatter.33.cloned.1.call-update) | async-done | bytes 73744
  1372.9 141.2 %reduce-scatter.27.cloned.1.call-done = f32[24,3072]{1,0:T(8,128)} async-done(((f32[768,3072]{1,0:T(8,128)}), f32[24,3072]{1,0:T(8,128)}) %reduce-scatter.27.cloned.1.call-update) | async-done | bytes 294928 | tf_op jit(solution)/shard_map/reduce_scatter | solution.py:327
  1514.1 141.8 %reduce-scatter.29.cloned.1.call-done = f32[96,768]{1,0:T(8,128)} async-done(((f32[3072,768]{1,0:T(8,128)}), f32[96,768]{1,0:T(8,128)}) %reduce-scatter.29.cloned.1.call-update) | async-done | bytes 294928 | tf_op jit(solution)/shard_map/reduce_scatter | solution.py:329
  (411 shorter events, 349.1 us)
Async XLA Ops:
  7.3 60.5 %all-gather.19.cloned.1.call-start = ((), (), s32[]{:S(2)}) async-start(), calls=%async_computation.12 | async-start | bytes 1216512 | tf_op jit(solution)/shard_map/all_gather | solution.py:272
  8.0 115.6 %all-gather.15.cloned.1.call-start = ((), (), s32[]{:S(2)}) async-start(), calls=%async_computation.10 | async-start | bytes 1216512 | tf_op jit(solution)/shard_map/all_gather | solution.py:273
  8.8 282.4 %all-gather.17.cloned.1.call-start = ((), (), s32[]{:S(2)}) async-start(), calls=%async_computation.11 | async-start | bytes 1216512 | tf_op jit(solution)/shard_map/all_gather | solution.py:270
  9.5 288.2 %all-gather.33.cloned.1.call-start = ((), (), s32[]{:S(2)}) async-start(), calls=%async_computation.26 | async-start | bytes 3932160 | tf_op jit(solution)/shard_map/all_gather | solution.py:127
  71.0 274.3 %all-gather.31.cloned.1.call-start = ((), (), s32[]{:S(2)}) async-start(), calls=%async_computation.25 | async-start | bytes 3932160 | tf_op jit(solution)/shard_map/all_gather | solution.py:128
  126.6 242.6 %all-gather.21.cloned.1.call-start = ((), (), s32[]{:S(2)}) async-start(), calls=%async_computation.13 | async-start | bytes 1216512 | tf_op jit(solution)/shard_map/all_gather | solution.py:275
  127.2 300.5 %all-gather.29.cloned.1.call-start = ((), (), s32[]{:S(2)}) async-start(), calls=%async_computation.24 | async-start | bytes 3932160 | tf_op jit(solution)/shard_map/all_gather | solution.py:127
  130.2 361.3 %all-gather.27.cloned.1.call-start = ((), (), s32[]{:S(2)}) async-start(), calls=%async_computation.23 | async-start | bytes 3932160 | tf_op jit(solution)/shard_map/all_gather | solution.py:128
  131.9 424.6 %all-gather.23.cloned.1.call-start = ((), (), s32[]{:S(2)}) async-start(), calls=%async_computation.14 | async-start | bytes 4866048 | tf_op jit(solution)/shard_map/all_gather | solution.py:279
  132.7 488.9 %all-gather.25.cloned.1.call-start = ((), (), s32[]{:S(2)}) async-start(), calls=%async_computation.15 | async-start | bytes 4866048 | tf_op jit(solution)/shard_map/all_gather | solution.py:281
  133.3 807.0 %reduce-scatter.19.cloned.1.call-start = ((), (), s32[]{:S(2)}) async-start(), calls=%async_computation.17 | async-start | bytes 3932160 | tf_op jit(solution)/shard_map/reduce_scatter | solution.py:213
  371.8 291.1 %copy-start.56 = (f32[512]{0:T(512)}, f32[512]{0:T(512)S(1)}, u32[]{:S(2)}) copy-start(f32[512]{0:T(512)S(1)} %broadcast_multiply_fusion.1) | copy-start | bytes 6148
  373.8 289.1 %copy-start.59 = (f32[512]{0:T(512)}, f32[512]{0:T(512)S(1)}, u32[]{:S(2)}) copy-start(f32[512]{0:T(512)S(1)} %fusion.102) | copy-start | bytes 6148
  515.9 147.0 %copy-start.62 = (f32[512]{0:T(512)}, f32[512]{0:T(512)S(1)}, u32[]{:S(2)}) copy-start(f32[512]{0:T(512)S(1)} %broadcast_multiply_fusion.3) | copy-start | bytes 6148
  516.3 146.7 %copy-start.82 = (f32[512]{0:T(512)}, f32[512]{0:T(512)S(1)}, u32[]{:S(2)}) copy-start(f32[512]{0:T(512)S(1)} %fusion.100) | copy-start | bytes 6148
  689.9 253.7 %reduce-scatter.23.cloned.1.call-start = ((), (), s32[]{:S(2)}) async-start(), calls=%async_computation.19 | async-start | bytes 3932160 | tf_op jit(solution)/shard_map/reduce_scatter | solution.py:213
  715.8 235.0 %reduce-scatter.17.cloned.1.call-start = ((), (), s32[]{:S(2)}) async-start(), calls=%async_computation.16 | async-start | bytes 3932160 | tf_op jit(solution)/shard_map/reduce_scatter | solution.py:210
  806.1 149.0 %reduce-scatter.21.cloned.1.call-start = ((), (), s32[]{:S(2)}) async-start(), calls=%async_computation.18 | async-start | bytes 3932160 | tf_op jit(solution)/shard_map/reduce_scatter | solution.py:210
  895.6 164.3 %reduce-scatter.25.cloned.1.call-start = ((), (), s32[]{:S(2)}) async-start(), calls=%async_computation.20 | async-start | bytes 2433024 | tf_op jit(solution)/shard_map/reduce_scatter | solution.py:323
  901.5 262.9 %reduce-scatter.31.cloned.1.call-start = ((), (), s32[]{:S(2)}) async-start(), calls=%async_computation.27 | async-start | bytes 2433024
  940.2 328.1 %reduce-scatter.35.cloned.1.call-start = ((), (), s32[]{:S(2)}) async-start(), calls=%async_computation.29 | async-start | bytes 2433024
  950.8 422.1 %reduce-scatter.33.cloned.1.call-start = ((), (), s32[]{:S(2)}) async-start(), calls=%async_computation.28 | async-start | bytes 2433024
  962.4 551.7 %reduce-scatter.27.cloned.1.call-start = ((), (), s32[]{:S(2)}) async-start(), calls=%async_computation.21 | async-start | bytes 9732096 | tf_op jit(solution)/shard_map/reduce_scatter | solution.py:327
  973.6 682.3 %reduce-scatter.29.cloned.1.call-start = ((), (), s32[]{:S(2)}) async-start(), calls=%async_computation.22 | async-start | bytes 9732096 | tf_op jit(solution)/shard_map/reduce_scatter | solution.py:329
  (105 other events, 1602.4 us)
Sparse Core Ops, SparseCore 0:
  10.9 56.7 all-gather.18
  70.6 53.0 all-gather.14
  126.4 53.0 all-gather.16
  181.5 62.4 all-gather.32
  246.0 62.1 all-gather.30
  310.8 52.8 all-gather.20
  365.3 62.3 all-gather.28
  429.2 62.1 all-gather.26
  494.3 62.1 all-gather.22
  559.1 62.3 all-gather.24
  690.0 59.0 reduce-scatter.18
  751.3 60.2 reduce-scatter.22
  813.9 60.2 reduce-scatter.16
  895.7 59.2 reduce-scatter.20
  960.8 99.0 reduce-scatter.24
  1066.5 97.9 reduce-scatter.30
  1170.1 98.1 reduce-scatter.34
  1274.9 97.9 reduce-scatter.32
  1379.3 134.6 reduce-scatter.26
  1521.4 134.4 reduce-scatter.28
where the time goes:
time: 1670 us; the launch traced here: 1660 us
  waiting for transfers between devices  818 us (49%)
  matrix products  402 us (24%)
  local copies, waits for them, and re-layouts  204 us (12%)
  other arithmetic  141 us (8%)
  blocking collectives  81.4 us (5%)
    unnamed x23, waiting for transfers between devices  317 us
    broadcast_in_dim x5, local copies, waits for them, and re-layouts, masked_scores(): scores = jnp.where(allowed[:, :, None, :, None], scores, NEG)  154 us
    reduce_scatter x1, waiting for transfers between devices, shards(): lax.psum_scatter(totals[11], ('dp', 'seq'), scatter_dimension=0, tiled=True)  142 us
    reduce_scatter x1, waiting for transfers between devices, shards(): lax.psum_scatter(totals[9], ('dp', 'seq'), scatter_dimension=0, tiled=True)  141 us
    convert_element_type x2, other arithmetic, attend_back(): grad_scores = (prob * (grad_prob - inner)).astype(jnp.bfloat16)  82.2 us
    unnamed x2, blocking collectives  81.4 us
    dot_general x12, matrix products, project(): jnp.einsum('std,de->ste', rows_in, weight, preferred_element_type=jnp.flo...  67 us
    dot_general x2, matrix products, attend_back(): jnp.einsum('qhe,khe->hqk', grad_heads, v_heads, preferred_element_type=jn...  65 us
  transfers between devices with their start and end apart: 20, of which 13 were waited for; matrix products, arithmetic and copies ran while one was open for 40% of the time, Pallas kernels for 0%

commit v1 on v0

v1 whole, which is shorter than its diff:
```python
from functools import partial

import jax
import jax.numpy as jnp
from jax import lax
from jax.experimental import pallas as pl
from jax.experimental.pallas import tpu as pltpu
from jax.sharding import PartitionSpec as P

HEADS = 12
HEAD = 64
BLOCK = 64
SLOTS = 8
EPS = 1e-06
NEG = -1e30
LOW = jnp.bfloat16
WIDE = jnp.float32

NT = (((1,), (1,)), ((), ()))
TN = (((0,), (0,)), ((), ()))
NN = (((1,), (0,)), ((), ()))


def dot(left, right, dims):
    return lax.dot_general(left, right, dims, preferred_element_type=WIDE)


def swap(array):
    size = lax.axis_size("dp")
    return lax.ppermute(array, "dp", [(i, i ^ 1) for i in range(size)])


def flip_chip(array, bit):
    size = lax.axis_size("dp")
    return lax.ppermute(array, "dp", [(i, i ^ (2 << bit)) for i in range(size)])


def flip_seq(array, k):
    size = lax.axis_size("seq")
    return lax.ppermute(array, "seq", [(i, i ^ k) for i in range(size)])


def rounds():
    dp, seq = lax.axis_size("dp"), lax.axis_size("seq")
    for a in range(2):
        for b in range(2):
            pairs = []
            for d in range(dp):
                for z in range(seq):
                    to_dp = (d & ~1) | (b ^ (z >> 1))
                    to_seq = 2 * (d & 1) + (a ^ (z & 1))
                    pairs.append((d * seq + z, to_dp * seq + to_seq))
            yield a, b, pairs


def bring(piece_of):
    z = lax.axis_index("seq")
    got = []
    for a, b, pairs in rounds():
        piece = piece_of(a ^ (z & 1), b ^ (z >> 1))
        got.append(lax.ppermute(piece, ("dp", "seq"), pairs))
    return got


def send_back(pieces):
    z = lax.axis_index("seq")
    got = []
    for at, (a, b, pairs) in enumerate(rounds()):
        got.append(lax.ppermute(pieces[at], ("dp", "seq"), [(t, s) for s, t in pairs]))
    odd, high = (z & 1) == 1, (z >> 1) == 1
    parts = []
    for s in range(2):
        for half in range(2):
            near = jnp.where(odd, got[2 * (1 - s) + half], got[2 * s + half])
            far = jnp.where(odd, got[2 * (1 - s) + 1 - half], got[2 * s + 1 - half])
            parts.append(jnp.where(high, far, near))
    return jnp.stack([jnp.concatenate(parts[:2], 0), jnp.concatenate(parts[2:], 0)])


def pick(array, index, axis):
    return lax.dynamic_slice_in_dim(array, index, 1, axis)


def gather_chips(shard):
    z = lax.axis_index("seq")
    chip = lax.axis_index("dp") >> 1
    pieces = [shard] + [flip_seq(shard, k) for k in range(1, lax.axis_size("seq"))]
    for bit in range(2):
        set_bit = ((z >> bit) & 1) == 1
        pieces = [
            jnp.where(set_bit, pieces[i ^ (1 << bit)], pieces[i]) for i in range(len(pieces))
        ]
    whole = jnp.stack(pieces, 1)[None]
    size = lax.axis_size("dp") // 2
    bit = 0
    while (1 << bit) < size:
        other = flip_chip(whole, bit)
        set_bit = ((chip >> bit) & 1) == 1
        whole = jnp.concatenate(
            [jnp.where(set_bit, other, whole), jnp.where(set_bit, whole, other)], 0
        )
        bit += 1
    return whole


def reduce_chips(parts, first):
    chip = lax.axis_index("dp") >> 1
    z = lax.axis_index("seq")
    size = parts.shape[0]
    count = size.bit_length() - 1
    tail = parts.shape[1:]
    parts = parts.reshape((2,) * count + tail)
    order = list(range(count))
    if first and count > 1:
        order = order[1:] + order[:1]
    for bit in order:
        axis = count - 1 - bit
        mine = (chip >> bit) & 1
        other = flip_chip(pick(parts, 1 - mine, axis), bit)
        parts = (pick(parts, mine, axis).astype(WIDE) + other.astype(WIDE)).astype(LOW)
    parts = parts.reshape(tail)
    total = pick(parts, z, 1).astype(WIDE)
    for k in range(1, tail[1]):
        total = total + flip_seq(pick(parts, z ^ k, 1), k).astype(WIDE)
    return total[:, 0]


def reduce_all(parts, first):
    core = lax.axis_index("dp") & 1
    other = swap(pick(parts, 1 - core, 1))
    parts = (pick(parts, core, 1).astype(WIDE) + other.astype(WIDE)).astype(LOW)
    return reduce_chips(parts, first)[0]


def block_rows(ref, block, lanes):
    return ref[pl.ds(pl.multiple_of(block * BLOCK, BLOCK), BLOCK), lanes]


def diagonal(pair_rows, low):
    zero = jnp.zeros_like(pair_rows)
    return jnp.concatenate(
        [jnp.where(low, pair_rows, zero), jnp.where(low, zero, pair_rows)], axis=0
    )


def gather_blocks(ref, ids, lanes, low):
    parts = []
    for one, two in ids:
        if two is None:
            parts.append(block_rows(ref, one, lanes))
        else:
            parts.append(
                jnp.where(low, block_rows(ref, one, lanes), block_rows(ref, two, lanes))
            )
    return jnp.concatenate(parts, axis=0)


def slot_ids(near_ref, rand_ref, globs, i, pair, blocks):
    ids = [(near_ref[i], None), (i, None), (near_ref[blocks + i], None)]
    ids += [(globs[0], None), (globs[1], None)]
    for r in range(3):
        ids.append(
            (
                rand_ref[((2 * pair) * blocks + i) * 3 + r],
                rand_ref[((2 * pair + 1) * blocks + i) * 3 + r],
            )
        )
    return ids


def lanes_of(part, pair, pairs):
    first = 128 * (part * pairs + pair)
    return slice(first, first + 128)


def attend_kernel(pairs, blocks, step, near_ref, rand_ref, glob_ref, bias_ref, qkv_ref, out_ref, log_ref):
    low = lax.broadcasted_iota(jnp.int32, (1, 2 * HEAD), 1) < HEAD
    globs = (glob_ref[0], glob_ref[1])

    def scores_of(i, pair):
        ids = slot_ids(near_ref, rand_ref, globs, i, pair, blocks)
        queries = diagonal(block_rows(qkv_ref, i, lanes_of(0, pair, pairs)), low)
        return dot(gather_blocks(qkv_ref, ids, lanes_of(1, pair, pairs), low), queries, NT)

    def softmax_of(i, pair, scores):
        highest = jnp.max(scores, axis=0, keepdims=True)
        weights = jnp.exp(scores - highest)
        total = jnp.sum(weights, axis=0, keepdims=True)
        log_ref[i, pair : pair + 1] = highest + jnp.log(total)
        return (weights * (1.0 / total)).astype(LOW)

    def put(i, pair, mixed):
        at = pl.ds(pl.multiple_of(i * BLOCK, BLOCK), BLOCK)
        out_ref[at, lanes_of(0, pair, pairs)] = jnp.where(
            low, mixed[:BLOCK], mixed[BLOCK:]
        ).astype(LOW)

    def body(at, carry):
        units = [(at * step + d, pair) for d in range(step) for pair in range(pairs)]
        scores = [scores_of(*unit) for unit in units]
        probs = []
        for (i, pair), score in zip(units, scores):
            bias = bias_ref[i, pair]
            score = jnp.concatenate(
                [score[BLOCK * j : BLOCK * j + BLOCK] + bias[j : j + 1] for j in range(SLOTS)],
                axis=0,
            )
            probs.append(softmax_of(i, pair, score))
        for (i, pair), prob in zip(units, probs):
            ids = slot_ids(near_ref, rand_ref, globs, i, pair, blocks)
            values = gather_blocks(qkv_ref, ids, lanes_of(2, pair, pairs), low)
            put(i, pair, dot(prob, values, TN))
        return carry

    lax.fori_loop(0, blocks // step, body, 0)

    def whole_row(n, carry):
        i = glob_ref[n]
        scores = []
        for pair in range(pairs):
            queries = diagonal(block_rows(qkv_ref, i, lanes_of(0, pair, pairs)), low)
            scores.append(dot(qkv_ref[:, lanes_of(1, pair, pairs)], queries, NT))
        probs = [softmax_of(i, pair, scores[pair]) for pair in range(pairs)]
        for pair in range(pairs):
            put(i, pair, dot(probs[pair], qkv_ref[:, lanes_of(2, pair, pairs)], TN))
        return carry

    lax.fori_loop(0, 2, whole_row, 0)


def attend_back_kernel(
    pairs, blocks, step, near_ref, rand_ref, glob_ref, bias_ref, log_ref, qkv_ref, grad_ref, out_ref, acc_ref
):
    low = lax.broadcasted_iota(jnp.int32, (1, 2 * HEAD), 1) < HEAD
    globs = (glob_ref[0], glob_ref[1])
    acc_ref[...] = jnp.zeros_like(acc_ref)

    def add(part, pair, block, value):
        at = pl.ds(pl.multiple_of(block * BLOCK, BLOCK), BLOCK)
        lanes = lanes_of(part, pair, pairs)
        acc_ref[at, lanes] = acc_ref[at, lanes] + value

    def operands(i, pair):
        queries = diagonal(block_rows(qkv_ref, i, lanes_of(0, pair, pairs)), low)
        grads = diagonal(block_rows(grad_ref, i, lanes_of(0, pair, pairs)), low)
        return queries, grads

    def softmax_back(prob, grad_prob):
        scaled = prob * grad_prob
        inner = jnp.sum(scaled, axis=0, keepdims=True)
        return prob.astype(LOW), (scaled - prob * inner).astype(LOW)

    def put(i, pair, mixed):
        at = pl.ds(pl.multiple_of(i * BLOCK, BLOCK), BLOCK)
        out_ref[at, lanes_of(0, pair, pairs)] = (
            jnp.where(low, mixed[:BLOCK], mixed[BLOCK:]) * HEAD ** (-0.5)
        ).astype(LOW)

    def body(at, carry):
        units = [(at * step + d, pair) for d in range(step) for pair in range(pairs)]
        first = []
        for i, pair in units:
            ids = slot_ids(near_ref, rand_ref, globs, i, pair, blocks)
            queries, grads = operands(i, pair)
            first.append(
                (
                    dot(gather_blocks(qkv_ref, ids, lanes_of(1, pair, pairs), low), queries, NT),
                    dot(gather_blocks(qkv_ref, ids, lanes_of(2, pair, pairs), low), grads, NT),
                )
            )
        second = []
        for (i, pair), (score, grad_prob) in zip(units, first):
            shift = bias_ref[i, pair] - log_ref[i, pair : pair + 1]
            prob = jnp.concatenate(
                [
                    jnp.exp(score[BLOCK * j : BLOCK * j + BLOCK] + shift[j : j + 1])
                    for j in range(SLOTS)
                ],
                axis=0,
            )
            second.append(softmax_back(prob, grad_prob))
        third = []
        for (i, pair), (prob, grad_score) in zip(units, second):
            ids = slot_ids(near_ref, rand_ref, globs, i, pair, blocks)
            queries, grads = operands(i, pair)
            keys = gather_blocks(qkv_ref, ids, lanes_of(1, pair, pairs), low)
            put(i, pair, dot(grad_score, keys, TN))
            third.append((dot(grad_score, queries, NN), dot(prob, grads, NN)))
        for (i, pair), values in zip(units, third):
            ids = slot_ids(near_ref, rand_ref, globs, i, pair, blocks)
            for j, (one, two) in enumerate(ids):
                for part, value in enumerate(values):
                    value = value[BLOCK * j : BLOCK * j + BLOCK]
                    if two is None:
                        add(part, pair, one, value)
                    else:
                        add(part, pair, one, jnp.where(low, value, 0.0))
                        add(part, pair, two, jnp.where(low, 0.0, value))
        return carry

    lax.fori_loop(0, blocks // step, body, 0)

    def whole_row(n, carry):
        i = glob_ref[n]
        first = []
        for pair in range(pairs):
            queries, grads = operands(i, pair)
            first.append(
                (
                    dot(qkv_ref[:, lanes_of(1, pair, pairs)], queries, NT),
                    dot(qkv_ref[:, lanes_of(2, pair, pairs)], grads, NT),
                )
            )
        second = []
        for pair, (score, grad_prob) in enumerate(first):
            prob = jnp.exp(score - log_ref[i, pair : pair + 1])
            second.append(softmax_back(prob, grad_prob))
        for pair, (prob, grad_score) in enumerate(second):
            queries, grads = operands(i, pair)
            acc_ref[:, lanes_of(0, pair, pairs)] += dot(grad_score, queries, NN)
            acc_ref[:, lanes_of(1, pair, pairs)] += dot(prob, grads, NN)
            put(i, pair, dot(grad_score, qkv_ref[:, lanes_of(1, pair, pairs)], TN))
        return carry

    lax.fori_loop(0, jnp.where(globs[0] == globs[1], 1, 2), whole_row, 0)
    out_ref[:, 128 * pairs :] = acc_ref[...].astype(LOW)


IN_SMEM = pl.BlockSpec(memory_space=pltpu.SMEM)
IN_VMEM = pl.BlockSpec(memory_space=pltpu.VMEM)


def attend(near, rand, globs, bias, qkv):
    length, width = qkv.shape
    pairs, blocks = width // 384, length // BLOCK
    return pl.pallas_call(
        partial(attend_kernel, pairs, blocks, 4),
        out_shape=(
            jax.ShapeDtypeStruct((length, width // 3), LOW),
            jax.ShapeDtypeStruct((blocks, 8, 128), WIDE),
        ),
        in_specs=[IN_SMEM, IN_SMEM, IN_SMEM, IN_VMEM, IN_VMEM],
        out_specs=(IN_VMEM, IN_VMEM),
        compiler_params=pltpu.CompilerParams(vmem_limit_bytes=48 << 20),
        cost_estimate=pl.CostEstimate(
            flops=20_000_000_000, bytes_accessed=8_000_000, transcendentals=0
        ),
        name="attend",
    )(near, rand, globs, bias, qkv)


def attend_back(near, rand, globs, bias, log_total, qkv, grads):
    length, width = qkv.shape
    pairs, blocks = width // 384, length // BLOCK
    return pl.pallas_call(
        partial(attend_back_kernel, pairs, blocks, 2),
        out_shape=jax.ShapeDtypeStruct((length, width), LOW),
        in_specs=[IN_SMEM, IN_SMEM, IN_SMEM, IN_VMEM, IN_VMEM, IN_VMEM, IN_VMEM],
        out_specs=IN_VMEM,
        scratch_shapes=[pltpu.VMEM((length, 2 * width // 3), WIDE)],
        compiler_params=pltpu.CompilerParams(vmem_limit_bytes=52 << 20),
        cost_estimate=pl.CostEstimate(
            flops=36_000_000_000, bytes_accessed=16_000_000, transcendentals=0
        ),
        name="attend_back",
    )(near, rand, globs, bias, log_total, qkv, grads)


def place_of(block, core, z, blocks):
    quarter, inner = block // (blocks // 4), block % (blocks // 4)
    size = blocks // 8
    half, row = inner // size, inner % size
    a = (quarter & 1) ^ (z & 1)
    b = (quarter >> 1) ^ half
    return (half ^ core) * (blocks // 2) + (2 * a + b) * size + row


def block_at(place, core, z, blocks):
    size = blocks // 8
    half = (place // (blocks // 2)) ^ core
    turn, row = (place % (blocks // 2)) // size, place % size
    quarter = 2 * ((turn & 1) ^ half) + ((turn >> 1) ^ (z & 1))
    return quarter * (blocks // 4) + half * size + row


def tables(rand, globs, blocks):
    core = lax.axis_index("dp") & 1
    z = lax.axis_index("seq")
    here = block_at(jnp.arange(blocks, dtype=jnp.int32), core, z, blocks)
    heads = rand.shape[0]
    one, two = globs[0], globs[1]

    def near(block):
        return jnp.abs(block - here) <= 1

    every = jnp.ones((heads, blocks), bool)
    ok = [every & (here > 0), every, every & (here < blocks - 1)]
    ok += [every & ~near(one), every & ~near(two) & (one != two)]
    seen = []
    for r in range(3):
        block = rand[:, :, r]
        good = ~near(block) & (block != one) & (block != two)
        for before in seen:
            good = good & (block != before)
        seen.append(block)
        ok.append(good)
    whole_row = (here == one) | (here == two)
    ok = jnp.stack(ok, -1) & ~whole_row[None, :, None]
    bias = jnp.where(ok, 0.0, NEG).astype(WIDE)
    bias = bias.reshape(heads // 2, 2, blocks, SLOTS).transpose(2, 0, 3, 1)
    bias = jnp.repeat(bias, HEAD, axis=3)
    put = partial(place_of, core=core, z=z, blocks=blocks)
    sides = jnp.concatenate([put(jnp.maximum(here - 1, 0)), put(jnp.minimum(here + 1, blocks - 1))])
    return sides, put(rand).reshape(-1), put(globs), bias


def norm_parts(summed):
    center = summed - jnp.mean(summed, -1, keepdims=True)
    spread = jnp.mean(center * center, -1, keepdims=True)
    scale = lax.rsqrt(spread + EPS)
    return center * scale, scale


def norm_back(grad, unit, scale, gain):
    grad_unit = grad * gain
    mean_one = jnp.mean(grad_unit, -1, keepdims=True)
    mean_two = jnp.mean(grad_unit * unit, -1, keepdims=True)
    return (
        scale * (grad_unit - mean_one - unit * mean_two),
        jnp.sum(grad * unit, 0),
        jnp.sum(grad, 0),
    )


def gelu_parts(x):
    size = jnp.abs(x)
    t = 1.0 / (1.0 + (0.3275911 * 0.5**0.5) * size)
    bell = jnp.exp(-0.5 * x * x)
    series = 1.061405429
    for factor in (-1.453152027, 1.421413741, -0.284496736, 0.254829592):
        series = series * t + factor
    tail = 0.5 * series * t * bell
    share = jnp.where(x >= 0, 1.0 - tail, tail)
    return x * share, share + x * bell * 0.3989422804014327


def shards(
    inputs,
    cotangent,
    rand_blocks,
    global_blocks,
    w_query,
    b_query,
    w_key,
    w_value,
    b_value,
    w_out,
    b_out,
    gain_one,
    shift_one,
    w_up,
    b_up,
    w_down,
    b_down,
    gain_two,
    shift_two,
):
    n_dp, n_seq = lax.axis_size("dp"), lax.axis_size("seq")
    chips, devices = n_dp // 2, n_dp * n_seq
    core = lax.axis_index("dp") & 1
    z = lax.axis_index("seq")
    rows_in = w_query.shape[0]
    rows_ff = w_down.shape[0]
    width = w_query.shape[1]
    wide = w_up.shape[1]
    half_width = width // 2
    _, quarter, _ = inputs.shape
    part = quarter // 2
    length = quarter * n_seq
    blocks = length // BLOCK
    own = length // 2
    own_heads = HEADS // 2

    def piece_of(s, half):
        tokens = lax.dynamic_slice(inputs, (s, half * part, 0), (1, part, width))[0]
        numbers = lax.dynamic_slice(
            rand_blocks, (s, half * own_heads, 0, 0), (1, own_heads) + rand_blocks.shape[2:]
        ).reshape(-1)
        globs = pick(global_blocks, s, 0).reshape(-1)
        numbers = jnp.concatenate([numbers, globs]).astype(LOW)
        numbers = jnp.pad(numbers, (0, 16 * width - numbers.shape[0])).reshape(16, width)
        return jnp.concatenate([tokens, numbers], 0)

    pieces = bring(piece_of)
    tokens_own = jnp.concatenate([p[:part] for p in pieces], 0)
    local_blocks = rand_blocks.shape[2]
    count = own_heads * local_blocks * 3
    rand_parts = [
        p[part, :count].astype(jnp.int32).reshape(own_heads, local_blocks, 3) for p in pieces
    ]
    globs = pieces[0][part, count : count + 2].astype(jnp.int32)
    size = local_blocks // 2
    rand_rows = []
    for side in range(2):
        for turn in range(4):
            numbers = rand_parts[turn ^ side]
            rand_rows.append(lax.dynamic_slice_in_dim(numbers, (core ^ side) * size, size, 1))
    near, rand, glob_at, bias = tables(jnp.concatenate(rand_rows, 1), globs, blocks)

    def halves(at):
        return jnp.concatenate(
            [
                lax.dynamic_slice_in_dim(w, at * half_width, half_width, 1)
                for w in (w_query, w_key, w_value)
            ],
            1,
        )

    def small_rows(*vectors):
        lines = [jnp.pad(v, (0, 3 * half_width - v.shape[0]))[None] for v in vectors]
        return jnp.pad(jnp.concatenate(lines, 0), ((0, 8 - len(lines)), (0, 0)))

    biases = small_rows(b_query, b_value)
    keep = jnp.concatenate([halves(core), biases], 0)
    come = swap(jnp.concatenate([halves(1 - core), biases], 0))
    shard = jnp.stack([jnp.where(core == 0, keep, come), jnp.where(core == 0, come, keep)])
    qkv_all = gather_chips(shard)
    w_qkv = qkv_all[:, :, :, :rows_in].reshape(width, 3 * half_width)

    def own_half(line):
        vector = qkv_all[:, :, :, rows_in + line, :rows_in].reshape(width)
        return lax.dynamic_slice_in_dim(vector, core * half_width, half_width, 0)

    b_qkv = jnp.concatenate(
        [own_half(0), jnp.zeros((half_width,), LOW), own_half(1)]
    ).astype(WIDE)

    vectors = jnp.concatenate([b_out, gain_one, shift_one, b_down, gain_two, shift_two, b_up])
    vector_rows = 8
    vectors = jnp.pad(vectors, (0, vector_rows * width - vectors.shape[0])).reshape(vector_rows, width)
    up_rows = rows_in * wide // width
    packed = jnp.concatenate([w_out, vectors, w_up.reshape(up_rows, width), w_down], 0)
    packed = lax.all_gather(packed, ("dp", "seq"), axis=0, tiled=False)
    w_out_all = packed[:, :rows_in].reshape(width, width)
    vectors = packed[:, rows_in : rows_in + vector_rows].reshape(devices, -1).astype(WIDE)
    at = rows_in + vector_rows
    w_up_all = packed[:, at : at + up_rows].reshape(width, wide)
    w_down_all = packed[:, at + up_rows :].reshape(wide, width)
    b_out_all, gain_one_all, shift_one_all, b_down_all, gain_two_all, shift_two_all = (
        vectors[:, k * rows_in : (k + 1) * rows_in].reshape(width) for k in range(6)
    )
    b_up_all = vectors[:, 6 * rows_in : 6 * rows_in + rows_ff].reshape(wide)

    tokens = jnp.concatenate([tokens_own, swap(tokens_own)], 0)
    scale = jnp.concatenate(
        [jnp.full((half_width,), HEAD ** (-0.5)), jnp.ones((2 * half_width,))]
    ).astype(LOW)
    qkv = (dot(tokens, w_qkv, NN) + b_qkv).astype(LOW) * scale
    mixed, log_total = attend(near, rand, glob_at, bias, qkv)
    other = swap(mixed[own:])
    attended = jnp.where(
        core == 0,
        jnp.concatenate([mixed[:own], other], 1),
        jnp.concatenate([other, mixed[:own]], 1),
    )
    first_sum = tokens_own.astype(WIDE) + (dot(attended, w_out_all, NN) + b_out_all)
    unit_one, scale_one = norm_parts(first_sum)
    normed = unit_one * gain_one_all + shift_one_all
    normed_low = normed.astype(LOW)
    hidden_pre = dot(normed_low, w_up_all, NN) + b_up_all
    hidden, slope = gelu_parts(hidden_pre)
    hidden, slope = hidden.astype(LOW), slope.astype(LOW)
    second_sum = normed + (dot(hidden, w_down_all, NN) + b_down_all)
    unit_two, scale_two = norm_parts(second_sum)
    result = (unit_two * gain_two_all + shift_two_all).astype(LOW)
    output = send_back(list(jnp.split(result, 4, 0)))

    def cotangent_piece(s, half):
        return lax.dynamic_slice(cotangent, (s, half * part, 0), (1, part, width))[0]

    grad_result = jnp.concatenate(bring(cotangent_piece), 0).astype(WIDE)
    grad_second, grad_gain_two, grad_shift_two = norm_back(
        grad_result, unit_two, scale_two, gain_two_all
    )
    grad_down = grad_second.astype(LOW)
    grad_b_down = jnp.sum(grad_down.astype(WIDE), 0)
    grad_w_down = dot(hidden, grad_down, TN).astype(LOW)
    own_down = reduce_all(grad_w_down.reshape(chips, 2, n_seq, rows_ff, width), 0)
    grad_pre = (dot(grad_down, w_down_all, NT) * slope.astype(WIDE)).astype(LOW)
    grad_b_up = jnp.sum(grad_pre.astype(WIDE), 0)
    grad_w_up = dot(normed_low, grad_pre, TN).astype(LOW)
    own_up = reduce_all(grad_w_up.reshape(chips, 2, n_seq, rows_in, wide), 1)
    grad_normed = grad_second + dot(grad_pre, w_up_all, NT)
    grad_first, grad_gain_one, grad_shift_one = norm_back(
        grad_normed, unit_one, scale_one, gain_one_all
    )
    grad_branch = grad_first.astype(LOW)
    grad_b_out = jnp.sum(grad_branch.astype(WIDE), 0)
    grad_w_out = dot(attended, grad_branch, TN).astype(LOW)
    grad_vectors = [
        v.reshape(devices, rows_in)
        for v in (grad_b_out, grad_gain_one, grad_shift_one, grad_b_down, grad_gain_two, grad_shift_two)
    ]
    grad_vectors = jnp.concatenate(grad_vectors + [grad_b_up.reshape(devices, rows_ff)], 1)
    grad_vectors = jnp.pad(
        grad_vectors, ((0, 0), (0, vector_rows * width - grad_vectors.shape[1]))
    ).reshape(devices, vector_rows, width)
    out_parts = jnp.concatenate(
        [grad_w_out.reshape(devices, rows_in, width), grad_vectors.astype(LOW)], 1
    )
    own_out = reduce_all(out_parts.reshape(chips, 2, n_seq, rows_in + vector_rows, width), 0)
    grad_attended = dot(grad_branch, w_out_all, NT).astype(LOW)
    mine = lax.dynamic_slice_in_dim(grad_attended, core * half_width, half_width, 1)
    theirs = lax.dynamic_slice_in_dim(grad_attended, (1 - core) * half_width, half_width, 1)
    grad_mixed = jnp.concatenate([mine, swap(theirs)], 0)
    grad_qkv = attend_back(near, rand, glob_at, bias, log_total, qkv, grad_mixed)

    grad_rows = dot(grad_qkv, w_qkv, NT)
    come = swap(grad_rows[own:].astype(LOW))
    grad_tokens = (grad_first + grad_rows[:own] + come.astype(WIDE)).astype(LOW)
    grad_inputs = send_back(list(jnp.split(grad_tokens, 4, 0)))

    grad_w_qkv = dot(tokens, grad_qkv, TN).astype(LOW)
    sums = jnp.sum(grad_qkv.astype(WIDE), 0).reshape(3, half_width)
    empty = jnp.zeros((half_width,), WIDE)

    def spread_half(vector):
        vector = jnp.where(
            core == 0, jnp.concatenate([vector, empty]), jnp.concatenate([empty, vector])
        )
        return vector.reshape(devices, 1, rows_in)

    lines = jnp.concatenate([spread_half(sums[0]), spread_half(sums[2])], 1).astype(LOW)
    lines = jnp.pad(lines, ((0, 0), (0, 6), (0, 3 * half_width - rows_in)))
    qkv_parts = jnp.concatenate(
        [grad_w_qkv.reshape(devices, rows_in, 3 * half_width), lines], 1
    ).reshape(chips, 2, n_seq, rows_in + 8, 3 * half_width)
    own_qkv = reduce_chips(qkv_parts, 0)
    come = swap(pick(own_qkv, 1 - core, 0))[0]
    keep = pick(own_qkv, core, 0)[0]
    left, right = jnp.where(core == 0, keep, come), jnp.where(core == 0, come, keep)

    def joined(k):
        lanes = slice(k * half_width, (k + 1) * half_width)
        return jnp.concatenate([left[:rows_in, lanes], right[:rows_in, lanes]], 1)

    both = keep[rows_in : rows_in + 2, :rows_in] + come[rows_in : rows_in + 2, :rows_in]
    small = own_out[rows_in:].reshape(-1)

    def vector_of(k):
        return small[k * rows_in : (k + 1) * rows_in]

    return (
        output,
        grad_inputs,
        joined(0),
        both[0],
        joined(1),
        joined(2),
        both[1],
        own_out[:rows_in],
        vector_of(0),
        vector_of(1),
        vector_of(2),
        own_up,
        small[6 * rows_in : 6 * rows_in + rows_ff],
        own_down,
        vector_of(3),
        vector_of(4),
        vector_of(5),
    )


def solution(mesh):
    both = ("dp", "seq")
    matrix, vector = P(both, None), P(both)
    tokens = P("dp", "seq", None)
    return jax.shard_map(
        shards,
        mesh=mesh,
        in_specs=(tokens, tokens, P("dp", None, "seq", None), P("dp", None))
        + (matrix, vector, matrix, matrix, vector, matrix, vector, vector, vector)
        + (matrix, vector, matrix, vector, vector, vector),
        out_specs=(tokens, tokens)
        + (matrix, vector, matrix, matrix, vector, matrix, vector, vector, vector)
        + (matrix, vector, matrix, vector, vector, vector),
        check_vma=False,
    )
```

time: 1670 us -> 629 us (0.38)
  waiting for transfers between devices: 818 us -> 168 us
  matrix products: 402 us -> 99.6 us
  starting transfers between devices: 1.06 us -> 124 us
  local copies, waits for them, and re-layouts: 204 us -> 88.2 us
  blocking collectives: 81.4 us -> 0 us
  other arithmetic: 141 us -> 67.4 us
  Pallas kernels: 0 us -> 55.8 us
    unnamed x23 -> x1, waiting for transfers between devices: 317 us -> 0.02 us
    dot_general x48 -> x12, matrix products: 402 us -> 99.6 us  [dot(): return lax.dot_general(left, right, dims, preferred_element_type=WIDE)]
    reduce_scatter x7 -> x0, waiting for transfers between devices: 300 us -> none  [the longest x1 142 us: shards(): lax.psum_scatter(totals[11], ('dp', 'seq'), scatter_dimension=0, tiled=True)]
    all_gather x10 -> x1, waiting for transfers between devices: 201 us -> 0.01 us  [shards(): packed = lax.all_gather(packed, ('dp', 'seq'), axis=0, tiled=False)]
    ppermute x0 -> x50, waiting for transfers between devices: none -> 168 us  [the longest x15 63.8 us: flip_seq(): return lax.ppermute(array, 'seq', [(i, i ^ k) for i in range(size)])]
    broadcast_in_dim x5 -> x4, local copies, waits for them, and re-layouts: 154 us -> 1.94 us  [the longest x1 1.92 us: tables(): bias = jnp.repeat(bias, HEAD, axis=3)]
    ppermute x0 -> x50, starting transfers between devices: none -> 124 us  [the longest x9 44 us: swap(): return lax.ppermute(array, 'dp', [(i, i ^ 1) for i in range(size)])]
    unnamed x2 -> x0, blocking collectives: 81.4 us -> none
  transfers between devices with their start and end apart: 20 -> 51, of which waited for: 13 -> 19; matrix products, arithmetic and copies ran while one was open for 40% -> 22% of each run, Pallas kernels for 0% -> 9%
where the time goes in v1:
time: 629 us; the launch traced here: 621 us
  waiting for transfers between devices  168 us (27%)
  starting transfers between devices  124 us (20%)
  matrix products  99.6 us (16%)
  local copies, waits for them, and re-layouts  88.2 us (14%)
  other arithmetic  67.4 us (11%)
  Pallas kernels  55.8 us (9%)
  between operations  17.3 us (3%)
    dot_general x12, matrix products, dot(): return lax.dot_general(left, right, dims, preferred_element_type=WIDE)  99.6 us
    ppermute x15, waiting for transfers between devices, flip_seq(): return lax.ppermute(array, 'seq', [(i, i ^ k) for i in range(size)])  63.8 us
    ppermute x10, waiting for transfers between devices, flip_chip(): return lax.ppermute(array, 'dp', [(i, i ^ 2 << bit) for i in range(size)])  54.1 us
    ppermute x8, waiting for transfers between devices, bring(): got.append(lax.ppermute(piece, ('dp', 'seq'), pairs))  46 us
    ppermute x9, starting transfers between devices, swap(): return lax.ppermute(array, 'dp', [(i, i ^ 1) for i in range(size)])  44 us
    pallas_call x1, Pallas kernels, attend_back(): pl.pallas_call(partial(attend_back_kernel, pairs, blocks, 2), out_shape=j...  36.6 us
    ppermute x15, starting transfers between devices, flip_seq(): return lax.ppermute(array, 'seq', [(i, i ^ k) for i in range(size)])  26.1 us
    ppermute x10, starting transfers between devices, flip_chip(): return lax.ppermute(array, 'dp', [(i, i ^ 2 << bit) for i in range(size)])  24.7 us
  transfers between devices with their start and end apart: 51, of which 19 were waited for; matrix products, arithmetic and copies ran while one was open for 22% of the time, Pallas kernels for 9%

profile of v1, /device:TPU:0, one launch (start us, length us, event | category | flops | bytes accessed | tf_op | source)
XLA Modules:
  0.0 620.7 jit_solution(306246268079041669)
XLA Ops:
  53.0 30.5 %collective-permute-done.7 = bf16[2,32,1152]{2,1,0:T(8,128)(2,1)} collective-permute-done((bf16[2,32,1152]{2,1,0:T(8,128)(2,1)S(1)}, bf16[2,32,1152]{2,1,0:T(8,128)(2,1)}, u32[]{:S(2)}, u32[]{:S(2)}) %collective-permute-start.7) | collective-permute-done | bytes 147488 | tf_op jit(solution)/shard_map/ppermute | solution.py:40
  86.3 11.9 %collective-permute-done.17 = bf16[256,768]{0,1:T(8,128)(2,1)S(1)} collective-permute-done((bf16[256,768]{0,1:T(8,128)(2,1)}, bf16[256,768]{0,1:T(8,128)(2,1)S(1)}, u32[]{:S(2)}, u32[]{:S(2)}) %collective-permute-start.17) | collective-permute-done | bytes 393248 | tf_op jit(solution)/shard_map/ppermute | solution.py:61
  98.1 15.3 %collective-permute-done.18 = bf16[256,768]{0,1:T(8,128)(2,1)S(1)} collective-permute-done((bf16[256,768]{0,1:T(8,128)(2,1)}, bf16[256,768]{0,1:T(8,128)(2,1)S(1)}, u32[]{:S(2)}, u32[]{:S(2)}) %collective-permute-start.18) | collective-permute-done | bytes 393248 | tf_op jit(solution)/shard_map/ppermute | solution.py:61
  113.4 10.3 %collective-permute-start.3 = (bf16[272,768]{1,0:T(8,128)(2,1)}, bf16[272,768]{1,0:T(8,128)(2,1)}, u32[]{:S(2)}, u32[]{:S(2)}) collective-permute-start(bf16[272,768]{1,0:T(8,128)(2,1)} %pad_maximum_fusion.9), channel_id=1, source_target_pairs={{0,5},{1,4},{2,1},{3,0},{4,7},{5,6},{6,3},{7,2},{8,13},{9,12},{10,... | collective-permute-start | bytes 1253384 | tf_op jit(solution)/shard_map/ppermute | solution.py:61
  125.2 9.0 %collective-permute-start.9 = (bf16[1,2,4,32,1152]{4,3,2,1,0:T(8,128)(2,1)}, bf16[1,2,4,32,1152]{4,3,2,1,0:T(8,128)(2,1)}, u32[]{:S(2)}, u32[]{:S(2)}) collective-permute-start(bf16[1,2,4,32,1152]{4,3,2,1,0:T(8,128)(2,1)} %maximum_bitcast_fusion.4), channel_id=1, source_target_pairs={{0,8},{4,12},{8,0},{12,4},{16,24},{20,28},{24,16},{28,20},{1,9},{5... | collective-permute-start | bytes 1769480 | tf_op jit(solution)/shard_map/ppermute | solution.py:35
  136.4 12.3 %collective-permute-done.1 = bf16[272,768]{1,0:T(8,128)(2,1)} collective-permute-done((bf16[272,768]{1,0:T(8,128)(2,1)S(1)}, bf16[272,768]{1,0:T(8,128)(2,1)}, u32[]{:S(2)}, u32[]{:S(2)}) %collective-permute-start.1) | collective-permute-done | bytes 417824 | tf_op jit(solution)/shard_map/ppermute | solution.py:61
  181.3 23.9 %collective-permute-done.10 = bf16[2,2,4,32,1152]{4,3,2,1,0:T(8,128)(2,1)S(1)} collective-permute-done((bf16[2,2,4,32,1152]{4,3,2,1,0:T(8,128)(2,1)S(1)}, bf16[2,2,4,32,1152]{4,3,2,1,0:T(8,128)(2,1)S(1)}, u32[]{:S(2)}, u32[]{:S(2)}) %collective-permute-start.10) | collective-permute-done | bytes 1179680 | tf_op jit(solution)/shard_map/ppermute | solution.py:35
  210.8 6.7 %fusion.6.qkv_ref = bf16[2048,1152]{1,0:T(8,128)(2,1)} fusion(bf16[2048,768]{0,1:T(8,128)(2,1)S(1)} %copy-done.47, bf16[768,1152]{1,0:T(8,128)(2,1)S(1)} %bitcast.200, f32[1152]{0:T(1024)S(1)} %maximum_convert_fusion, bf16[1152]{0:T(1024)(128)(2,1)} %constant.291.clone.1), kind=kOutput, calls=%fused_computation.12 | convolution fusion | flops 3630956544 | bytes 9640704 | tf_op jit(solution)/shard_map/dot_general | solution.py:25
  217.5 19.1 %attend.1 = (bf16[2048,384]{1,0:T(8,128)(2,1)S(1)}, f32[32,8,128]{2,1,0:T(8,128)S(1)}) custom-call(s32[64]{0:T(128)S(1)} %pad_add_fusion.near_ref, s32[576]{0:T(1024)S(1)} %fusion.44.rand_ref, s32[2]{0:T(128)S(1)} %fusion.60.glob_ref, f32[32,3,8,128]{3,2,1,0:T(8,128)S(1)} %reshape.505.bias_ref, bf16[2048,1152]{1,0:T(8,128)(2,1)} %fusion.6.qkv_ref), custom_call_target="tpu_custom_call" | custom-call | flops 20000000000 | bytes 8000000 | tf_op jit(solution)/shard_map/attend/pallas_call | solution.py:336
  241.9 8.1 %fusion.76 = (bf16[32,96,768]{2,1,0:T(8,128)(2,1)}, bf16[32,96,768]{2,1,0:T(8,128)(2,1)}) fusion(bf16[32,224,768]{2,1,0:T(8,128)(2,1)} %bitcast.166), kind=kLoop, calls=%fused_computation.337 | loop fusion | bytes 18874368 | tf_op jit(solution)/shard_map/slice | solution.py:548
  255.3 8.9 %reshape.510 = bf16[768,3072]{1,0:T(8,128)(2,1)} reshape(bf16[32,96,768]{2,1,0:T(8,128)(2,1)} %get-tuple-element.127) | data formatting | bytes 9437184 | tf_op jit(solution)/shard_map/reshape | solution.py:547
  264.3 19.9 %multiply_convert_fusion.1 = (bf16[1024,3072]{1,0:T(8,128)(2,1)S(1)}, f32[1024,3072]{1,0:T(8,128)}) fusion(f32[3072]{0:T(1024)S(1)} %add.646, bf16[768,3072]{1,0:T(8,128)(2,1)} %reshape.510, f32[1024,768]{0,1:T(8,128)} %copy-done.2, f32[768]{0:T(1024)S(1)} %add.643, f32[768]{0:T(1024)S(1)} %mul.351, f32[1024]{0:T(1024)S(1)} %add_rsqrt_fusion.1, ...), kind=kOutput, calls=%fused_computation.9 | convolution fusion | flops 4908122112 | bytes 26765312 | tf_op jit(solution)/shard_map/dot_general | solution.py:25
  284.2 9.4 %fusion.87 = (f32[1024]{0:T(1024)S(1)}, f32[1024,768]{0,1:T(8,128)S(1)}) fusion(f32[768]{0:T(1024)S(1)} %add.658, bf16[1024,3072]{1,0:T(8,128)(2,1)S(1)} %get-tuple-element.235, bf16[3072,768]{1,0:T(8,128)(2,1)} %bitcast.189, f32[768]{0:T(1024)S(1)} %add.643, f32[768]{0:T(1024)S(1)} %mul.351, f32[1024]{0:T(1024)S(1)} %add_rsqrt_fusion.1, ...), kind=kOutput, calls=%fused_computation.348 | convolution fusion | flops 4837342208 | bytes 17323008 | tf_op jit(solution)/shard_map/dot_general | solution.py:25
  302.2 7.0 %convolution_convert_fusion = bf16[3072,768]{1,0:T(8,128)(2,1)} fusion(bf16[1024,3072]{1,0:T(8,128)(2,1)S(1)} %copy-done.60, bf16[1024,768]{0,1:T(8,128)(2,1)S(1)} %get-tuple-element.119), kind=kOutput, calls=%fused_computation.13 | convolution fusion | flops 4834197504 | bytes 12582912 | tf_op jit(solution)/shard_map/dot_general | solution.py:25
  309.2 19.3 %fusion.88 = (bf16[3072]{0:T(1024)(128)(2,1)}, bf16[1024,3072]{1,0:T(8,128)(2,1)}) fusion(f32[1024,3072]{1,0:T(8,128)} %get-tuple-element.236, f32[3072]{0:T(1024)S(1)} %add.646, bf16[1024,768]{0,1:T(8,128)(2,1)} %copy-done.30, bf16[3072,768]{1,0:T(8,128)(2,1)S(1)} %bitcast.192), kind=kOutput, calls=%fused_computation.349 | convolution fusion | flops 4923061248 | bytes 25184256 | tf_op jit(solution)/shard_map/dot_general | solution.py:25
  328.5 10.3 %convolution_convert_fusion.1 = bf16[768,3072]{1,0:T(8,128)(2,1)} fusion(bf16[1024,3072]{1,0:T(8,128)(2,1)} %get-tuple-element.241, f32[1024,768]{0,1:T(8,128)S(1)} %copy-done.4, f32[768]{0:T(1024)S(1)} %add.643, f32[768]{0:T(1024)S(1)} %mul.351, f32[1024]{0:T(1024)S(1)} %add_rsqrt_fusion.1, f32[1024]{0:T(1024)S(1)} %broadcast_multiply_fusion.5), kind=kOutput, calls=%fused_computation.14 | convolution fusion | flops 4838129664 | bytes 14170112 | tf_op jit(solution)/shard_map/dot_general | solution.py:25
  338.8 7.4 %multiply_reduce_fusion = (bf16[768]{0:T(1024)(128)(2,1)}, f32[1024]{0:T(1024)S(1)}, f32[1024]{0:T(1024)S(1)}, bf16[768]{0:T(1024)(128)(2,1)}, f32[1024,768]{0,1:T(8,128)S(1)}) fusion(f32[1024,768]{0,1:T(8,128)S(1)} %copy-done.4, f32[1024]{0:T(1024)S(1)} %add_rsqrt_fusion.1, f32[1024]{0:T(1024)S(1)} %broadcast_multiply_fusion.5, f32[768]{0:T(1024)S(1)} %mul.351, ...), kind=kOutput, calls=%fused_computation.31 | convolution fusion | flops 4851494912 | bytes 22062080 | tf_op jit(solution)/shard_map/dot_general | solution.py:25
  374.6 18.9 %collective-permute-start.38 = (bf16[4,1,4,24,3072]{4,3,2,1,0:T(8,128)(2,1)}, bf16[4,1,4,24,3072]{4,3,2,1,0:T(8,128)(2,1)}, u32[]{:S(2)}, u32[]{:S(2)}) collective-permute-start(bf16[4,1,4,24,3072]{4,3,2,1,0:T(8,128)(2,1)} %constant_dynamic-slice_fusion.5), channel_id=1, source_target_pairs={{0,4},{4,0},{8,12},{12,8},{16,20},{20,16},{24,28},{28,24},{1,5},{5... | collective-permute-start | bytes 7077896 | tf_op jit(solution)/shard_map/ppermute | solution.py:30
  398.1 36.6 %attend_back.1 = bf16[2048,1152]{1,0:T(8,128)(2,1)} custom-call(s32[64]{0:T(128)S(1)} %pad_add_fusion.near_ref, s32[576]{0:T(1024)S(1)} %fusion.44.rand_ref, s32[2]{0:T(128)S(1)} %fusion.60.glob_ref, f32[32,3,8,128]{3,2,1,0:T(8,128)S(1)} %reshape.505.bias_ref, f32[32,8,128]{2,1,0:T(8,128)S(1)} %get-tuple-element.20.log_ref, ...), custom_call_target="tpu_custom_call" | custom-call | flops 35999997952 | bytes 16000000 | tf_op jit(solution)/shard_map/attend_back/pallas_call | solution.py:355
  447.1 9.8 %collective-permute-done.33 = bf16[2,1,1,4,32,768]{5,4,3,2,1,0:T(8,128)(2,1)S(1)} collective-permute-done((bf16[2,1,1,4,32,768]{5,4,3,2,1,0:T(8,128)(2,1)S(1)}, bf16[2,1,1,4,32,768]{5,4,3,2,1,0:T(8,128)(2,1)S(1)}, u32[]{:S(2)}, u32[]{:S(2)}) %collective-permute-start.33) | collective-permute-done | bytes 393248 | tf_op jit(solution)/shard_map/ppermute | solution.py:35
  515.5 11.6 %collective-permute-done.29 = bf16[2,1,32,1152]{3,2,0,1:T(8,128)(2,1)S(1)} collective-permute-done((bf16[2,1,32,1152]{3,2,0,1:T(8,128)(2,1)S(1)}, bf16[2,1,32,1152]{3,2,0,1:T(8,128)(2,1)S(1)}, u32[]{:S(2)}, u32[]{:S(2)}) %collective-permute-start.29) | collective-permute-done | bytes 147488 | tf_op jit(solution)/shard_map/ppermute | solution.py:40
  534.0 21.8 %collective-permute-start.31 = (f32[1,32,1152]{2,1,0:T(8,128)}, f32[1,32,1152]{2,1,0:T(8,128)}, u32[]{:S(2)}, u32[]{:S(2)}) collective-permute-start(f32[1,32,1152]{2,1,0:T(8,128)} %dynamic-slice_bitcast_fusion.10), channel_id=1, source_target_pairs={{0,4},{4,0},{8,12},{12,8},{16,20},{20,16},{24,28},{28,24},{1,5},{5... | collective-permute-start | bytes 442376 | tf_op jit(solution)/shard_map/ppermute | solution.py:30
  571.9 10.7 %collective-permute-done.46 = bf16[1,1,1,4,96,768]{5,4,3,2,1,0:T(8,128)(2,1)S(1)} collective-permute-done((bf16[1,1,1,4,96,768]{5,4,3,2,1,0:T(8,128)(2,1)S(1)}, bf16[1,1,1,4,96,768]{5,4,3,2,1,0:T(8,128)(2,1)S(1)}, u32[]{:S(2)}, u32[]{:S(2)}) %collective-permute-start.46) | collective-permute-done | bytes 589856 | tf_op jit(solution)/shard_map/ppermute | solution.py:35
  601.4 11.4 %collective-permute-done.42 = bf16[1,1,24,3072]{3,2,1,0:T(8,128)(2,1)S(1)} collective-permute-done((bf16[1,1,24,3072]{3,2,1,0:T(8,128)(2,1)S(1)}, bf16[1,1,24,3072]{3,2,1,0:T(8,128)(2,1)S(1)}, u32[]{:S(2)}, u32[]{:S(2)}) %collective-permute-start.42) | collective-permute-done | bytes 147488 | tf_op jit(solution)/shard_map/ppermute | solution.py:40
  (475 shorter events, 253.3 us)
Async XLA Ops:
  7.2 230.7 %all-gather.3.cloned.1.call-start = ((), (), s32[]{:S(2)}) async-start(), calls=%async_computation | async-start | bytes 11354112 | tf_op jit(solution)/shard_map/all_gather | solution.py:543
  26.7 108.5 %collective-permute-start = (bf16[272,768]{1,0:T(8,128)(2,1)}, bf16[272,768]{1,0:T(8,128)(2,1)}, u32[]{:S(2)}, u32[]{:S(2)}) collective-permute-start(bf16[272,768]{1,0:T(8,128)(2,1)} %pad_maximum_fusion.6), channel_id=1, source_target_pairs={{0,0},{1,1},{2,4},{3,5},{4,2},{5,3},{6,6},{7,7},{8,8},{9,9},{10,12... | collective-permute-start | bytes 1253384 | tf_op jit(solution)/shard_map/ppermute | solution.py:61
  34.4 50.3 %collective-permute-start.16 = (bf16[256,768]{0,1:T(8,128)(2,1)}, bf16[256,768]{0,1:T(8,128)(2,1)S(1)}, u32[]{:S(2)}, u32[]{:S(2)}) collective-permute-start(bf16[256,768]{0,1:T(8,128)(2,1)} %bitcast.26), channel_id=1, source_target_pairs={{0,0},{1,1},{2,4},{3,5},{4,2},{5,3},{6,6},{7,7},{8,8},{9,9},{10,12... | collective-permute-start | bytes 1179656 | tf_op jit(solution)/shard_map/ppermute | solution.py:61
  45.4 38.1 %collective-permute-start.7 = (bf16[2,32,1152]{2,1,0:T(8,128)(2,1)S(1)}, bf16[2,32,1152]{2,1,0:T(8,128)(2,1)}, u32[]{:S(2)}, u32[]{:S(2)}) collective-permute-start(bf16[2,32,1152]{2,1,0:T(8,128)(2,1)S(1)} %pad_maximum_fusion.11), channel_id=1, source_target_pairs={{0,2},{1,3},{2,0},{3,1},{4,6},{5,7},{6,4},{7,5},{8,10},{9,11},{10,... | collective-permute-start | bytes 442376 | tf_op jit(solution)/shard_map/ppermute | solution.py:40
  45.4 38.1 %collective-permute-start.8 = (bf16[2,32,1152]{2,1,0:T(8,128)(2,1)S(1)}, bf16[2,32,1152]{2,1,0:T(8,128)(2,1)}, u32[]{:S(2)}, u32[]{:S(2)}) collective-permute-start(bf16[2,32,1152]{2,1,0:T(8,128)(2,1)S(1)} %pad_maximum_fusion.11), channel_id=1, source_target_pairs={{0,1},{1,0},{2,3},{3,2},{4,5},{5,4},{6,7},{7,6},{8,9},{9,8},{10,11... | collective-permute-start | bytes 442376 | tf_op jit(solution)/shard_map/ppermute | solution.py:40
  53.0 45.1 %collective-permute-start.17 = (bf16[256,768]{0,1:T(8,128)(2,1)}, bf16[256,768]{0,1:T(8,128)(2,1)S(1)}, u32[]{:S(2)}, u32[]{:S(2)}) collective-permute-start(bf16[256,768]{0,1:T(8,128)(2,1)} %bitcast.27), channel_id=1, source_target_pairs={{0,4},{1,5},{2,0},{3,1},{4,6},{5,7},{6,2},{7,3},{8,12},{9,13},{10,... | collective-permute-start | bytes 1179656 | tf_op jit(solution)/shard_map/ppermute | solution.py:61
  83.5 29.9 %collective-permute-start.18 = (bf16[256,768]{0,1:T(8,128)(2,1)}, bf16[256,768]{0,1:T(8,128)(2,1)S(1)}, u32[]{:S(2)}, u32[]{:S(2)}) collective-permute-start(bf16[256,768]{0,1:T(8,128)(2,1)} %bitcast.28), channel_id=1, source_target_pairs={{0,1},{1,0},{2,5},{3,4},{4,3},{5,2},{6,7},{7,6},{8,9},{9,8},{10,13... | collective-permute-start | bytes 1179656 | tf_op jit(solution)/shard_map/ppermute | solution.py:61
  83.5 41.7 %collective-permute-start.19 = (bf16[256,768]{0,1:T(8,128)(2,1)}, bf16[256,768]{0,1:T(8,128)(2,1)S(1)}, u32[]{:S(2)}, u32[]{:S(2)}) collective-permute-start(bf16[256,768]{0,1:T(8,128)(2,1)} %bitcast.29), channel_id=1, source_target_pairs={{0,5},{1,4},{2,1},{3,0},{4,7},{5,6},{6,3},{7,2},{8,13},{9,12},{10,... | collective-permute-start | bytes 1179656 | tf_op jit(solution)/shard_map/ppermute | solution.py:61
  84.7 64.0 %collective-permute-start.1 = (bf16[272,768]{1,0:T(8,128)(2,1)S(1)}, bf16[272,768]{1,0:T(8,128)(2,1)}, u32[]{:S(2)}, u32[]{:S(2)}) collective-permute-start(bf16[272,768]{1,0:T(8,128)(2,1)S(1)} %pad_maximum_fusion.7), channel_id=1, source_target_pairs={{0,4},{1,5},{2,0},{3,1},{4,6},{5,7},{6,2},{7,3},{8,12},{9,13},{10,... | collective-permute-start | bytes 1253384 | tf_op jit(solution)/shard_map/ppermute | solution.py:61
  98.1 51.8 %collective-permute-start.2 = (bf16[272,768]{1,0:T(8,128)(2,1)S(1)}, bf16[272,768]{1,0:T(8,128)(2,1)}, u32[]{:S(2)}, u32[]{:S(2)}) collective-permute-start(bf16[272,768]{1,0:T(8,128)(2,1)S(1)} %pad_maximum_fusion.8), channel_id=1, source_target_pairs={{0,1},{1,0},{2,5},{3,4},{4,3},{5,2},{6,7},{7,6},{8,9},{9,8},{10,13... | collective-permute-start | bytes 1253384 | tf_op jit(solution)/shard_map/ppermute | solution.py:61
  113.4 44.3 %collective-permute-start.3 = (bf16[272,768]{1,0:T(8,128)(2,1)}, bf16[272,768]{1,0:T(8,128)(2,1)}, u32[]{:S(2)}, u32[]{:S(2)}) collective-permute-start(bf16[272,768]{1,0:T(8,128)(2,1)} %pad_maximum_fusion.9), channel_id=1, source_target_pairs={{0,5},{1,4},{2,1},{3,0},{4,7},{5,6},{6,3},{7,2},{8,13},{9,12},{10,... | collective-permute-start | bytes 1253384 | tf_op jit(solution)/shard_map/ppermute | solution.py:61
  125.2 49.9 %collective-permute-start.9 = (bf16[1,2,4,32,1152]{4,3,2,1,0:T(8,128)(2,1)}, bf16[1,2,4,32,1152]{4,3,2,1,0:T(8,128)(2,1)}, u32[]{:S(2)}, u32[]{:S(2)}) collective-permute-start(bf16[1,2,4,32,1152]{4,3,2,1,0:T(8,128)(2,1)} %maximum_bitcast_fusion.4), channel_id=1, source_target_pairs={{0,8},{4,12},{8,0},{12,4},{16,24},{20,28},{24,16},{28,20},{1,9},{5... | collective-permute-start | bytes 1769480 | tf_op jit(solution)/shard_map/ppermute | solution.py:35
  176.6 28.6 %collective-permute-start.10 = (bf16[2,2,4,32,1152]{4,3,2,1,0:T(8,128)(2,1)S(1)}, bf16[2,2,4,32,1152]{4,3,2,1,0:T(8,128)(2,1)S(1)}, u32[]{:S(2)}, u32[]{:S(2)}) collective-permute-start(bf16[2,2,4,32,1152]{4,3,2,1,0:T(8,128)(2,1)S(1)} %pad_maximum_fusion.5), channel_id=1, source_target_pairs={{0,16},{4,20},{8,24},{12,28},{16,0},{20,4},{24,8},{28,12},{1,17},{... | collective-permute-start | bytes 3538952 | tf_op jit(solution)/shard_map/ppermute | solution.py:35
  355.5 40.0 %collective-permute-start.20 = (bf16[1024,384]{1,0:T(8,128)(2,1)}, bf16[1024,384]{1,0:T(8,128)(2,1)}, u32[]{:S(2)}, u32[]{:S(2)}) collective-permute-start(bf16[1024,384]{1,0:T(8,128)(2,1)} %get-tuple-element.140), channel_id=1, source_target_pairs={{0,4},{4,0},{8,12},{12,8},{16,20},{20,16},{24,28},{28,24},{1,5},{5... | collective-permute-start | bytes 2359304 | tf_op jit(solution)/shard_map/ppermute | solution.py:30
  363.2 30.3 %collective-permute-start.14 = (bf16[256,768]{0,1:T(8,128)(2,1)S(1)}, bf16[256,768]{0,1:T(8,128)(2,1)S(1)}, u32[]{:S(2)}, u32[]{:S(2)}) collective-permute-start(bf16[256,768]{0,1:T(8,128)(2,1)S(1)} %get-tuple-element.149), channel_id=1, source_target_pairs={{1,0},{0,1},{5,2},{4,3},{3,4},{2,5},{7,6},{6,7},{9,8},{8,9},{13,10... | collective-permute-start | bytes 1179656 | tf_op jit(solution)/shard_map/ppermute | solution.py:69
  364.8 28.7 %collective-permute-start.15 = (bf16[256,768]{0,1:T(8,128)(2,1)S(1)}, bf16[256,768]{0,1:T(8,128)(2,1)S(1)}, u32[]{:S(2)}, u32[]{:S(2)}) collective-permute-start(bf16[256,768]{0,1:T(8,128)(2,1)S(1)} %get-tuple-element.150), channel_id=1, source_target_pairs={{0,0},{1,1},{4,2},{5,3},{2,4},{3,5},{6,6},{7,7},{8,8},{9,9},{12,10... | collective-permute-start | bytes 1179656 | tf_op jit(solution)/shard_map/ppermute | solution.py:69
  373.0 123.0 %collective-permute-start.44 = (bf16[4,1,4,96,768]{4,3,2,1,0:T(8,128)(2,1)}, bf16[4,1,4,96,768]{4,3,2,1,0:T(8,128)(2,1)}, u32[]{:S(2)}, u32[]{:S(2)}) collective-permute-start(bf16[4,1,4,96,768]{4,3,2,1,0:T(8,128)(2,1)} %constant_dynamic-slice_fusion.2), channel_id=1, source_target_pairs={{0,4},{4,0},{8,12},{12,8},{16,20},{20,16},{24,28},{28,24},{1,5},{5... | collective-permute-start | bytes 7077896 | tf_op jit(solution)/shard_map/ppermute | solution.py:30
  374.6 128.3 %collective-permute-start.38 = (bf16[4,1,4,24,3072]{4,3,2,1,0:T(8,128)(2,1)}, bf16[4,1,4,24,3072]{4,3,2,1,0:T(8,128)(2,1)}, u32[]{:S(2)}, u32[]{:S(2)}) collective-permute-start(bf16[4,1,4,24,3072]{4,3,2,1,0:T(8,128)(2,1)} %constant_dynamic-slice_fusion.5), channel_id=1, source_target_pairs={{0,4},{4,0},{8,12},{12,8},{16,20},{20,16},{24,28},{28,24},{1,5},{5... | collective-permute-start | bytes 7077896 | tf_op jit(solution)/shard_map/ppermute | solution.py:30
  393.5 49.3 %collective-permute-start.32 = (bf16[4,1,4,32,768]{4,3,2,1,0:T(8,128)(2,1)}, bf16[4,1,4,32,768]{4,3,2,1,0:T(8,128)(2,1)}, u32[]{:S(2)}, u32[]{:S(2)}) collective-permute-start(bf16[4,1,4,32,768]{4,3,2,1,0:T(8,128)(2,1)} %fusion.20), channel_id=1, source_target_pairs={{0,4},{4,0},{8,12},{12,8},{16,20},{20,16},{24,28},{28,24},{1,5},{5... | collective-permute-start | bytes 2359304 | tf_op jit(solution)/shard_map/ppermute | solution.py:30
  466.4 27.5 %collective-permute-start.26 = (bf16[2,1,2,4,32,1152]{5,4,3,2,1,0:T(8,128)(2,1)}, bf16[2,1,2,4,32,1152]{5,4,3,2,1,0:T(8,128)(2,1)S(1)}, u32[]{:S(2)}, u32[]{:S(2)}) collective-permute-start(bf16[2,1,2,4,32,1152]{5,4,3,2,1,0:T(8,128)(2,1)} %fusion.18), channel_id=1, source_target_pairs={{0,8},{4,12},{8,0},{12,4},{16,24},{20,28},{24,16},{28,20},{1,9},{5... | collective-permute-start | bytes 3538952 | tf_op jit(solution)/shard_map/ppermute | solution.py:35
  501.1 63.4 %collective-permute-start.45 = (bf16[2,1,1,4,96,768]{5,4,3,2,1,0:T(8,128)(2,1)}, bf16[2,1,1,4,96,768]{5,4,3,2,1,0:T(8,128)(2,1)}, u32[]{:S(2)}, u32[]{:S(2)}) collective-permute-start(bf16[2,1,1,4,96,768]{5,4,3,2,1,0:T(8,128)(2,1)} %constant_dynamic-slice_fusion.1), channel_id=1, source_target_pairs={{0,8},{4,12},{8,0},{12,4},{16,24},{20,28},{24,16},{28,20},{1,9},{5... | collective-permute-start | bytes 3538952 | tf_op jit(solution)/shard_map/ppermute | solution.py:35
  527.1 28.7 %collective-permute-start.24 = (bf16[256,768]{0,1:T(8,128)(2,1)S(1)}, bf16[256,768]{0,1:T(8,128)(2,1)S(1)}, u32[]{:S(2)}, u32[]{:S(2)}) collective-permute-start(bf16[256,768]{0,1:T(8,128)(2,1)S(1)} %get-tuple-element.135), channel_id=1, source_target_pairs={{1,0},{0,1},{5,2},{4,3},{3,4},{2,5},{7,6},{6,7},{9,8},{8,9},{13,10... | collective-permute-start | bytes 1179656 | tf_op jit(solution)/shard_map/ppermute | solution.py:69
  527.1 28.7 %collective-permute-start.25 = (bf16[256,768]{0,1:T(8,128)(2,1)S(1)}, bf16[256,768]{0,1:T(8,128)(2,1)S(1)}, u32[]{:S(2)}, u32[]{:S(2)}) collective-permute-start(bf16[256,768]{0,1:T(8,128)(2,1)S(1)} %get-tuple-element.136), channel_id=1, source_target_pairs={{0,0},{1,1},{4,2},{5,3},{2,4},{3,5},{6,6},{7,7},{8,8},{9,9},{12,10... | collective-permute-start | bytes 1179656 | tf_op jit(solution)/shard_map/ppermute | solution.py:69
  528.7 39.3 %collective-permute-start.39 = (bf16[1,2,1,4,24,3072]{5,4,3,2,1,0:T(8,128)(2,1)S(1)}, bf16[1,2,1,4,24,3072]{5,4,3,2,1,0:T(8,128)(2,1)}, u32[]{:S(2)}, u32[]{:S(2)}) collective-permute-start(bf16[1,2,1,4,24,3072]{5,4,3,2,1,0:T(8,128)(2,1)S(1)} %constant_dynamic-slice_fusion.4), channel_id=1, source_target_pairs={{0,16},{4,20},{8,24},{12,28},{16,0},{20,4},{24,8},{28,12},{1,17},{... | collective-permute-start | bytes 3538952 | tf_op jit(solution)/shard_map/ppermute | solution.py:35
  (100 other events, 1567.0 us)
Sparse Core Ops, SparseCore 0:
  15.1 131.0 all-gather.2

commit v2 on v1

v2 whole, which is shorter than its diff:
```python
from functools import partial

import jax
import jax.numpy as jnp
from jax import lax
from jax.experimental import pallas as pl
from jax.experimental.pallas import tpu as pltpu
from jax.sharding import PartitionSpec as P

HEADS = 12
HEAD = 64
BLOCK = 64
SLOTS = 8
EPS = 1e-06
NEG = -1e30
LOW = jnp.bfloat16
WIDE = jnp.float32

NT = (((1,), (1,)), ((), ()))
TN = (((0,), (0,)), ((), ()))
NN = (((1,), (0,)), ((), ()))


def dot(left, right, dims):
    return lax.dot_general(left, right, dims, preferred_element_type=WIDE)


def swap(array):
    size = lax.axis_size("dp")
    return lax.ppermute(array, "dp", [(i, i ^ 1) for i in range(size)])


def flip_seq(array, k):
    size = lax.axis_size("seq")
    return lax.ppermute(array, "seq", [(i, i ^ k) for i in range(size)])


def rounds():
    dp, seq = lax.axis_size("dp"), lax.axis_size("seq")
    for a in range(2):
        pairs = []
        for d in range(dp):
            for z in range(seq):
                to_dp = (d & ~1) | (z >> 1)
                to_seq = 2 * (d & 1) + (a ^ (z & 1))
                pairs.append((d * seq + z, to_dp * seq + to_seq))
        yield a, pairs


def bring(piece_of):
    z = lax.axis_index("seq")
    return [lax.ppermute(piece_of(a ^ (z & 1)), ("dp", "seq"), pairs) for a, pairs in rounds()]


def send_back(rows):
    z = lax.axis_index("seq")
    size = rows.shape[0] // 2
    got = [
        lax.ppermute(rows[size * a : size * a + size], ("dp", "seq"), [(t, s) for s, t in pairs])
        for a, pairs in rounds()
    ]
    odd = (z & 1) == 1
    return jnp.stack([jnp.where(odd, got[1], got[0]), jnp.where(odd, got[0], got[1])])


def pick(array, index, axis):
    return lax.dynamic_slice_in_dim(array, index, 1, axis)


def gather_seq(shard):
    z = lax.axis_index("seq")
    mirror = flip_seq(shard, 3)
    near = flip_seq(jnp.stack([shard, mirror]), 1)
    pieces = [shard, near[0], near[1], mirror]
    for bit in range(2):
        set_bit = ((z >> bit) & 1) == 1
        pieces = [
            jnp.where(set_bit, pieces[i ^ (1 << bit)], pieces[i]) for i in range(len(pieces))
        ]
    return pieces, mirror


def chip_groups():
    count = (lax.axis_size("dp") // 2).bit_length() - 1
    return [(bit, min(2, count - bit)) for bit in range(0, count, 2)]


def flip_chip(array, away):
    size = lax.axis_size("dp")
    return lax.ppermute(array, "dp", [(i, i ^ (2 * away)) for i in range(size)])


def gather_chips(part):
    parts = [part]
    for bit, bits in chip_groups():
        parts = parts + [flip_chip(p, k << bit) for k in range(1, 1 << bits) for p in parts]
    return parts


def in_chip_order(parts):
    chip = lax.axis_index("dp") >> 1
    parts = jnp.stack(parts)
    return [pick(parts, q ^ chip, 0)[0] for q in range(parts.shape[0])]


def in_device_order(mine, theirs):
    core = lax.axis_index("dp") & 1
    parts = []
    for own, other in zip(in_chip_order(mine), in_chip_order(theirs)):
        parts += [jnp.where(core == 0, own, other), jnp.where(core == 0, other, own)]
    return jnp.concatenate(parts, 0)


def join(*values):
    return lax.optimization_barrier(values)


def tie(values, *others):
    return lax.optimization_barrier((values, others))[0]


def added(*arrays):
    return sum(array.astype(WIDE) for array in arrays).astype(LOW)


def reduce_chips(parts):
    chip = lax.axis_index("dp") >> 1
    for bit, bits in chip_groups():
        ways = 1 << bits
        parts = parts.reshape((-1, ways) + parts.shape[1:])
        mine = (chip >> bit) & (ways - 1)
        others = [flip_chip(pick(parts, mine ^ k, 1)[:, 0], k << bit) for k in range(1, ways)]
        parts = added(pick(parts, mine, 1)[:, 0], *others)
    return parts[0]


def reduce_seq(parts):
    z = lax.axis_index("seq")
    near = flip_seq(jnp.concatenate([pick(parts, z ^ 1, 0), pick(parts, z ^ 2, 0)], 0), 1)
    mirror = added(pick(parts, z ^ 3, 0)[0], near[1])
    return pick(parts, z, 0)[0].astype(WIDE) + near[0].astype(WIDE) + flip_seq(mirror, 3).astype(WIDE)


def norm_parts(summed):
    center = summed - jnp.mean(summed, -1, keepdims=True)
    spread = jnp.mean(center * center, -1, keepdims=True)
    scale = lax.rsqrt(spread + EPS)
    return center * scale, scale


def norm_back(grad, unit, scale, gain):
    grad_unit = grad * gain
    mean_one = jnp.mean(grad_unit, -1, keepdims=True)
    mean_two = jnp.mean(grad_unit * unit, -1, keepdims=True)
    return scale * (grad_unit - mean_one - unit * mean_two)


def gelu_parts(x):
    size = jnp.abs(x)
    t = 1.0 / (1.0 + (0.3275911 * 0.5**0.5) * size)
    bell = jnp.exp(-0.5 * x * x)
    series = 1.061405429
    for factor in (-1.453152027, 1.421413741, -0.284496736, 0.254829592):
        series = series * t + factor
    tail = 0.5 * series * t * bell
    share = jnp.where(x >= 0, 1.0 - tail, tail)
    return x * share, share + x * bell * 0.3989422804014327


def block_rows(ref, block, lanes):
    return ref[pl.ds(pl.multiple_of(block * BLOCK, BLOCK), BLOCK), lanes]


def diagonal(pair_rows, low):
    zero = jnp.zeros_like(pair_rows)
    return jnp.concatenate(
        [jnp.where(low, pair_rows, zero), jnp.where(low, zero, pair_rows)], axis=0
    )


def gather_blocks(ref, ids, lanes, low):
    parts = []
    for one, two in ids:
        if two is None:
            parts.append(block_rows(ref, one, lanes))
        else:
            parts.append(
                jnp.where(low, block_rows(ref, one, lanes), block_rows(ref, two, lanes))
            )
    return jnp.concatenate(parts, axis=0)


def slot_ids(near_ref, rand_ref, globs, i, head, blocks):
    ids = [(near_ref[i], None), (i, None), (near_ref[blocks + i], None)]
    ids += [(globs[0], None), (globs[1], None)]
    for r in range(3):
        ids.append(
            (
                rand_ref[(head * blocks + i) * 3 + r],
                rand_ref[((head + 1) * blocks + i) * 3 + r],
            )
        )
    return ids


def lanes_of(part, pair):
    first = 128 * (3 * pair + part)
    return slice(first, first + 128)


def flat_lanes(pair):
    return slice(128 * pair, 128 * pair + 128)


def start_copies(copies, sems):
    started = [
        pltpu.make_async_copy(source, target, sems.at[k])
        for k, (source, target) in enumerate(copies)
    ]
    for copy in started:
        copy.start()
    return started


def project_kernel(chips, direct, at_ref, tokens_ref, b_ref, *refs):
    sources, (first_ref, rest_ref, w_ref, sems) = refs[:-4], refs[-4:]
    if direct:
        span = w_ref.shape[0] // (2 * chips)
        copies = [
            (
                sources[away].at[k, :span],
                w_ref.at[pl.ds(pl.multiple_of((2 * (at_ref[0] ^ away) + k) * span, span), span)],
            )
            for away in range(chips)
            for k in range(2)
        ]
    else:
        copies = [(sources[0], w_ref)]
    for copy in start_copies(copies, sems):
        copy.wait()
    tile = 256
    lane = lax.broadcasted_iota(jnp.int32, (1, w_ref.shape[1]), 1)
    scale = jnp.where(lane % 384 < 128, HEAD ** (-0.5), 1.0)

    def body(at, carry):
        rows = pl.ds(pl.multiple_of(at * tile, tile), tile)
        values = (dot(tokens_ref[rows], w_ref[...], NN) + b_ref[...]).astype(LOW).astype(WIDE)
        values = (values * scale).astype(LOW)
        cut = first_ref.shape[1]
        first_ref[rows] = values[:, :cut]
        rest_ref[rows] = values[:, cut:]
        return carry

    lax.fori_loop(0, tokens_ref.shape[0] // tile, body, 0)


def attend_kernel(
    first_pair, pairs, blocks, step, near_ref, rand_ref, glob_ref, bias_ref, qkv_ref, out_ref, log_ref
):
    low = lax.broadcasted_iota(jnp.int32, (1, 2 * HEAD), 1) < HEAD
    globs = (glob_ref[0], glob_ref[1])

    def scores_of(i, pair):
        ids = slot_ids(near_ref, rand_ref, globs, i, 2 * (first_pair + pair), blocks)
        queries = diagonal(block_rows(qkv_ref, i, lanes_of(0, pair)), low)
        return dot(gather_blocks(qkv_ref, ids, lanes_of(1, pair), low), queries, NT)

    def softmax_of(i, pair, scores):
        highest = jnp.max(scores, axis=0, keepdims=True)
        weights = jnp.exp(scores - highest)
        total = jnp.sum(weights, axis=0, keepdims=True)
        log_ref[i, pair : pair + 1] = highest + jnp.log(total)
        return (weights * (1.0 / total)).astype(LOW)

    def put(i, pair, mixed):
        at = pl.ds(pl.multiple_of(i * BLOCK, BLOCK), BLOCK)
        out_ref[at, flat_lanes(pair)] = jnp.where(low, mixed[:BLOCK], mixed[BLOCK:]).astype(LOW)

    def body(at, carry):
        units = [(at * step + d, pair) for d in range(step) for pair in range(pairs)]
        scores = [scores_of(*unit) for unit in units]
        probs = []
        for (i, pair), score in zip(units, scores):
            bias = bias_ref[i, first_pair + pair]
            score = jnp.concatenate(
                [score[BLOCK * j : BLOCK * j + BLOCK] + bias[j : j + 1] for j in range(SLOTS)],
                axis=0,
            )
            probs.append(softmax_of(i, pair, score))
        for (i, pair), prob in zip(units, probs):
            ids = slot_ids(near_ref, rand_ref, globs, i, 2 * (first_pair + pair), blocks)
            values = gather_blocks(qkv_ref, ids, lanes_of(2, pair), low)
            put(i, pair, dot(prob, values, TN))
        return carry

    lax.fori_loop(0, blocks // step, body, 0)

    def whole_row(n, carry):
        i = glob_ref[n]
        scores = []
        for pair in range(pairs):
            queries = diagonal(block_rows(qkv_ref, i, lanes_of(0, pair)), low)
            scores.append(dot(qkv_ref[:, lanes_of(1, pair)], queries, NT))
        probs = [softmax_of(i, pair, scores[pair]) for pair in range(pairs)]
        for pair in range(pairs):
            put(i, pair, dot(probs[pair], qkv_ref[:, lanes_of(2, pair)], TN))
        return carry

    lax.fori_loop(0, 2, whole_row, 0)


def attend_back_kernel(
    first_pair,
    pairs,
    blocks,
    step,
    near_ref,
    rand_ref,
    glob_ref,
    bias_ref,
    log_ref,
    qkv_ref,
    mine_ref,
    come_ref,
    *refs,
):
    if first_pair:
        before_ref, w_ref, whole_ref, rows_own_ref, rows_other_ref, sums_ref = refs[:6]
        out_ref = whole_ref.at[:, 384 * first_pair :]
    else:
        out_ref = refs[0]
    grad_ref, acc_ref = refs[-2:]
    low = lax.broadcasted_iota(jnp.int32, (1, 2 * HEAD), 1) < HEAD
    globs = (glob_ref[0], glob_ref[1])
    acc_ref[...] = jnp.zeros_like(acc_ref)
    half = mine_ref.shape[0]
    lanes = slice(128 * first_pair, 128 * (first_pair + pairs))
    grad_ref[:half] = mine_ref[:, lanes]
    grad_ref[half:] = come_ref[:, lanes]

    def add(part, pair, block, value):
        at = pl.ds(pl.multiple_of(block * BLOCK, BLOCK), BLOCK)
        lanes = flat_lanes(2 * pair + part)
        acc_ref[at, lanes] = acc_ref[at, lanes] + value

    def operands(i, pair):
        queries = diagonal(block_rows(qkv_ref, i, lanes_of(0, pair)), low)
        grads = diagonal(block_rows(grad_ref, i, flat_lanes(pair)), low)
        return queries, grads

    def softmax_back(prob, grad_prob):
        scaled = prob * grad_prob
        inner = jnp.sum(scaled, axis=0, keepdims=True)
        return prob.astype(LOW), (scaled - prob * inner).astype(LOW)

    def put(i, pair, mixed):
        at = pl.ds(pl.multiple_of(i * BLOCK, BLOCK), BLOCK)
        out_ref[at, lanes_of(0, pair)] = (
            jnp.where(low, mixed[:BLOCK], mixed[BLOCK:]) * HEAD ** (-0.5)
        ).astype(LOW)

    def body(at, carry):
        units = [(at * step + d, pair) for d in range(step) for pair in range(pairs)]
        first = []
        for i, pair in units:
            ids = slot_ids(near_ref, rand_ref, globs, i, 2 * (first_pair + pair), blocks)
            queries, grads = operands(i, pair)
            first.append(
                (
                    dot(gather_blocks(qkv_ref, ids, lanes_of(1, pair), low), queries, NT),
                    dot(gather_blocks(qkv_ref, ids, lanes_of(2, pair), low), grads, NT),
                )
            )
        second = []
        for (i, pair), (score, grad_prob) in zip(units, first):
            shift = bias_ref[i, first_pair + pair] - log_ref[i, pair : pair + 1]
            prob = jnp.concatenate(
                [
                    jnp.exp(score[BLOCK * j : BLOCK * j + BLOCK] + shift[j : j + 1])
                    for j in range(SLOTS)
                ],
                axis=0,
            )
            second.append(softmax_back(prob, grad_prob))
        third = []
        for (i, pair), (prob, grad_score) in zip(units, second):
            ids = slot_ids(near_ref, rand_ref, globs, i, 2 * (first_pair + pair), blocks)
            queries, grads = operands(i, pair)
            keys = gather_blocks(qkv_ref, ids, lanes_of(1, pair), low)
            put(i, pair, dot(grad_score, keys, TN))
            third.append((dot(grad_score, queries, NN), dot(prob, grads, NN)))
        for (i, pair), values in zip(units, third):
            ids = slot_ids(near_ref, rand_ref, globs, i, 2 * (first_pair + pair), blocks)
            for j, (one, two) in enumerate(ids):
                for part, value in enumerate(values):
                    value = value[BLOCK * j : BLOCK * j + BLOCK]
                    if two is None:
                        add(part, pair, one, value)
                    else:
                        add(part, pair, one, jnp.where(low, value, 0.0))
                        add(part, pair, two, jnp.where(low, 0.0, value))
        return carry

    lax.fori_loop(0, blocks // step, body, 0)

    def whole_row(n, carry):
        i = glob_ref[n]
        first = []
        for pair in range(pairs):
            queries, grads = operands(i, pair)
            first.append(
                (
                    dot(qkv_ref[:, lanes_of(1, pair)], queries, NT),
                    dot(qkv_ref[:, lanes_of(2, pair)], grads, NT),
                )
            )
        second = []
        for pair, (score, grad_prob) in enumerate(first):
            prob = jnp.exp(score - log_ref[i, pair : pair + 1])
            second.append(softmax_back(prob, grad_prob))
        for pair, (prob, grad_score) in enumerate(second):
            queries, grads = operands(i, pair)
            acc_ref[:, flat_lanes(2 * pair)] += dot(grad_score, queries, NN)
            acc_ref[:, flat_lanes(2 * pair + 1)] += dot(prob, grads, NN)
            put(i, pair, dot(grad_score, qkv_ref[:, lanes_of(1, pair)], TN))
        return carry

    lax.fori_loop(0, jnp.where(globs[0] == globs[1], 1, 2), whole_row, 0)
    for pair in range(pairs):
        out_ref[:, 384 * pair + 128 : 384 * pair + 384] = acc_ref[
            :, 256 * pair : 256 * pair + 256
        ].astype(LOW)
    if first_pair:
        whole_ref[:, : 384 * first_pair] = before_ref[...]
        rows_back(256, whole_ref, w_ref, rows_own_ref, rows_other_ref, sums_ref)


def rows_back(tile, grads_ref, w_ref, own_ref, other_ref, sums_ref):
    sums_ref[...] = jnp.zeros_like(sums_ref)
    for side, rows_ref in enumerate((own_ref, other_ref)):

        def body(at, carry, side=side, rows_ref=rows_ref):
            rows = pl.ds(pl.multiple_of(side * own_ref.shape[0] + at * tile, tile), tile)
            grads = grads_ref[rows]
            sums_ref[...] += jnp.sum(grads.astype(WIDE), 0, keepdims=True)
            rows = pl.ds(pl.multiple_of(at * tile, tile), tile)
            rows_ref[rows] = dot(grads, w_ref[...], NT).astype(rows_ref.dtype)
            return carry

        lax.fori_loop(0, own_ref.shape[0] // tile, body, 0)


def token_kernel(
    tile,
    chips,
    direct,
    at_ref,
    mixed_first_ref,
    mixed_rest_ref,
    other_first_ref,
    other_rest_ref,
    tokens_ref,
    grad_ref,
    vectors_ref,
    *refs,
):
    sources, refs = refs[:-17], refs[-17:]
    output_ref, first_ref, mine_ref, theirs_ref, *grad_refs, g_vectors_ref = refs[:7]
    w_in_ref, w_down_ref, hidden_ref, pre_ref, normed_ref, down_ref, branch_ref, line_ref = refs[7:15]
    sems, out_sems = refs[15:]
    own, half = mine_ref.shape
    wide, width = w_down_ref.shape
    chunks = wide // width
    chip, core = at_ref[0], at_ref[1]
    span, span_ff = width // (2 * chips), wide // (2 * chips)
    low_rows = span * (chunks + 1)
    if direct:
        copies = []
        for k in range(2):
            for away in range(chips):
                source = sources[k * chips + away]
                place = 2 * (chip ^ away) + (core if k == 0 else 1 - core)
                rows = pl.ds(pl.multiple_of(place * span, span), span)
                copies += [
                    (source.at[span * c : span * c + span], w_in_ref.at[c, rows])
                    for c in range(chunks + 1)
                ]
                rows = pl.ds(pl.multiple_of(place * span_ff, span_ff), span_ff)
                copies.append((source.at[low_rows : low_rows + span_ff], w_down_ref.at[rows]))
    else:
        copies = [(sources[0], w_in_ref), (sources[1], w_down_ref)]
    for copy in start_copies(copies, sems):
        copy.wait()
    w_out_ref = w_in_ref.at[chunks]
    here = pl.ds(pl.multiple_of(core * half, 128), half)
    there = pl.ds(pl.multiple_of((1 - core) * half, 128), half)
    b_out, gain_one, shift_one, b_down, gain_two, shift_two = (
        vectors_ref[k : k + 1] for k in range(6)
    )
    g_vectors_ref[...] = jnp.zeros_like(g_vectors_ref)
    columns = [(c, slice(width * c, width * c + width)) for c in range(chunks)]

    def add_sums(**sums):
        for k, value in sums.items():
            k = int(k[1:])
            g_vectors_ref[k : k + 1] += jnp.sum(value, 0, keepdims=True)

    def token_tile(at, carry):
        rows = pl.ds(pl.multiple_of(at * tile, tile), tile)
        mixed = jnp.concatenate([mixed_first_ref[rows], mixed_rest_ref[rows]], 1)
        other = jnp.concatenate([other_first_ref[rows], other_rest_ref[rows]], 1)
        branch = dot(mixed, w_out_ref[here], NN) + dot(other, w_out_ref[there], NN)
        unit_one, scale_one = norm_parts(tokens_ref[rows].astype(WIDE) + (branch + b_out))
        normed = unit_one * gain_one + shift_one
        normed_low = normed.astype(LOW)
        normed_ref[rows] = normed_low
        down = b_down
        for c, lanes in columns:
            bias = vectors_ref[6 + c : 7 + c]
            hidden, slope = gelu_parts(dot(normed_low, w_in_ref[c], NN) + bias)
            hidden = hidden.astype(LOW)
            hidden_ref[rows, lanes] = hidden
            pre_ref[rows, lanes] = slope.astype(LOW)
            down = down + dot(hidden, w_down_ref[lanes], NN)
        unit_two, scale_two = norm_parts(normed + down)
        output_ref[rows] = (unit_two * gain_two + shift_two).astype(LOW)
        grad = grad_ref[rows].astype(WIDE)
        add_sums(_4=grad * unit_two, _5=grad)
        grad_second = norm_back(grad, unit_two, scale_two, gain_two)
        grad_down = grad_second.astype(LOW)
        down_ref[rows] = grad_down
        add_sums(_3=grad_down.astype(WIDE))
        grad_normed = grad_second
        for c, lanes in columns:
            grad_pre = dot(grad_down, w_down_ref[lanes], NT) * pre_ref[rows, lanes].astype(WIDE)
            grad_pre = grad_pre.astype(LOW)
            pre_ref[rows, lanes] = grad_pre
            g_vectors_ref[6 + c : 7 + c] += jnp.sum(grad_pre.astype(WIDE), 0, keepdims=True)
            grad_normed = grad_normed + dot(grad_pre, w_in_ref[c], NT)
        add_sums(_1=grad_normed * unit_one, _2=grad_normed)
        grad_first = norm_back(grad_normed, unit_one, scale_one, gain_one)
        first_ref[rows] = grad_first
        grad_branch = grad_first.astype(LOW)
        branch_ref[rows] = grad_branch
        add_sums(_0=grad_branch.astype(WIDE))
        mine_ref[rows] = dot(grad_branch, w_out_ref[here], NT).astype(LOW)
        theirs_ref[rows] = dot(grad_branch, w_out_ref[there], NT).astype(LOW)
        return carry

    lax.fori_loop(0, own // tile, token_tile, 0)
    mixed = jnp.concatenate([mixed_first_ref[:own], mixed_rest_ref[:own]], 1)
    other = jnp.concatenate([other_first_ref[...], other_rest_ref[...]], 1)
    w_out_ref[here] = dot(mixed, branch_ref[...], TN).astype(LOW)
    w_out_ref[there] = dot(other, branch_ref[...], TN).astype(LOW)
    moving = []

    def leave(copies):
        for source, target in copies:
            copy = pltpu.make_async_copy(source, target, out_sems.at[len(moving)])
            copy.start()
            moving.append(copy)

    def leave_rows(c):
        if not direct:
            return leave([(w_in_ref.at[c], grad_refs[0].at[c])])
        for k, target in enumerate(grad_refs):
            for q in range(chips):
                place = 2 * q + (core if k == 0 else 1 - core)
                rows = pl.ds(pl.multiple_of(place * span, span), span)
                leave([(w_in_ref.at[c, rows], target.at[q, span * c : span * c + span])])

    leave_rows(chunks)
    if direct:
        line_ref[...] = g_vectors_ref[...].astype(LOW)
        for target in grad_refs:
            for q in range(chips):
                leave([(line_ref, target.at[q, low_rows + span_ff : low_rows + span_ff + 16])])
    for c, lanes in columns:
        w_down_ref[lanes] = dot(hidden_ref[:, lanes], down_ref[...], TN).astype(LOW)
        if direct:
            for k, target in enumerate(grad_refs):
                place = 2 * c + (core if k == 0 else 1 - core)
                rows = pl.ds(pl.multiple_of(place * span_ff, span_ff), span_ff)
                leave([(w_down_ref.at[rows], target.at[c, low_rows : low_rows + span_ff])])
        else:
            leave([(w_down_ref.at[lanes], grad_refs[1].at[lanes])])
        w_in_ref[c] = dot(normed_ref[...], pre_ref[:, lanes], TN).astype(LOW)
        leave_rows(c)
    for copy in moving:
        copy.wait()


IN_SMEM = pl.BlockSpec(memory_space=pltpu.SMEM)
IN_VMEM = pl.BlockSpec(memory_space=pltpu.VMEM)


IN_ANY = pl.BlockSpec(memory_space=pl.ANY)


def project_tokens(at, tokens, b_qkv, weights, direct):
    length, width = tokens.shape
    half = width // 2
    chips = lax.axis_size("dp") // 2
    return pl.pallas_call(
        partial(project_kernel, chips, direct),
        out_shape=(
            jax.ShapeDtypeStruct((length, 384), LOW),
            jax.ShapeDtypeStruct((length, 3 * half - 384), LOW),
            jax.ShapeDtypeStruct((width, 3 * half), LOW),
        ),
        in_specs=[IN_SMEM] + [IN_VMEM] * 2 + [IN_ANY] * len(weights),
        out_specs=(IN_VMEM,) * 3,
        scratch_shapes=[pltpu.SemaphoreType.DMA((2 * chips,))],
        compiler_params=pltpu.CompilerParams(vmem_limit_bytes=48 << 20),
        cost_estimate=pl.CostEstimate(
            flops=4_000_000_000, bytes_accessed=12_000_000, transcendentals=0
        ),
        name="project",
    )(at, tokens, b_qkv, *weights)


def attend(first_pair, near, rand, globs, bias, qkv):
    length, width = qkv.shape
    pairs, blocks = width // 384, length // BLOCK
    return pl.pallas_call(
        partial(attend_kernel, first_pair, pairs, blocks, 8 // pairs),
        out_shape=(
            jax.ShapeDtypeStruct((length, 128 * pairs), LOW),
            jax.ShapeDtypeStruct((blocks, 8, 128), WIDE),
        ),
        in_specs=[IN_SMEM] * 3 + [IN_VMEM] * 2,
        out_specs=(IN_VMEM,) * 2,
        compiler_params=pltpu.CompilerParams(vmem_limit_bytes=48 << 20),
        cost_estimate=pl.CostEstimate(
            flops=6_000_000_000 * pairs, bytes_accessed=3_000_000 * pairs, transcendentals=0
        ),
        name="attend",
    )(near, rand, globs, bias, qkv)


def attend_back(first_pair, near, rand, globs, bias, log_total, qkv, mine, come, *more):
    length, width = qkv.shape
    pairs, blocks = width // 384, length // BLOCK
    grads = jax.ShapeDtypeStruct((length, width + 384 * first_pair), LOW)
    if more:
        rows, wide = length // 2, more[1].shape[0]
        grads = (
            grads,
            jax.ShapeDtypeStruct((rows, wide), WIDE),
            jax.ShapeDtypeStruct((rows, wide), LOW),
            jax.ShapeDtypeStruct((1, grads.shape[1]), WIDE),
        )
    return pl.pallas_call(
        partial(attend_back_kernel, first_pair, pairs, blocks, 4 // pairs),
        out_shape=grads,
        in_specs=[IN_SMEM] * 3 + [IN_VMEM] * (5 + len(more)),
        out_specs=(IN_VMEM,) * 4 if more else IN_VMEM,
        scratch_shapes=[
            pltpu.VMEM((length, 128 * pairs), LOW),
            pltpu.VMEM((length, 256 * pairs), WIDE),
        ],
        compiler_params=pltpu.CompilerParams(vmem_limit_bytes=56 << 20),
        cost_estimate=pl.CostEstimate(
            flops=12_000_000_000 * pairs, bytes_accessed=6_000_000 * pairs, transcendentals=0
        ),
        name="attend_back",
    )(near, rand, globs, bias, log_total, qkv, mine, come, *more)


def token_layer(at, mixed, other, tokens, grads, vectors, weights, direct):
    own, width = tokens.shape
    half = width // 2
    chips = lax.axis_size("dp") // 2
    wide = 4 * width
    chunks = wide // width
    if direct:
        rows = ((chunks + 1) * width + wide) // (2 * chips) + 16
        grads_like = (jax.ShapeDtypeStruct((chips, rows, width), LOW),) * 2
    else:
        grads_like = (
            jax.ShapeDtypeStruct((chunks + 1, width, width), LOW),
            jax.ShapeDtypeStruct((wide, width), LOW),
        )
    return pl.pallas_call(
        partial(token_kernel, 256, chips, direct),
        out_shape=(
            jax.ShapeDtypeStruct((own, width), LOW),
            jax.ShapeDtypeStruct((own, width), WIDE),
            jax.ShapeDtypeStruct((own, half), LOW),
            jax.ShapeDtypeStruct((own, half), LOW),
        )
        + grads_like
        + (jax.ShapeDtypeStruct((16, width), WIDE),),
        in_specs=[IN_SMEM] + [IN_VMEM] * 7 + [IN_ANY] * len(weights),
        out_specs=(IN_VMEM,) * 4 + (IN_ANY,) * 2 + (IN_VMEM,),
        scratch_shapes=[
            pltpu.VMEM((chunks + 1, width, width), LOW),
            pltpu.VMEM((wide, width), LOW),
            pltpu.VMEM((own, wide), LOW),
            pltpu.VMEM((own, wide), LOW),
            pltpu.VMEM((own, width), LOW),
            pltpu.VMEM((own, width), LOW),
            pltpu.VMEM((own, width), LOW),
            pltpu.VMEM((16, width), LOW),
            pltpu.SemaphoreType.DMA((2 * chips * (chunks + 2),)),
            pltpu.SemaphoreType.DMA((2 * chips * (chunks + 2) + 2 * chunks,)),
        ],
        compiler_params=pltpu.CompilerParams(vmem_limit_bytes=60 << 20),
        cost_estimate=pl.CostEstimate(
            flops=36_000_000_000, bytes_accessed=32_000_000, transcendentals=0
        ),
        name="token_layer",
    )(at, *mixed, *other, tokens, grads, vectors, *weights)


def place_of(block, core, z, blocks):
    quarter, row = block // (blocks // 4), block % (blocks // 4)
    a = (quarter & 1) ^ (z & 1)
    return ((quarter >> 1) ^ core) * (blocks // 2) + a * (blocks // 4) + row


def block_at(place, core, z, blocks):
    quarter = 2 * ((place // (blocks // 2)) ^ core) + ((place % (blocks // 2)) // (blocks // 4) ^ (z & 1))
    return quarter * (blocks // 4) + place % (blocks // 4)


def tables(rand, globs, blocks):
    core = lax.axis_index("dp") & 1
    z = lax.axis_index("seq")
    here = block_at(jnp.arange(blocks, dtype=jnp.int32), core, z, blocks)
    heads = rand.shape[0]
    one, two = globs[0], globs[1]

    def near(block):
        return jnp.abs(block - here) <= 1

    every = jnp.ones((heads, blocks), bool)
    ok = [every & (here > 0), every, every & (here < blocks - 1)]
    ok += [every & ~near(one), every & ~near(two) & (one != two)]
    seen = []
    for r in range(3):
        block = rand[:, :, r]
        good = ~near(block) & (block != one) & (block != two)
        for before in seen:
            good = good & (block != before)
        seen.append(block)
        ok.append(good)
    whole_row = (here == one) | (here == two)
    ok = jnp.stack(ok, -1) & ~whole_row[None, :, None]
    bias = jnp.where(ok, 0.0, NEG).astype(WIDE)
    bias = bias.reshape(heads // 2, 2, blocks, SLOTS).transpose(2, 0, 3, 1)
    bias = jnp.repeat(bias, HEAD, axis=3)
    put = partial(place_of, core=core, z=z, blocks=blocks)
    sides = jnp.concatenate([put(jnp.maximum(here - 1, 0)), put(jnp.minimum(here + 1, blocks - 1))])
    return sides, put(rand).reshape(-1), put(globs), bias


def shards(
    inputs,
    cotangent,
    rand_blocks,
    global_blocks,
    w_query,
    b_query,
    w_key,
    w_value,
    b_value,
    w_out,
    b_out,
    gain_one,
    shift_one,
    w_up,
    b_up,
    w_down,
    b_down,
    gain_two,
    shift_two,
):
    n_dp, n_seq = lax.axis_size("dp"), lax.axis_size("seq")
    chips, devices = n_dp // 2, n_dp * n_seq
    core = lax.axis_index("dp") & 1
    z = lax.axis_index("seq")
    device = lax.axis_index("dp") * n_seq + z
    rows_in, width = w_query.shape
    rows_ff, wide = w_down.shape[0], w_up.shape[1]
    chunks = wide // width
    half_width = width // 2
    _, quarter, _ = inputs.shape
    length = quarter * n_seq
    blocks = length // BLOCK
    own = length // 2
    own_heads = HEADS // 2
    span, span_ff = n_seq * rows_in, n_seq * rows_ff
    direct = span % 16 == 0 and chips == chunks

    here = jnp.arange(devices, dtype=jnp.int32)[:, None] == device

    def placed(vector):
        return jnp.where(here, vector[None], jnp.zeros((), LOW)).reshape(-1, width)

    q_line, v_line = placed(b_query), placed(b_value)

    pairs = half_width // 128

    def side(at):
        no_line = jnp.zeros((1, width), LOW)
        parts = []
        for pair in range(pairs):
            first = at * half_width + 128 * pair
            lanes = slice(first, first + 128)
            for w, line in ((w_query, q_line), (w_key, no_line), (w_value, v_line)):
                parts.append(jnp.concatenate([w[:, lanes], line[:, lanes]], 0))
        return jnp.pad(jnp.concatenate(parts, 1), ((0, 7), (0, 0)))

    left, right = side(0), side(1)
    keep = jnp.where(core == 0, left, right)
    come = swap(jnp.where(core == 0, right, left))
    shard = jnp.stack([jnp.where(core == 0, keep, come), jnp.where(core == 0, come, keep)])
    qkv_z, first_move = gather_seq(shard)

    packed = jnp.concatenate(
        [w_up[:, width * c : width * c + width] for c in range(chunks)]
        + [w_out, w_down]
        + [placed(v) for v in (b_out, gain_one, shift_one, b_down, gain_two, shift_two, b_up)]
        + [jnp.zeros((16 - 6 - chunks, width), LOW)],
        0,
    )
    wide_z, first_move = gather_seq(tie(packed, first_move))

    whole = []
    for k in range(2):
        lines = sum(p[k, rows_in:].astype(WIDE) for p in qkv_z).astype(LOW)
        whole += [p[k, :rows_in] for p in qkv_z] + [lines, jnp.zeros_like(lines)]
    qkv_parts = gather_chips(jnp.concatenate(whole, 0).reshape(2, span + 16, 3 * half_width))
    lines = sum(jnp.sum(p[:, span].astype(WIDE), 0, keepdims=True) for p in qkv_parts)

    tied_inputs = tie(inputs, first_move)

    def piece_of(s):
        tokens = pick(tied_inputs, s, 0)[0]
        numbers = pick(rand_blocks, s, 0).reshape(-1)
        globs = pick(global_blocks, s, 0).reshape(-1)
        numbers = jnp.concatenate([numbers, globs]).astype(LOW)
        numbers = jnp.pad(numbers, (0, 16 * width - numbers.shape[0])).reshape(16, width)
        return jnp.concatenate([tokens, numbers], 0)

    pieces = bring(piece_of)
    local_blocks = rand_blocks.shape[2]
    count = HEADS * local_blocks * 3
    tokens_own = jnp.concatenate([p[:quarter] for p in pieces], 0)
    numbers = jnp.stack([p[quarter] for p in pieces])
    tokens_other, other_numbers = swap(tokens_own), swap(numbers)
    numbers = jnp.concatenate([numbers, other_numbers], 0).astype(jnp.int32)
    globs = numbers[0, count : count + 2]
    rand = numbers[:, :count].reshape(4, HEADS, local_blocks, 3)
    rand = lax.dynamic_slice_in_dim(rand, core * own_heads, own_heads, 1)
    rand = rand.transpose(1, 0, 2, 3).reshape(own_heads, blocks, 3)
    near, rand, glob_at, bias = tables(rand, globs, blocks)
    tokens = jnp.concatenate([tokens_own, tokens_other], 0)

    rows_a = (chunks + 1) * rows_in
    rows = []
    for c in range(chunks + 1):
        rows += [p[c * rows_in : (c + 1) * rows_in] for p in wide_z]
    rows += [p[rows_a : rows_a + rows_ff] for p in wide_z]
    rows.append(sum(p[rows_a + rows_ff :].astype(WIDE) for p in wide_z).astype(LOW))
    parts = gather_chips(tie(jnp.concatenate(rows, 0), qkv_parts))
    rows_a, rows_b = (chunks + 1) * span, (chunks + 1) * span + span_ff
    at = jnp.stack([lax.axis_index("dp") >> 1, core]).astype(jnp.int32)
    if direct:
        qkv_weights = tuple(qkv_parts)
    else:
        ordered = in_chip_order(qkv_parts)
        qkv_weights = (jnp.concatenate([p[k, :span] for p in ordered for k in range(2)], 0),)

    qkv_first, qkv_rest, w_qkv = project_tokens(at, tokens, lines, qkv_weights, direct)
    mixed_first, log_first = attend(0, near, rand, glob_at, bias, qkv_first)
    mixed_first, qkv_rest, *parts = join(mixed_first, qkv_rest, *parts)
    other_first = swap(mixed_first[own:])
    other_parts = [swap(p) for p in parts]
    mixed_rest, log_rest = attend(1, near, rand, glob_at, bias, qkv_rest)
    vectors = sum(p[rows_b:].astype(WIDE) for p in parts + other_parts)
    if direct:
        weights = tuple(parts + other_parts)
    else:
        weights = (
            jnp.stack(
                [
                    in_device_order(
                        *([p[span * c : span * c + span] for p in ps] for ps in (parts, other_parts))
                    )
                    for c in range(chunks + 1)
                ]
            ),
            in_device_order(*([p[rows_a:rows_b] for p in ps] for ps in (parts, other_parts))),
        )
    tied_cotangent = tie(cotangent, tokens_own)
    grad_result = jnp.concatenate(bring(lambda s: pick(tied_cotangent, s, 0)[0]), 0)
    result, grad_first, mine, theirs, grad_keep, grad_send, grad_vectors = token_layer(
        at,
        (mixed_first, mixed_rest),
        (other_first, swap(mixed_rest[own:])),
        tokens_own,
        grad_result,
        vectors,
        weights,
        direct,
    )
    come = swap(theirs)
    output = send_back(result)

    if not direct:
        parts_a = grad_keep.reshape(chunks + 1, chips, 2, span, width)
        parts_b = grad_send.reshape(chips, 2, span_ff, width)
        vector_rows = jnp.broadcast_to(grad_vectors.astype(LOW), (chips, 16, width))
        grad_keep, grad_send = (
            jnp.concatenate(
                [pick(parts_a[c], which, 1)[:, 0] for c in range(chunks + 1)]
                + [pick(parts_b, which, 1)[:, 0], vector_rows],
                1,
            )
            for which in (core, 1 - core)
        )
    grad_other = swap(grad_send)

    back_first = attend_back(0, near, rand, glob_at, bias, log_first, qkv_first, mine, come)
    back_first, grad_other = join(back_first, grad_other)
    chip_sums = added(grad_keep, grad_other)
    qkv_rest, chip_sums = join(qkv_rest, chip_sums)
    own_sums = reduce_chips(chip_sums)
    grad_qkv, grad_own, grad_theirs, sums = attend_back(
        1, near, rand, glob_at, bias, log_rest, qkv_rest, mine, come, back_first, w_qkv
    )
    come = swap(grad_theirs)
    grad_qkv, own_sums = join(grad_qkv, own_sums)
    grad_tokens = (grad_first + grad_own + come.astype(WIDE)).astype(LOW)
    grad_inputs = send_back(grad_tokens)
    grad_w_qkv = dot(tokens, grad_qkv, TN).astype(LOW)
    lines = jnp.broadcast_to(sums.astype(LOW), (chips, 2, n_seq, 8, 3 * half_width))
    parts = jnp.concatenate(
        [grad_w_qkv.reshape(chips, 2, n_seq, rows_in, 3 * half_width), lines], 3
    )
    own_qkv = reduce_seq(reduce_chips(parts).transpose(1, 0, 2, 3))
    come = swap(pick(own_qkv, 1 - core, 0))[0]
    keep = pick(own_qkv, core, 0)[0]
    left, right = jnp.where(core == 0, keep, come), jnp.where(core == 0, come, keep)

    by_seq = own_sums[:rows_a].reshape(chunks + 1, n_seq, rows_in, width)
    by_seq = jnp.concatenate(
        [by_seq[c] for c in range(chunks + 1)]
        + [
            own_sums[rows_a:rows_b].reshape(n_seq, rows_ff, width),
            jnp.broadcast_to(own_sums[rows_b:], (n_seq, 16, width)),
        ],
        1,
    )
    own_sums = reduce_seq(by_seq)
    rows_a = (chunks + 1) * rows_in
    own_up = jnp.concatenate(
        [own_sums[c * rows_in : (c + 1) * rows_in] for c in range(chunks)], 1
    )
    small = own_sums[rows_a + rows_ff :]

    def joined(k, rows):
        lanes = [lanes_of(k, pair) for pair in range(pairs)]
        return jnp.concatenate([one[rows, at] for one in (left, right) for at in lanes], 1)

    def own_part(vector, size):
        return lax.dynamic_slice_in_dim(vector.reshape(-1), device * size, size, 0)

    matrix_rows, line = slice(0, rows_in), slice(rows_in, rows_in + 1)
    return (
        output,
        grad_inputs,
        joined(0, matrix_rows),
        own_part(joined(0, line), rows_in),
        joined(1, matrix_rows),
        joined(2, matrix_rows),
        own_part(joined(2, line), rows_in),
        own_sums[chunks * rows_in : rows_a],
        own_part(small[0], rows_in),
        own_part(small[1], rows_in),
        own_part(small[2], rows_in),
        own_up,
        own_part(small[6 : 6 + chunks], rows_ff),
        own_sums[rows_a : rows_a + rows_ff],
        own_part(small[3], rows_in),
        own_part(small[4], rows_in),
        own_part(small[5], rows_in),
    )


def solution(mesh):
    both = ("dp", "seq")
    matrix, vector = P(both, None), P(both)
    tokens = P("dp", "seq", None)
    return jax.shard_map(
        shards,
        mesh=mesh,
        in_specs=(tokens, tokens, P("dp", None, "seq", None), P("dp", None))
        + (matrix, vector, matrix, matrix, vector, matrix, vector, vector, vector)
        + (matrix, vector, matrix, vector, vector, vector),
        out_specs=(tokens, tokens)
        + (matrix, vector, matrix, matrix, vector, matrix, vector, vector, vector)
        + (matrix, vector, matrix, vector, vector, vector),
        check_vma=False,
    )
```

time: 629 us -> 428 us (0.68)
  matrix products: 99.6 us -> 6.12 us
  Pallas kernels: 55.8 us -> 144 us
  waiting for transfers between devices: 168 us -> 86.2 us
  local copies, waits for them, and re-layouts: 88.2 us -> 49.2 us
  other arithmetic: 67.4 us -> 32.2 us
  starting transfers between devices: 124 us -> 98.6 us
  between operations: 17.3 us -> 3.32 us
    dot_general x12 -> x1, matrix products: 99.6 us -> 6.12 us  [dot(): return lax.dot_general(left, right, dims, preferred_element_type=WIDE)]
    pallas_call x2 -> x6, Pallas kernels: 55.8 us -> 144 us  [the longest x1 61.1 us: token_layer(): pl.pallas_call(partial(token_kernel, 256, chips, direct), out_shape=(jax....]
    ppermute x26 -> x20, waiting for transfers between devices: 104 us -> 50.6 us  [the longest x12 31.1 us: flip_chip(): return lax.ppermute(array, 'dp', [(i, i ^ 2 * away) for i in range(size)])]
    ppermute x15 -> x8, waiting for transfers between devices: 63.8 us -> 35.5 us  [flip_seq(): return lax.ppermute(array, 'seq', [(i, i ^ k) for i in range(size)])]
    ppermute x26 -> x20, starting transfers between devices: 54.3 us -> 26.5 us  [the longest x12 14.1 us: flip_chip(): return lax.ppermute(array, 'dp', [(i, i ^ 2 * away) for i in range(size)])]
    reduce_sum x11 -> x4, other arithmetic: 14.4 us -> 0.1 us  [shards(): jnp.sum(p[:, span].astype(WIDE), 0, keepdims=True)]
    reshape x17 -> x6, local copies, waits for them, and re-layouts: 13.4 us -> 0.84 us  [the longest x2 0.37 us: piece_of(): numbers = pick(rand_blocks, s, 0).reshape(-1)]
    convert_element_type x17 -> x7, other arithmetic: 19.7 us -> 7.28 us  [the longest x4 5.94 us: added(): return sum((array.astype(WIDE) for array in arrays)).astype(LOW)]
  transfers between devices with their start and end apart: 51 -> 41, of which waited for: 19 -> 14; matrix products, arithmetic and copies ran while one was open for 22% -> 16% of each run, Pallas kernels for 9% -> 20%
where the time goes in v2:
time: 428 us; the launch traced here: 420 us
  Pallas kernels  144 us (34%)
  starting transfers between devices  98.6 us (23%)
  waiting for transfers between devices  86.2 us (20%)
  local copies, waits for them, and re-layouts  49.2 us (11%)
  other arithmetic  32.2 us (8%)
  matrix products  6.12 us (1%)
    pallas_call x1, Pallas kernels, token_layer(): pl.pallas_call(partial(token_kernel, 256, chips, direct), out_shape=(jax....  61.1 us
    pallas_call x2, Pallas kernels, attend_back(): pl.pallas_call(partial(attend_back_kernel, first_pair, pairs, blocks, 4 /...  49.5 us
    ppermute x8, starting transfers between devices, flip_seq(): return lax.ppermute(array, 'seq', [(i, i ^ k) for i in range(size)])  38.2 us
    ppermute x8, waiting for transfers between devices, flip_seq(): return lax.ppermute(array, 'seq', [(i, i ^ k) for i in range(size)])  35.5 us
    ppermute x13, starting transfers between devices, swap(): return lax.ppermute(array, 'dp', [(i, i ^ 1) for i in range(size)])  33.8 us
    ppermute x12, waiting for transfers between devices, flip_chip(): return lax.ppermute(array, 'dp', [(i, i ^ 2 * away) for i in range(size)])  31.1 us
    pallas_call x2, Pallas kernels, attend(): pl.pallas_call(partial(attend_kernel, first_pair, pairs, blocks, 8 // pai...  22 us
    unnamed x130, local copies, waits for them, and re-layouts  21.9 us
  transfers between devices with their start and end apart: 41, of which 14 were waited for; matrix products, arithmetic and copies ran while one was open for 16% of the time, Pallas kernels for 20%

profile of v2, /device:TPU:0, one launch (start us, length us, event | category | flops | bytes accessed | tf_op | source)
XLA Modules:
  0.0 419.7 jit_solution(9638336982404149312)
XLA Ops:
  8.9 4.7 %collective-permute-start.1 = (bf16[2,32,1152]{2,1,0:T(8,128)(2,1)S(1)}, bf16[2,32,1152]{2,1,0:T(8,128)(2,1)S(1)}, u32[]{:S(2)}, u32[]{:S(2)}) collective-permute-start(bf16[2,32,1152]{2,1,0:T(8,128)(2,1)S(1)} %get-tuple-element.168), channel_id=1, source_target_pairs={{0,3},{1,2},{2,1},{3,0},{4,7},{5,6},{6,5},{7,4},{8,11},{9,10},{10,... | collective-permute-start | bytes 442376 | tf_op jit(solution)/shard_map/ppermute | solution.py:35
  13.6 4.6 %collective-permute-done.1 = bf16[2,32,1152]{2,1,0:T(8,128)(2,1)S(1)} collective-permute-done((bf16[2,32,1152]{2,1,0:T(8,128)(2,1)S(1)}, bf16[2,32,1152]{2,1,0:T(8,128)(2,1)S(1)}, u32[]{:S(2)}, u32[]{:S(2)}) %collective-permute-start.1) | collective-permute-done | bytes 147488 | tf_op jit(solution)/shard_map/ppermute | solution.py:35
  24.0 4.5 %collective-permute-done.7 = bf16[2,2,32,1152]{3,2,1,0:T(8,128)(2,1)S(1)} collective-permute-done((bf16[2,2,32,1152]{3,2,1,0:T(8,128)(2,1)S(1)}, bf16[2,2,32,1152]{3,2,1,0:T(8,128)(2,1)S(1)}, u32[]{:S(2)}, u32[]{:S(2)}) %collective-permute-start.7) | collective-permute-done | bytes 294944 | tf_op jit(solution)/shard_map/ppermute | solution.py:35
  32.4 5.5 %collective-permute-done.2 = bf16[232,768]{1,0:T(8,128)(2,1)S(1)} collective-permute-done((bf16[232,768]{1,0:T(8,128)(2,1)S(1)}, bf16[232,768]{1,0:T(8,128)(2,1)S(1)}, u32[]{:S(2)}, u32[]{:S(2)}) %collective-permute-start.2) | collective-permute-done | bytes 356384 | tf_op jit(solution)/shard_map/ppermute | solution.py:35
  45.3 7.8 %collective-permute-done.9.refs_2_ = bf16[2,112,1152]{2,1,0:T(8,128)(2,1)S(1)} collective-permute-done((bf16[2,112,1152]{2,1,0:T(8,128)(2,1)S(1)}, bf16[2,112,1152]{2,1,0:T(8,128)(2,1)S(1)}, u32[]{:S(2)}, u32[]{:S(2)}) %collective-permute-start.9) | collective-permute-done | bytes 516128 | tf_op jit(solution)/shard_map/ppermute | solution.py:90
  53.3 14.9 %collective-permute-done.11 = bf16[2,232,768]{2,1,0:T(8,128)(2,1)S(1)} collective-permute-done((bf16[2,232,768]{2,1,0:T(8,128)(2,1)S(1)}, bf16[2,232,768]{2,1,0:T(8,128)(2,1)S(1)}, u32[]{:S(2)}, u32[]{:S(2)}) %collective-permute-start.11) | collective-permute-done | bytes 712736 | tf_op jit(solution)/shard_map/ppermute | solution.py:35
  99.4 7.6 %collective-permute-start.17 = (bf16[512,768]{1,0:T(8,128)(2,1)}, bf16[512,768]{1,0:T(8,128)(2,1)}, u32[]{:S(2)}, u32[]{:S(2)}) collective-permute-start(bf16[512,768]{1,0:T(8,128)(2,1)} %get-tuple-element.99), channel_id=1, source_target_pairs={{0,0},{1,1},{2,4},{3,5},{4,2},{5,3},{6,6},{7,7},{8,8},{9,9},{10,12... | collective-permute-start | bytes 2359304 | tf_op jit(solution)/shard_map/ppermute | solution.py:52
  115.1 11.5 %project.1 = (bf16[2048,384]{1,0:T(8,128)(2,1)S(1)}, bf16[2048,768]{1,0:T(8,128)(2,1)}, bf16[768,1152]{1,0:T(8,128)(2,1)S(1)}) custom-call(s32[2]{0:T(128)S(1)} %pad_add_fusion.at_ref, bf16[2048,768]{1,0:T(8,128)(2,1)} %pad_maximum_fusion.tokens_ref, f32[1,1152]{1,0:T(1,128)S(1)} %add.453.b_ref, bf16[2,112,1152]{2,1,0:T(8,128)(2,1)S(1)} %bitcast.226, ...), custom_call_target="tpu_custom_call" | custom-call | flops 4000000000 | bytes 12000000 | tf_op jit(solution)/shard_map/project/pallas_call | solution.py:604
  127.9 8.2 %attend.2 = (bf16[2048,128]{1,0:T(8,128)(2,1)S(1)}, f32[32,8,128]{2,1,0:T(8,128)S(1)}) custom-call(s32[64]{0:T(128)S(1)} %pad_add_fusion.1.near_ref, s32[576]{0:T(1024)S(1)} %fusion.21.rand_ref, s32[2]{0:T(128)S(1)} %fusion.40.glob_ref, f32[32,3,8,128]{3,2,1,0:T(8,128)S(1)} %reshape.583.bias_ref, bf16[2048,384]{1,0:T(8,128)(2,1)S(1)} %get-tuple-element.52.qkv_ref), custom_call_target="tpu_custom_call" | custom-call | flops 6000000000 | bytes 3000000 | tf_op jit(solution)/shard_map/attend/pallas_call | solution.py:625
  136.1 5.4 %collective-permute-done.13.refs_2_ = bf16[880,768]{1,0:T(8,128)(2,1)} collective-permute-done((bf16[880,768]{1,0:T(8,128)(2,1)}, bf16[880,768]{1,0:T(8,128)(2,1)}, u32[]{:S(2)}, u32[]{:S(2)}) %collective-permute-start.13) | collective-permute-done | bytes 1351712 | tf_op jit(solution)/shard_map/ppermute | solution.py:90
  144.8 13.8 %attend.3 = (bf16[2048,256]{1,0:T(8,128)(2,1)S(1)}, f32[32,8,128]{2,1,0:T(8,128)S(1)}) custom-call(s32[64]{0:T(128)S(1)} %pad_add_fusion.1.near_ref, s32[576]{0:T(1024)S(1)} %fusion.21.rand_ref, s32[2]{0:T(128)S(1)} %fusion.40.glob_ref, f32[32,3,8,128]{3,2,1,0:T(8,128)S(1)} %reshape.583.bias_ref, bf16[2048,768]{1,0:T(8,128)(2,1)S(1)} %copy-done.7), custom_call_target="tpu_custom_call" | custom-call | flops 12000000000 | bytes 6000000 | tf_op jit(solution)/shard_map/attend/pallas_call | solution.py:625
  168.2 61.1 %token_layer.1 = (bf16[1024,768]{1,0:T(8,128)(2,1)}, f32[1024,768]{1,0:T(8,128)}, bf16[1024,384]{1,0:T(8,128)(2,1)}, bf16[1024,384]{1,0:T(8,128)(2,1)}, bf16[4,8...) custom-call(s32[2]{0:T(128)} %copy-done.5, bf16[2048,128]{1,0:T(8,128)(2,1)} %copy-done.2, ...), custom_call_target="tpu_custom_call" | custom-call | flops 35999997952 | bytes 32000000 | tf_op jit(solution)/shard_map/token_layer/pallas_call | solution.py:684
  235.5 18.0 %collective-permute-done.23 = bf16[512,768]{1,0:T(8,128)(2,1)S(1)} collective-permute-done((bf16[512,768]{1,0:T(8,128)(2,1)S(1)}, bf16[512,768]{1,0:T(8,128)(2,1)S(1)}, u32[]{:S(2)}, u32[]{:S(2)}) %collective-permute-start.23) | collective-permute-done | bytes 786464 | tf_op jit(solution)/shard_map/ppermute | solution.py:59
  255.9 14.3 %attend_back.2.refs_0_ = bf16[2048,384]{1,0:T(8,128)(2,1)} custom-call(s32[64]{0:T(128)} %copy-done.6, s32[576]{0:T(1024)} %copy-done.3, s32[2]{0:T(128)} %copy-done.4, f32[32,3,8,128]{3,2,1,0:T(8,128)} %copy-done, f32[32,8,128]{2,1,0:T(8,128)} %copy-done.10, bf16[2048,384]{1,0:T(8,128)(2,1)} %copy-done.9, bf16[1024,384]{1,0:T(8,128)(2,1)} %get-tuple-element.69.mine_ref, ...), custom_call_target="tpu_custom_call" | custom-call | flops 12000000000 | bytes 6000000 | tf_op jit(solution)/shard_map/attend_back/pallas_call | solution.py:653
  270.2 5.5 %add_convert_fusion = bf16[4,880,768]{2,1,0:T(8,128)(2,1)S(1)} fusion(bf16[4,880,768]{2,1,0:T(8,128)(2,1)} %collective-permute-done.26, bf16[4,880,768]{2,1,0:T(8,128)(2,1)} %get-tuple-element.67), kind=kLoop, calls=%fused_computation | loop fusion | flops 10813440 | bytes 16220160 | tf_op jit(solution)/shard_map/convert_element_type | solution.py:123
  281.0 35.2 %attend_back.3 = (bf16[2048,1152]{1,0:T(8,128)(2,1)}, f32[1024,768]{1,0:T(8,128)}, bf16[1024,768]{1,0:T(8,128)(2,1)}, f32[1,1152]{1,0:T(1,128)}) custom-call(s32[64]{0:T(128)} %copy-done.6, s32[576]{0:T(1024)} %copy-done.3, s32[2]{0:T(128)} %copy-done.4, f32[32,3,8,128]{3,2,1,0:T(8,128)} %copy-done, f32[32,8,128]{2,1,0:T(8,128)} %copy-done.11, ...), custom_call_target="tpu_custom_call" | custom-call | flops 24000000000 | bytes 12000000 | tf_op jit(solution)/shard_map/attend_back/pallas_call | solution.py:653
  316.2 12.4 %collective-permute-start.27 = (bf16[1024,768]{1,0:T(8,128)(2,1)}, bf16[1024,768]{1,0:T(8,128)(2,1)S(1)}, u32[]{:S(2)}, u32[]{:S(2)}) collective-permute-start(bf16[1024,768]{1,0:T(8,128)(2,1)} %get-tuple-element.77), channel_id=1, source_target_pairs={{0,4},{4,0},{8,12},{12,8},{16,20},{20,16},{24,28},{28,24},{1,5},{5... | collective-permute-start | bytes 4718600 | tf_op jit(solution)/shard_map/ppermute | solution.py:30
  335.8 6.1 %convolution_convert_fusion = bf16[768,1152]{1,0:T(8,128)(2,1)S(1)} fusion(bf16[2048,1152]{1,0:T(8,128)(2,1)S(1)} %copy-done.33, bf16[1024,768]{1,0:T(8,128)(2,1)} %collective-permute-done.6, bf16[512,768]{1,0:T(8,128)(2,1)} %slice.702, bf16[512,768]{1,0:T(8,128)(2,1)S(1)} %slice.701), kind=kOutput, calls=%fused_computation.5 | convolution fusion | flops 3634200576 | bytes 9633792 | tf_op jit(solution)/shard_map/dot_general | solution.py:25
  347.4 4.7 %collective-permute-done.33 = bf16[1,2,4,32,1152]{4,3,1,2,0:T(8,128)(2,1)S(1)} collective-permute-done((bf16[1,2,4,32,1152]{4,3,1,2,0:T(8,128)(2,1)S(1)}, bf16[1,2,4,32,1152]{4,3,1,2,0:T(8,128)(2,1)S(1)}, u32[]{:S(2)}, u32[]{:S(2)}) %collective-permute-start.33) | collective-permute-done | bytes 589856 | tf_op jit(solution)/shard_map/ppermute | solution.py:90
  352.8 8.1 %collective-permute-done.34 = bf16[1,2,4,32,1152]{4,3,1,2,0:T(8,128)(2,1)S(1)} collective-permute-done((bf16[1,2,4,32,1152]{4,3,1,2,0:T(8,128)(2,1)S(1)}, bf16[1,2,4,32,1152]{4,3,1,2,0:T(8,128)(2,1)S(1)}, u32[]{:S(2)}, u32[]{:S(2)}) %collective-permute-start.34) | collective-permute-done | bytes 589856 | tf_op jit(solution)/shard_map/ppermute | solution.py:90
  365.5 12.7 %collective-permute-start.40 = (bf16[232,768]{1,0:T(8,128)(2,1)S(1)}, bf16[232,768]{1,0:T(8,128)(2,1)S(1)}, u32[]{:S(2)}, u32[]{:S(2)}) collective-permute-start(bf16[232,768]{1,0:T(8,128)(2,1)S(1)} %fusion.5), channel_id=1, source_target_pairs={{0,3},{1,2},{2,1},{3,0},{4,7},{5,6},{6,5},{7,4},{8,11},{9,10},{10,... | collective-permute-start | bytes 1069064 | tf_op jit(solution)/shard_map/ppermute | solution.py:35
  378.3 13.0 %collective-permute-start.37 = (bf16[2,32,1152]{2,1,0:T(8,128)(2,1)S(1)}, bf16[2,32,1152]{2,1,0:T(8,128)(2,1)S(1)}, u32[]{:S(2)}, u32[]{:S(2)}) collective-permute-start(bf16[2,32,1152]{2,1,0:T(8,128)(2,1)S(1)} %fusion.6), channel_id=1, source_target_pairs={{0,3},{1,2},{2,1},{3,0},{4,7},{5,6},{6,5},{7,4},{8,11},{9,10},{10,... | collective-permute-start | bytes 442376 | tf_op jit(solution)/shard_map/ppermute | solution.py:35
  392.7 6.0 %collective-permute-done.37 = bf16[2,32,1152]{2,1,0:T(8,128)(2,1)S(1)} collective-permute-done((bf16[2,32,1152]{2,1,0:T(8,128)(2,1)S(1)}, bf16[2,32,1152]{2,1,0:T(8,128)(2,1)S(1)}, u32[]{:S(2)}, u32[]{:S(2)}) %collective-permute-start.37) | collective-permute-done | bytes 147488 | tf_op jit(solution)/shard_map/ppermute | solution.py:35
  398.8 12.3 %collective-permute-start.38 = (f32[1,32,1152]{2,1,0:T(8,128)S(1)}, f32[1,32,1152]{2,1,0:T(8,128)S(1)}, u32[]{:S(2)}, u32[]{:S(2)}) collective-permute-start(f32[1,32,1152]{2,1,0:T(8,128)S(1)} %constant_dynamic-slice_fusion.10), channel_id=1, source_target_pairs={{0,4},{4,0},{8,12},{12,8},{16,20},{20,16},{24,28},{28,24},{1,5},{5... | collective-permute-start | bytes 442376 | tf_op jit(solution)/shard_map/ppermute | solution.py:30
  (343 shorter events, 118.4 us)
Async XLA Ops:
  31.4 21.9 %collective-permute-start.8 = (bf16[2,112,1152]{2,1,0:T(8,128)(2,1)S(1)}, bf16[2,112,1152]{2,1,0:T(8,128)(2,1)S(1)}, u32[]{:S(2)}, u32[]{:S(2)}) collective-permute-start(bf16[2,112,1152]{2,1,0:T(8,128)(2,1)S(1)} %bitcast.223), channel_id=1, source_target_pairs={{0,8},{4,12},{8,0},{12,4},{16,24},{20,28},{24,16},{28,20},{1,9},{5... | collective-permute-start | bytes 1548296 | tf_op jit(solution)/shard_map/ppermute | solution.py:90
  31.9 21.2 %collective-permute-start.9 = (bf16[2,112,1152]{2,1,0:T(8,128)(2,1)S(1)}, bf16[2,112,1152]{2,1,0:T(8,128)(2,1)S(1)}, u32[]{:S(2)}, u32[]{:S(2)}) collective-permute-start(bf16[2,112,1152]{2,1,0:T(8,128)(2,1)S(1)} %bitcast.224), channel_id=1, source_target_pairs={{0,16},{4,20},{8,24},{12,28},{16,0},{20,4},{24,8},{28,12},{1,17},{... | collective-permute-start | bytes 1548296 | tf_op jit(solution)/shard_map/ppermute | solution.py:90
  38.0 30.1 %collective-permute-start.11 = (bf16[2,232,768]{2,1,0:T(8,128)(2,1)S(1)}, bf16[2,232,768]{2,1,0:T(8,128)(2,1)S(1)}, u32[]{:S(2)}, u32[]{:S(2)}) collective-permute-start(bf16[2,232,768]{2,1,0:T(8,128)(2,1)S(1)} %pad_maximum_fusion.7), channel_id=1, source_target_pairs={{0,1},{1,0},{2,3},{3,2},{4,5},{5,4},{6,7},{7,6},{8,9},{9,8},{10,11... | collective-permute-start | bytes 2138120 | tf_op jit(solution)/shard_map/ppermute | solution.py:35
  40.3 51.1 %collective-permute-start.4 = (bf16[528,768]{1,0:T(8,128)(2,1)}, bf16[528,768]{1,0:T(8,128)(2,1)}, u32[]{:S(2)}, u32[]{:S(2)}) collective-permute-start(bf16[528,768]{1,0:T(8,128)(2,1)} %pad_maximum_fusion.6), channel_id=1, source_target_pairs={{0,1},{1,0},{2,5},{3,4},{4,3},{5,2},{6,7},{7,6},{8,9},{9,8},{10,13... | collective-permute-start | bytes 2433032 | tf_op jit(solution)/shard_map/ppermute | solution.py:52
  44.5 42.8 %collective-permute-start.3 = (bf16[528,768]{1,0:T(8,128)(2,1)S(1)}, bf16[528,768]{1,0:T(8,128)(2,1)S(1)}, u32[]{:S(2)}, u32[]{:S(2)}) collective-permute-start(bf16[528,768]{1,0:T(8,128)(2,1)S(1)} %pad_maximum_fusion.5), channel_id=1, source_target_pairs={{0,0},{1,1},{2,4},{3,5},{4,2},{5,3},{6,6},{7,7},{8,8},{9,9},{10,12... | collective-permute-start | bytes 2433032 | tf_op jit(solution)/shard_map/ppermute | solution.py:52
  83.9 52.2 %collective-permute-start.12 = (bf16[880,768]{1,0:T(8,128)(2,1)}, bf16[880,768]{1,0:T(8,128)(2,1)}, u32[]{:S(2)}, u32[]{:S(2)}) collective-permute-start(bf16[880,768]{1,0:T(8,128)(2,1)} %constant_dynamic-update-slice_fusion.38.refs_0_), channel_id=1, source_target_pairs={{0,8},{4,12},{8,0},{12,4},{16,24},{20,28},{24,16},{28,20},{1,9},{5... | collective-permute-start | bytes 4055048 | tf_op jit(solution)/shard_map/ppermute | solution.py:90
  85.4 56.1 %collective-permute-start.13 = (bf16[880,768]{1,0:T(8,128)(2,1)}, bf16[880,768]{1,0:T(8,128)(2,1)}, u32[]{:S(2)}, u32[]{:S(2)}) collective-permute-start(bf16[880,768]{1,0:T(8,128)(2,1)} %constant_dynamic-update-slice_fusion.38.refs_0_), channel_id=1, source_target_pairs={{0,16},{4,20},{8,24},{12,28},{16,0},{20,4},{24,8},{28,12},{1,17},{... | collective-permute-start | bytes 4055048 | tf_op jit(solution)/shard_map/ppermute | solution.py:90
  86.9 54.6 %collective-permute-start.14 = (bf16[880,768]{1,0:T(8,128)(2,1)}, bf16[880,768]{1,0:T(8,128)(2,1)}, u32[]{:S(2)}, u32[]{:S(2)}) collective-permute-start(bf16[880,768]{1,0:T(8,128)(2,1)} %constant_dynamic-update-slice_fusion.38.refs_0_), channel_id=1, source_target_pairs={{0,24},{4,28},{8,16},{12,20},{16,8},{20,12},{24,0},{28,4},{1,25},{... | collective-permute-start | bytes 4055048 | tf_op jit(solution)/shard_map/ppermute | solution.py:90
  99.4 44.9 %collective-permute-start.17 = (bf16[512,768]{1,0:T(8,128)(2,1)}, bf16[512,768]{1,0:T(8,128)(2,1)}, u32[]{:S(2)}, u32[]{:S(2)}) collective-permute-start(bf16[512,768]{1,0:T(8,128)(2,1)} %get-tuple-element.99), channel_id=1, source_target_pairs={{0,0},{1,1},{2,4},{3,5},{4,2},{5,3},{6,6},{7,7},{8,8},{9,9},{10,12... | collective-permute-start | bytes 2359304 | tf_op jit(solution)/shard_map/ppermute | solution.py:52
  141.6 23.1 %collective-permute-start.20 = (bf16[880,768]{1,0:T(8,128)(2,1)}, bf16[880,768]{1,0:T(8,128)(2,1)S(1)}, u32[]{:S(2)}, u32[]{:S(2)}) collective-permute-start(bf16[880,768]{1,0:T(8,128)(2,1)} %collective-permute-done.12.refs_1_), channel_id=1, source_target_pairs={{0,4},{4,0},{8,12},{12,8},{16,20},{20,16},{24,28},{28,24},{1,5},{5... | collective-permute-start | bytes 4055048 | tf_op jit(solution)/shard_map/ppermute | solution.py:30
  144.3 20.4 %collective-permute-start.21 = (bf16[880,768]{1,0:T(8,128)(2,1)}, bf16[880,768]{1,0:T(8,128)(2,1)S(1)}, u32[]{:S(2)}, u32[]{:S(2)}) collective-permute-start(bf16[880,768]{1,0:T(8,128)(2,1)} %collective-permute-done.13.refs_2_), channel_id=1, source_target_pairs={{0,4},{4,0},{8,12},{12,8},{16,20},{20,16},{24,28},{28,24},{1,5},{5... | collective-permute-start | bytes 4055048 | tf_op jit(solution)/shard_map/ppermute | solution.py:30
  144.3 20.5 %collective-permute-start.22 = (bf16[880,768]{1,0:T(8,128)(2,1)}, bf16[880,768]{1,0:T(8,128)(2,1)S(1)}, u32[]{:S(2)}, u32[]{:S(2)}) collective-permute-start(bf16[880,768]{1,0:T(8,128)(2,1)} %collective-permute-done.14.refs_3_), channel_id=1, source_target_pairs={{0,4},{4,0},{8,12},{12,8},{16,20},{20,16},{24,28},{28,24},{1,5},{5... | collective-permute-start | bytes 4055048 | tf_op jit(solution)/shard_map/ppermute | solution.py:30
  229.3 40.9 %collective-permute-start.26 = (bf16[4,880,768]{2,1,0:T(8,128)(2,1)}, bf16[4,880,768]{2,1,0:T(8,128)(2,1)}, u32[]{:S(2)}, u32[]{:S(2)}) collective-permute-start(bf16[4,880,768]{2,1,0:T(8,128)(2,1)} %get-tuple-element.71), channel_id=1, source_target_pairs={{0,4},{4,0},{8,12},{12,8},{16,20},{20,16},{24,28},{28,24},{1,5},{5... | collective-permute-start | bytes 16220168 | tf_op jit(solution)/shard_map/ppermute | solution.py:30
  230.9 22.6 %collective-permute-start.23 = (bf16[512,768]{1,0:T(8,128)(2,1)S(1)}, bf16[512,768]{1,0:T(8,128)(2,1)S(1)}, u32[]{:S(2)}, u32[]{:S(2)}) collective-permute-start(bf16[512,768]{1,0:T(8,128)(2,1)S(1)} %get-tuple-element.97), channel_id=1, source_target_pairs={{1,0},{0,1},{5,2},{4,3},{3,4},{2,5},{7,6},{6,7},{9,8},{8,9},{13,10... | collective-permute-start | bytes 2359304 | tf_op jit(solution)/shard_map/ppermute | solution.py:59
  231.0 22.5 %collective-permute-start.24 = (bf16[512,768]{1,0:T(8,128)(2,1)S(1)}, bf16[512,768]{1,0:T(8,128)(2,1)}, u32[]{:S(2)}, u32[]{:S(2)}) collective-permute-start(bf16[512,768]{1,0:T(8,128)(2,1)S(1)} %get-tuple-element.98), channel_id=1, source_target_pairs={{0,0},{1,1},{4,2},{5,3},{2,4},{3,5},{6,6},{7,7},{8,8},{9,9},{12,10... | collective-permute-start | bytes 2359304 | tf_op jit(solution)/shard_map/ppermute | solution.py:59
  232.6 23.4 %collective-permute-start.25 = (bf16[1024,384]{1,0:T(8,128)(2,1)}, bf16[1024,384]{1,0:T(8,128)(2,1)}, u32[]{:S(2)}, u32[]{:S(2)}) collective-permute-start(bf16[1024,384]{1,0:T(8,128)(2,1)} %get-tuple-element.70), channel_id=1, source_target_pairs={{0,4},{4,0},{8,12},{12,8},{16,20},{20,16},{24,28},{28,24},{1,5},{5... | collective-permute-start | bytes 2359304 | tf_op jit(solution)/shard_map/ppermute | solution.py:30
  277.5 51.8 %collective-permute-start.30 = (bf16[1,880,768]{2,1,0:T(8,128)(2,1)}, bf16[1,880,768]{2,1,0:T(8,128)(2,1)}, u32[]{:S(2)}, u32[]{:S(2)}) collective-permute-start(bf16[1,880,768]{2,1,0:T(8,128)(2,1)} %get-tuple-element.85), channel_id=1, source_target_pairs={{0,8},{4,12},{8,0},{12,4},{16,24},{20,28},{24,16},{28,20},{1,9},{5... | collective-permute-start | bytes 4055048 | tf_op jit(solution)/shard_map/ppermute | solution.py:90
  278.2 51.1 %collective-permute-start.31 = (bf16[1,880,768]{2,1,0:T(8,128)(2,1)}, bf16[1,880,768]{2,1,0:T(8,128)(2,1)}, u32[]{:S(2)}, u32[]{:S(2)}) collective-permute-start(bf16[1,880,768]{2,1,0:T(8,128)(2,1)} %get-tuple-element.87), channel_id=1, source_target_pairs={{0,16},{4,20},{8,24},{12,28},{16,0},{20,4},{24,8},{28,12},{1,17},{... | collective-permute-start | bytes 4055048 | tf_op jit(solution)/shard_map/ppermute | solution.py:90
  279.1 50.2 %collective-permute-start.32 = (bf16[1,880,768]{2,1,0:T(8,128)(2,1)S(1)}, bf16[1,880,768]{2,1,0:T(8,128)(2,1)}, u32[]{:S(2)}, u32[]{:S(2)}) collective-permute-start(bf16[1,880,768]{2,1,0:T(8,128)(2,1)S(1)} %get-tuple-element.86), channel_id=1, source_target_pairs={{0,24},{4,28},{8,16},{12,20},{16,8},{20,12},{24,0},{28,4},{1,25},{... | collective-permute-start | bytes 4055048 | tf_op jit(solution)/shard_map/ppermute | solution.py:90
  316.2 29.5 %collective-permute-start.27 = (bf16[1024,768]{1,0:T(8,128)(2,1)}, bf16[1024,768]{1,0:T(8,128)(2,1)S(1)}, u32[]{:S(2)}, u32[]{:S(2)}) collective-permute-start(bf16[1024,768]{1,0:T(8,128)(2,1)} %get-tuple-element.77), channel_id=1, source_target_pairs={{0,4},{4,0},{8,12},{12,8},{16,20},{20,16},{24,28},{28,24},{1,5},{5... | collective-permute-start | bytes 4718600 | tf_op jit(solution)/shard_map/ppermute | solution.py:30
  334.5 30.9 %collective-permute-start.39 = (bf16[2,232,768]{2,1,0:T(8,128)(2,1)S(1)}, bf16[2,232,768]{2,1,0:T(8,128)(2,1)S(1)}, u32[]{:S(2)}, u32[]{:S(2)}) collective-permute-start(bf16[2,232,768]{2,1,0:T(8,128)(2,1)S(1)} %pad_maximum_fusion.8), channel_id=1, source_target_pairs={{0,1},{1,0},{2,3},{3,2},{4,5},{5,4},{6,7},{7,6},{8,9},{9,8},{10,11... | collective-permute-start | bytes 2138120 | tf_op jit(solution)/shard_map/ppermute | solution.py:35
  346.5 44.8 %collective-permute-start.28 = (bf16[512,768]{1,0:T(8,128)(2,1)S(1)}, bf16[512,768]{1,0:T(8,128)(2,1)S(1)}, u32[]{:S(2)}, u32[]{:S(2)}) collective-permute-start(bf16[512,768]{1,0:T(8,128)(2,1)S(1)} %get-tuple-element.93), channel_id=1, source_target_pairs={{1,0},{0,1},{5,2},{4,3},{3,4},{2,5},{7,6},{6,7},{9,8},{8,9},{13,10... | collective-permute-start | bytes 2359304 | tf_op jit(solution)/shard_map/ppermute | solution.py:59
  352.1 39.2 %collective-permute-start.29 = (bf16[512,768]{1,0:T(8,128)(2,1)S(1)}, bf16[512,768]{1,0:T(8,128)(2,1)S(1)}, u32[]{:S(2)}, u32[]{:S(2)}) collective-permute-start(bf16[512,768]{1,0:T(8,128)(2,1)S(1)} %get-tuple-element.94), channel_id=1, source_target_pairs={{0,0},{1,1},{4,2},{5,3},{2,4},{3,5},{6,6},{7,7},{8,8},{9,9},{12,10... | collective-permute-start | bytes 2359304 | tf_op jit(solution)/shard_map/ppermute | solution.py:59
  365.5 45.6 %collective-permute-start.40 = (bf16[232,768]{1,0:T(8,128)(2,1)S(1)}, bf16[232,768]{1,0:T(8,128)(2,1)S(1)}, u32[]{:S(2)}, u32[]{:S(2)}) collective-permute-start(bf16[232,768]{1,0:T(8,128)(2,1)S(1)} %fusion.5), channel_id=1, source_target_pairs={{0,3},{1,2},{2,1},{3,0},{4,7},{5,6},{6,5},{7,4},{8,11},{9,10},{10,... | collective-permute-start | bytes 1069064 | tf_op jit(solution)/shard_map/ppermute | solution.py:35
  (53 other events, 661.4 us)

commit v3 on v2

v3 whole, which is shorter than its diff:
```python
from functools import partial

import jax
import jax.numpy as jnp
from jax import lax
from jax.experimental import pallas as pl
from jax.experimental.pallas import tpu as pltpu
from jax.sharding import PartitionSpec as P

HEADS = 12
HEAD = 64
BLOCK = 64
SLOTS = 8
EPS = 1e-06
NEG = -1e30
LOW = jnp.bfloat16
WIDE = jnp.float32

NT = (((1,), (1,)), ((), ()))
TN = (((0,), (0,)), ((), ()))
NN = (((1,), (0,)), ((), ()))


def dot(left, right, dims):
    return lax.dot_general(left, right, dims, preferred_element_type=WIDE)


def swap(array):
    size = lax.axis_size("dp")
    return lax.ppermute(array, "dp", [(i, i ^ 1) for i in range(size)])


def flip_seq(array, k):
    size = lax.axis_size("seq")
    return lax.ppermute(array, "seq", [(i, i ^ k) for i in range(size)])


def rounds():
    dp, seq = lax.axis_size("dp"), lax.axis_size("seq")
    for a in range(2):
        pairs = []
        for d in range(dp):
            for z in range(seq):
                to_dp = (d & ~1) | (z >> 1)
                to_seq = 2 * (d & 1) + (a ^ (z & 1))
                pairs.append((d * seq + z, to_dp * seq + to_seq))
        yield a, pairs


def bring(piece_of):
    z = lax.axis_index("seq")
    return [lax.ppermute(piece_of(a ^ (z & 1)), ("dp", "seq"), pairs) for a, pairs in rounds()]


def start_back(rows):
    size = rows.shape[0] // 2
    return [rows[size * a : size * a + size] for a in range(2)]


def finish_back(parts, which):
    a, pairs = list(rounds())[which]
    return lax.ppermute(parts[a], ("dp", "seq"), [(t, s) for s, t in pairs])


def send_back(rows):
    parts = start_back(rows)
    return [finish_back(parts, a) for a in range(2)]


def in_sequences(got):
    odd = (lax.axis_index("seq") & 1) == 1
    return jnp.stack([jnp.where(odd, got[1], got[0]), jnp.where(odd, got[0], got[1])])


def pick(array, index, axis):
    return lax.dynamic_slice_in_dim(array, index, 1, axis)


def gather_seq(shard, before=None):
    mirror = flip_seq(shard, 3)
    pair = jnp.stack([shard, mirror])
    if before is not None:
        pair = tie(pair, before)
    return shard, flip_seq(pair, 1), mirror


def in_seq_order(shard, near, mirror):
    z = lax.axis_index("seq")
    pieces = [shard, near[0], near[1], mirror]
    for bit in range(2):
        set_bit = ((z >> bit) & 1) == 1
        pieces = [
            jnp.where(set_bit, pieces[i ^ (1 << bit)], pieces[i]) for i in range(len(pieces))
        ]
    return pieces


def chip_groups():
    count = (lax.axis_size("dp") // 2).bit_length() - 1
    return [(bit, min(2, count - bit)) for bit in range(0, count, 2)]


def flip_chip(array, away):
    size = lax.axis_size("dp")
    return lax.ppermute(array, "dp", [(i, i ^ (2 * away)) for i in range(size)])


def gather_chips(part):
    parts = [part]
    for bit, bits in chip_groups():
        parts = parts + [flip_chip(p, k << bit) for k in range(1, 1 << bits) for p in parts]
    return parts


def in_chip_order(parts):
    chip = lax.axis_index("dp") >> 1
    parts = jnp.stack(parts)
    return [pick(parts, q ^ chip, 0)[0] for q in range(parts.shape[0])]


def in_device_order(mine, theirs):
    core = lax.axis_index("dp") & 1
    parts = []
    for own, other in zip(in_chip_order(mine), in_chip_order(theirs)):
        parts += [jnp.where(core == 0, own, other), jnp.where(core == 0, other, own)]
    return jnp.concatenate(parts, 0)


def join(*values):
    return lax.optimization_barrier(values)


def gather_quads(upper, lower):
    return [upper, flip_chip(upper, 1), lower, flip_chip(lower, 2)]


def finish_quads(upper, upper_x, lower, lower_y):
    upper, lower = jnp.stack([upper, upper_x]), jnp.stack([lower, lower_y])
    return [upper, flip_chip(upper, 2), lower, flip_chip(lower, 1)]


def tie(values, *others):
    return lax.optimization_barrier((values, others))[0]


def added(*arrays):
    return sum(array.astype(WIDE) for array in arrays).astype(LOW)


def reduce_chips(parts):
    chip = lax.axis_index("dp") >> 1
    for bit, bits in chip_groups():
        ways = 1 << bits
        parts = parts.reshape((-1, ways) + parts.shape[1:])
        mine = (chip >> bit) & (ways - 1)
        others = [flip_chip(pick(parts, mine ^ k, 1)[:, 0], k << bit) for k in range(1, ways)]
        parts = added(pick(parts, mine, 1)[:, 0], *others)
    return parts[0]


def reduce_seq(parts):
    z = lax.axis_index("seq")
    near = flip_seq(jnp.concatenate([pick(parts, z ^ 1, 0), pick(parts, z ^ 2, 0)], 0), 1)
    mirror = added(pick(parts, z ^ 3, 0)[0], near[1])
    return pick(parts, z, 0)[0].astype(WIDE) + near[0].astype(WIDE) + flip_seq(mirror, 3).astype(WIDE)


def norm_parts(summed):
    center = summed - jnp.mean(summed, -1, keepdims=True)
    spread = jnp.mean(center * center, -1, keepdims=True)
    scale = lax.rsqrt(spread + EPS)
    return center * scale, scale


def norm_back(grad, unit, scale, gain):
    grad_unit = grad * gain
    mean_one = jnp.mean(grad_unit, -1, keepdims=True)
    mean_two = jnp.mean(grad_unit * unit, -1, keepdims=True)
    return scale * (grad_unit - mean_one - unit * mean_two)


def gelu_parts(x):
    size = jnp.abs(x)
    t = 1.0 / (1.0 + (0.3275911 * 0.5**0.5) * size)
    bell = jnp.exp(-0.5 * x * x)
    series = 0.5 * 1.061405429
    for factor in (-1.453152027, 1.421413741, -0.284496736, 0.254829592):
        series = series * t + 0.5 * factor
    tail = series * t * bell
    share = jnp.where(x >= 0, 1.0 - tail, tail)
    return x * share, share + x * bell * 0.3989422804014327


def block_rows(ref, block, lanes):
    return ref[pl.ds(pl.multiple_of(block * BLOCK, BLOCK), BLOCK), lanes]


def diagonal(pair_rows, low):
    zero = jnp.zeros_like(pair_rows)
    return jnp.concatenate(
        [jnp.where(low, pair_rows, zero), jnp.where(low, zero, pair_rows)], axis=0
    )


def gather_blocks(ref, ids, lanes, low):
    parts = []
    for one, two in ids:
        if two is None:
            parts.append(block_rows(ref, one, lanes))
        else:
            parts.append(
                jnp.where(low, block_rows(ref, one, lanes), block_rows(ref, two, lanes))
            )
    return jnp.concatenate(parts, axis=0)


def slot_ids(near_ref, rand_ref, globs, i, head, blocks):
    ids = [(near_ref[i], None), (i, None), (near_ref[blocks + i], None)]
    ids += [(globs[0], None), (globs[1], None)]
    for r in range(3):
        ids.append(
            (
                rand_ref[(head * blocks + i) * 3 + r],
                rand_ref[((head + 1) * blocks + i) * 3 + r],
            )
        )
    return ids


def lanes_of(part, pair):
    first = 128 * (3 * pair + part)
    return slice(first, first + 128)


def flat_lanes(pair):
    return slice(128 * pair, 128 * pair + 128)


def start_copies(copies, sems):
    started = [
        pltpu.make_async_copy(source, target, sems.at[k])
        for k, (source, target) in enumerate(copies)
    ]
    for copy in started:
        copy.start()
    return started


def project_kernel(chips, direct, at_ref, *refs):
    pieces, b_ref = refs[:4], refs[4]
    sources, (first_ref, rest_ref, tokens_ref, w_ref, sems) = refs[5:-5], refs[-5:]
    if direct:
        span = w_ref.shape[0] // (2 * chips)
        copies = [
            (
                sources[away].at[k, :span],
                w_ref.at[pl.ds(pl.multiple_of((2 * (at_ref[0] ^ away) + k) * span, span), span)],
            )
            for away in range(chips)
            for k in range(2)
        ]
    else:
        copies = [(sources[0], w_ref)]
    for copy in start_copies(copies, sems):
        copy.wait()
    tile = 256
    lane = lax.broadcasted_iota(jnp.int32, (1, w_ref.shape[1]), 1)
    scale = jnp.where(lane % 384 < 128, HEAD ** (-0.5), 1.0)

    size = pieces[0].shape[0]
    for k, piece_ref in enumerate(pieces):

        def body(at, carry, k=k, piece_ref=piece_ref):
            tokens = piece_ref[pl.ds(pl.multiple_of(at * tile, tile), tile)]
            rows = pl.ds(pl.multiple_of(k * size + at * tile, tile), tile)
            tokens_ref[rows] = tokens
            values = (dot(tokens, w_ref[...], NN) + b_ref[...]).astype(LOW).astype(WIDE)
            values = (values * scale).astype(LOW)
            cut = first_ref.shape[1]
            first_ref[rows] = values[:, :cut]
            rest_ref[rows] = values[:, cut:]
            return carry

        lax.fori_loop(0, size // tile, body, 0, unroll=True)


def attend_kernel(
    first_pair, pairs, blocks, step, near_ref, rand_ref, glob_ref, bias_ref, qkv_ref, out_ref, log_ref
):
    low = lax.broadcasted_iota(jnp.int32, (1, 2 * HEAD), 1) < HEAD
    globs = (glob_ref[0], glob_ref[1])

    def scores_of(i, pair):
        ids = slot_ids(near_ref, rand_ref, globs, i, 2 * (first_pair + pair), blocks)
        queries = diagonal(block_rows(qkv_ref, i, lanes_of(0, pair)), low)
        return dot(gather_blocks(qkv_ref, ids, lanes_of(1, pair), low), queries, NT)

    def softmax_of(i, pair, scores):
        highest = jnp.max(scores, axis=0, keepdims=True)
        weights = jnp.exp(scores - highest)
        total = jnp.sum(weights, axis=0, keepdims=True)
        log_ref[i, pair : pair + 1] = highest + jnp.log(total)
        return (weights * (1.0 / total)).astype(LOW)

    def put(i, pair, mixed):
        at = pl.ds(pl.multiple_of(i * BLOCK, BLOCK), BLOCK)
        out_ref[at, flat_lanes(pair)] = jnp.where(low, mixed[:BLOCK], mixed[BLOCK:]).astype(LOW)

    def body(at, carry):
        units = [(at * step + d, pair) for d in range(step) for pair in range(pairs)]
        scores = [scores_of(*unit) for unit in units]
        probs = []
        for (i, pair), score in zip(units, scores):
            bias = bias_ref[i, first_pair + pair]
            score = jnp.concatenate(
                [score[BLOCK * j : BLOCK * j + BLOCK] + bias[j : j + 1] for j in range(SLOTS)],
                axis=0,
            )
            probs.append(softmax_of(i, pair, score))
        for (i, pair), prob in zip(units, probs):
            ids = slot_ids(near_ref, rand_ref, globs, i, 2 * (first_pair + pair), blocks)
            values = gather_blocks(qkv_ref, ids, lanes_of(2, pair), low)
            put(i, pair, dot(prob, values, TN))
        return carry

    lax.fori_loop(0, blocks // step, body, 0)

    def whole_row(n, carry):
        i = glob_ref[n]
        scores = []
        for pair in range(pairs):
            queries = diagonal(block_rows(qkv_ref, i, lanes_of(0, pair)), low)
            scores.append(dot(qkv_ref[:, lanes_of(1, pair)], queries, NT))
        probs = [softmax_of(i, pair, scores[pair]) for pair in range(pairs)]
        for pair in range(pairs):
            put(i, pair, dot(probs[pair], qkv_ref[:, lanes_of(2, pair)], TN))
        return carry

    lax.fori_loop(0, 2, whole_row, 0)


def attend_back_kernel(
    blocks,
    step,
    near_ref,
    rand_ref,
    glob_ref,
    bias_ref,
    log_first_ref,
    log_rest_ref,
    qkv_first_ref,
    qkv_rest_ref,
    mine_ref,
    come_ref,
    w_ref,
    grad_first_ref,
    out_ref,
    rows_own_ref,
    rows_other_ref,
    sums_ref,
    grad_ref,
    acc_ref,
):
    low = lax.broadcasted_iota(jnp.int32, (1, 2 * HEAD), 1) < HEAD
    globs = (glob_ref[0], glob_ref[1])
    acc_ref[...] = jnp.zeros_like(acc_ref)
    half = mine_ref.shape[0]
    grad_ref[:half] = mine_ref[...]
    grad_ref[half:] = come_ref[...]
    pairs = mine_ref.shape[1] // 128
    cut = qkv_first_ref.shape[1] // 384

    def source(pair, part):
        ref, at = (qkv_first_ref, pair) if pair < cut else (qkv_rest_ref, pair - cut)
        return ref.at[:, lanes_of(part, at)]

    def log_of(i, pair):
        ref, at = (log_first_ref, pair) if pair < cut else (log_rest_ref, pair - cut)
        return ref[i, at : at + 1]

    every = slice(None)

    def add(part, pair, block, value):
        at = pl.ds(pl.multiple_of(block * BLOCK, BLOCK), BLOCK)
        lanes = flat_lanes(2 * pair + part)
        acc_ref[at, lanes] = acc_ref[at, lanes] + value

    def operands(i, pair):
        queries = diagonal(block_rows(source(pair, 0), i, every), low)
        grads = diagonal(block_rows(grad_ref, i, flat_lanes(pair)), low)
        return queries, grads

    def softmax_back(prob, grad_prob):
        scaled = prob * grad_prob
        inner = jnp.sum(scaled, axis=0, keepdims=True)
        return prob.astype(LOW), (scaled - prob * inner).astype(LOW)

    def put(i, pair, mixed):
        at = pl.ds(pl.multiple_of(i * BLOCK, BLOCK), BLOCK)
        out_ref[at, lanes_of(0, pair)] = (
            jnp.where(low, mixed[:BLOCK], mixed[BLOCK:]) * HEAD ** (-0.5)
        ).astype(LOW)

    def body(at, carry):
        units = [(at * step + d, pair) for d in range(step) for pair in range(pairs)]
        first = []
        for i, pair in units:
            ids = slot_ids(near_ref, rand_ref, globs, i, 2 * pair, blocks)
            queries, grads = operands(i, pair)
            first.append(
                (
                    dot(gather_blocks(source(pair, 1), ids, every, low), queries, NT),
                    dot(gather_blocks(source(pair, 2), ids, every, low), grads, NT),
                )
            )
        second = []
        for (i, pair), (score, grad_prob) in zip(units, first):
            shift = bias_ref[i, pair] - log_of(i, pair)
            prob = jnp.concatenate(
                [
                    jnp.exp(score[BLOCK * j : BLOCK * j + BLOCK] + shift[j : j + 1])
                    for j in range(SLOTS)
                ],
                axis=0,
            )
            second.append(softmax_back(prob, grad_prob))
        third = []
        for (i, pair), (prob, grad_score) in zip(units, second):
            ids = slot_ids(near_ref, rand_ref, globs, i, 2 * pair, blocks)
            queries, grads = operands(i, pair)
            keys = gather_blocks(source(pair, 1), ids, every, low)
            put(i, pair, dot(grad_score, keys, TN))
            third.append((dot(grad_score, queries, NN), dot(prob, grads, NN)))
        for (i, pair), values in zip(units, third):
            ids = slot_ids(near_ref, rand_ref, globs, i, 2 * pair, blocks)
            for j, (one, two) in enumerate(ids):
                for part, value in enumerate(values):
                    value = value[BLOCK * j : BLOCK * j + BLOCK]
                    if two is None:
                        add(part, pair, one, value)
                    else:
                        add(part, pair, one, jnp.where(low, value, 0.0))
                        add(part, pair, two, jnp.where(low, 0.0, value))
        return carry

    lax.fori_loop(0, blocks // step, body, 0)

    def whole_row(n, carry):
        i = glob_ref[n]
        first = []
        for pair in range(pairs):
            queries, grads = operands(i, pair)
            first.append(
                (
                    dot(source(pair, 1)[...], queries, NT),
                    dot(source(pair, 2)[...], grads, NT),
                )
            )
        second = []
        for pair, (score, grad_prob) in enumerate(first):
            prob = jnp.exp(score - log_of(i, pair))
            second.append(softmax_back(prob, grad_prob))
        for pair, (prob, grad_score) in enumerate(second):
            queries, grads = operands(i, pair)
            acc_ref[:, flat_lanes(2 * pair)] += dot(grad_score, queries, NN)
            acc_ref[:, flat_lanes(2 * pair + 1)] += dot(prob, grads, NN)
            put(i, pair, dot(grad_score, source(pair, 1)[...], TN))
        return carry

    lax.fori_loop(0, jnp.where(globs[0] == globs[1], 1, 2), whole_row, 0)
    for pair in range(pairs):
        out_ref[:, 384 * pair + 128 : 384 * pair + 384] = acc_ref[
            :, 256 * pair : 256 * pair + 256
        ].astype(LOW)

    sums_ref[...] = jnp.zeros_like(sums_ref)
    tile = 512
    for side, rows_ref in enumerate((rows_own_ref, rows_other_ref)):

        def token_rows(at, carry, side=side, rows_ref=rows_ref):
            grads = out_ref[pl.ds(pl.multiple_of(side * half + at * tile, tile), tile)]
            sums_ref[...] += jnp.sum(grads.astype(WIDE), 0, keepdims=True)
            rows = pl.ds(pl.multiple_of(at * tile, tile), tile)
            total = dot(grads, w_ref[...], NT)
            if side == 0:
                total = total + grad_first_ref[rows].astype(WIDE)
            rows_ref[rows] = total.astype(LOW)
            return carry

        lax.fori_loop(0, half // tile, token_rows, 0)


def pack_kernel(seq, chunks, cut, at_ref, shard_ref, near_ref, mirror_ref, upper_ref, lower_ref):
    rows = shard_ref.shape[0] - 16
    rows_in = rows // (chunks + 4)
    rows_ff = rows - chunks * rows_in
    pieces = [shard_ref, near_ref.at[0], near_ref.at[1], mirror_ref]
    total = sum(piece[rows:].astype(WIDE) for piece in pieces)

    def put(first, value):
        target, first = (upper_ref, first) if first < cut else (lower_ref, first - cut)
        target[first : first + value.shape[0]] = value

    put(rows * seq, total.astype(LOW))
    for z in range(seq):

        @pl.when(at_ref[2] == z)
        def _(z=z):
            for k, piece in enumerate(pieces):
                for c in range(chunks):
                    put((c * seq + (z ^ k)) * rows_in, piece[c * rows_in : c * rows_in + rows_in])
                put(chunks * seq * rows_in + (z ^ k) * rows_ff, piece[chunks * rows_in : rows])


def unpack_kernel(seq, chunks, at_ref, in_ref, down_ref, near_ref, keep_ref):
    rows_in, rows_ff = in_ref.shape[1] // seq, down_ref.shape[0] // seq
    for z in range(seq):

        @pl.when(at_ref[2] == z)
        def _(z=z):
            for k in range(seq):
                target = (keep_ref, near_ref)[k in (1, 2)].at[int(k > 1)]
                first = (z ^ k) * rows_in
                for c in range(chunks):
                    target[c * rows_in : c * rows_in + rows_in] = in_ref[c, first : first + rows_in]
                first = (z ^ k) * rows_ff
                target[chunks * rows_in :] = down_ref[first : first + rows_ff]


def weight_copies(chips, direct, chip, core, sources, w_in_ref, w_down_ref, lines_ref):
    if not direct:
        return [(sources[0], w_in_ref), (sources[1], w_down_ref), (sources[2], lines_ref)]
    wide, width = w_down_ref.shape
    chunks = wide // width
    span, span_ff = width // (2 * chips), wide // (2 * chips)
    cut = span // 2
    copies = []
    for k in range(2):
        for away in range(chips):
            place = 2 * (chip ^ away) + (core if k == 0 else 1 - core)
            upper = sources[4 * k + (away >> 1)].at[away & 1]
            lower = sources[4 * k + 2 + (away & 1)].at[away >> 1]
            rows = pl.ds(pl.multiple_of(place * span, span), span)
            copies += [
                (upper.at[span * c : span * c + span], w_in_ref.at[c, rows]) for c in range(chunks)
            ]
            for half, source in enumerate((upper.at[span * chunks :], lower.at[:cut])):
                rows = pl.ds(pl.multiple_of(place * span + half * cut, cut), cut)
                copies.append((source, w_in_ref.at[chunks, rows]))
            rows = pl.ds(pl.multiple_of(place * span_ff, span_ff), span_ff)
            copies.append((lower.at[cut : cut + span_ff], w_down_ref.at[rows]))
            copies.append((lower.at[cut + span_ff :], lines_ref.at[k * chips + away]))
    return copies


def forward_kernel(
    chips,
    direct,
    at_ref,
    mixed_first_ref,
    mixed_rest_ref,
    other_first_ref,
    other_rest_ref,
    tokens_ref,
    grad_first_ref,
    grad_last_ref,
    *refs,
):
    sources, refs = refs[:-15], refs[-15:]
    output_ref, slope_ref, normed_ref, unit_one_ref, grad_second_ref, scale_ref, g_down_ref, sums_ref = refs[:8]
    w_in_ref, w_down_ref, lines_ref, hidden_ref, down_ref, sems, out_sems = refs[8:]
    wide, width = w_down_ref.shape
    half, chunks = width // 2, wide // width
    core = at_ref[1]
    copies = weight_copies(chips, direct, at_ref[0], core, sources, w_in_ref, w_down_ref, lines_ref)

    @pl.when(pl.program_id(0) == 0)
    def _():
        sums_ref[...] = jnp.zeros_like(sums_ref)
        for copy in start_copies(copies, sems):
            copy.wait()

    at, last = pl.program_id(0), pl.num_programs(0) - 1
    tile = tokens_ref.shape[0]
    rows = pl.ds(pl.multiple_of(at * tile, tile), tile)
    vectors = jnp.sum(lines_ref[...].astype(WIDE), 0)
    b_out, gain_one, shift_one, b_down, gain_two, shift_two = (vectors[k : k + 1] for k in range(6))
    here = pl.ds(pl.multiple_of(core * half, 128), half)
    there = pl.ds(pl.multiple_of((1 - core) * half, 128), half)
    mixed = jnp.concatenate([mixed_first_ref[...], mixed_rest_ref[...]], 1)
    other = jnp.concatenate([other_first_ref[...], other_rest_ref[...]], 1)
    branch = dot(mixed, w_in_ref[chunks, here], NN) + dot(other, w_in_ref[chunks, there], NN)
    unit_one, scale_one = norm_parts(tokens_ref[...].astype(WIDE) + (branch + b_out))
    normed = unit_one * gain_one + shift_one
    normed_low = normed.astype(LOW)
    normed_ref[...] = normed_low
    unit_one_ref[...] = unit_one
    down = b_down
    for c in range(0, chunks, 2):
        lanes = slice(width * c, width * c + 2 * width)
        weights = jnp.concatenate([w_in_ref[c], w_in_ref[c + 1]], 1)
        bias = jnp.concatenate([vectors[6 + c : 7 + c], vectors[7 + c : 8 + c]], 1)
        hidden, slope = gelu_parts(dot(normed_low, weights, NN) + bias)
        hidden = hidden.astype(LOW)
        hidden_ref[rows, lanes] = hidden
        slope_ref[:, lanes] = slope.astype(LOW)
        down = down + dot(hidden, w_down_ref[lanes], NN)
    unit_two, scale_two = norm_parts(normed + down)
    output_ref[...] = (unit_two * gain_two + shift_two).astype(LOW)
    lane = lax.broadcasted_iota(jnp.int32, (1, 128), 1)
    scale_ref[...] = jnp.where(lane < 128, scale_one, 0.0)
    grad = jnp.where(2 * at <= last, grad_first_ref[...], grad_last_ref[...]).astype(WIDE)
    sums_ref[4:5] += jnp.sum(grad * unit_two, 0, keepdims=True)
    sums_ref[5:6] += jnp.sum(grad, 0, keepdims=True)
    grad_second = norm_back(grad, unit_two, scale_two, gain_two)
    grad_second_ref[...] = grad_second
    grad_down = grad_second.astype(LOW)
    down_ref[rows] = grad_down
    sums_ref[3:4] += jnp.sum(grad_down.astype(WIDE), 0, keepdims=True)

    @pl.when(at == last)
    def _():
        moving = []
        for c in range(chunks):
            lanes = slice(width * c, width * c + width)
            w_down_ref[lanes] = dot(hidden_ref[:, lanes], down_ref[...], TN).astype(LOW)
            copy = pltpu.make_async_copy(w_down_ref.at[lanes], g_down_ref.at[lanes], out_sems.at[c])
            copy.start()
            moving.append(copy)
        for copy in moving:
            copy.wait()


def backward_kernel(
    tile,
    chips,
    direct,
    at_ref,
    mixed_first_ref,
    mixed_rest_ref,
    other_first_ref,
    other_rest_ref,
    slope_ref,
    unit_one_ref,
    grad_second_ref,
    scale_ref,
    normed_hbm,
    *refs,
):
    sources, refs = refs[:-15], refs[-15:]
    first_ref, mine_ref, theirs_ref, g_in_ref, sums_ref = refs[:5]
    w_in_ref, w_down_ref, lines_ref, vectors_ref, pre_ref, branch_ref, normed_ref = refs[5:12]
    sems, extra_sem, out_sems = refs[12:]
    own, width = normed_ref.shape
    wide = w_down_ref.shape[0]
    half, chunks = width // 2, wide // width
    chip, core = at_ref[0], at_ref[1]
    at, last = pl.program_id(0), pl.num_programs(0) - 1
    rows = pl.ds(pl.multiple_of(at * tile, tile), tile)
    copies = weight_copies(chips, direct, chip, core, sources, w_in_ref, w_down_ref, lines_ref)
    extra = pltpu.make_async_copy(normed_hbm, normed_ref, extra_sem.at[0])
    here = pl.ds(pl.multiple_of(core * half, 128), half)
    there = pl.ds(pl.multiple_of((1 - core) * half, 128), half)

    @pl.when(at == 0)
    def _():
        started = start_copies(copies, sems)
        extra.start()
        sums_ref[...] = jnp.zeros_like(sums_ref)
        for copy in started:
            copy.wait()
        vectors_ref[...] = jnp.sum(lines_ref[...].astype(WIDE), 0)

    def add_sum(k, value):
        sums_ref[k : k + 1] += jnp.sum(value, 0, keepdims=True)

    grad_normed = grad_second_ref[...]
    grad_down = grad_normed.astype(LOW)
    for c in range(chunks):
        lanes = slice(width * c, width * c + width)
        grad_pre = dot(grad_down, w_down_ref[lanes], NT) * slope_ref[:, lanes].astype(WIDE)
        grad_pre = grad_pre.astype(LOW)
        pre_ref[rows, lanes] = grad_pre
        add_sum(6 + c, grad_pre.astype(WIDE))
        grad_normed = grad_normed + dot(grad_pre, w_in_ref[c], NT)
    unit_one = unit_one_ref[...]
    add_sum(1, grad_normed * unit_one)
    add_sum(2, grad_normed)
    grad_branch = norm_back(grad_normed, unit_one, scale_ref[:, 0:1], vectors_ref[1:2]).astype(LOW)
    first_ref[...] = grad_branch
    branch_ref[rows] = grad_branch
    add_sum(0, grad_branch.astype(WIDE))
    mine_ref[...] = dot(grad_branch, w_in_ref[chunks, here], NT).astype(LOW)
    theirs_ref[...] = dot(grad_branch, w_in_ref[chunks, there], NT).astype(LOW)

    @pl.when(at == last)
    def _():
        extra.wait()
        moving = []

        def leave(c):
            copy = pltpu.make_async_copy(w_in_ref.at[c], g_in_ref.at[c], out_sems.at[c])
            copy.start()
            moving.append(copy)

        for c in range(chunks):
            lanes = slice(width * c, width * c + width)
            w_in_ref[c] = dot(normed_ref[...], pre_ref[:, lanes], TN).astype(LOW)
            leave(c)
        mixed = jnp.concatenate([mixed_first_ref[...], mixed_rest_ref[...]], 1)
        other = jnp.concatenate([other_first_ref[...], other_rest_ref[...]], 1)
        w_in_ref[chunks, here] = dot(mixed, branch_ref[...], TN).astype(LOW)
        w_in_ref[chunks, there] = dot(other, branch_ref[...], TN).astype(LOW)
        leave(chunks)
        for copy in moving:
            copy.wait()


IN_SMEM = pl.BlockSpec(memory_space=pltpu.SMEM)
IN_VMEM = pl.BlockSpec(memory_space=pltpu.VMEM)


IN_ANY = pl.BlockSpec(memory_space=pl.ANY)


def project_tokens(at, pieces, b_qkv, weights, direct):
    length, width = 4 * pieces[0].shape[0], pieces[0].shape[1]
    half = width // 2
    chips = lax.axis_size("dp") // 2
    return pl.pallas_call(
        partial(project_kernel, chips, direct),
        out_shape=(
            jax.ShapeDtypeStruct((length, 384), LOW),
            jax.ShapeDtypeStruct((length, 3 * half - 384), LOW),
            jax.ShapeDtypeStruct((length, width), LOW),
            jax.ShapeDtypeStruct((width, 3 * half), LOW),
        ),
        in_specs=[IN_SMEM] + [IN_VMEM] * 5 + [IN_ANY] * len(weights),
        out_specs=(IN_VMEM,) * 4,
        scratch_shapes=[pltpu.SemaphoreType.DMA((2 * chips,))],
        compiler_params=pltpu.CompilerParams(vmem_limit_bytes=48 << 20),
        cost_estimate=pl.CostEstimate(
            flops=4_000_000_000, bytes_accessed=12_000_000, transcendentals=0
        ),
        name="project",
    )(at, *pieces, b_qkv, *weights)


def attend(first_pair, near, rand, globs, bias, qkv):
    length, width = qkv.shape
    pairs, blocks = width // 384, length // BLOCK
    return pl.pallas_call(
        partial(attend_kernel, first_pair, pairs, blocks, 8 // pairs),
        out_shape=(
            jax.ShapeDtypeStruct((length, 128 * pairs), LOW),
            jax.ShapeDtypeStruct((blocks, 8, 128), WIDE),
        ),
        in_specs=[IN_SMEM] * 3 + [IN_VMEM] * 2,
        out_specs=(IN_VMEM,) * 2,
        compiler_params=pltpu.CompilerParams(vmem_limit_bytes=48 << 20),
        cost_estimate=pl.CostEstimate(
            flops=6_000_000_000 * pairs, bytes_accessed=3_000_000 * pairs, transcendentals=0
        ),
        name="attend",
    )(near, rand, globs, bias, qkv)


def attend_back(near, rand, globs, bias, logs, qkvs, mine, come, w_qkv, grad_first):
    length, (wide, width) = qkvs[0].shape[0], w_qkv.shape
    pairs, blocks = width // 384, length // BLOCK
    rows = jax.ShapeDtypeStruct((length // 2, wide), LOW)
    return pl.pallas_call(
        partial(attend_back_kernel, blocks, 2),
        out_shape=(
            jax.ShapeDtypeStruct((length, width), LOW),
            rows,
            rows,
            jax.ShapeDtypeStruct((1, width), WIDE),
        ),
        in_specs=[IN_SMEM] * 3 + [IN_VMEM] * 9,
        out_specs=(IN_VMEM,) * 4,
        scratch_shapes=[
            pltpu.VMEM((length, 128 * pairs), LOW),
            pltpu.VMEM((length, 256 * pairs), WIDE),
        ],
        compiler_params=pltpu.CompilerParams(vmem_limit_bytes=56 << 20),
        cost_estimate=pl.CostEstimate(
            flops=40_000_000_000, bytes_accessed=20_000_000, transcendentals=0
        ),
        name="attend_back",
    )(near, rand, globs, bias, *logs, *qkvs, mine, come, w_qkv, grad_first)


def pack_rows(at, shard, near, mirror, chunks, cut):
    rows, width = 4 * (shard.shape[0] - 16) + 16, shard.shape[1]
    return pl.pallas_call(
        partial(pack_kernel, 4, chunks, cut),
        out_shape=(
            jax.ShapeDtypeStruct((cut, width), LOW),
            jax.ShapeDtypeStruct((rows - cut, width), LOW),
        ),
        in_specs=[IN_SMEM] + [IN_VMEM] * 3,
        out_specs=(IN_VMEM, IN_VMEM),
        name="pack",
    )(at, shard, near, mirror)


TILE = 256


def tiles(width, first=0, many=None):
    if many is None:
        return pl.BlockSpec((TILE, width), lambda i: (i, 0))
    return pl.BlockSpec((TILE, width), lambda i: (jnp.clip(i - first, 0, many - 1), 0))


def weight_space(chips, direct, chunks, width):
    return [
        pltpu.VMEM((chunks + 1, width, width), LOW),
        pltpu.VMEM((chunks * width, width), LOW),
        pltpu.VMEM((2 * chips if direct else 1, 16, width), LOW),
    ]


def unpack_rows(at, rows_in, rows_down):
    chunks, span, width = rows_in.shape
    like = jax.ShapeDtypeStruct((2, (chunks * span + rows_down.shape[0]) // 4, width), LOW)
    return pl.pallas_call(
        partial(unpack_kernel, 4, chunks),
        out_shape=(like, like),
        in_specs=[IN_SMEM] + [IN_VMEM] * 2,
        out_specs=(IN_VMEM, IN_VMEM),
        name="unpack",
    )(at, rows_in, rows_down)


def layer_forward(at, mixed, other, tokens, grads, weights, direct, chunks):
    own, width = other[0].shape[0], tokens.shape[1]
    chips, wide = lax.axis_size("dp") // 2, chunks * width
    many = own // TILE // 2

    def rows(width, kind=LOW):
        return jax.ShapeDtypeStruct((own, width), kind)

    return pl.pallas_call(
        partial(forward_kernel, chips, direct),
        grid=(own // TILE,),
        out_shape=(rows(width), rows(wide), rows(width))
        + (rows(width, WIDE), rows(width, WIDE), rows(128, WIDE))
        + (jax.ShapeDtypeStruct((wide, width), LOW), jax.ShapeDtypeStruct((16, width), WIDE)),
        in_specs=[IN_SMEM]
        + [tiles(p.shape[1]) for p in (*mixed, *other, tokens)]
        + [tiles(width, 0, many), tiles(width, many, many)]
        + [IN_ANY] * len(weights),
        out_specs=tuple(tiles(w) for w in (width, wide, width, width, width, 128))
        + (IN_ANY, pl.BlockSpec((16, width), lambda i: (0, 0))),
        scratch_shapes=weight_space(chips, direct, chunks, width)
        + [
            pltpu.VMEM((own, wide), LOW),
            pltpu.VMEM((own, width), LOW),
            pltpu.SemaphoreType.DMA((2 * chips * (chunks + 4),)),
            pltpu.SemaphoreType.DMA((chunks,)),
        ],
        compiler_params=pltpu.CompilerParams(vmem_limit_bytes=58 << 20),
        cost_estimate=pl.CostEstimate(
            flops=22_000_000_000, bytes_accessed=36_000_000, transcendentals=0
        ),
        name="layer_forward",
    )(at, *mixed, *other, tokens, *grads, *weights)


def layer_backward(at, mixed, other, slope, unit_one, grad_second, scale, normed, weights, direct):
    own, width = normed.shape
    wide = slope.shape[1]
    half, chunks = width // 2, wide // width
    chips = lax.axis_size("dp") // 2
    whole = pl.BlockSpec((own, 128), lambda i: (0, 0)), pl.BlockSpec((own, half - 128), lambda i: (0, 0))
    return pl.pallas_call(
        partial(backward_kernel, TILE, chips, direct),
        grid=(own // TILE,),
        out_shape=(
            jax.ShapeDtypeStruct((own, width), LOW),
            jax.ShapeDtypeStruct((own, half), LOW),
            jax.ShapeDtypeStruct((own, half), LOW),
            jax.ShapeDtypeStruct((chunks + 1, width, width), LOW),
            jax.ShapeDtypeStruct((16, width), WIDE),
        ),
        in_specs=[IN_SMEM]
        + [whole[0], whole[1]] * 2
        + [tiles(wide), tiles(width), tiles(width), tiles(128)]
        + [IN_ANY] * (1 + len(weights)),
        out_specs=(tiles(width), tiles(half), tiles(half), IN_ANY)
        + (pl.BlockSpec((16, width), lambda i: (0, 0)),),
        scratch_shapes=weight_space(chips, direct, chunks, width)
        + [
            pltpu.VMEM((16, width), WIDE),
            pltpu.VMEM((own, wide), LOW),
            pltpu.VMEM((own, width), LOW),
            pltpu.VMEM((own, width), LOW),
            pltpu.SemaphoreType.DMA((2 * chips * (chunks + 4),)),
            pltpu.SemaphoreType.DMA((1,)),
            pltpu.SemaphoreType.DMA((chunks + 1,)),
        ],
        compiler_params=pltpu.CompilerParams(vmem_limit_bytes=58 << 20),
        cost_estimate=pl.CostEstimate(
            flops=22_000_000_000, bytes_accessed=40_000_000, transcendentals=0
        ),
        name="layer_backward",
    )(at, *mixed, *other, slope, unit_one, grad_second, scale, normed, *weights)


def place_of(block, core, z, blocks):
    quarter, row = block // (blocks // 4), block % (blocks // 4)
    a = (quarter & 1) ^ (z & 1)
    return ((quarter >> 1) ^ core) * (blocks // 2) + a * (blocks // 4) + row


def block_at(place, core, z, blocks):
    quarter = 2 * ((place // (blocks // 2)) ^ core) + ((place % (blocks // 2)) // (blocks // 4) ^ (z & 1))
    return quarter * (blocks // 4) + place % (blocks // 4)


def tables(rand, globs, blocks):
    core = lax.axis_index("dp") & 1
    z = lax.axis_index("seq")
    here = block_at(jnp.arange(blocks, dtype=jnp.int32), core, z, blocks)
    heads = rand.shape[0]
    one, two = globs[0], globs[1]

    def near(block):
        return jnp.abs(block - here) <= 1

    every = jnp.ones((heads, blocks), bool)
    ok = [every & (here > 0), every, every & (here < blocks - 1)]
    ok += [every & ~near(one), every & ~near(two) & (one != two)]
    seen = []
    for r in range(3):
        block = rand[:, :, r]
        good = ~near(block) & (block != one) & (block != two)
        for before in seen:
            good = good & (block != before)
        seen.append(block)
        ok.append(good)
    whole_row = (here == one) | (here == two)
    ok = jnp.stack(ok, -1) & ~whole_row[None, :, None]
    bias = jnp.where(ok, 0.0, NEG).astype(WIDE)
    bias = bias.reshape(heads // 2, 2, blocks, SLOTS).transpose(2, 0, 3, 1)
    bias = jnp.repeat(bias, HEAD, axis=3)
    put = partial(place_of, core=core, z=z, blocks=blocks)
    sides = jnp.concatenate([put(jnp.maximum(here - 1, 0)), put(jnp.minimum(here + 1, blocks - 1))])
    return sides, put(rand).reshape(-1), put(globs), bias


def shards(
    inputs,
    cotangent,
    rand_blocks,
    global_blocks,
    w_query,
    b_query,
    w_key,
    w_value,
    b_value,
    w_out,
    b_out,
    gain_one,
    shift_one,
    w_up,
    b_up,
    w_down,
    b_down,
    gain_two,
    shift_two,
):
    n_dp, n_seq = lax.axis_size("dp"), lax.axis_size("seq")
    chips, devices = n_dp // 2, n_dp * n_seq
    core = lax.axis_index("dp") & 1
    z = lax.axis_index("seq")
    device = lax.axis_index("dp") * n_seq + z
    rows_in, width = w_query.shape
    rows_ff, wide = w_down.shape[0], w_up.shape[1]
    chunks = wide // width
    half_width = width // 2
    _, quarter, _ = inputs.shape
    length = quarter * n_seq
    blocks = length // BLOCK
    own = length // 2
    own_heads = HEADS // 2
    span, span_ff = n_seq * rows_in, n_seq * rows_ff
    direct = span % 16 == 0 and chips == chunks

    here = jnp.arange(devices, dtype=jnp.int32)[:, None] == device

    def placed(vector):
        return jnp.where(here, vector[None], jnp.zeros((), LOW)).reshape(-1, width)

    q_line, v_line = placed(b_query), placed(b_value)

    pairs = half_width // 128

    def side(at):
        no_line = jnp.zeros((1, width), LOW)
        parts = []
        for pair in range(pairs):
            first = at * half_width + 128 * pair
            lanes = slice(first, first + 128)
            for w, line in ((w_query, q_line), (w_key, no_line), (w_value, v_line)):
                parts.append(jnp.concatenate([w[:, lanes], line[:, lanes]], 0))
        return jnp.pad(jnp.concatenate(parts, 1), ((0, 7), (0, 0)))

    left, right = side(0), side(1)
    keep = jnp.where(core == 0, left, right)
    come = swap(jnp.where(core == 0, right, left))
    shard = jnp.stack([jnp.where(core == 0, keep, come), jnp.where(core == 0, come, keep)])
    def numbers_of(s):
        numbers = pick(rand_blocks, s, 0).reshape(-1)
        numbers = jnp.concatenate([numbers, pick(global_blocks, s, 0).reshape(-1)])
        return jnp.pad(numbers, (0, -numbers.shape[0] % 128))

    numbers = jnp.stack(bring(numbers_of))
    qkv_z = gather_seq(tie(shard, numbers))

    packed = jnp.concatenate(
        [w_up[:, width * c : width * c + width] for c in range(chunks)]
        + [w_out, w_down]
        + [placed(v) for v in (b_out, gain_one, shift_one, b_down, gain_two, shift_two, b_up)]
        + [jnp.zeros((16 - 6 - chunks, width), LOW)],
        0,
    )
    wide_z = gather_seq(tie(packed, shard), qkv_z[2])
    at = jnp.stack([lax.axis_index("dp") >> 1, core, z]).astype(jnp.int32)

    numbers = tie(numbers, wide_z[2])
    numbers = jnp.concatenate([numbers, swap(numbers)], 0)
    local_blocks = rand_blocks.shape[2]
    count = HEADS * local_blocks * 3
    globs = numbers[0, count : count + 2]
    rand = numbers[:, :count].reshape(4, HEADS, local_blocks, 3)
    rand = lax.dynamic_slice_in_dim(rand, core * own_heads, own_heads, 1)
    rand = rand.transpose(1, 0, 2, 3).reshape(own_heads, blocks, 3)
    sides, rand, glob_at, bias = tables(rand, globs, blocks)

    qkv_z = in_seq_order(*qkv_z)
    whole = []
    for k in range(2):
        lines = sum(p[k, rows_in:].astype(WIDE) for p in qkv_z).astype(LOW)
        whole += [p[k, :rows_in] for p in qkv_z] + [lines, jnp.zeros_like(lines)]
    qkv_parts = gather_chips(jnp.concatenate(whole, 0).reshape(2, span + 16, 3 * half_width))

    tied_inputs = tie(inputs, qkv_z[2])
    pieces = bring(lambda s: pick(tied_inputs, s, 0)[0])

    if direct:
        cut = chunks * span + span // 2
        near, pieces[0], *qkv_parts = join(wide_z[1], pieces[0], *qkv_parts)
        whole = pack_rows(at, wide_z[0], near, wide_z[2], chunks + 1, cut)
    else:
        wide_z = in_seq_order(*wide_z)
        rows_a = (chunks + 1) * rows_in
        rows = []
        for c in range(chunks + 1):
            rows += [p[c * rows_in : (c + 1) * rows_in] for p in wide_z]
        rows += [p[rows_a : rows_a + rows_ff] for p in wide_z]
        rows.append(sum(p[rows_a + rows_ff :].astype(WIDE) for p in wide_z).astype(LOW))
        whole = jnp.concatenate(rows, 0)
    if direct:
        parts = gather_quads(*whole)
        joined_up = join(*parts, *pieces)
        parts, pieces = joined_up[:4], joined_up[4:]
    else:
        parts = gather_chips(tie(whole, qkv_parts))
    lines = sum(jnp.sum(p[:, span].astype(WIDE), 0, keepdims=True) for p in qkv_parts)
    pieces = [*pieces, *(swap(p) for p in pieces)]
    rows_a, rows_b = (chunks + 1) * span, (chunks + 1) * span + span_ff
    if direct:
        qkv_weights = tuple(qkv_parts)
    else:
        ordered = in_chip_order(qkv_parts)
        qkv_weights = (jnp.concatenate([p[k, :span] for p in ordered for k in range(2)], 0),)

    if direct:
        parts = finish_quads(*parts)
    qkv_first, qkv_rest, tokens, w_qkv = project_tokens(at, pieces, lines, qkv_weights, direct)
    mixed_first, log_first = attend(0, sides, rand, glob_at, bias, qkv_first)
    tied_cotangent = tie(cotangent, *pieces)
    grad_result = bring(lambda s: pick(tied_cotangent, s, 0)[0])
    mixed_first, qkv_rest, *parts = join(mixed_first, qkv_rest, *parts)
    other_first = swap(mixed_first[own:])
    other_parts = [swap(p) for p in parts]
    mixed_rest, log_rest = attend(1, sides, rand, glob_at, bias, qkv_rest)
    if direct:
        weights = tuple(parts + other_parts)
    else:
        weights = (
            jnp.stack(
                [
                    in_device_order(
                        *([p[span * c : span * c + span] for p in ps] for ps in (parts, other_parts))
                    )
                    for c in range(chunks + 1)
                ]
            ),
            in_device_order(*([p[rows_a:rows_b] for p in ps] for ps in (parts, other_parts))),
            sum(p[rows_b:].astype(WIDE) for p in parts + other_parts).astype(LOW)[None],
        )
    other = other_first, swap(mixed_rest[own:])
    result, slope, normed, unit_one, grad_second, scale, grad_down, down_sums = layer_forward(
        at, (mixed_first, mixed_rest), other, tokens, grad_result, weights, direct, chunks
    )
    output = send_back(result)

    grad_down = lax.psum_scatter(grad_down, "dp", scatter_dimension=0, tiled=True)
    *backward, grad_in, in_sums = layer_backward(
        at,
        (mixed_first, mixed_rest),
        other,
        slope,
        unit_one,
        grad_second,
        scale,
        normed,
        weights,
        direct,
    )
    grad_first, mine, theirs, grad_in, in_sums, *output = join(*backward, grad_in, in_sums, *output)
    grad_in = lax.psum_scatter(grad_in, "dp", scatter_dimension=1, tiled=True)

    come = swap(theirs)
    grad_qkv, grad_own, grad_theirs, sums = attend_back(
        sides,
        rand,
        glob_at,
        bias,
        (log_first, log_rest),
        (qkv_first, qkv_rest),
        mine,
        come,
        w_qkv,
        grad_first,
    )
    come = swap(grad_theirs)
    grad_w_qkv = dot(tokens, grad_qkv, TN).astype(LOW)
    grad_w_qkv, grad_own, come = join(grad_w_qkv, grad_own, come)
    grad_inputs = start_back(added(grad_own, come))
    vectors = (down_sums + in_sums)[: 6 + chunks].reshape(-1)
    vectors = jnp.pad(vectors, (0, -vectors.shape[0] % (3 * half_width))).reshape(-1, 3 * half_width)
    lines = jnp.concatenate([sums, vectors], 0).astype(LOW)
    lines = jnp.broadcast_to(lines, (chips, 2, n_seq) + lines.shape)
    parts = jnp.concatenate(
        [grad_w_qkv.reshape(chips, 2, n_seq, rows_in, 3 * half_width), lines], 3
    )
    come = swap(pick(parts, 1 - core, 1)[:, 0])
    first_back = finish_back(grad_inputs, 0)
    come, first_back = join(come, first_back)
    near_sums, keep_sums = unpack_rows(at, grad_in, grad_down)
    near_sums = flip_seq(near_sums, 1)
    parts = jnp.stack([pick(parts, core, 1)[:, 0], come], 1)
    grad_inputs, parts = tie((grad_inputs, parts), first_back)
    grad_inputs = first_back, finish_back(grad_inputs, 1)
    parts = reduce_chips(parts)
    parts, near_sums = join(parts, near_sums)
    own_qkv = reduce_seq(parts.transpose(1, 0, 2, 3))
    keep, come = own_qkv[0], own_qkv[1]
    left, right = jnp.where(core == 0, keep, come), jnp.where(core == 0, come, keep)

    mirror = flip_seq(added(keep_sums[1], near_sums[1]), 3)
    own_sums = sum(p.astype(WIDE) for p in (keep_sums[0], near_sums[0], mirror))
    rows_a = (chunks + 1) * rows_in
    own_up = jnp.concatenate(
        [own_sums[c * rows_in : (c + 1) * rows_in] for c in range(chunks)], 1
    )
    small = (keep + come)[rows_in + 1 :].reshape(-1)[: (6 + chunks) * width].reshape(-1, width)

    def joined(k, rows):
        lanes = [lanes_of(k, pair) for pair in range(pairs)]
        return jnp.concatenate([one[rows, at] for one in (left, right) for at in lanes], 1)

    def own_part(vector, size):
        return lax.dynamic_slice_in_dim(vector.reshape(-1), device * size, size, 0)

    matrix_rows, line = slice(0, rows_in), slice(rows_in, rows_in + 1)
    return (
        in_sequences(output),
        in_sequences(grad_inputs),
        joined(0, matrix_rows),
        own_part(joined(0, line), rows_in),
        joined(1, matrix_rows),
        joined(2, matrix_rows),
        own_part(joined(2, line), rows_in),
        own_sums[chunks * rows_in : rows_a],
        own_part(small[0], rows_in),
        own_part(small[1], rows_in),
        own_part(small[2], rows_in),
        own_up,
        own_part(small[6 : 6 + chunks], rows_ff),
        own_sums[rows_a : rows_a + rows_ff],
        own_part(small[3], rows_in),
        own_part(small[4], rows_in),
        own_part(small[5], rows_in),
    )


def solution(mesh):
    both = ("dp", "seq")
    matrix, vector = P(both, None), P(both)
    tokens = P("dp", "seq", None)
    return jax.shard_map(
        shards,
        mesh=mesh,
        in_specs=(tokens, tokens, P("dp", None, "seq", None), P("dp", None))
        + (matrix, vector, matrix, matrix, vector, matrix, vector, vector, vector)
        + (matrix, vector, matrix, vector, vector, vector),
        out_specs=(tokens, tokens)
        + (matrix, vector, matrix, matrix, vector, matrix, vector, vector, vector)
        + (matrix, vector, matrix, vector, vector, vector),
        check_vma=False,
    )
```

time: 428 us -> 401 us (0.937)
  waiting for transfers between devices: 86.2 us -> 65.2 us
  local copies, waits for them, and re-layouts: 49.2 us -> 33.1 us
  between operations: 3.32 us -> 16.9 us
  other arithmetic: 32.2 us -> 21.9 us
  Pallas kernels: 144 us -> 151 us
    ppermute x8, waiting for transfers between devices: 35.5 us -> 6.67 us  [flip_seq(): return lax.ppermute(array, 'seq', [(i, i ^ k) for i in range(size)])]
    ppermute x13, starting transfers between devices: 33.8 us -> 7.17 us  [swap(): return lax.ppermute(array, 'dp', [(i, i ^ 1) for i in range(size)])]
    ppermute x8, starting transfers between devices: 38.2 us -> 61 us  [flip_seq(): return lax.ppermute(array, 'seq', [(i, i ^ k) for i in range(size)])]
    ppermute x4, waiting for transfers between devices: 18 us -> 0.01 us  [finish_back(): return lax.ppermute(parts[a], ('dp', 'seq'), [(t, s) for s, t in pairs])]
    unnamed x130 -> x114, local copies, waits for them, and re-layouts: 21.9 us -> 10.4 us
    concatenate x7 -> x4, other arithmetic: 10.5 us -> 0.18 us  [the longest x2 0.15 us: numbers_of(): numbers = jnp.concatenate([numbers, pick(global_blocks, s, 0).reshape(-1)])]
    reduce_scatter x0 -> x2, waiting for transfers between devices: none -> 9.85 us  [the longest x1 9.85 us: shards(): grad_in = lax.psum_scatter(grad_in, 'dp', scatter_dimension=1, tiled=True)]
    ppermute x4 -> x6, waiting for transfers between devices: 1.46 us -> 10 us  [bring(): lax.ppermute(piece_of(a ^ z & 1), ('dp', 'seq'), pairs)]
  transfers between devices with their start and end apart: 41 -> 43, of which waited for: 14 -> 13; matrix products, arithmetic and copies ran while one was open for 16% -> 11% of each run, Pallas kernels for 20% -> 29%
where the time goes in v3:
time: 401 us; the launch traced here: 394 us
  Pallas kernels  151 us (38%)
  starting transfers between devices  97.3 us (24%)
  waiting for transfers between devices  65.2 us (16%)
  local copies, waits for them, and re-layouts  33.1 us (8%)
  other arithmetic  21.9 us (5%)
  between operations  16.9 us (4%)
  matrix products  7.62 us (2%)
    ppermute x8, starting transfers between devices, flip_seq(): return lax.ppermute(array, 'seq', [(i, i ^ k) for i in range(size)])  61 us
    pallas_call x1, Pallas kernels, attend_back(): pl.pallas_call(partial(attend_back_kernel, blocks, 2), out_shape=(jax.Sha...  43 us
    pallas_call x1, Pallas kernels, layer_forward(): pl.pallas_call(partial(forward_kernel, chips, direct), grid=(own // TILE,...  38.7 us
    ppermute x10, waiting for transfers between devices, flip_chip(): return lax.ppermute(array, 'dp', [(i, i ^ 2 * away) for i in range(size)])  34.5 us
    pallas_call x1, Pallas kernels, layer_backward(): pl.pallas_call(partial(backward_kernel, TILE, chips, direct), grid=(own /...  31.6 us
    pallas_call x2, Pallas kernels, attend(): pl.pallas_call(partial(attend_kernel, first_pair, pairs, blocks, 8 // pai...  22 us
    ppermute x10, starting transfers between devices, flip_chip(): return lax.ppermute(array, 'dp', [(i, i ^ 2 * away) for i in range(size)])  12.4 us
    pallas_call x1, Pallas kernels, project_tokens(): pl.pallas_call(partial(project_kernel, chips, direct), out_shape=(jax.Sha...  11.1 us
  transfers between devices with their start and end apart: 43, of which 13 were waited for; matrix products, arithmetic and copies ran while one was open for 11% of the time, Pallas kernels for 29%

profile of v3, /device:TPU:0, one launch (start us, length us, event | category | flops | bytes accessed | tf_op | source)
XLA Modules:
  0.0 393.5 jit_solution(11480839331802048176)
XLA Ops:
  14.5 2.6 collective-permute-start.1
  19.0 6.8 %collective-permute-start.5 = (bf16[2,32,1152]{2,1,0:T(8,128)(2,1)S(1)}, bf16[2,32,1152]{2,1,0:T(8,128)(2,1)S(1)}, u32[]{:S(2)}, u32[]{:S(2)}) collective-permute-start(bf16[2,32,1152]{2,1,0:T(8,128)(2,1)S(1)} %pad_maximum_fusion.9), channel_id=1, source_target_pairs={{0,3},{1,2},{2,1},{3,0},{4,7},{5,6},{6,5},{7,4},{8,11},{9,10},{10,... | collective-permute-start | bytes 442376 | tf_op jit(solution)/shard_map/ppermute | solution.py:35
  29.0 10.8 %collective-permute-start.7 = (bf16[2,2,32,1152]{3,2,1,0:T(8,128)(2,1)S(1)}, bf16[2,2,32,1152]{3,2,1,0:T(8,128)(2,1)S(1)}, u32[]{:S(2)}, u32[]{:S(2)}) collective-permute-start(bf16[2,2,32,1152]{3,2,1,0:T(8,128)(2,1)S(1)} %pad_maximum_fusion.6), channel_id=1, source_target_pairs={{0,1},{1,0},{2,3},{3,2},{4,5},{5,4},{6,7},{7,6},{8,9},{9,8},{10,11... | collective-permute-start | bytes 884744 | tf_op jit(solution)/shard_map/ppermute | solution.py:35
  44.9 7.2 %collective-permute-start.6 = (bf16[2,232,768]{2,1,0:T(8,128)(2,1)}, bf16[2,232,768]{2,1,0:T(8,128)(2,1)}, u32[]{:S(2)}, u32[]{:S(2)}) collective-permute-start(bf16[2,232,768]{2,1,0:T(8,128)(2,1)} %pad_maximum_fusion.5), channel_id=1, source_target_pairs={{0,1},{1,0},{2,3},{3,2},{4,5},{5,4},{6,7},{7,6},{8,9},{9,8},{10,11... | collective-permute-start | bytes 2138120 | tf_op jit(solution)/shard_map/ppermute | solution.py:35
  62.3 19.9 %collective-permute-done.10.refs_7_ = bf16[2,112,1152]{2,1,0:T(8,128)(2,1)S(1)} collective-permute-done((bf16[2,112,1152]{2,1,0:T(8,128)(2,1)S(1)}, bf16[2,112,1152]{2,1,0:T(8,128)(2,1)S(1)}, u32[]{:S(2)}, u32[]{:S(2)}) %collective-permute-start.10) | collective-permute-done | bytes 516128 | tf_op jit(solution)/shard_map/ppermute | solution.py:105
  83.5 2.5 pack.1
  93.0 10.0 %collective-permute-done.14.refs_1_ = bf16[512,768]{1,0:T(8,128)(2,1)} collective-permute-done((bf16[512,768]{1,0:T(8,128)(2,1)}, bf16[512,768]{1,0:T(8,128)(2,1)}, u32[]{:S(2)}, u32[]{:S(2)}) %collective-permute-start.14) | collective-permute-done | bytes 786464 | tf_op jit(solution)/shard_map/ppermute | solution.py:52
  112.0 11.1 %project.1 = (bf16[2048,384]{1,0:T(8,128)(2,1)}, bf16[2048,768]{1,0:T(8,128)(2,1)}, bf16[2048,768]{1,0:T(8,128)(2,1)}, bf16[768,1152]{1,0:T(8,128)(2,1)}) custom-call(s32[3]{0:T(128)S(1)} %copy-done.3, bf16[512,768]{1,0:T(8,128)(2,1)S(1)} %collective-permute-done.8.refs_0_, bf16[512,768]{1,0:T(8,128)(2,1)} %collective-permute-done.14.refs_1_, ...), custom_call_target="tpu_custom_call" | custom-call | flops 4000000000 | bytes 12000000 | tf_op jit(solution)/shard_map/project/pallas_call | solution.py:730
  124.5 8.2 %attend.2 = (bf16[2048,128]{1,0:T(8,128)(2,1)S(1)}, f32[32,8,128]{2,1,0:T(8,128)S(1)}) custom-call(s32[64]{0:T(128)S(1)} %pad_add_fusion.5.near_ref, s32[576]{0:T(1024)S(1)} %fusion.11.rand_ref, s32[2]{0:T(128)S(1)} %fusion.30.glob_ref, f32[32,3,8,128]{3,2,1,0:T(8,128)S(1)} %reshape.565.bias_ref, bf16[2048,384]{1,0:T(8,128)(2,1)S(1)} %copy-done.8), custom_call_target="tpu_custom_call" | custom-call | flops 6000000000 | bytes 3000000 | tf_op jit(solution)/shard_map/attend/pallas_call | solution.py:752
  132.8 7.6 %collective-permute-done.17.refs_1_ = bf16[2,432,768]{2,1,0:T(8,128)(2,1)S(1)} collective-permute-done((bf16[2,432,768]{2,1,0:T(8,128)(2,1)S(1)}, bf16[2,432,768]{2,1,0:T(8,128)(2,1)S(1)}, u32[]{:S(2)}, u32[]{:S(2)}) %collective-permute-start.17) | collective-permute-done | bytes 1327136 | tf_op jit(solution)/shard_map/ppermute | solution.py:105
  142.4 13.8 %attend.3 = (bf16[2048,256]{1,0:T(8,128)(2,1)S(1)}, f32[32,8,128]{2,1,0:T(8,128)S(1)}) custom-call(s32[64]{0:T(128)S(1)} %pad_add_fusion.5.near_ref, s32[576]{0:T(1024)S(1)} %fusion.11.rand_ref, s32[2]{0:T(128)S(1)} %fusion.30.glob_ref, f32[32,3,8,128]{3,2,1,0:T(8,128)S(1)} %reshape.565.bias_ref, bf16[2048,768]{1,0:T(8,128)(2,1)S(1)} %copy-done.7), custom_call_target="tpu_custom_call" | custom-call | flops 12000000000 | bytes 6000000 | tf_op jit(solution)/shard_map/attend/pallas_call | solution.py:752
  160.7 38.7 %layer_forward.1 = (bf16[1024,768]{1,0:T(8,128)(2,1)}, bf16[1024,3072]{1,0:T(8,128)(2,1)}, bf16[1024,768]{1,0:T(8,128)(2,1)}, f32[1024,768]{1,0:T(8,128)}, f32[1...) custom-call(s32[3]{0:T(128)} %pad_add_fusion.4.at_ref, ...), custom_call_target="tpu_custom_call" | custom-call | flops 22000001024 | bytes 36000000 | tf_op jit(solution)/shard_map/layer_forward/pallas_call | solution.py:845
  201.6 7.6 %collective-permute-start.28 = (bf16[512,768]{1,0:T(8,128)(2,1)S(1)}, bf16[512,768]{1,0:T(8,128)(2,1)S(1)}, u32[]{:S(2)}, u32[]{:S(2)}) collective-permute-start(bf16[512,768]{1,0:T(8,128)(2,1)S(1)} %get-tuple-element.168), channel_id=1, source_target_pairs={{1,0},{0,1},{5,2},{4,3},{3,4},{2,5},{7,6},{6,7},{9,8},{8,9},{13,10... | collective-permute-start | bytes 2359304 | tf_op jit(solution)/shard_map/ppermute | solution.py:62
  209.3 31.6 %layer_backward.1 = (bf16[1024,768]{1,0:T(8,128)(2,1)}, bf16[1024,384]{1,0:T(8,128)(2,1)}, bf16[1024,384]{1,0:T(8,128)(2,1)}, bf16[5,768,768]{2,1,0:T(8,128)(2,1)}, f32[16,768]{1,0:T(8,128)}) custom-call(s32[3]{0:T(128)} %pad_add_fusion.4.at_ref, bf16[2048,128]{1,0:T(8,128)(2,1)} %copy-done.2, bf16[2048,256]{1,0:T(8,128)(2,1)} %copy-done.1, ...), custom_call_target="tpu_custom_call" | custom-call | flops 22000001024 | bytes 40000000 | tf_op jit(solution)/shard_map/layer_backward/pallas_call | solution.py:878
  242.7 3.1 collective-permute-start.29
  248.8 43.0 %attend_back.1 = (bf16[2048,1152]{1,0:T(8,128)(2,1)}, bf16[1024,768]{1,0:T(8,128)(2,1)}, bf16[1024,768]{1,0:T(8,128)(2,1)}, f32[1,1152]{1,0:T(1,128)}) custom-call(s32[64]{0:T(128)} %copy-done.6, s32[576]{0:T(1024)} %copy-done.4, s32[2]{0:T(128)} %copy-done.5, f32[32,3,8,128]{3,2,1,0:T(8,128)} %copy-done, f32[32,8,128]{2,1,0:T(8,128)} %copy-done.9, ...), custom_call_target="tpu_custom_call" | custom-call | flops 40000000000 | bytes 20000000 | tf_op jit(solution)/shard_map/attend_back/pallas_call | solution.py:772
  292.9 7.6 %convolution_convert_fusion = bf16[768,1152]{1,0:T(8,128)(2,1)S(1)} fusion(bf16[2048,768]{1,0:T(8,128)(2,1)} %get-tuple-element.111.tokens_ref, bf16[2048,1152]{1,0:T(8,128)(2,1)} %get-tuple-element.136), kind=kOutput, calls=%fused_computation | convolution fusion | flops 3624763392 | bytes 9633792 | tf_op jit(solution)/shard_map/dot_general | solution.py:25
  315.7 9.8 %reduce-scatter.3.cloned.1.call-done.in_ref = bf16[5,96,768]{2,1,0:T(8,128)(2,1)} async-done(((bf16[5,768,768]{2,1,0:T(8,128)(2,1)}), bf16[5,96,768]{2,1,0:T(8,128)(2,1)}) %reduce-scatter.3.cloned.1.call-update) | async-done | bytes 737296 | tf_op jit(solution)/shard_map/reduce_scatter | solution.py:1126
  325.6 2.5 unpack.1
  329.6 4.0 %collective-permute-done.36 = bf16[1,2,4,32,1152]{4,3,1,2,0:T(8,128)(2,1)} collective-permute-done((bf16[1,2,4,32,1152]{4,3,1,2,0:T(8,128)(2,1)}, bf16[1,2,4,32,1152]{4,3,1,2,0:T(8,128)(2,1)}, u32[]{:S(2)}, u32[]{:S(2)}) %collective-permute-start.36) | collective-permute-done | bytes 589856 | tf_op jit(solution)/shard_map/ppermute | solution.py:105
  336.6 4.0 %collective-permute-done.37 = bf16[2,216,768]{2,1,0:T(8,128)(2,1)S(1)} collective-permute-done((bf16[2,216,768]{2,1,0:T(8,128)(2,1)}, bf16[2,216,768]{2,1,0:T(8,128)(2,1)S(1)}, u32[]{:S(2)}, u32[]{:S(2)}) %collective-permute-start.37) | collective-permute-done | bytes 663584 | tf_op jit(solution)/shard_map/ppermute | solution.py:35
  340.7 2.4 collective-permute-start.38
  344.6 18.2 %collective-permute-start.40 = (bf16[216,768]{1,0:T(8,128)(2,1)S(1)}, bf16[216,768]{1,0:T(8,128)(2,1)S(1)}, u32[]{:S(2)}, u32[]{:S(2)}) collective-permute-start(bf16[216,768]{1,0:T(8,128)(2,1)S(1)} %fusion.4), channel_id=1, source_target_pairs={{0,3},{1,2},{2,1},{3,0},{4,7},{5,6},{6,5},{7,4},{8,11},{9,10},{10,... | collective-permute-start | bytes 995336 | tf_op jit(solution)/shard_map/ppermute | solution.py:35
  362.8 14.0 %collective-permute-start.39 = (bf16[2,32,1152]{2,1,0:T(8,128)(2,1)S(1)}, bf16[2,32,1152]{2,1,0:T(8,128)(2,1)S(1)}, u32[]{:S(2)}, u32[]{:S(2)}) collective-permute-start(bf16[2,32,1152]{2,1,0:T(8,128)(2,1)S(1)} %fusion.5), channel_id=1, source_target_pairs={{0,3},{1,2},{2,1},{3,0},{4,7},{5,6},{6,5},{7,4},{8,11},{9,10},{10,... | collective-permute-start | bytes 442376 | tf_op jit(solution)/shard_map/ppermute | solution.py:35
  (323 shorter events, 89.4 us)
Async XLA Ops:
  7.2 308.5 %reduce-scatter.5.cloned.1.call-start = ((), (), s32[]{:S(2)}) async-start(), calls=%async_computation.3 | async-start | bytes 5308416 | tf_op jit(solution)/shard_map/reduce_scatter | solution.py:1112
  29.0 24.6 %collective-permute-start.7 = (bf16[2,2,32,1152]{3,2,1,0:T(8,128)(2,1)S(1)}, bf16[2,2,32,1152]{3,2,1,0:T(8,128)(2,1)S(1)}, u32[]{:S(2)}, u32[]{:S(2)}) collective-permute-start(bf16[2,2,32,1152]{3,2,1,0:T(8,128)(2,1)S(1)} %pad_maximum_fusion.6), channel_id=1, source_target_pairs={{0,1},{1,0},{2,3},{3,2},{4,5},{5,4},{6,7},{7,6},{8,9},{9,8},{10,11... | collective-permute-start | bytes 884744 | tf_op jit(solution)/shard_map/ppermute | solution.py:35
  39.8 20.1 %collective-permute-start.4 = (s32[2,384]{1,0:T(2,128)S(1)}, s32[2,384]{1,0:T(2,128)S(1)}, u32[]{:S(2)}, u32[]{:S(2)}) collective-permute-start(s32[2,384]{1,0:T(2,128)S(1)} %pad_add_fusion.1), channel_id=1, source_target_pairs={{0,4},{4,0},{8,12},{12,8},{16,20},{20,16},{24,28},{28,24},{1,5},{5... | collective-permute-start | bytes 9224 | tf_op jit(solution)/shard_map/ppermute | solution.py:30
  44.9 38.6 %collective-permute-start.6 = (bf16[2,232,768]{2,1,0:T(8,128)(2,1)}, bf16[2,232,768]{2,1,0:T(8,128)(2,1)}, u32[]{:S(2)}, u32[]{:S(2)}) collective-permute-start(bf16[2,232,768]{2,1,0:T(8,128)(2,1)} %pad_maximum_fusion.5), channel_id=1, source_target_pairs={{0,1},{1,0},{2,3},{3,2},{4,5},{5,4},{6,7},{7,6},{8,9},{9,8},{10,11... | collective-permute-start | bytes 2138120 | tf_op jit(solution)/shard_map/ppermute | solution.py:35
  55.1 28.3 %collective-permute-start.8 = (bf16[512,768]{1,0:T(8,128)(2,1)}, bf16[512,768]{1,0:T(8,128)(2,1)S(1)}, u32[]{:S(2)}, u32[]{:S(2)}) collective-permute-start(bf16[512,768]{1,0:T(8,128)(2,1)} %get-tuple-element.173), channel_id=1, source_target_pairs={{0,0},{1,1},{2,4},{3,5},{4,2},{5,3},{6,6},{7,7},{8,8},{9,9},{10,12... | collective-permute-start | bytes 2359304 | tf_op jit(solution)/shard_map/ppermute | solution.py:52
  56.9 25.3 %collective-permute-start.10 = (bf16[2,112,1152]{2,1,0:T(8,128)(2,1)S(1)}, bf16[2,112,1152]{2,1,0:T(8,128)(2,1)S(1)}, u32[]{:S(2)}, u32[]{:S(2)}) collective-permute-start(bf16[2,112,1152]{2,1,0:T(8,128)(2,1)S(1)} %bitcast.177), channel_id=1, source_target_pairs={{0,16},{4,20},{8,24},{12,28},{16,0},{20,4},{24,8},{28,12},{1,17},{... | collective-permute-start | bytes 1548296 | tf_op jit(solution)/shard_map/ppermute | solution.py:105
  58.5 23.8 %collective-permute-start.11 = (bf16[2,112,1152]{2,1,0:T(8,128)(2,1)S(1)}, bf16[2,112,1152]{2,1,0:T(8,128)(2,1)S(1)}, u32[]{:S(2)}, u32[]{:S(2)}) collective-permute-start(bf16[2,112,1152]{2,1,0:T(8,128)(2,1)S(1)} %bitcast.178), channel_id=1, source_target_pairs={{0,24},{4,28},{8,16},{12,20},{16,8},{20,12},{24,0},{28,4},{1,25},{... | collective-permute-start | bytes 1548296 | tf_op jit(solution)/shard_map/ppermute | solution.py:105
  59.9 23.6 %collective-permute-start.9 = (bf16[2,112,1152]{2,1,0:T(8,128)(2,1)S(1)}, bf16[2,112,1152]{2,1,0:T(8,128)(2,1)S(1)}, u32[]{:S(2)}, u32[]{:S(2)}) collective-permute-start(bf16[2,112,1152]{2,1,0:T(8,128)(2,1)S(1)} %bitcast.179), channel_id=1, source_target_pairs={{0,8},{4,12},{8,0},{12,4},{16,24},{20,28},{24,16},{28,20},{1,9},{5... | collective-permute-start | bytes 1548296 | tf_op jit(solution)/shard_map/ppermute | solution.py:105
  82.2 20.7 %collective-permute-start.14 = (bf16[512,768]{1,0:T(8,128)(2,1)}, bf16[512,768]{1,0:T(8,128)(2,1)}, u32[]{:S(2)}, u32[]{:S(2)}) collective-permute-start(bf16[512,768]{1,0:T(8,128)(2,1)} %get-tuple-element.172), channel_id=1, source_target_pairs={{0,1},{1,0},{2,5},{3,4},{4,3},{5,2},{6,7},{7,6},{8,9},{9,8},{10,13... | collective-permute-start | bytes 2359304 | tf_op jit(solution)/shard_map/ppermute | solution.py:52
  86.0 18.7 %collective-permute-start.13 = (bf16[448,768]{1,0:T(8,128)(2,1)}, bf16[448,768]{1,0:T(8,128)(2,1)}, u32[]{:S(2)}, u32[]{:S(2)}) collective-permute-start(bf16[448,768]{1,0:T(8,128)(2,1)} %get-tuple-element.106), channel_id=1, source_target_pairs={{0,16},{4,20},{8,24},{12,28},{16,0},{20,4},{24,8},{28,12},{1,17},{... | collective-permute-start | bytes 2064392 | tf_op jit(solution)/shard_map/ppermute | solution.py:105
  106.7 33.6 %collective-permute-start.18 = (bf16[2,448,768]{2,1,0:T(8,128)(2,1)S(1)}, bf16[2,448,768]{2,1,0:T(8,128)(2,1)S(1)}, u32[]{:S(2)}, u32[]{:S(2)}) collective-permute-start(bf16[2,448,768]{2,1,0:T(8,128)(2,1)S(1)} %pad_maximum_fusion.3.refs_2_), channel_id=1, source_target_pairs={{0,8},{4,12},{8,0},{12,4},{16,24},{20,28},{24,16},{28,20},{1,9},{5... | collective-permute-start | bytes 4128776 | tf_op jit(solution)/shard_map/ppermute | solution.py:105
  109.5 30.8 %collective-permute-start.17 = (bf16[2,432,768]{2,1,0:T(8,128)(2,1)S(1)}, bf16[2,432,768]{2,1,0:T(8,128)(2,1)S(1)}, u32[]{:S(2)}, u32[]{:S(2)}) collective-permute-start(bf16[2,432,768]{2,1,0:T(8,128)(2,1)S(1)} %pad_maximum_fusion.4.refs_0_), channel_id=1, source_target_pairs={{0,16},{4,20},{8,24},{12,28},{16,0},{20,4},{24,8},{28,12},{1,17},{... | collective-permute-start | bytes 3981320 | tf_op jit(solution)/shard_map/ppermute | solution.py:105
  110.5 30.5 %collective-permute-start.21 = (bf16[512,768]{1,0:T(8,128)(2,1)S(1)}, bf16[512,768]{1,0:T(8,128)(2,1)S(1)}, u32[]{:S(2)}, u32[]{:S(2)}) collective-permute-start(bf16[512,768]{1,0:T(8,128)(2,1)S(1)} %get-tuple-element.171), channel_id=1, source_target_pairs={{0,0},{1,1},{2,4},{3,5},{4,2},{5,3},{6,6},{7,7},{8,8},{9,9},{10,12... | collective-permute-start | bytes 2359304 | tf_op jit(solution)/shard_map/ppermute | solution.py:52
  111.7 29.9 %collective-permute-start.22 = (bf16[512,768]{1,0:T(8,128)(2,1)S(1)}, bf16[512,768]{1,0:T(8,128)(2,1)}, u32[]{:S(2)}, u32[]{:S(2)}) collective-permute-start(bf16[512,768]{1,0:T(8,128)(2,1)S(1)} %get-tuple-element.170), channel_id=1, source_target_pairs={{0,1},{1,0},{2,5},{3,4},{4,3},{5,2},{6,7},{7,6},{8,9},{9,8},{10,13... | collective-permute-start | bytes 2359304 | tf_op jit(solution)/shard_map/ppermute | solution.py:52
  140.4 18.6 %collective-permute-start.25 = (bf16[2,448,768]{2,1,0:T(8,128)(2,1)S(1)}, bf16[2,448,768]{2,1,0:T(8,128)(2,1)S(1)}, u32[]{:S(2)}, u32[]{:S(2)}) collective-permute-start(bf16[2,448,768]{2,1,0:T(8,128)(2,1)S(1)} %pad_maximum_fusion.3.refs_2_), channel_id=1, source_target_pairs={{0,4},{4,0},{8,12},{12,8},{16,20},{20,16},{24,28},{28,24},{1,5},{5... | collective-permute-start | bytes 4128776 | tf_op jit(solution)/shard_map/ppermute | solution.py:30
  199.4 126.1 %reduce-scatter.3.cloned.1.call-start = ((), (), s32[]{:S(2)}) async-start(), calls=%async_computation.2 | async-start | bytes 6635520 | tf_op jit(solution)/shard_map/reduce_scatter | solution.py:1126
  200.9 40.0 %collective-permute-start.27 = (bf16[512,768]{1,0:T(8,128)(2,1)S(1)}, bf16[512,768]{1,0:T(8,128)(2,1)S(1)}, u32[]{:S(2)}, u32[]{:S(2)}) collective-permute-start(bf16[512,768]{1,0:T(8,128)(2,1)S(1)} %get-tuple-element.169), channel_id=1, source_target_pairs={{0,0},{1,1},{4,2},{5,3},{2,4},{3,5},{6,6},{7,7},{8,8},{9,9},{12,10... | collective-permute-start | bytes 2359304 | tf_op jit(solution)/shard_map/ppermute | solution.py:62
  201.6 39.3 %collective-permute-start.28 = (bf16[512,768]{1,0:T(8,128)(2,1)S(1)}, bf16[512,768]{1,0:T(8,128)(2,1)S(1)}, u32[]{:S(2)}, u32[]{:S(2)}) collective-permute-start(bf16[512,768]{1,0:T(8,128)(2,1)S(1)} %get-tuple-element.168), channel_id=1, source_target_pairs={{1,0},{0,1},{5,2},{4,3},{3,4},{2,5},{7,6},{6,7},{9,8},{8,9},{13,10... | collective-permute-start | bytes 2359304 | tf_op jit(solution)/shard_map/ppermute | solution.py:62
  308.4 21.3 %collective-permute-start.34 = (bf16[1,2,4,32,1152]{4,3,1,2,0:T(8,128)(2,1)}, bf16[1,2,4,32,1152]{4,3,1,2,0:T(8,128)(2,1)}, u32[]{:S(2)}, u32[]{:S(2)}) collective-permute-start(bf16[1,2,4,32,1152]{4,3,1,2,0:T(8,128)(2,1)} %get-tuple-element.157), channel_id=1, source_target_pairs={{0,8},{4,12},{8,0},{12,4},{16,24},{20,28},{24,16},{28,20},{1,9},{5... | collective-permute-start | bytes 1769480 | tf_op jit(solution)/shard_map/ppermute | solution.py:105
  309.7 19.9 %collective-permute-start.35 = (bf16[1,2,4,32,1152]{4,3,1,2,0:T(8,128)(2,1)}, bf16[1,2,4,32,1152]{4,3,1,2,0:T(8,128)(2,1)}, u32[]{:S(2)}, u32[]{:S(2)}) collective-permute-start(bf16[1,2,4,32,1152]{4,3,1,2,0:T(8,128)(2,1)} %get-tuple-element.159), channel_id=1, source_target_pairs={{0,16},{4,20},{8,24},{12,28},{16,0},{20,4},{24,8},{28,12},{1,17},{... | collective-permute-start | bytes 1769480 | tf_op jit(solution)/shard_map/ppermute | solution.py:105
  311.1 22.5 %collective-permute-start.36 = (bf16[1,2,4,32,1152]{4,3,1,2,0:T(8,128)(2,1)}, bf16[1,2,4,32,1152]{4,3,1,2,0:T(8,128)(2,1)}, u32[]{:S(2)}, u32[]{:S(2)}) collective-permute-start(bf16[1,2,4,32,1152]{4,3,1,2,0:T(8,128)(2,1)} %get-tuple-element.158), channel_id=1, source_target_pairs={{0,24},{4,28},{8,16},{12,20},{16,8},{20,12},{24,0},{28,4},{1,25},{... | collective-permute-start | bytes 1769480 | tf_op jit(solution)/shard_map/ppermute | solution.py:105
  311.9 23.5 %collective-permute-start.33 = (bf16[512,768]{1,0:T(8,128)(2,1)S(1)}, bf16[512,768]{1,0:T(8,128)(2,1)}, u32[]{:S(2)}, u32[]{:S(2)}) collective-permute-start(bf16[512,768]{1,0:T(8,128)(2,1)S(1)} %copy-done.19), channel_id=1, source_target_pairs={{1,0},{0,1},{5,2},{4,3},{3,4},{2,5},{7,6},{6,7},{9,8},{8,9},{13,10... | collective-permute-start | bytes 2359304 | tf_op jit(solution)/shard_map/ppermute | solution.py:62
  340.7 22.0 %collective-permute-start.38 = (bf16[2,2,32,1152]{3,2,1,0:T(8,128)(2,1)S(1)}, bf16[2,2,32,1152]{3,2,1,0:T(8,128)(2,1)S(1)}, u32[]{:S(2)}, u32[]{:S(2)}) collective-permute-start(bf16[2,2,32,1152]{3,2,1,0:T(8,128)(2,1)S(1)} %pad_maximum_fusion.7), channel_id=1, source_target_pairs={{0,1},{1,0},{2,3},{3,2},{4,5},{5,4},{6,7},{7,6},{8,9},{9,8},{10,11... | collective-permute-start | bytes 884744 | tf_op jit(solution)/shard_map/ppermute | solution.py:35
  344.6 32.2 %collective-permute-start.40 = (bf16[216,768]{1,0:T(8,128)(2,1)S(1)}, bf16[216,768]{1,0:T(8,128)(2,1)S(1)}, u32[]{:S(2)}, u32[]{:S(2)}) collective-permute-start(bf16[216,768]{1,0:T(8,128)(2,1)S(1)} %fusion.4), channel_id=1, source_target_pairs={{0,3},{1,2},{2,1},{3,0},{4,7},{5,6},{6,5},{7,4},{8,11},{9,10},{10,... | collective-permute-start | bytes 995336 | tf_op jit(solution)/shard_map/ppermute | solution.py:35
  (60 other events, 866.6 us)
Sparse Core Ops, SparseCore 0:
  199.6 58.5 reduce-scatter.4
  262.1 63.4 reduce-scatter.2

commit v4 on v3

--- a/solution.py
+++ b/solution.py
@@ -47,9 +47,14 @@
         yield a, pairs
 
 
+def bring_round(piece_of, which):
+    a, pairs = list(rounds())[which]
+    z = lax.axis_index("seq")
+    return lax.ppermute(piece_of(a ^ (z & 1)), ("dp", "seq"), pairs)
+
+
 def bring(piece_of):
-    z = lax.axis_index("seq")
-    return [lax.ppermute(piece_of(a ^ (z & 1)), ("dp", "seq"), pairs) for a, pairs in rounds()]
+    return [bring_round(piece_of, which) for which in range(2)]
 
 
 def start_back(rows):
@@ -132,11 +137,6 @@
 
 def gather_quads(upper, lower):
     return [upper, flip_chip(upper, 1), lower, flip_chip(lower, 2)]
-
-
-def finish_quads(upper, upper_x, lower, lower_y):
-    upper, lower = jnp.stack([upper, upper_x]), jnp.stack([lower, lower_y])
-    return [upper, flip_chip(upper, 2), lower, flip_chip(lower, 1)]
 
 
 def tie(values, *others):
@@ -248,7 +248,7 @@
 
 def project_kernel(chips, direct, at_ref, *refs):
     pieces, b_ref = refs[:4], refs[4]
-    sources, (first_ref, rest_ref, tokens_ref, w_ref, sems) = refs[5:-5], refs[-5:]
+    sources, (qkv_ref, tokens_ref, w_ref, sems) = refs[5:-4], refs[-4:]
     if direct:
         span = w_ref.shape[0] // (2 * chips)
         copies = [
@@ -261,37 +261,39 @@
         ]
     else:
         copies = [(sources[0], w_ref)]
-    for copy in start_copies(copies, sems):
-        copy.wait()
-    tile = 256
+
+    @pl.when(pl.program_id(0) == 0)
+    def _():
+        for copy in start_copies(copies, sems):
+            copy.wait()
+
     lane = lax.broadcasted_iota(jnp.int32, (1, w_ref.shape[1]), 1)
     scale = jnp.where(lane % 384 < 128, HEAD ** (-0.5), 1.0)
-
-    size = pieces[0].shape[0]
-    for k, piece_ref in enumerate(pieces):
-
-        def body(at, carry, k=k, piece_ref=piece_ref):
-            tokens = piece_ref[pl.ds(pl.multiple_of(at * tile, tile), tile)]
-            rows = pl.ds(pl.multiple_of(k * size + at * tile, tile), tile)
-            tokens_ref[rows] = tokens
-            values = (dot(tokens, w_ref[...], NN) + b_ref[...]).astype(LOW).astype(WIDE)
-            values = (values * scale).astype(LOW)
-            cut = first_ref.shape[1]
-            first_ref[rows] = values[:, :cut]
-            rest_ref[rows] = values[:, cut:]
-            return carry
-
-        lax.fori_loop(0, size // tile, body, 0, unroll=True)
+    at = pl.program_id(0) * len(pieces) // pl.num_programs(0)
+    rows = pieces[0][...]
+    for k in range(1, len(pieces)):
+        rows = jnp.where(at == k, pieces[k][...], rows)
+    tokens_ref[...] = rows
+    values = (dot(rows, w_ref[...], NN) + b_ref[...]).astype(LOW).astype(WIDE)
+    qkv_ref[...] = (values * scale).astype(LOW)
+
+
+def with_sems(groups, sems):
+    done, copies = 0, []
+    for group in groups:
+        copies.append([pltpu.make_async_copy(*pair, sems.at[done + k]) for k, pair in enumerate(group)])
+        done += len(group)
+    return copies
 
 
 def attend_kernel(
-    first_pair, pairs, blocks, step, near_ref, rand_ref, glob_ref, bias_ref, qkv_ref, out_ref, log_ref
+    pairs, blocks, step, near_ref, rand_ref, glob_ref, bias_ref, qkv_ref, out_ref, log_ref
 ):
     low = lax.broadcasted_iota(jnp.int32, (1, 2 * HEAD), 1) < HEAD
     globs = (glob_ref[0], glob_ref[1])
 
     def scores_of(i, pair):
-        ids = slot_ids(near_ref, rand_ref, globs, i, 2 * (first_pair + pair), blocks)
+        ids = slot_ids(near_ref, rand_ref, globs, i, 2 * pair, blocks)
         queries = diagonal(block_rows(qkv_ref, i, lanes_of(0, pair)), low)
         return dot(gather_blocks(qkv_ref, ids, lanes_of(1, pair), low), queries, NT)
 
@@ -311,14 +313,14 @@
         scores = [scores_of(*unit) for unit in units]
         probs = []
         for (i, pair), score in zip(units, scores):
-            bias = bias_ref[i, first_pair + pair]
+            bias = bias_ref[i, pair]
             score = jnp.concatenate(
                 [score[BLOCK * j : BLOCK * j + BLOCK] + bias[j : j + 1] for j in range(SLOTS)],
                 axis=0,
             )
             probs.append(softmax_of(i, pair, score))
         for (i, pair), prob in zip(units, probs):
-            ids = slot_ids(near_ref, rand_ref, globs, i, 2 * (first_pair + pair), blocks)
+            ids = slot_ids(near_ref, rand_ref, globs, i, 2 * pair, blocks)
             values = gather_blocks(qkv_ref, ids, lanes_of(2, pair), low)
             put(i, pair, dot(prob, values, TN))
         return carry
@@ -346,10 +348,8 @@
     rand_ref,
     glob_ref,
     bias_ref,
-    log_first_ref,
-    log_rest_ref,
-    qkv_first_ref,
-    qkv_rest_ref,
+    log_ref,
+    qkv_ref,
     mine_ref,
     come_ref,
     w_ref,
@@ -368,15 +368,12 @@
     grad_ref[:half] = mine_ref[...]
     grad_ref[half:] = come_ref[...]
     pairs = mine_ref.shape[1] // 128
-    cut = qkv_first_ref.shape[1] // 384
 
     def source(pair, part):
-        ref, at = (qkv_first_ref, pair) if pair < cut else (qkv_rest_ref, pair - cut)
-        return ref.at[:, lanes_of(part, at)]
+        return qkv_ref.at[:, lanes_of(part, pair)]
 
     def log_of(i, pair):
-        ref, at = (log_first_ref, pair) if pair < cut else (log_rest_ref, pair - cut)
-        return ref[i, at : at + 1]
+        return log_ref[i, pair : pair + 1]
 
     every = slice(None)
 
@@ -512,89 +509,110 @@
                 put(chunks * seq * rows_in + (z ^ k) * rows_ff, piece[chunks * rows_in : rows])
 
 
-def unpack_kernel(seq, chunks, at_ref, in_ref, down_ref, near_ref, keep_ref):
-    rows_in, rows_ff = in_ref.shape[1] // seq, down_ref.shape[0] // seq
+def pack_columns_kernel(seq, rows_in, at_ref, shard_ref, near_ref, mirror_ref, out_ref):
+    pieces = [shard_ref, near_ref.at[0], near_ref.at[1], mirror_ref]
+    total = sum(piece[:, rows_in:].astype(WIDE) for piece in pieces).astype(LOW)
+    out_ref[:, seq * rows_in :] = jnp.concatenate([total, jnp.zeros_like(total)], 1)
+    for z in range(seq):
+
+        @pl.when(at_ref[2] == z)
+        def _(z=z):
+            for k, piece in enumerate(pieces):
+                first = (z ^ k) * rows_in
+                out_ref[:, first : first + rows_in] = piece[:, :rows_in]
+
+
+def unpack_kernel(seq, chunks, many, at_ref, *refs):
+    sources, (near_ref, keep_ref) = refs[:-2], refs[-2:]
+    rows = near_ref.shape[1]
+    rows_in = rows // (chunks + 4)
+    rows_ff = rows - chunks * rows_in
+
+    cut = sources[0].shape[0]
+
+    def total(first, size):
+        refs, first = (sources[:many], first) if first < cut else (sources[many:], first - cut)
+        return sum(ref[first : first + size].astype(WIDE) for ref in refs).astype(LOW)
+
     for z in range(seq):
 
         @pl.when(at_ref[2] == z)
         def _(z=z):
             for k in range(seq):
                 target = (keep_ref, near_ref)[k in (1, 2)].at[int(k > 1)]
-                first = (z ^ k) * rows_in
                 for c in range(chunks):
-                    target[c * rows_in : c * rows_in + rows_in] = in_ref[c, first : first + rows_in]
-                first = (z ^ k) * rows_ff
-                target[chunks * rows_in :] = down_ref[first : first + rows_ff]
+                    part = total((c * seq + (z ^ k)) * rows_in, rows_in)
+                    target[c * rows_in : c * rows_in + rows_in] = part
+                target[chunks * rows_in :] = total(chunks * seq * rows_in + (z ^ k) * rows_ff, rows_ff)
 
 
 def weight_copies(chips, direct, chip, core, sources, w_in_ref, w_down_ref, lines_ref):
     if not direct:
-        return [(sources[0], w_in_ref), (sources[1], w_down_ref), (sources[2], lines_ref)]
+        return [(sources[0], w_in_ref), (sources[2], lines_ref)], [], [(sources[1], w_down_ref)]
     wide, width = w_down_ref.shape
     chunks = wide // width
     span, span_ff = width // (2 * chips), wide // (2 * chips)
     cut = span // 2
-    copies = []
+    groups = [], [], []
     for k in range(2):
         for away in range(chips):
             place = 2 * (chip ^ away) + (core if k == 0 else 1 - core)
             upper = sources[4 * k + (away >> 1)].at[away & 1]
             lower = sources[4 * k + 2 + (away & 1)].at[away >> 1]
             rows = pl.ds(pl.multiple_of(place * span, span), span)
-            copies += [
+            groups[1].extend(
                 (upper.at[span * c : span * c + span], w_in_ref.at[c, rows]) for c in range(chunks)
-            ]
+            )
             for half, source in enumerate((upper.at[span * chunks :], lower.at[:cut])):
                 rows = pl.ds(pl.multiple_of(place * span + half * cut, cut), cut)
-                copies.append((source, w_in_ref.at[chunks, rows]))
+                groups[0].append((source, w_in_ref.at[chunks, rows]))
             rows = pl.ds(pl.multiple_of(place * span_ff, span_ff), span_ff)
-            copies.append((lower.at[cut : cut + span_ff], w_down_ref.at[rows]))
-            copies.append((lower.at[cut + span_ff :], lines_ref.at[k * chips + away]))
-    return copies
+            groups[2].append((lower.at[cut : cut + span_ff], w_down_ref.at[rows]))
+            groups[0].append((lower.at[cut + span_ff :], lines_ref.at[k * chips + away]))
+    return groups
 
 
 def forward_kernel(
     chips,
     direct,
     at_ref,
-    mixed_first_ref,
-    mixed_rest_ref,
-    other_first_ref,
-    other_rest_ref,
+    mixed_ref,
+    other_ref,
     tokens_ref,
-    grad_first_ref,
-    grad_last_ref,
     *refs,
 ):
-    sources, refs = refs[:-15], refs[-15:]
-    output_ref, slope_ref, normed_ref, unit_one_ref, grad_second_ref, scale_ref, g_down_ref, sums_ref = refs[:8]
-    w_in_ref, w_down_ref, lines_ref, hidden_ref, down_ref, sems, out_sems = refs[8:]
+    sources, refs = refs[:-11], refs[-11:]
+    output_ref, hidden_ref, slope_ref, normed_ref, unit_one_ref, unit_two_ref, scales_ref = refs[:7]
+    w_in_ref, w_down_ref, lines_ref, sems = refs[7:]
     wide, width = w_down_ref.shape
     half, chunks = width // 2, wide // width
     core = at_ref[1]
-    copies = weight_copies(chips, direct, at_ref[0], core, sources, w_in_ref, w_down_ref, lines_ref)
+    groups = weight_copies(chips, direct, at_ref[0], core, sources, w_in_ref, w_down_ref, lines_ref)
+    groups = with_sems(groups, sems)
 
     @pl.when(pl.program_id(0) == 0)
     def _():
-        sums_ref[...] = jnp.zeros_like(sums_ref)
-        for copy in start_copies(copies, sems):
+        for copy in sum(groups, []):
+            copy.start()
+        for copy in groups[0]:
             copy.wait()
 
-    at, last = pl.program_id(0), pl.num_programs(0) - 1
-    tile = tokens_ref.shape[0]
-    rows = pl.ds(pl.multiple_of(at * tile, tile), tile)
     vectors = jnp.sum(lines_ref[...].astype(WIDE), 0)
     b_out, gain_one, shift_one, b_down, gain_two, shift_two = (vectors[k : k + 1] for k in range(6))
     here = pl.ds(pl.multiple_of(core * half, 128), half)
     there = pl.ds(pl.multiple_of((1 - core) * half, 128), half)
-    mixed = jnp.concatenate([mixed_first_ref[...], mixed_rest_ref[...]], 1)
-    other = jnp.concatenate([other_first_ref[...], other_rest_ref[...]], 1)
-    branch = dot(mixed, w_in_ref[chunks, here], NN) + dot(other, w_in_ref[chunks, there], NN)
+    branch = dot(mixed_ref[...], w_in_ref[chunks, here], NN) + dot(other_ref[...], w_in_ref[chunks, there], NN)
     unit_one, scale_one = norm_parts(tokens_ref[...].astype(WIDE) + (branch + b_out))
     normed = unit_one * gain_one + shift_one
     normed_low = normed.astype(LOW)
     normed_ref[...] = normed_low
     unit_one_ref[...] = unit_one
+
+    @pl.when(pl.program_id(0) == 0)
+    def _():
+        for copy in groups[1] + groups[2]:
+            copy.wait()
+
     down = b_down
     for c in range(0, chunks, 2):
         lanes = slice(width * c, width * c + 2 * width)
@@ -602,33 +620,14 @@
         bias = jnp.concatenate([vectors[6 + c : 7 + c], vectors[7 + c : 8 + c]], 1)
         hidden, slope = gelu_parts(dot(normed_low, weights, NN) + bias)
         hidden = hidden.astype(LOW)
-        hidden_ref[rows, lanes] = hidden
+        hidden_ref[:, lanes] = hidden
         slope_ref[:, lanes] = slope.astype(LOW)
         down = down + dot(hidden, w_down_ref[lanes], NN)
     unit_two, scale_two = norm_parts(normed + down)
     output_ref[...] = (unit_two * gain_two + shift_two).astype(LOW)
     lane = lax.broadcasted_iota(jnp.int32, (1, 128), 1)
-    scale_ref[...] = jnp.where(lane < 128, scale_one, 0.0)
-    grad = jnp.where(2 * at <= last, grad_first_ref[...], grad_last_ref[...]).astype(WIDE)
-    sums_ref[4:5] += jnp.sum(grad * unit_two, 0, keepdims=True)
-    sums_ref[5:6] += jnp.sum(grad, 0, keepdims=True)
-    grad_second = norm_back(grad, unit_two, scale_two, gain_two)
-    grad_second_ref[...] = grad_second
-    grad_down = grad_second.astype(LOW)
-    down_ref[rows] = grad_down
-    sums_ref[3:4] += jnp.sum(grad_down.astype(WIDE), 0, keepdims=True)
-
-    @pl.when(at == last)
-    def _():
-        moving = []
-        for c in range(chunks):
-            lanes = slice(width * c, width * c + width)
-            w_down_ref[lanes] = dot(hidden_ref[:, lanes], down_ref[...], TN).astype(LOW)
-            copy = pltpu.make_async_copy(w_down_ref.at[lanes], g_down_ref.at[lanes], out_sems.at[c])
-            copy.start()
-            moving.append(copy)
-        for copy in moving:
-            copy.wait()
+    scales_ref[...] = jnp.where(lane < 64, scale_one, scale_two)
+    unit_two_ref[...] = unit_two
 
 
 def backward_kernel(
@@ -636,46 +635,59 @@
     chips,
     direct,
     at_ref,
-    mixed_first_ref,
-    mixed_rest_ref,
-    other_first_ref,
-    other_rest_ref,
+    mixed_ref,
+    other_ref,
+    grad_first_ref,
+    grad_last_ref,
     slope_ref,
     unit_one_ref,
-    grad_second_ref,
-    scale_ref,
+    unit_two_ref,
+    scales_ref,
+    hidden_hbm,
     normed_hbm,
     *refs,
 ):
-    sources, refs = refs[:-15], refs[-15:]
-    first_ref, mine_ref, theirs_ref, g_in_ref, sums_ref = refs[:5]
-    w_in_ref, w_down_ref, lines_ref, vectors_ref, pre_ref, branch_ref, normed_ref = refs[5:12]
-    sems, extra_sem, out_sems = refs[12:]
+    sources, refs = refs[:-18], refs[-18:]
+    first_ref, mine_ref, theirs_ref, sums_ref, *grad_refs = refs[:6]
+    w_in_ref, w_down_ref, lines_ref, vectors_ref, pre_ref, branch_ref = refs[6:12]
+    normed_ref, hidden_ref, down_ref, sems, extra_sems, out_sems = refs[12:]
     own, width = normed_ref.shape
     wide = w_down_ref.shape[0]
     half, chunks = width // 2, wide // width
     chip, core = at_ref[0], at_ref[1]
     at, last = pl.program_id(0), pl.num_programs(0) - 1
     rows = pl.ds(pl.multiple_of(at * tile, tile), tile)
-    copies = weight_copies(chips, direct, chip, core, sources, w_in_ref, w_down_ref, lines_ref)
-    extra = pltpu.make_async_copy(normed_hbm, normed_ref, extra_sem.at[0])
+    groups = weight_copies(chips, direct, chip, core, sources, w_in_ref, w_down_ref, lines_ref)
+    groups = with_sems(groups, sems)
+    extra = [
+        pltpu.make_async_copy(hidden_hbm, hidden_ref, extra_sems.at[0]),
+        pltpu.make_async_copy(normed_hbm, normed_ref, extra_sems.at[1]),
+    ]
     here = pl.ds(pl.multiple_of(core * half, 128), half)
     there = pl.ds(pl.multiple_of((1 - core) * half, 128), half)
 
     @pl.when(at == 0)
     def _():
-        started = start_copies(copies, sems)
-        extra.start()
+        for copy in groups[2] + groups[1] + groups[0]:
+            copy.start()
+        for copy in extra:
+            copy.start()
         sums_ref[...] = jnp.zeros_like(sums_ref)
-        for copy in started:
+        for copy in groups[2] + groups[1] + groups[0]:
             copy.wait()
         vectors_ref[...] = jnp.sum(lines_ref[...].astype(WIDE), 0)
 
     def add_sum(k, value):
         sums_ref[k : k + 1] += jnp.sum(value, 0, keepdims=True)
 
-    grad_normed = grad_second_ref[...]
+    grad = jnp.where(2 * at <= last, grad_first_ref[...], grad_last_ref[...]).astype(WIDE)
+    unit_two = unit_two_ref[...]
+    add_sum(4, grad * unit_two)
+    add_sum(5, grad)
+    grad_normed = norm_back(grad, unit_two, scales_ref[:, 64:65], vectors_ref[4:5])
     grad_down = grad_normed.astype(LOW)
+    down_ref[rows] = grad_down
+    add_sum(3, grad_down.astype(WIDE))
     for c in range(chunks):
         lanes = slice(width * c, width * c + width)
         grad_pre = dot(grad_down, w_down_ref[lanes], NT) * slope_ref[:, lanes].astype(WIDE)
@@ -686,7 +698,7 @@
     unit_one = unit_one_ref[...]
     add_sum(1, grad_normed * unit_one)
     add_sum(2, grad_normed)
-    grad_branch = norm_back(grad_normed, unit_one, scale_ref[:, 0:1], vectors_ref[1:2]).astype(LOW)
+    grad_branch = norm_back(grad_normed, unit_one, scales_ref[:, 0:1], vectors_ref[1:2]).astype(LOW)
     first_ref[...] = grad_branch
     branch_ref[rows] = grad_branch
     add_sum(0, grad_branch.astype(WIDE))
@@ -695,23 +707,42 @@
 
     @pl.when(at == last)
     def _():
-        extra.wait()
+        for copy in extra:
+            copy.wait()
         moving = []
-
-        def leave(c):
-            copy = pltpu.make_async_copy(w_in_ref.at[c], g_in_ref.at[c], out_sems.at[c])
-            copy.start()
-            moving.append(copy)
+        span, span_ff = width // (2 * chips), wide // (2 * chips)
+        first = span * (chunks + 1)
+
+        def leave(pairs):
+            for source, target in pairs:
+                copy = pltpu.make_async_copy(source, target, out_sems.at[len(moving)])
+                copy.start()
+                moving.append(copy)
+
+        def leave_rows(c):
+            if not direct:
+                return leave([(w_in_ref.at[c], grad_refs[0].at[c])])
+            for k, target in enumerate(grad_refs):
+                for q in range(chips):
+                    place = 2 * q + (core if k == 0 else 1 - core)
+                    source = w_in_ref.at[c, pl.ds(pl.multiple_of(place * span, span), span)]
+                    leave([(source, target.at[q, span * c : span * c + span])])
 
         for c in range(chunks):
             lanes = slice(width * c, width * c + width)
+            w_down_ref[lanes] = dot(hidden_ref[:, lanes], down_ref[...], TN).astype(LOW)
+            if direct:
+                for k, target in enumerate(grad_refs):
+                    place = 2 * c + (core if k == 0 else 1 - core)
+                    source = w_down_ref.at[pl.ds(pl.multiple_of(place * span_ff, span_ff), span_ff)]
+                    leave([(source, target.at[c, first : first + span_ff])])
+            else:
+                leave([(w_down_ref.at[lanes], grad_refs[1].at[lanes])])
             w_in_ref[c] = dot(normed_ref[...], pre_ref[:, lanes], TN).astype(LOW)
-            leave(c)
-        mixed = jnp.concatenate([mixed_first_ref[...], mixed_rest_ref[...]], 1)
-        other = jnp.concatenate([other_first_ref[...], other_rest_ref[...]], 1)
-        w_in_ref[chunks, here] = dot(mixed, branch_ref[...], TN).astype(LOW)
-        w_in_ref[chunks, there] = dot(other, branch_ref[...], TN).astype(LOW)
-        leave(chunks)
+            leave_rows(c)
+        w_in_ref[chunks, here] = dot(mixed_ref[...], branch_ref[...], TN).astype(LOW)
+        w_in_ref[chunks, there] = dot(other_ref[...], branch_ref[...], TN).astype(LOW)
+        leave_rows(chunks)
         for copy in moving:
             copy.wait()
 
@@ -721,36 +752,51 @@
 
 
 IN_ANY = pl.BlockSpec(memory_space=pl.ANY)
+
+
+TILE = 256
+
+
+def tiles(width, first=0, many=None):
+    if many is None:
+        return pl.BlockSpec((TILE, width), lambda i: (i, 0))
+    return pl.BlockSpec((TILE, width), lambda i: (jnp.clip(i - first, 0, many - 1), 0))
 
 
 def project_tokens(at, pieces, b_qkv, weights, direct):
     length, width = 4 * pieces[0].shape[0], pieces[0].shape[1]
     half = width // 2
     chips = lax.axis_size("dp") // 2
+    many = pieces[0].shape[0] // TILE
+
+    def all_of(*shape):
+        return pl.BlockSpec(shape, lambda i: (0, 0))
+
     return pl.pallas_call(
         partial(project_kernel, chips, direct),
+        grid=(length // TILE,),
         out_shape=(
-            jax.ShapeDtypeStruct((length, 384), LOW),
-            jax.ShapeDtypeStruct((length, 3 * half - 384), LOW),
+            jax.ShapeDtypeStruct((length, 3 * half), LOW),
             jax.ShapeDtypeStruct((length, width), LOW),
             jax.ShapeDtypeStruct((width, 3 * half), LOW),
         ),
-        in_specs=[IN_SMEM] + [IN_VMEM] * 5 + [IN_ANY] * len(weights),
-        out_specs=(IN_VMEM,) * 4,
+        in_specs=[IN_SMEM]
+        + [tiles(width, many * k, many) for k in range(4)]
+        + [all_of(1, 3 * half)]
+        + [IN_ANY] * len(weights),
+        out_specs=(tiles(3 * half), tiles(width), all_of(width, 3 * half)),
         scratch_shapes=[pltpu.SemaphoreType.DMA((2 * chips,))],
         compiler_params=pltpu.CompilerParams(vmem_limit_bytes=48 << 20),
-        cost_estimate=pl.CostEstimate(
-            flops=4_000_000_000, bytes_accessed=12_000_000, transcendentals=0
-        ),
+        cost_estimate=pl.CostEstimate(flops=1, bytes_accessed=1, transcendentals=0),
         name="project",
     )(at, *pieces, b_qkv, *weights)
 
 
-def attend(first_pair, near, rand, globs, bias, qkv):
+def attend(near, rand, globs, bias, qkv):
     length, width = qkv.shape
     pairs, blocks = width // 384, length // BLOCK
     return pl.pallas_call(
-        partial(attend_kernel, first_pair, pairs, blocks, 8 // pairs),
+        partial(attend_kernel, pairs, blocks, 4),
         out_shape=(
             jax.ShapeDtypeStruct((length, 128 * pairs), LOW),
             jax.ShapeDtypeStruct((blocks, 8, 128), WIDE),
@@ -758,15 +804,13 @@
         in_specs=[IN_SMEM] * 3 + [IN_VMEM] * 2,
         out_specs=(IN_VMEM,) * 2,
         compiler_params=pltpu.CompilerParams(vmem_limit_bytes=48 << 20),
-        cost_estimate=pl.CostEstimate(
-            flops=6_000_000_000 * pairs, bytes_accessed=3_000_000 * pairs, transcendentals=0
-        ),
+        cost_estimate=pl.CostEstimate(flops=1, bytes_accessed=1, transcendentals=0),
         name="attend",
     )(near, rand, globs, bias, qkv)
 
 
-def attend_back(near, rand, globs, bias, logs, qkvs, mine, come, w_qkv, grad_first):
-    length, (wide, width) = qkvs[0].shape[0], w_qkv.shape
+def attend_back(near, rand, globs, bias, log_total, qkv, mine, come, w_qkv, grad_first):
+    length, (wide, width) = qkv.shape[0], w_qkv.shape
     pairs, blocks = width // 384, length // BLOCK
     rows = jax.ShapeDtypeStruct((length // 2, wide), LOW)
     return pl.pallas_call(
@@ -777,18 +821,29 @@
             rows,
             jax.ShapeDtypeStruct((1, width), WIDE),
         ),
-        in_specs=[IN_SMEM] * 3 + [IN_VMEM] * 9,
+        in_specs=[IN_SMEM] * 3 + [IN_VMEM] * 7,
         out_specs=(IN_VMEM,) * 4,
         scratch_shapes=[
             pltpu.VMEM((length, 128 * pairs), LOW),
             pltpu.VMEM((length, 256 * pairs), WIDE),
         ],
         compiler_params=pltpu.CompilerParams(vmem_limit_bytes=56 << 20),
-        cost_estimate=pl.CostEstimate(
-            flops=40_000_000_000, bytes_accessed=20_000_000, transcendentals=0
-        ),
+        cost_estimate=pl.CostEstimate(flops=1, bytes_accessed=1, transcendentals=0),
         name="attend_back",
-    )(near, rand, globs, bias, *logs, *qkvs, mine, come, w_qkv, grad_first)
+    )(near, rand, globs, bias, log_total, qkv, mine, come, w_qkv, grad_first)
+
+
+def pack_columns(at, shard, near, mirror, rows_in):
+    two, rows, width = shard.shape
+    rows = 4 * rows_in + 2 * (rows - rows_in)
+    return pl.pallas_call(
+        partial(pack_columns_kernel, 4, rows_in),
+        out_shape=jax.ShapeDtypeStruct((two, rows, width), LOW),
+        in_specs=[IN_SMEM] + [IN_VMEM] * 3,
+        out_specs=IN_VMEM,
+        cost_estimate=pl.CostEstimate(flops=1, bytes_accessed=1, transcendentals=0),
+        name="pack_columns",
+    )(at, shard, near, mirror)
 
 
 def pack_rows(at, shard, near, mirror, chunks, cut):
@@ -801,17 +856,9 @@
         ),
         in_specs=[IN_SMEM] + [IN_VMEM] * 3,
         out_specs=(IN_VMEM, IN_VMEM),
+        cost_estimate=pl.CostEstimate(flops=1, bytes_accessed=1, transcendentals=0),
         name="pack",
     )(at, shard, near, mirror)
-
-
-TILE = 256
-
-
-def tiles(width, first=0, many=None):
-    if many is None:
-        return pl.BlockSpec((TILE, width), lambda i: (i, 0))
-    return pl.BlockSpec((TILE, width), lambda i: (jnp.clip(i - first, 0, many - 1), 0))
 
 
 def weight_space(chips, direct, chunks, width):
@@ -822,22 +869,22 @@
     ]
 
 
-def unpack_rows(at, rows_in, rows_down):
-    chunks, span, width = rows_in.shape
-    like = jax.ShapeDtypeStruct((2, (chunks * span + rows_down.shape[0]) // 4, width), LOW)
+def unpack_rows(at, upper, lower, chunks):
+    rows, width = upper[0].shape[0] + lower[0].shape[0], upper[0].shape[1]
+    like = jax.ShapeDtypeStruct((2, rows // 4, width), LOW)
     return pl.pallas_call(
-        partial(unpack_kernel, 4, chunks),
+        partial(unpack_kernel, 4, chunks, len(upper)),
         out_shape=(like, like),
-        in_specs=[IN_SMEM] + [IN_VMEM] * 2,
+        in_specs=[IN_SMEM] + [IN_VMEM] * (len(upper) + len(lower)),
         out_specs=(IN_VMEM, IN_VMEM),
+        cost_estimate=pl.CostEstimate(flops=1, bytes_accessed=1, transcendentals=0),
         name="unpack",
-    )(at, rows_in, rows_down)
-
-
-def layer_forward(at, mixed, other, tokens, grads, weights, direct, chunks):
-    own, width = other[0].shape[0], tokens.shape[1]
+    )(at, *upper, *lower)
+
+
+def layer_forward(at, mixed, other, tokens, weights, direct, chunks):
+    own, width = other.shape[0], tokens.shape[1]
     chips, wide = lax.axis_size("dp") // 2, chunks * width
-    many = own // TILE // 2
 
     def rows(width, kind=LOW):
         return jax.ShapeDtypeStruct((own, width), kind)
@@ -845,36 +892,35 @@
     return pl.pallas_call(
         partial(forward_kernel, chips, direct),
         grid=(own // TILE,),
-        out_shape=(rows(width), rows(wide), rows(width))
-        + (rows(width, WIDE), rows(width, WIDE), rows(128, WIDE))
-        + (jax.ShapeDtypeStruct((wide, width), LOW), jax.ShapeDtypeStruct((16, width), WIDE)),
+        out_shape=(rows(width), rows(wide), rows(wide), rows(width))
+        + (rows(width, WIDE), rows(width, WIDE), rows(128, WIDE)),
         in_specs=[IN_SMEM]
-        + [tiles(p.shape[1]) for p in (*mixed, *other, tokens)]
-        + [tiles(width, 0, many), tiles(width, many, many)]
+        + [tiles(p.shape[1]) for p in (mixed, other, tokens)]
         + [IN_ANY] * len(weights),
-        out_specs=tuple(tiles(w) for w in (width, wide, width, width, width, 128))
-        + (IN_ANY, pl.BlockSpec((16, width), lambda i: (0, 0))),
+        out_specs=tuple(tiles(w) for w in (width, wide, wide, width, width, width, 128)),
         scratch_shapes=weight_space(chips, direct, chunks, width)
-        + [
-            pltpu.VMEM((own, wide), LOW),
-            pltpu.VMEM((own, width), LOW),
-            pltpu.SemaphoreType.DMA((2 * chips * (chunks + 4),)),
-            pltpu.SemaphoreType.DMA((chunks,)),
-        ],
+        + [pltpu.SemaphoreType.DMA((2 * chips * (chunks + 4),))],
         compiler_params=pltpu.CompilerParams(vmem_limit_bytes=58 << 20),
-        cost_estimate=pl.CostEstimate(
-            flops=22_000_000_000, bytes_accessed=36_000_000, transcendentals=0
-        ),
+        cost_estimate=pl.CostEstimate(flops=1, bytes_accessed=1, transcendentals=0),
         name="layer_forward",
-    )(at, *mixed, *other, tokens, *grads, *weights)
-
-
-def layer_backward(at, mixed, other, slope, unit_one, grad_second, scale, normed, weights, direct):
+    )(at, mixed, other, tokens, *weights)
+
+
+def layer_backward(at, mixed, other, grads, slope, units, scales, hidden, normed, weights, direct):
     own, width = normed.shape
     wide = slope.shape[1]
     half, chunks = width // 2, wide // width
     chips = lax.axis_size("dp") // 2
-    whole = pl.BlockSpec((own, 128), lambda i: (0, 0)), pl.BlockSpec((own, half - 128), lambda i: (0, 0))
+    many = own // TILE // 2
+    whole = pl.BlockSpec((own, half), lambda i: (0, 0))
+    if direct:
+        rows = ((chunks + 1) * width + wide) // (2 * chips)
+        grads_like = (jax.ShapeDtypeStruct((chips, rows, width), LOW),) * 2
+    else:
+        grads_like = (
+            jax.ShapeDtypeStruct((chunks + 1, width, width), LOW),
+            jax.ShapeDtypeStruct((wide, width), LOW),
+        )
     return pl.pallas_call(
         partial(backward_kernel, TILE, chips, direct),
         grid=(own // TILE,),
@@ -882,31 +928,33 @@
             jax.ShapeDtypeStruct((own, width), LOW),
             jax.ShapeDtypeStruct((own, half), LOW),
             jax.ShapeDtypeStruct((own, half), LOW),
-            jax.ShapeDtypeStruct((chunks + 1, width, width), LOW),
             jax.ShapeDtypeStruct((16, width), WIDE),
-        ),
+        )
+        + grads_like,
         in_specs=[IN_SMEM]
-        + [whole[0], whole[1]] * 2
+        + [whole, whole]
+        + [tiles(width, 0, many), tiles(width, many, many)]
         + [tiles(wide), tiles(width), tiles(width), tiles(128)]
-        + [IN_ANY] * (1 + len(weights)),
-        out_specs=(tiles(width), tiles(half), tiles(half), IN_ANY)
-        + (pl.BlockSpec((16, width), lambda i: (0, 0)),),
+        + [IN_ANY] * (2 + len(weights)),
+        out_specs=(tiles(width), tiles(half), tiles(half))
+        + (pl.BlockSpec((16, width), lambda i: (0, 0)),)
+        + (IN_ANY,) * 2,
         scratch_shapes=weight_space(chips, direct, chunks, width)
         + [
             pltpu.VMEM((16, width), WIDE),
             pltpu.VMEM((own, wide), LOW),
             pltpu.VMEM((own, width), LOW),
             pltpu.VMEM((own, width), LOW),
+            pltpu.VMEM((own, wide), LOW),
+            pltpu.VMEM((own, width), LOW),
             pltpu.SemaphoreType.DMA((2 * chips * (chunks + 4),)),
-            pltpu.SemaphoreType.DMA((1,)),
-            pltpu.SemaphoreType.DMA((chunks + 1,)),
+            pltpu.SemaphoreType.DMA((2,)),
+            pltpu.SemaphoreType.DMA((2 * chips * (chunks + 1) + 2 * chunks,)),
         ],
         compiler_params=pltpu.CompilerParams(vmem_limit_bytes=58 << 20),
-        cost_estimate=pl.CostEstimate(
-            flops=22_000_000_000, bytes_accessed=40_000_000, transcendentals=0
-        ),
+        cost_estimate=pl.CostEstimate(flops=1, bytes_accessed=1, transcendentals=0),
         name="layer_backward",
-    )(at, *mixed, *other, slope, unit_one, grad_second, scale, normed, *weights)
+    )(at, mixed, other, *grads, slope, *units, scales, hidden, normed, *weights)
 
 
 def place_of(block, core, z, blocks):
@@ -1030,7 +1078,18 @@
     wide_z = gather_seq(tie(packed, shard), qkv_z[2])
     at = jnp.stack([lax.axis_index("dp") >> 1, core, z]).astype(jnp.int32)
 
-    numbers = tie(numbers, wide_z[2])
+    direct = span % 16 == 0 and chips == chunks
+    if direct:
+        whole = pack_columns(at, *qkv_z, rows_in)
+    else:
+        qkv_z = in_seq_order(*qkv_z)
+        whole = []
+        for k in range(2):
+            lines = sum(p[k, rows_in:].astype(WIDE) for p in qkv_z).astype(LOW)
+            whole += [p[k, :rows_in] for p in qkv_z] + [lines, jnp.zeros_like(lines)]
+        whole = jnp.concatenate(whole, 0).reshape(2, span + 16, 3 * half_width)
+    qkv_parts = gather_chips(whole)
+    numbers = tie(numbers, whole)
     numbers = jnp.concatenate([numbers, swap(numbers)], 0)
     local_blocks = rand_blocks.shape[2]
     count = HEADS * local_blocks * 3
@@ -1040,19 +1099,15 @@
     rand = rand.transpose(1, 0, 2, 3).reshape(own_heads, blocks, 3)
     sides, rand, glob_at, bias = tables(rand, globs, blocks)
 
-    qkv_z = in_seq_order(*qkv_z)
-    whole = []
-    for k in range(2):
-        lines = sum(p[k, rows_in:].astype(WIDE) for p in qkv_z).astype(LOW)
-        whole += [p[k, :rows_in] for p in qkv_z] + [lines, jnp.zeros_like(lines)]
-    qkv_parts = gather_chips(jnp.concatenate(whole, 0).reshape(2, span + 16, 3 * half_width))
 
     tied_inputs = tie(inputs, qkv_z[2])
     pieces = bring(lambda s: pick(tied_inputs, s, 0)[0])
 
     if direct:
         cut = chunks * span + span // 2
-        near, pieces[0], *qkv_parts = join(wide_z[1], pieces[0], *qkv_parts)
+        near, pieces[0], bias, sides, rand, glob_at, *qkv_parts = join(
+            wide_z[1], pieces[0], bias, sides, rand, glob_at, *qkv_parts
+        )
         whole = pack_rows(at, wide_z[0], near, wide_z[2], chunks + 1, cut)
     else:
         wide_z = in_seq_order(*wide_z)
@@ -1064,12 +1119,11 @@
         rows.append(sum(p[rows_a + rows_ff :].astype(WIDE) for p in wide_z).astype(LOW))
         whole = jnp.concatenate(rows, 0)
     if direct:
-        parts = gather_quads(*whole)
-        joined_up = join(*parts, *pieces)
-        parts, pieces = joined_up[:4], joined_up[4:]
+        lines = sum(jnp.sum(p[:, span].astype(WIDE), 0, keepdims=True) for p in qkv_parts)
+        *parts, lines, pieces[0], pieces[1] = join(*gather_quads(*whole), lines, *pieces)
     else:
         parts = gather_chips(tie(whole, qkv_parts))
-    lines = sum(jnp.sum(p[:, span].astype(WIDE), 0, keepdims=True) for p in qkv_parts)
+        lines = sum(jnp.sum(p[:, span].astype(WIDE), 0, keepdims=True) for p in qkv_parts)
     pieces = [*pieces, *(swap(p) for p in pieces)]
     rows_a, rows_b = (chunks + 1) * span, (chunks + 1) * span + span_ff
     if direct:
@@ -1079,15 +1133,19 @@
         qkv_weights = (jnp.concatenate([p[k, :span] for p in ordered for k in range(2)], 0),)
 
     if direct:
-        parts = finish_quads(*parts)
-    qkv_first, qkv_rest, tokens, w_qkv = project_tokens(at, pieces, lines, qkv_weights, direct)
-    mixed_first, log_first = attend(0, sides, rand, glob_at, bias, qkv_first)
-    tied_cotangent = tie(cotangent, *pieces)
-    grad_result = bring(lambda s: pick(tied_cotangent, s, 0)[0])
-    mixed_first, qkv_rest, *parts = join(mixed_first, qkv_rest, *parts)
-    other_first = swap(mixed_first[own:])
-    other_parts = [swap(p) for p in parts]
-    mixed_rest, log_rest = attend(1, sides, rand, glob_at, bias, qkv_rest)
+        upper, lower = jnp.stack(parts[:2]), jnp.stack(parts[2:])
+        parts = [upper, flip_chip(upper, 2), lower, flip_chip(lower, 1)]
+        other_parts = [swap(upper), None, swap(lower), None]
+    qkv, tokens, w_qkv = project_tokens(at, pieces, lines, qkv_weights, direct)
+    mixed, log_total = attend(sides, rand, glob_at, bias, qkv)
+    tied = tie(cotangent, qkv)
+    first_grads = bring_round(lambda s: pick(tied, s, 0)[0], 0)
+    mixed, log_total, first_grads, *parts = join(mixed, log_total, first_grads, *parts)
+    other = swap(mixed[own:])
+    if direct:
+        other_parts[1], other_parts[3] = swap(parts[1]), swap(parts[3])
+    else:
+        other_parts = [swap(p) for p in parts]
     if direct:
         weights = tuple(parts + other_parts)
     else:
@@ -1103,60 +1161,84 @@
             in_device_order(*([p[rows_a:rows_b] for p in ps] for ps in (parts, other_parts))),
             sum(p[rows_b:].astype(WIDE) for p in parts + other_parts).astype(LOW)[None],
         )
-    other = other_first, swap(mixed_rest[own:])
-    result, slope, normed, unit_one, grad_second, scale, grad_down, down_sums = layer_forward(
-        at, (mixed_first, mixed_rest), other, tokens, grad_result, weights, direct, chunks
-    )
+    tied = tie(cotangent, mixed)
+    grad_result = first_grads, bring_round(lambda s: pick(tied, s, 0)[0], 1)
+    forward = layer_forward(at, mixed, other, tokens, weights, direct, chunks)
+    forward, grad_result = join(forward, grad_result)
+    result, hidden, slope, normed, unit_one, unit_two, scales = forward
     output = send_back(result)
-
-    grad_down = lax.psum_scatter(grad_down, "dp", scatter_dimension=0, tiled=True)
-    *backward, grad_in, in_sums = layer_backward(
+    backward = layer_backward(
         at,
-        (mixed_first, mixed_rest),
+        mixed,
         other,
+        grad_result,
         slope,
-        unit_one,
-        grad_second,
-        scale,
+        (unit_one, unit_two),
+        scales,
+        hidden,
         normed,
         weights,
         direct,
     )
-    grad_first, mine, theirs, grad_in, in_sums, *output = join(*backward, grad_in, in_sums, *output)
-    grad_in = lax.psum_scatter(grad_in, "dp", scatter_dimension=1, tiled=True)
+    backward, output = join(backward, output)
+    grad_first, mine, theirs, in_sums, grad_in, grad_down = backward
 
     come = swap(theirs)
+    if direct:
+        chip = lax.axis_index("dp") >> 1
+        x, y = chip & 1, chip >> 1
+        grad_other, come = join(swap(grad_down), come)
+        sums = added(grad_in, grad_other).reshape(2, 2, -1, width)
+        cut = chunks * span + span // 2
+        upper, lower = sums[:, :, :cut], sums[:, :, cut:]
+        moves = [pick(upper, x, 1), pick(upper, 1 - x, 1), pick(lower, y, 0), pick(lower, 1 - y, 0)]
+        mine, come, *moves = join(mine, come, *moves)
+        moves[1], moves[3] = flip_chip(moves[1], 1), flip_chip(moves[3], 2)
     grad_qkv, grad_own, grad_theirs, sums = attend_back(
         sides,
         rand,
         glob_at,
         bias,
-        (log_first, log_rest),
-        (qkv_first, qkv_rest),
+        log_total,
+        qkv,
         mine,
         come,
         w_qkv,
         grad_first,
     )
-    come = swap(grad_theirs)
+    if direct:
+        grad_qkv, grad_own, grad_theirs, sums, *moves = join(grad_qkv, grad_own, grad_theirs, sums, *moves)
+    come_rows = swap(grad_theirs)
     grad_w_qkv = dot(tokens, grad_qkv, TN).astype(LOW)
-    grad_w_qkv, grad_own, come = join(grad_w_qkv, grad_own, come)
-    grad_inputs = start_back(added(grad_own, come))
-    vectors = (down_sums + in_sums)[: 6 + chunks].reshape(-1)
+    vectors = in_sums[: 6 + chunks].reshape(-1)
     vectors = jnp.pad(vectors, (0, -vectors.shape[0] % (3 * half_width))).reshape(-1, 3 * half_width)
     lines = jnp.concatenate([sums, vectors], 0).astype(LOW)
     lines = jnp.broadcast_to(lines, (chips, 2, n_seq) + lines.shape)
     parts = jnp.concatenate(
         [grad_w_qkv.reshape(chips, 2, n_seq, rows_in, 3 * half_width), lines], 3
     )
-    come = swap(pick(parts, 1 - core, 1)[:, 0])
+    keep, come = (pick(parts, which, 1)[:, 0] for which in (core, 1 - core))
+    if direct:
+        keep, come, *moves = join(keep, come, *moves)
+        upper, lower = added(*moves[:2]), added(*moves[2:])
+        moves = [pick(upper, y, 0), pick(upper, 1 - y, 0), pick(lower, x, 1), pick(lower, 1 - x, 1)]
+        grad_own, *moves = join(grad_own, *(move.reshape(-1, width) for move in moves))
+        moves[1], moves[3] = flip_chip(moves[1], 2), flip_chip(moves[3], 1)
+    come = swap(come)
+    grad_tokens = added(grad_own, come_rows)
+    parts = jnp.stack([keep, come], 1)
+    grad_inputs = start_back(grad_tokens)
     first_back = finish_back(grad_inputs, 0)
-    come, first_back = join(come, first_back)
-    near_sums, keep_sums = unpack_rows(at, grad_in, grad_down)
+    if direct:
+        first_back, *moves = join(first_back, *moves)
+        near_sums, keep_sums = unpack_rows(at, moves[:2], moves[2:], chunks + 1)
+    else:
+        rows = lax.psum_scatter(grad_in, "dp", scatter_dimension=1, tiled=True)
+        rows = rows.reshape((chunks + 1) * span, width)
+        down = lax.psum_scatter(grad_down, "dp", scatter_dimension=0, tiled=True)
+        near_sums, keep_sums = unpack_rows(at, [rows], [down], chunks + 1)
+    grad_inputs = first_back, finish_back(tie(grad_inputs, near_sums), 1)
     near_sums = flip_seq(near_sums, 1)
-    parts = jnp.stack([pick(parts, core, 1)[:, 0], come], 1)
-    grad_inputs, parts = tie((grad_inputs, parts), first_back)
-    grad_inputs = first_back, finish_back(grad_inputs, 1)
     parts = reduce_chips(parts)
     parts, near_sums = join(parts, near_sums)
     own_qkv = reduce_seq(parts.transpose(1, 0, 2, 3))

time: 401 us -> 388 us (0.968)
  starting transfers between devices: 97.3 us -> 66.6 us
  waiting for transfers between devices: 65.2 us -> 91.6 us
  between operations: 16.9 us -> 3.52 us
  other arithmetic: 21.9 us -> 29.5 us
  Pallas kernels: 151 us -> 146 us
    ppermute x8, starting transfers between devices: 61 us -> 21.5 us  [flip_seq(): return lax.ppermute(array, 'seq', [(i, i ^ k) for i in range(size)])]
    ppermute x4, waiting for transfers between devices: 0.01 us -> 20.7 us  [finish_back(): return lax.ppermute(parts[a], ('dp', 'seq'), [(t, s) for s, t in pairs])]
    ppermute x10 -> x14, waiting for transfers between devices: 34.5 us -> 50.1 us  [flip_chip(): return lax.ppermute(array, 'dp', [(i, i ^ 2 * away) for i in range(size)])]
    ppermute x6, waiting for transfers between devices: 10 us -> 0.02 us  [bring_round(): return lax.ppermute(piece_of(a ^ z & 1), ('dp', 'seq'), pairs)]
    reduce_scatter x2 -> x0, waiting for transfers between devices: 9.85 us -> none  [the longest x1 9.85 us: shards(): grad_in = lax.psum_scatter(grad_in, 'dp', scatter_dimension=1, tiled=True)]
    pallas_call x1, Pallas kernels: 38.7 us -> 29 us  [layer_forward(): pl.pallas_call(partial(forward_kernel, chips, direct), grid=(own // TILE,...]
    ppermute x13, waiting for transfers between devices: 4.08 us -> 13.1 us  [swap(): return lax.ppermute(array, 'dp', [(i, i ^ 1) for i in range(size)])]
    convert_element_type x3 -> x6, other arithmetic: 0.6 us -> 7.9 us  [added(): return sum((array.astype(WIDE) for array in arrays)).astype(LOW)]
  transfers between devices with their start and end apart: 43 -> 45, of which waited for: 13 -> 15; matrix products, arithmetic and copies ran while one was open for 11% -> 12% of each run, Pallas kernels for 29% -> 38%
where the time goes in v4:
time: 388 us; the launch traced here: 381 us
  Pallas kernels  146 us (38%)
  waiting for transfers between devices  91.6 us (24%)
  starting transfers between devices  66.6 us (17%)
  local copies, waits for them, and re-layouts  36.2 us (9%)
  other arithmetic  29.5 us (8%)
  matrix products  7.02 us (2%)
    ppermute x14, waiting for transfers between devices, flip_chip(): return lax.ppermute(array, 'dp', [(i, i ^ 2 * away) for i in range(size)])  50.1 us
    pallas_call x1, Pallas kernels, attend_back(): pl.pallas_call(partial(attend_back_kernel, blocks, 2), out_shape=(jax.Sha...  42.5 us
    pallas_call x1, Pallas kernels, layer_backward(): pl.pallas_call(partial(backward_kernel, TILE, chips, direct), grid=(own /...  37.3 us
    pallas_call x1, Pallas kernels, layer_forward(): pl.pallas_call(partial(forward_kernel, chips, direct), grid=(own // TILE,...  29 us
    ppermute x8, starting transfers between devices, flip_seq(): return lax.ppermute(array, 'seq', [(i, i ^ k) for i in range(size)])  21.5 us
    ppermute x4, waiting for transfers between devices, finish_back(): return lax.ppermute(parts[a], ('dp', 'seq'), [(t, s) for s, t in pairs])  20.7 us
    pallas_call x1, Pallas kernels, attend(): pl.pallas_call(partial(attend_kernel, pairs, blocks, 4), out_shape=(jax.S...  19.2 us
    ppermute x14, starting transfers between devices, flip_chip(): return lax.ppermute(array, 'dp', [(i, i ^ 2 * away) for i in range(size)])  16.6 us
  transfers between devices with their start and end apart: 45, of which 15 were waited for; matrix products, arithmetic and copies ran while one was open for 12% of the time, Pallas kernels for 38%

profile of v4, /device:TPU:0, one launch (start us, length us, event | category | flops | bytes accessed | tf_op | source)
XLA Modules:
  0.0 380.7 jit_solution(16211899800893874303)
XLA Ops:
  8.0 2.6 collective-permute-start.3
  12.6 6.7 %collective-permute-start.4 = (bf16[2,32,1152]{2,1,0:T(8,128)(2,1)S(1)}, bf16[2,32,1152]{2,1,0:T(8,128)(2,1)S(1)}, u32[]{:S(2)}, u32[]{:S(2)}) collective-permute-start(bf16[2,32,1152]{2,1,0:T(8,128)(2,1)S(1)} %pad_maximum_fusion.8.shard_ref), channel_id=1, source_target_pairs={{0,3},{1,2},{2,1},{3,0},{4,7},{5,6},{6,5},{7,4},{8,11},{9,10},{10,... | collective-permute-start | bytes 442376 | tf_op jit(solution)/shard_map/ppermute | solution.py:35
  22.6 10.8 %collective-permute-start.7 = (bf16[2,2,32,1152]{3,2,1,0:T(8,128)(2,1)S(1)}, bf16[2,2,32,1152]{3,2,1,0:T(8,128)(2,1)}, u32[]{:S(2)}, u32[]{:S(2)}) collective-permute-start(bf16[2,2,32,1152]{3,2,1,0:T(8,128)(2,1)S(1)} %pad_maximum_fusion.5), channel_id=1, source_target_pairs={{0,1},{1,0},{2,3},{3,2},{4,5},{5,4},{6,7},{7,6},{8,9},{9,8},{10,11... | collective-permute-start | bytes 884744 | tf_op jit(solution)/shard_map/ppermute | solution.py:35
  34.0 2.6 dynamic-slice_bitcast_fusion.2
  58.3 12.5 %collective-permute-done.10.refs_7_ = bf16[2,112,1152]{2,1,0:T(8,128)(2,1)} collective-permute-done((bf16[2,112,1152]{2,1,0:T(8,128)(2,1)}, bf16[2,112,1152]{2,1,0:T(8,128)(2,1)}, u32[]{:S(2)}, u32[]{:S(2)}) %collective-permute-start.10) | collective-permute-done | bytes 516128 | tf_op jit(solution)/shard_map/ppermute | solution.py:110
  72.1 2.5 pack.1
  80.0 12.1 %collective-permute-done.12 = bf16[432,768]{1,0:T(8,128)(2,1)S(1)} collective-permute-done((bf16[432,768]{1,0:T(8,128)(2,1)}, bf16[432,768]{1,0:T(8,128)(2,1)S(1)}, u32[]{:S(2)}, u32[]{:S(2)}) %collective-permute-start.12) | collective-permute-done | bytes 663584 | tf_op jit(solution)/shard_map/ppermute | solution.py:110
  96.5 10.8 %project.1 = (bf16[2048,1152]{1,0:T(8,128)(2,1)}, bf16[2048,768]{1,0:T(8,128)(2,1)}, bf16[768,1152]{1,0:T(8,128)(2,1)}) custom-call(s32[3]{0:T(128)S(1)} %copy-done.7, bf16[512,768]{1,0:T(8,128)(2,1)S(1)} %collective-permute-done.6.refs_0_, bf16[512,768]{1,0:T(8,128)(2,1)} %collective-permute-done.14.refs_1_, ...), custom_call_target="tpu_custom_call" | custom-call | flops 1 | bytes 1 | tf_op jit(solution)/shard_map/project/pallas_call | solution.py:775
  110.9 19.2 %attend.1 = (bf16[2048,384]{1,0:T(8,128)(2,1)S(1)}, f32[32,8,128]{2,1,0:T(8,128)S(1)}) custom-call(s32[64]{0:T(128)S(1)} %pad_add_fusion.5.near_ref, s32[576]{0:T(1024)S(1)} %fusion.13.rand_ref, s32[2]{0:T(128)S(1)} %fusion.32.glob_ref, f32[32,3,8,128]{3,2,1,0:T(8,128)S(1)} %reshape.560.bias_ref, bf16[2048,1152]{1,0:T(8,128)(2,1)} %get-tuple-element.146.qkv_ref), custom_call_target="tpu_custom_call" | custom-call | flops 1 | bytes 1 | tf_op jit(solution)/shard_map/attend/pallas_call | solution.py:798
  133.1 3.3 collective-permute-done.20.other_ref
  138.9 29.0 %layer_forward.1 = (bf16[1024,768]{1,0:T(8,128)(2,1)}, bf16[1024,3072]{1,0:T(8,128)(2,1)}, bf16[1024,3072]{1,0:T(8,128)(2,1)}, bf16[1024,768]{1,0:T(8,128)(2,1)}...) custom-call(s32[3]{0:T(128)} %pad_add_fusion.4.at_ref, bf16[2048,384]{1,0:T(8,128)(2,1)} %copy-done.2, ...), custom_call_target="tpu_custom_call" | custom-call | flops 1 | bytes 1 | tf_op jit(solution)/shard_map/layer_forward/pallas_call | solution.py:892
  172.5 37.3 %layer_backward.1 = (bf16[1024,768]{1,0:T(8,128)(2,1)}, bf16[1024,384]{1,0:T(8,128)(2,1)}, bf16[1024,384]{1,0:T(8,128)(2,1)}, f32[16,768]{1,0:T(8,128)}, bf16[4,...) custom-call(s32[3]{0:T(128)} %pad_add_fusion.4.at_ref, bf16[2048,384]{1,0:T(8,128)(2,1)} %copy-done.2, ...), custom_call_target="tpu_custom_call" | custom-call | flops 1 | bytes 1 | tf_op jit(solution)/shard_map/layer_backward/pallas_call | solution.py:924
  210.7 3.4 collective-permute-start.28
  214.4 8.0 %collective-permute-done.29.come_ref = bf16[1024,384]{1,0:T(8,128)(2,1)S(1)} collective-permute-done((bf16[1024,384]{1,0:T(8,128)(2,1)}, bf16[1024,384]{1,0:T(8,128)(2,1)S(1)}, u32[]{:S(2)}, u32[]{:S(2)}) %collective-permute-start.29) | collective-permute-done | bytes 786464 | tf_op jit(solution)/shard_map/ppermute | solution.py:30
  224.0 5.3 %add_convert_fusion = bf16[4,864,768]{2,1,0:T(8,128)(2,1)S(1)} fusion(bf16[4,864,768]{2,1,0:T(8,128)(2,1)} %collective-permute-done.28, bf16[4,864,768]{2,1,0:T(8,128)(2,1)} %get-tuple-element.191), kind=kLoop, calls=%fused_computation | loop fusion | flops 10616832 | bytes 15925248 | tf_op jit(solution)/shard_map/convert_element_type | solution.py:147
  234.5 42.5 %attend_back.1 = (bf16[2048,1152]{1,0:T(8,128)(2,1)}, bf16[1024,768]{1,0:T(8,128)(2,1)}, bf16[1024,768]{1,0:T(8,128)(2,1)}, f32[1,1152]{1,0:T(1,128)}) custom-call(s32[64]{0:T(128)} %copy-done.9, s32[576]{0:T(1024)} %copy-done.6, s32[2]{0:T(128)} %copy-done.8, f32[32,3,8,128]{3,2,1,0:T(8,128)} %copy-done.3, f32[32,8,128]{2,1,0:T(8,128)} %copy-done.5, ...), custom_call_target="tpu_custom_call" | custom-call | flops 1 | bytes 1 | tf_op jit(solution)/shard_map/attend_back/pallas_call | solution.py:816
  277.1 7.0 %convolution_convert_fusion = bf16[768,1152]{1,0:T(8,128)(2,1)S(1)} fusion(bf16[2048,768]{1,0:T(8,128)(2,1)S(1)} %copy-done.19, bf16[2048,1152]{1,0:T(8,128)(2,1)} %get-tuple-element.206), kind=kOutput, calls=%fused_computation.1 | convolution fusion | flops 3624763392 | bytes 9633792 | tf_op jit(solution)/shard_map/dot_general | solution.py:25
  293.5 7.4 %collective-permute-start.33 = (bf16[512,768]{1,0:T(8,128)(2,1)}, bf16[512,768]{1,0:T(8,128)(2,1)}, u32[]{:S(2)}, u32[]{:S(2)}) collective-permute-start(bf16[512,768]{1,0:T(8,128)(2,1)} %get-tuple-element.251), channel_id=1, source_target_pairs={{0,0},{1,1},{4,2},{5,3},{2,4},{3,5},{6,6},{7,7},{8,8},{9,9},{12,10... | collective-permute-start | bytes 2359304 | tf_op jit(solution)/shard_map/ppermute | solution.py:67
  311.4 7.7 %collective-permute-done.35.refs_3_ = bf16[432,768]{1,0:T(8,128)(2,1)} collective-permute-done((bf16[432,768]{1,0:T(8,128)(2,1)}, bf16[432,768]{1,0:T(8,128)(2,1)}, u32[]{:S(2)}, u32[]{:S(2)}) %collective-permute-start.35) | collective-permute-done | bytes 663584 | tf_op jit(solution)/shard_map/ppermute | solution.py:110
  319.1 3.1 unpack.1
  325.6 6.2 %collective-permute-done.38 = bf16[1,2,4,32,1152]{4,3,1,2,0:T(8,128)(2,1)} collective-permute-done((bf16[1,2,4,32,1152]{4,3,1,2,0:T(8,128)(2,1)}, bf16[1,2,4,32,1152]{4,3,1,2,0:T(8,128)(2,1)}, u32[]{:S(2)}, u32[]{:S(2)}) %collective-permute-start.38) | collective-permute-done | bytes 589856 | tf_op jit(solution)/shard_map/ppermute | solution.py:110
  331.8 8.3 %collective-permute-done.40 = bf16[1,2,4,32,1152]{4,3,1,2,0:T(8,128)(2,1)} collective-permute-done((bf16[1,2,4,32,1152]{4,3,1,2,0:T(8,128)(2,1)}, bf16[1,2,4,32,1152]{4,3,1,2,0:T(8,128)(2,1)}, u32[]{:S(2)}, u32[]{:S(2)}) %collective-permute-start.40) | collective-permute-done | bytes 589856 | tf_op jit(solution)/shard_map/ppermute | solution.py:110
  342.9 20.7 %collective-permute-done.36 = bf16[512,768]{1,0:T(8,128)(2,1)S(1)} collective-permute-done((bf16[512,768]{1,0:T(8,128)(2,1)S(1)}, bf16[512,768]{1,0:T(8,128)(2,1)S(1)}, u32[]{:S(2)}, u32[]{:S(2)}) %collective-permute-start.36) | collective-permute-done | bytes 786464 | tf_op jit(solution)/shard_map/ppermute | solution.py:67
  369.3 4.7 %collective-permute-done.43 = bf16[2,32,1152]{2,1,0:T(8,128)(2,1)S(1)} collective-permute-done((bf16[2,32,1152]{2,1,0:T(8,128)(2,1)S(1)}, bf16[2,32,1152]{2,1,0:T(8,128)(2,1)S(1)}, u32[]{:S(2)}, u32[]{:S(2)}) %collective-permute-start.43) | collective-permute-done | bytes 147488 | tf_op jit(solution)/shard_map/ppermute | solution.py:35
  (323 shorter events, 103.3 us)
Async XLA Ops:
  22.6 19.3 %collective-permute-start.7 = (bf16[2,2,32,1152]{3,2,1,0:T(8,128)(2,1)S(1)}, bf16[2,2,32,1152]{3,2,1,0:T(8,128)(2,1)}, u32[]{:S(2)}, u32[]{:S(2)}) collective-permute-start(bf16[2,2,32,1152]{3,2,1,0:T(8,128)(2,1)S(1)} %pad_maximum_fusion.5), channel_id=1, source_target_pairs={{0,1},{1,0},{2,3},{3,2},{4,5},{5,4},{6,7},{7,6},{8,9},{9,8},{10,11... | collective-permute-start | bytes 884744 | tf_op jit(solution)/shard_map/ppermute | solution.py:35
  39.4 32.7 %collective-permute-start.5 = (bf16[2,232,768]{2,1,0:T(8,128)(2,1)}, bf16[2,232,768]{2,1,0:T(8,128)(2,1)}, u32[]{:S(2)}, u32[]{:S(2)}) collective-permute-start(bf16[2,232,768]{2,1,0:T(8,128)(2,1)} %pad_maximum_fusion.4), channel_id=1, source_target_pairs={{0,1},{1,0},{2,3},{3,2},{4,5},{5,4},{6,7},{7,6},{8,9},{9,8},{10,11... | collective-permute-start | bytes 2138120 | tf_op jit(solution)/shard_map/ppermute | solution.py:35
  45.8 25.0 %collective-permute-start.10 = (bf16[2,112,1152]{2,1,0:T(8,128)(2,1)}, bf16[2,112,1152]{2,1,0:T(8,128)(2,1)}, u32[]{:S(2)}, u32[]{:S(2)}) collective-permute-start(bf16[2,112,1152]{2,1,0:T(8,128)(2,1)} %pack_columns.1.refs_5_), channel_id=1, source_target_pairs={{0,16},{4,20},{8,24},{12,28},{16,0},{20,4},{24,8},{28,12},{1,17},{... | collective-permute-start | bytes 1548296 | tf_op jit(solution)/shard_map/ppermute | solution.py:110
  47.3 23.5 %collective-permute-start.11 = (bf16[2,112,1152]{2,1,0:T(8,128)(2,1)}, bf16[2,112,1152]{2,1,0:T(8,128)(2,1)}, u32[]{:S(2)}, u32[]{:S(2)}) collective-permute-start(bf16[2,112,1152]{2,1,0:T(8,128)(2,1)} %pack_columns.1.refs_5_), channel_id=1, source_target_pairs={{0,24},{4,28},{8,16},{12,20},{16,8},{20,12},{24,0},{28,4},{1,25},{... | collective-permute-start | bytes 1548296 | tf_op jit(solution)/shard_map/ppermute | solution.py:110
  51.5 20.5 %collective-permute-start.9 = (bf16[2,112,1152]{2,1,0:T(8,128)(2,1)}, bf16[2,112,1152]{2,1,0:T(8,128)(2,1)}, u32[]{:S(2)}, u32[]{:S(2)}) collective-permute-start(bf16[2,112,1152]{2,1,0:T(8,128)(2,1)} %pack_columns.1.refs_5_), channel_id=1, source_target_pairs={{0,8},{4,12},{8,0},{12,4},{16,24},{20,28},{24,16},{28,20},{1,9},{5... | collective-permute-start | bytes 1548296 | tf_op jit(solution)/shard_map/ppermute | solution.py:110
  54.3 25.7 %collective-permute-start.14 = (bf16[512,768]{1,0:T(8,128)(2,1)}, bf16[512,768]{1,0:T(8,128)(2,1)}, u32[]{:S(2)}, u32[]{:S(2)}) collective-permute-start(bf16[512,768]{1,0:T(8,128)(2,1)} %get-tuple-element.256), channel_id=1, source_target_pairs={{0,1},{1,0},{2,5},{3,4},{4,3},{5,2},{6,7},{7,6},{8,9},{9,8},{10,13... | collective-permute-start | bytes 2359304 | tf_op jit(solution)/shard_map/ppermute | solution.py:53
  93.9 36.2 %collective-permute-start.19 = (bf16[2,448,768]{2,1,0:T(8,128)(2,1)S(1)}, bf16[2,448,768]{2,1,0:T(8,128)(2,1)S(1)}, u32[]{:S(2)}, u32[]{:S(2)}) collective-permute-start(bf16[2,448,768]{2,1,0:T(8,128)(2,1)S(1)} %pad_maximum_fusion.2.refs_2_), channel_id=1, source_target_pairs={{0,8},{4,12},{8,0},{12,4},{16,24},{20,28},{24,16},{28,20},{1,9},{5... | collective-permute-start | bytes 4128776 | tf_op jit(solution)/shard_map/ppermute | solution.py:110
  95.6 34.5 %collective-permute-start.18 = (bf16[2,432,768]{2,1,0:T(8,128)(2,1)S(1)}, bf16[2,432,768]{2,1,0:T(8,128)(2,1)}, u32[]{:S(2)}, u32[]{:S(2)}) collective-permute-start(bf16[2,432,768]{2,1,0:T(8,128)(2,1)S(1)} %pad_maximum_fusion.3.refs_0_), channel_id=1, source_target_pairs={{0,16},{4,20},{8,24},{12,28},{16,0},{20,4},{24,8},{28,12},{1,17},{... | collective-permute-start | bytes 3981320 | tf_op jit(solution)/shard_map/ppermute | solution.py:110
  107.4 22.7 %collective-permute-start.17 = (bf16[512,768]{1,0:T(8,128)(2,1)S(1)}, bf16[512,768]{1,0:T(8,128)(2,1)S(1)}, u32[]{:S(2)}, u32[]{:S(2)}) collective-permute-start(bf16[512,768]{1,0:T(8,128)(2,1)S(1)} %dynamic-slice_bitcast_fusion.1), channel_id=1, source_target_pairs={{0,0},{1,1},{2,4},{3,5},{4,2},{5,3},{6,6},{7,7},{8,8},{9,9},{10,12... | collective-permute-start | bytes 2359304 | tf_op jit(solution)/shard_map/ppermute | solution.py:53
  108.6 23.1 %collective-permute-start.21 = (bf16[2,432,768]{2,1,0:T(8,128)(2,1)S(1)}, bf16[2,432,768]{2,1,0:T(8,128)(2,1)S(1)}, u32[]{:S(2)}, u32[]{:S(2)}) collective-permute-start(bf16[2,432,768]{2,1,0:T(8,128)(2,1)S(1)} %pad_maximum_fusion.3.refs_0_), channel_id=1, source_target_pairs={{0,4},{4,0},{8,12},{12,8},{16,20},{20,16},{24,28},{28,24},{1,5},{5... | collective-permute-start | bytes 3981320 | tf_op jit(solution)/shard_map/ppermute | solution.py:30
  110.8 22.3 %collective-permute-start.23 = (bf16[2,448,768]{2,1,0:T(8,128)(2,1)S(1)}, bf16[2,448,768]{2,1,0:T(8,128)(2,1)S(1)}, u32[]{:S(2)}, u32[]{:S(2)}) collective-permute-start(bf16[2,448,768]{2,1,0:T(8,128)(2,1)S(1)} %pad_maximum_fusion.2.refs_2_), channel_id=1, source_target_pairs={{0,4},{4,0},{8,12},{12,8},{16,20},{20,16},{24,28},{28,24},{1,5},{5... | collective-permute-start | bytes 4128776 | tf_op jit(solution)/shard_map/ppermute | solution.py:30
  131.7 36.2 %collective-permute-start.25 = (bf16[512,768]{1,0:T(8,128)(2,1)S(1)}, bf16[512,768]{1,0:T(8,128)(2,1)S(1)}, u32[]{:S(2)}, u32[]{:S(2)}) collective-permute-start(bf16[512,768]{1,0:T(8,128)(2,1)S(1)} %dynamic-slice_bitcast_fusion), channel_id=1, source_target_pairs={{0,1},{1,0},{2,5},{3,4},{4,3},{5,2},{6,7},{7,6},{8,9},{9,8},{10,13... | collective-permute-start | bytes 2359304 | tf_op jit(solution)/shard_map/ppermute | solution.py:53
  170.3 39.5 %collective-permute-start.26 = (bf16[512,768]{1,0:T(8,128)(2,1)S(1)}, bf16[512,768]{1,0:T(8,128)(2,1)S(1)}, u32[]{:S(2)}, u32[]{:S(2)}) collective-permute-start(bf16[512,768]{1,0:T(8,128)(2,1)S(1)} %get-tuple-element.255), channel_id=1, source_target_pairs={{0,0},{1,1},{4,2},{5,3},{2,4},{3,5},{6,6},{7,7},{8,8},{9,9},{12,10... | collective-permute-start | bytes 2359304 | tf_op jit(solution)/shard_map/ppermute | solution.py:67
  171.0 38.8 %collective-permute-start.27 = (bf16[512,768]{1,0:T(8,128)(2,1)S(1)}, bf16[512,768]{1,0:T(8,128)(2,1)S(1)}, u32[]{:S(2)}, u32[]{:S(2)}) collective-permute-start(bf16[512,768]{1,0:T(8,128)(2,1)S(1)} %get-tuple-element.254), channel_id=1, source_target_pairs={{1,0},{0,1},{5,2},{4,3},{3,4},{2,5},{7,6},{6,7},{9,8},{8,9},{13,10... | collective-permute-start | bytes 2359304 | tf_op jit(solution)/shard_map/ppermute | solution.py:67
  232.6 44.4 %collective-permute-start.30 = (bf16[2,1,432,768]{3,2,1,0:T(8,128)(2,1)}, bf16[2,1,432,768]{3,2,1,0:T(8,128)(2,1)S(1)}, u32[]{:S(2)}, u32[]{:S(2)}) collective-permute-start(bf16[2,1,432,768]{3,2,1,0:T(8,128)(2,1)} %get-tuple-element.202), channel_id=1, source_target_pairs={{0,8},{4,12},{8,0},{12,4},{16,24},{20,28},{24,16},{28,20},{1,9},{5... | collective-permute-start | bytes 3981320 | tf_op jit(solution)/shard_map/ppermute | solution.py:110
  233.6 43.3 %collective-permute-start.31 = (bf16[1,2,432,768]{3,2,1,0:T(8,128)(2,1)}, bf16[1,2,432,768]{3,2,1,0:T(8,128)(2,1)}, u32[]{:S(2)}, u32[]{:S(2)}) collective-permute-start(bf16[1,2,432,768]{3,2,1,0:T(8,128)(2,1)} %get-tuple-element.204), channel_id=1, source_target_pairs={{0,16},{4,20},{8,24},{12,28},{16,0},{20,4},{24,8},{28,12},{1,17},{... | collective-permute-start | bytes 3981320 | tf_op jit(solution)/shard_map/ppermute | solution.py:110
  293.5 25.6 %collective-permute-start.33 = (bf16[512,768]{1,0:T(8,128)(2,1)}, bf16[512,768]{1,0:T(8,128)(2,1)}, u32[]{:S(2)}, u32[]{:S(2)}) collective-permute-start(bf16[512,768]{1,0:T(8,128)(2,1)} %get-tuple-element.251), channel_id=1, source_target_pairs={{0,0},{1,1},{4,2},{5,3},{2,4},{3,5},{6,6},{7,7},{8,8},{9,9},{12,10... | collective-permute-start | bytes 2359304 | tf_op jit(solution)/shard_map/ppermute | solution.py:67
  304.4 27.3 %collective-permute-start.38 = (bf16[1,2,4,32,1152]{4,3,1,2,0:T(8,128)(2,1)}, bf16[1,2,4,32,1152]{4,3,1,2,0:T(8,128)(2,1)}, u32[]{:S(2)}, u32[]{:S(2)}) collective-permute-start(bf16[1,2,4,32,1152]{4,3,1,2,0:T(8,128)(2,1)} %get-tuple-element.243), channel_id=1, source_target_pairs={{0,8},{4,12},{8,0},{12,4},{16,24},{20,28},{24,16},{28,20},{1,9},{5... | collective-permute-start | bytes 1769480 | tf_op jit(solution)/shard_map/ppermute | solution.py:110
  305.5 26.3 %collective-permute-start.39 = (bf16[1,2,4,32,1152]{4,3,1,2,0:T(8,128)(2,1)}, bf16[1,2,4,32,1152]{4,3,1,2,0:T(8,128)(2,1)}, u32[]{:S(2)}, u32[]{:S(2)}) collective-permute-start(bf16[1,2,4,32,1152]{4,3,1,2,0:T(8,128)(2,1)} %get-tuple-element.244), channel_id=1, source_target_pairs={{0,16},{4,20},{8,24},{12,28},{16,0},{20,4},{24,8},{28,12},{1,17},{... | collective-permute-start | bytes 1769480 | tf_op jit(solution)/shard_map/ppermute | solution.py:110
  308.2 31.9 %collective-permute-start.40 = (bf16[1,2,4,32,1152]{4,3,1,2,0:T(8,128)(2,1)}, bf16[1,2,4,32,1152]{4,3,1,2,0:T(8,128)(2,1)}, u32[]{:S(2)}, u32[]{:S(2)}) collective-permute-start(bf16[1,2,4,32,1152]{4,3,1,2,0:T(8,128)(2,1)} %get-tuple-element.245), channel_id=1, source_target_pairs={{0,24},{4,28},{8,16},{12,20},{16,8},{20,12},{24,0},{28,4},{1,25},{... | collective-permute-start | bytes 1769480 | tf_op jit(solution)/shard_map/ppermute | solution.py:110
  322.2 19.7 %collective-permute-start.41 = (bf16[2,216,768]{2,1,0:T(8,128)(2,1)}, bf16[2,216,768]{2,1,0:T(8,128)(2,1)S(1)}, u32[]{:S(2)}, u32[]{:S(2)}) collective-permute-start(bf16[2,216,768]{2,1,0:T(8,128)(2,1)} %get-tuple-element.227), channel_id=1, source_target_pairs={{0,1},{1,0},{2,3},{3,2},{4,5},{5,4},{6,7},{7,6},{8,9},{9,8},{10,11... | collective-permute-start | bytes 1990664 | tf_op jit(solution)/shard_map/ppermute | solution.py:35
  324.2 39.4 %collective-permute-start.36 = (bf16[512,768]{1,0:T(8,128)(2,1)S(1)}, bf16[512,768]{1,0:T(8,128)(2,1)S(1)}, u32[]{:S(2)}, u32[]{:S(2)}) collective-permute-start(bf16[512,768]{1,0:T(8,128)(2,1)S(1)} %copy-done.27), channel_id=1, source_target_pairs={{1,0},{0,1},{5,2},{4,3},{3,4},{2,5},{7,6},{6,7},{9,8},{8,9},{13,10... | collective-permute-start | bytes 2359304 | tf_op jit(solution)/shard_map/ppermute | solution.py:67
  342.0 25.0 %collective-permute-start.44 = (bf16[216,768]{1,0:T(8,128)(2,1)S(1)}, bf16[216,768]{1,0:T(8,128)(2,1)S(1)}, u32[]{:S(2)}, u32[]{:S(2)}) collective-permute-start(bf16[216,768]{1,0:T(8,128)(2,1)S(1)} %fusion.9), channel_id=1, source_target_pairs={{0,3},{1,2},{2,1},{3,0},{4,7},{5,6},{6,5},{7,4},{8,11},{9,10},{10,... | collective-permute-start | bytes 995336 | tf_op jit(solution)/shard_map/ppermute | solution.py:35
  342.6 24.4 %collective-permute-start.42 = (bf16[2,2,32,1152]{3,2,1,0:T(8,128)(2,1)S(1)}, bf16[2,2,32,1152]{3,2,1,0:T(8,128)(2,1)S(1)}, u32[]{:S(2)}, u32[]{:S(2)}) collective-permute-start(bf16[2,2,32,1152]{3,2,1,0:T(8,128)(2,1)S(1)} %pad_maximum_fusion.6), channel_id=1, source_target_pairs={{0,1},{1,0},{2,3},{3,2},{4,5},{5,4},{6,7},{7,6},{8,9},{9,8},{10,11... | collective-permute-start | bytes 884744 | tf_op jit(solution)/shard_map/ppermute | solution.py:35
  (64 other events, 946.2 us)

commit v5 on v4

--- a/solution.py
+++ b/solution.py
@@ -1209,6 +1209,15 @@
     if direct:
         grad_qkv, grad_own, grad_theirs, sums, *moves = join(grad_qkv, grad_own, grad_theirs, sums, *moves)
     come_rows = swap(grad_theirs)
+    if direct:
+        upper, lower = added(*moves[:2]), added(*moves[2:])
+        moves = [pick(upper, y, 0), pick(upper, 1 - y, 0), pick(lower, x, 1), pick(lower, 1 - x, 1)]
+        grad_own, *moves = join(grad_own, *(move.reshape(-1, width) for move in moves))
+        moves[1], moves[3] = flip_chip(moves[1], 2), flip_chip(moves[3], 1)
+    grad_tokens = added(grad_own, come_rows)
+    grad_tokens, grad_qkv = join(grad_tokens, grad_qkv)
+    grad_inputs = start_back(grad_tokens)
+    first_back = finish_back(grad_inputs, 0)
     grad_w_qkv = dot(tokens, grad_qkv, TN).astype(LOW)
     vectors = in_sums[: 6 + chunks].reshape(-1)
     vectors = jnp.pad(vectors, (0, -vectors.shape[0] % (3 * half_width))).reshape(-1, 3 * half_width)
@@ -1218,17 +1227,8 @@
         [grad_w_qkv.reshape(chips, 2, n_seq, rows_in, 3 * half_width), lines], 3
     )
     keep, come = (pick(parts, which, 1)[:, 0] for which in (core, 1 - core))
-    if direct:
-        keep, come, *moves = join(keep, come, *moves)
-        upper, lower = added(*moves[:2]), added(*moves[2:])
-        moves = [pick(upper, y, 0), pick(upper, 1 - y, 0), pick(lower, x, 1), pick(lower, 1 - x, 1)]
-        grad_own, *moves = join(grad_own, *(move.reshape(-1, width) for move in moves))
-        moves[1], moves[3] = flip_chip(moves[1], 2), flip_chip(moves[3], 1)
     come = swap(come)
-    grad_tokens = added(grad_own, come_rows)
     parts = jnp.stack([keep, come], 1)
-    grad_inputs = start_back(grad_tokens)
-    first_back = finish_back(grad_inputs, 0)
     if direct:
         first_back, *moves = join(first_back, *moves)
         near_sums, keep_sums = unpack_rows(at, moves[:2], moves[2:], chunks + 1)
@@ -1237,7 +1237,7 @@
         rows = rows.reshape((chunks + 1) * span, width)
         down = lax.psum_scatter(grad_down, "dp", scatter_dimension=0, tiled=True)
         near_sums, keep_sums = unpack_rows(at, [rows], [down], chunks + 1)
-    grad_inputs = first_back, finish_back(tie(grad_inputs, near_sums), 1)
+    grad_inputs = first_back, finish_back(grad_inputs, 1)
     near_sums = flip_seq(near_sums, 1)
     parts = reduce_chips(parts)
     parts, near_sums = join(parts, near_sums)
@@ -1259,6 +1259,8 @@
 
     def own_part(vector, size):
         return lax.dynamic_slice_in_dim(vector.reshape(-1), device * size, size, 0)
+
+    six = lax.dynamic_slice_in_dim(small[:6], device * rows_in, rows_in, 1)
 
     matrix_rows, line = slice(0, rows_in), slice(rows_in, rows_in + 1)
     return (
@@ -1270,15 +1272,15 @@
         joined(2, matrix_rows),
         own_part(joined(2, line), rows_in),
         own_sums[chunks * rows_in : rows_a],
-        own_part(small[0], rows_in),
-        own_part(small[1], rows_in),
-        own_part(small[2], rows_in),
+        six[0],
+        six[1],
+        six[2],
         own_up,
         own_part(small[6 : 6 + chunks], rows_ff),
         own_sums[rows_a : rows_a + rows_ff],
-        own_part(small[3], rows_in),
-        own_part(small[4], rows_in),
-        own_part(small[5], rows_in),
+        six[3],
+        six[4],
+        six[5],
     )
 
 

time: 388 us -> 376 us (0.969)
  local copies, waits for them, and re-layouts: 36.2 us -> 30.6 us
    ppermute x8, waiting for transfers between devices: 7.68 us -> 28.2 us  [flip_seq(): return lax.ppermute(array, 'seq', [(i, i ^ k) for i in range(size)])]
    ppermute x14, waiting for transfers between devices: 50.1 us -> 31.6 us  [flip_chip(): return lax.ppermute(array, 'dp', [(i, i ^ 2 * away) for i in range(size)])]
    ppermute x4, waiting for transfers between devices: 20.7 us -> 16 us  [finish_back(): return lax.ppermute(parts[a], ('dp', 'seq'), [(t, s) for s, t in pairs])]
  transfers between devices with their start and end apart: 45 -> 45, of which waited for: 15 -> 15; matrix products, arithmetic and copies ran while one was open for 12% -> 10% of each run, Pallas kernels for 38% -> 40%
where the time goes in v5:
time: 376 us; the launch traced here: 369 us
  Pallas kernels  146 us (39%)
  waiting for transfers between devices  88.9 us (24%)
  starting transfers between devices  65.8 us (18%)
  local copies, waits for them, and re-layouts  30.6 us (8%)
  other arithmetic  29.9 us (8%)
  matrix products  4.44 us (1%)
    pallas_call x1, Pallas kernels, attend_back(): pl.pallas_call(partial(attend_back_kernel, blocks, 2), out_shape=(jax.Sha...  42.3 us
    pallas_call x1, Pallas kernels, layer_backward(): pl.pallas_call(partial(backward_kernel, TILE, chips, direct), grid=(own /...  37.3 us
    ppermute x14, waiting for transfers between devices, flip_chip(): return lax.ppermute(array, 'dp', [(i, i ^ 2 * away) for i in range(size)])  31.6 us
    pallas_call x1, Pallas kernels, layer_forward(): pl.pallas_call(partial(forward_kernel, chips, direct), grid=(own // TILE,...  29 us
    ppermute x8, waiting for transfers between devices, flip_seq(): return lax.ppermute(array, 'seq', [(i, i ^ k) for i in range(size)])  28.2 us
    ppermute x8, starting transfers between devices, flip_seq(): return lax.ppermute(array, 'seq', [(i, i ^ k) for i in range(size)])  20.5 us
    pallas_call x1, Pallas kernels, attend(): pl.pallas_call(partial(attend_kernel, pairs, blocks, 4), out_shape=(jax.S...  19.2 us
    ppermute x14, starting transfers between devices, flip_chip(): return lax.ppermute(array, 'dp', [(i, i ^ 2 * away) for i in range(size)])  17.6 us
  transfers between devices with their start and end apart: 45, of which 15 were waited for; matrix products, arithmetic and copies ran while one was open for 10% of the time, Pallas kernels for 40%

profile of v5, /device:TPU:0, one launch (start us, length us, event | category | flops | bytes accessed | tf_op | source)
XLA Modules:
  0.0 369.3 jit_solution(3547757953771614333)
XLA Ops:
  8.0 2.6 collective-permute-start.3
  12.6 6.7 %collective-permute-start.4 = (bf16[2,32,1152]{2,1,0:T(8,128)(2,1)S(1)}, bf16[2,32,1152]{2,1,0:T(8,128)(2,1)S(1)}, u32[]{:S(2)}, u32[]{:S(2)}) collective-permute-start(bf16[2,32,1152]{2,1,0:T(8,128)(2,1)S(1)} %pad_maximum_fusion.8.shard_ref), channel_id=1, source_target_pairs={{0,3},{1,2},{2,1},{3,0},{4,7},{5,6},{6,5},{7,4},{8,11},{9,10},{10,... | collective-permute-start | bytes 442376 | tf_op jit(solution)/shard_map/ppermute | solution.py:35
  22.6 10.8 %collective-permute-start.7 = (bf16[2,2,32,1152]{3,2,1,0:T(8,128)(2,1)S(1)}, bf16[2,2,32,1152]{3,2,1,0:T(8,128)(2,1)}, u32[]{:S(2)}, u32[]{:S(2)}) collective-permute-start(bf16[2,2,32,1152]{3,2,1,0:T(8,128)(2,1)S(1)} %pad_maximum_fusion.5), channel_id=1, source_target_pairs={{0,1},{1,0},{2,3},{3,2},{4,5},{5,4},{6,7},{7,6},{8,9},{9,8},{10,11... | collective-permute-start | bytes 884744 | tf_op jit(solution)/shard_map/ppermute | solution.py:35
  34.0 2.6 dynamic-slice_bitcast_fusion.2
  58.3 12.5 %collective-permute-done.10.refs_7_ = bf16[2,112,1152]{2,1,0:T(8,128)(2,1)} collective-permute-done((bf16[2,112,1152]{2,1,0:T(8,128)(2,1)}, bf16[2,112,1152]{2,1,0:T(8,128)(2,1)}, u32[]{:S(2)}, u32[]{:S(2)}) %collective-permute-start.10) | collective-permute-done | bytes 516128 | tf_op jit(solution)/shard_map/ppermute | solution.py:110
  72.1 2.5 pack.1
  80.0 12.2 %collective-permute-done.12 = bf16[432,768]{1,0:T(8,128)(2,1)S(1)} collective-permute-done((bf16[432,768]{1,0:T(8,128)(2,1)}, bf16[432,768]{1,0:T(8,128)(2,1)S(1)}, u32[]{:S(2)}, u32[]{:S(2)}) %collective-permute-start.12) | collective-permute-done | bytes 663584 | tf_op jit(solution)/shard_map/ppermute | solution.py:110
  96.5 10.8 %project.1 = (bf16[2048,1152]{1,0:T(8,128)(2,1)}, bf16[2048,768]{1,0:T(8,128)(2,1)}, bf16[768,1152]{1,0:T(8,128)(2,1)}) custom-call(s32[3]{0:T(128)S(1)} %copy-done.7, bf16[512,768]{1,0:T(8,128)(2,1)S(1)} %collective-permute-done.6.refs_0_, bf16[512,768]{1,0:T(8,128)(2,1)} %collective-permute-done.14.refs_1_, ...), custom_call_target="tpu_custom_call" | custom-call | flops 1 | bytes 1 | tf_op jit(solution)/shard_map/project/pallas_call | solution.py:775
  110.9 19.2 %attend.1 = (bf16[2048,384]{1,0:T(8,128)(2,1)S(1)}, f32[32,8,128]{2,1,0:T(8,128)S(1)}) custom-call(s32[64]{0:T(128)S(1)} %pad_add_fusion.5.near_ref, s32[576]{0:T(1024)S(1)} %fusion.12.rand_ref, s32[2]{0:T(128)S(1)} %fusion.31.glob_ref, f32[32,3,8,128]{3,2,1,0:T(8,128)S(1)} %reshape.549.bias_ref, bf16[2048,1152]{1,0:T(8,128)(2,1)} %get-tuple-element.141.qkv_ref), custom_call_target="tpu_custom_call" | custom-call | flops 1 | bytes 1 | tf_op jit(solution)/shard_map/attend/pallas_call | solution.py:798
  133.1 3.3 collective-permute-done.20.other_ref
  138.9 29.0 %layer_forward.1 = (bf16[1024,768]{1,0:T(8,128)(2,1)}, bf16[1024,3072]{1,0:T(8,128)(2,1)}, bf16[1024,3072]{1,0:T(8,128)(2,1)}, bf16[1024,768]{1,0:T(8,128)(2,1)}...) custom-call(s32[3]{0:T(128)} %pad_add_fusion.4.at_ref, bf16[2048,384]{1,0:T(8,128)(2,1)} %copy-done.2, ...), custom_call_target="tpu_custom_call" | custom-call | flops 1 | bytes 1 | tf_op jit(solution)/shard_map/layer_forward/pallas_call | solution.py:892
  172.5 37.3 %layer_backward.1 = (bf16[1024,768]{1,0:T(8,128)(2,1)}, bf16[1024,384]{1,0:T(8,128)(2,1)}, bf16[1024,384]{1,0:T(8,128)(2,1)}, f32[16,768]{1,0:T(8,128)}, bf16[4,...) custom-call(s32[3]{0:T(128)} %pad_add_fusion.4.at_ref, bf16[2048,384]{1,0:T(8,128)(2,1)} %copy-done.2, ...), custom_call_target="tpu_custom_call" | custom-call | flops 1 | bytes 1 | tf_op jit(solution)/shard_map/layer_backward/pallas_call | solution.py:924
  210.6 3.4 collective-permute-start.28
  214.3 8.0 %collective-permute-done.29.come_ref = bf16[1024,384]{1,0:T(8,128)(2,1)S(1)} collective-permute-done((bf16[1024,384]{1,0:T(8,128)(2,1)}, bf16[1024,384]{1,0:T(8,128)(2,1)S(1)}, u32[]{:S(2)}, u32[]{:S(2)}) %collective-permute-start.29) | collective-permute-done | bytes 786464 | tf_op jit(solution)/shard_map/ppermute | solution.py:30
  223.9 5.3 %add_convert_fusion = bf16[4,864,768]{2,1,0:T(8,128)(2,1)S(1)} fusion(bf16[4,864,768]{2,1,0:T(8,128)(2,1)} %collective-permute-done.28, bf16[4,864,768]{2,1,0:T(8,128)(2,1)} %get-tuple-element.186), kind=kLoop, calls=%fused_computation | loop fusion | flops 10616832 | bytes 15925248 | tf_op jit(solution)/shard_map/convert_element_type | solution.py:147
  231.8 42.3 %attend_back.1 = (bf16[2048,1152]{1,0:T(8,128)(2,1)}, bf16[1024,768]{1,0:T(8,128)(2,1)}, bf16[1024,768]{1,0:T(8,128)(2,1)}, f32[1,1152]{1,0:T(1,128)}) custom-call(s32[64]{0:T(128)} %copy-done.9, s32[576]{0:T(1024)} %copy-done.6, s32[2]{0:T(128)} %copy-done.8, f32[32,3,8,128]{3,2,1,0:T(8,128)} %copy-done.3, f32[32,8,128]{2,1,0:T(8,128)} %copy-done.5, ...), custom_call_target="tpu_custom_call" | custom-call | flops 1 | bytes 1 | tf_op jit(solution)/shard_map/attend_back/pallas_call | solution.py:816
  283.0 4.4 %convolution_convert_fusion = bf16[768,1152]{1,0:T(8,128)(2,1)S(1)} fusion(bf16[2048,768]{1,0:T(8,128)(2,1)S(1)} %copy-done.18, bf16[2048,1152]{1,0:T(8,128)(2,1)S(1)} %copy-done.40), kind=kOutput, calls=%fused_computation.1 | convolution fusion | flops 3624763392 | bytes 9633792 | tf_op jit(solution)/shard_map/dot_general | solution.py:25
  292.6 7.5 %collective-permute-start.34 = (bf16[512,768]{1,0:T(8,128)(2,1)}, bf16[512,768]{1,0:T(8,128)(2,1)}, u32[]{:S(2)}, u32[]{:S(2)}) collective-permute-start(bf16[512,768]{1,0:T(8,128)(2,1)} %get-tuple-element.241), channel_id=1, source_target_pairs={{0,0},{1,1},{4,2},{5,3},{2,4},{3,5},{6,6},{7,7},{8,8},{9,9},{12,10... | collective-permute-start | bytes 2359304 | tf_op jit(solution)/shard_map/ppermute | solution.py:67
  302.9 3.5 collective-permute-done.35.refs_1_
  311.8 3.1 unpack.1
  315.1 16.0 %collective-permute-done.33 = bf16[512,768]{1,0:T(8,128)(2,1)} collective-permute-done((bf16[512,768]{1,0:T(8,128)(2,1)S(1)}, bf16[512,768]{1,0:T(8,128)(2,1)}, u32[]{:S(2)}, u32[]{:S(2)}) %collective-permute-start.33) | collective-permute-done | bytes 786464 | tf_op jit(solution)/shard_map/ppermute | solution.py:67
  335.5 7.3 %collective-permute-done.41 = bf16[2,216,768]{2,1,0:T(8,128)(2,1)S(1)} collective-permute-done((bf16[2,216,768]{2,1,0:T(8,128)(2,1)}, bf16[2,216,768]{2,1,0:T(8,128)(2,1)S(1)}, u32[]{:S(2)}, u32[]{:S(2)}) %collective-permute-start.41) | collective-permute-done | bytes 663584 | tf_op jit(solution)/shard_map/ppermute | solution.py:35
  344.4 13.9 %collective-permute-done.42 = bf16[2,2,32,1152]{3,2,1,0:T(8,128)(2,1)S(1)} collective-permute-done((bf16[2,2,32,1152]{3,2,1,0:T(8,128)(2,1)S(1)}, bf16[2,2,32,1152]{3,2,1,0:T(8,128)(2,1)S(1)}, u32[]{:S(2)}, u32[]{:S(2)}) %collective-permute-start.42) | collective-permute-done | bytes 294944 | tf_op jit(solution)/shard_map/ppermute | solution.py:35
  360.7 4.8 %collective-permute-done.43 = bf16[2,32,1152]{2,1,0:T(8,128)(2,1)S(1)} collective-permute-done((bf16[2,32,1152]{2,1,0:T(8,128)(2,1)S(1)}, bf16[2,32,1152]{2,1,0:T(8,128)(2,1)S(1)}, u32[]{:S(2)}, u32[]{:S(2)}) %collective-permute-start.43) | collective-permute-done | bytes 147488 | tf_op jit(solution)/shard_map/ppermute | solution.py:35
  (316 shorter events, 96.8 us)
Async XLA Ops:
  20.3 18.1 %collective-permute-start.1 = (bf16[232,768]{1,0:T(8,128)(2,1)S(1)}, bf16[232,768]{1,0:T(8,128)(2,1)S(1)}, u32[]{:S(2)}, u32[]{:S(2)}) collective-permute-start(bf16[232,768]{1,0:T(8,128)(2,1)S(1)} %concatenate.104.shard_ref), channel_id=1, source_target_pairs={{0,3},{1,2},{2,1},{3,0},{4,7},{5,6},{6,5},{7,4},{8,11},{9,10},{10,... | collective-permute-start | bytes 1069064 | tf_op jit(solution)/shard_map/ppermute | solution.py:35
  22.6 19.2 %collective-permute-start.7 = (bf16[2,2,32,1152]{3,2,1,0:T(8,128)(2,1)S(1)}, bf16[2,2,32,1152]{3,2,1,0:T(8,128)(2,1)}, u32[]{:S(2)}, u32[]{:S(2)}) collective-permute-start(bf16[2,2,32,1152]{3,2,1,0:T(8,128)(2,1)S(1)} %pad_maximum_fusion.5), channel_id=1, source_target_pairs={{0,1},{1,0},{2,3},{3,2},{4,5},{5,4},{6,7},{7,6},{8,9},{9,8},{10,11... | collective-permute-start | bytes 884744 | tf_op jit(solution)/shard_map/ppermute | solution.py:35
  39.3 32.7 %collective-permute-start.5 = (bf16[2,232,768]{2,1,0:T(8,128)(2,1)}, bf16[2,232,768]{2,1,0:T(8,128)(2,1)}, u32[]{:S(2)}, u32[]{:S(2)}) collective-permute-start(bf16[2,232,768]{2,1,0:T(8,128)(2,1)} %pad_maximum_fusion.4), channel_id=1, source_target_pairs={{0,1},{1,0},{2,3},{3,2},{4,5},{5,4},{6,7},{7,6},{8,9},{9,8},{10,11... | collective-permute-start | bytes 2138120 | tf_op jit(solution)/shard_map/ppermute | solution.py:35
  45.8 25.0 %collective-permute-start.10 = (bf16[2,112,1152]{2,1,0:T(8,128)(2,1)}, bf16[2,112,1152]{2,1,0:T(8,128)(2,1)}, u32[]{:S(2)}, u32[]{:S(2)}) collective-permute-start(bf16[2,112,1152]{2,1,0:T(8,128)(2,1)} %pack_columns.1.refs_5_), channel_id=1, source_target_pairs={{0,16},{4,20},{8,24},{12,28},{16,0},{20,4},{24,8},{28,12},{1,17},{... | collective-permute-start | bytes 1548296 | tf_op jit(solution)/shard_map/ppermute | solution.py:110
  47.3 23.5 %collective-permute-start.11 = (bf16[2,112,1152]{2,1,0:T(8,128)(2,1)}, bf16[2,112,1152]{2,1,0:T(8,128)(2,1)}, u32[]{:S(2)}, u32[]{:S(2)}) collective-permute-start(bf16[2,112,1152]{2,1,0:T(8,128)(2,1)} %pack_columns.1.refs_5_), channel_id=1, source_target_pairs={{0,24},{4,28},{8,16},{12,20},{16,8},{20,12},{24,0},{28,4},{1,25},{... | collective-permute-start | bytes 1548296 | tf_op jit(solution)/shard_map/ppermute | solution.py:110
  51.5 20.5 %collective-permute-start.9 = (bf16[2,112,1152]{2,1,0:T(8,128)(2,1)}, bf16[2,112,1152]{2,1,0:T(8,128)(2,1)}, u32[]{:S(2)}, u32[]{:S(2)}) collective-permute-start(bf16[2,112,1152]{2,1,0:T(8,128)(2,1)} %pack_columns.1.refs_5_), channel_id=1, source_target_pairs={{0,8},{4,12},{8,0},{12,4},{16,24},{20,28},{24,16},{28,20},{1,9},{5... | collective-permute-start | bytes 1548296 | tf_op jit(solution)/shard_map/ppermute | solution.py:110
  54.3 25.7 %collective-permute-start.14 = (bf16[512,768]{1,0:T(8,128)(2,1)}, bf16[512,768]{1,0:T(8,128)(2,1)}, u32[]{:S(2)}, u32[]{:S(2)}) collective-permute-start(bf16[512,768]{1,0:T(8,128)(2,1)} %get-tuple-element.246), channel_id=1, source_target_pairs={{0,1},{1,0},{2,5},{3,4},{4,3},{5,2},{6,7},{7,6},{8,9},{9,8},{10,13... | collective-permute-start | bytes 2359304 | tf_op jit(solution)/shard_map/ppermute | solution.py:53
  93.9 36.1 %collective-permute-start.19 = (bf16[2,448,768]{2,1,0:T(8,128)(2,1)S(1)}, bf16[2,448,768]{2,1,0:T(8,128)(2,1)S(1)}, u32[]{:S(2)}, u32[]{:S(2)}) collective-permute-start(bf16[2,448,768]{2,1,0:T(8,128)(2,1)S(1)} %pad_maximum_fusion.2.refs_2_), channel_id=1, source_target_pairs={{0,8},{4,12},{8,0},{12,4},{16,24},{20,28},{24,16},{28,20},{1,9},{5... | collective-permute-start | bytes 4128776 | tf_op jit(solution)/shard_map/ppermute | solution.py:110
  95.6 34.4 %collective-permute-start.18 = (bf16[2,432,768]{2,1,0:T(8,128)(2,1)S(1)}, bf16[2,432,768]{2,1,0:T(8,128)(2,1)}, u32[]{:S(2)}, u32[]{:S(2)}) collective-permute-start(bf16[2,432,768]{2,1,0:T(8,128)(2,1)S(1)} %pad_maximum_fusion.3.refs_0_), channel_id=1, source_target_pairs={{0,16},{4,20},{8,24},{12,28},{16,0},{20,4},{24,8},{28,12},{1,17},{... | collective-permute-start | bytes 3981320 | tf_op jit(solution)/shard_map/ppermute | solution.py:110
  107.4 22.7 %collective-permute-start.17 = (bf16[512,768]{1,0:T(8,128)(2,1)S(1)}, bf16[512,768]{1,0:T(8,128)(2,1)S(1)}, u32[]{:S(2)}, u32[]{:S(2)}) collective-permute-start(bf16[512,768]{1,0:T(8,128)(2,1)S(1)} %dynamic-slice_bitcast_fusion.1), channel_id=1, source_target_pairs={{0,0},{1,1},{2,4},{3,5},{4,2},{5,3},{6,6},{7,7},{8,8},{9,9},{10,12... | collective-permute-start | bytes 2359304 | tf_op jit(solution)/shard_map/ppermute | solution.py:53
  108.6 23.0 %collective-permute-start.21 = (bf16[2,432,768]{2,1,0:T(8,128)(2,1)S(1)}, bf16[2,432,768]{2,1,0:T(8,128)(2,1)S(1)}, u32[]{:S(2)}, u32[]{:S(2)}) collective-permute-start(bf16[2,432,768]{2,1,0:T(8,128)(2,1)S(1)} %pad_maximum_fusion.3.refs_0_), channel_id=1, source_target_pairs={{0,4},{4,0},{8,12},{12,8},{16,20},{20,16},{24,28},{28,24},{1,5},{5... | collective-permute-start | bytes 3981320 | tf_op jit(solution)/shard_map/ppermute | solution.py:30
  110.8 22.3 %collective-permute-start.23 = (bf16[2,448,768]{2,1,0:T(8,128)(2,1)S(1)}, bf16[2,448,768]{2,1,0:T(8,128)(2,1)S(1)}, u32[]{:S(2)}, u32[]{:S(2)}) collective-permute-start(bf16[2,448,768]{2,1,0:T(8,128)(2,1)S(1)} %pad_maximum_fusion.2.refs_2_), channel_id=1, source_target_pairs={{0,4},{4,0},{8,12},{12,8},{16,20},{20,16},{24,28},{28,24},{1,5},{5... | collective-permute-start | bytes 4128776 | tf_op jit(solution)/shard_map/ppermute | solution.py:30
  131.7 36.2 %collective-permute-start.25 = (bf16[512,768]{1,0:T(8,128)(2,1)S(1)}, bf16[512,768]{1,0:T(8,128)(2,1)S(1)}, u32[]{:S(2)}, u32[]{:S(2)}) collective-permute-start(bf16[512,768]{1,0:T(8,128)(2,1)S(1)} %dynamic-slice_bitcast_fusion), channel_id=1, source_target_pairs={{0,1},{1,0},{2,5},{3,4},{4,3},{5,2},{6,7},{7,6},{8,9},{9,8},{10,13... | collective-permute-start | bytes 2359304 | tf_op jit(solution)/shard_map/ppermute | solution.py:53
  170.3 39.4 %collective-permute-start.26 = (bf16[512,768]{1,0:T(8,128)(2,1)S(1)}, bf16[512,768]{1,0:T(8,128)(2,1)S(1)}, u32[]{:S(2)}, u32[]{:S(2)}) collective-permute-start(bf16[512,768]{1,0:T(8,128)(2,1)S(1)} %get-tuple-element.245), channel_id=1, source_target_pairs={{0,0},{1,1},{4,2},{5,3},{2,4},{3,5},{6,6},{7,7},{8,8},{9,9},{12,10... | collective-permute-start | bytes 2359304 | tf_op jit(solution)/shard_map/ppermute | solution.py:67
  171.0 38.7 %collective-permute-start.27 = (bf16[512,768]{1,0:T(8,128)(2,1)S(1)}, bf16[512,768]{1,0:T(8,128)(2,1)S(1)}, u32[]{:S(2)}, u32[]{:S(2)}) collective-permute-start(bf16[512,768]{1,0:T(8,128)(2,1)S(1)} %get-tuple-element.244), channel_id=1, source_target_pairs={{1,0},{0,1},{5,2},{4,3},{3,4},{2,5},{7,6},{6,7},{9,8},{8,9},{13,10... | collective-permute-start | bytes 2359304 | tf_op jit(solution)/shard_map/ppermute | solution.py:67
  230.0 44.2 %collective-permute-start.30 = (bf16[2,1,432,768]{3,2,1,0:T(8,128)(2,1)S(1)}, bf16[2,1,432,768]{3,2,1,0:T(8,128)(2,1)}, u32[]{:S(2)}, u32[]{:S(2)}) collective-permute-start(bf16[2,1,432,768]{3,2,1,0:T(8,128)(2,1)S(1)} %get-tuple-element.197), channel_id=1, source_target_pairs={{0,8},{4,12},{8,0},{12,4},{16,24},{20,28},{24,16},{28,20},{1,9},{5... | collective-permute-start | bytes 3981320 | tf_op jit(solution)/shard_map/ppermute | solution.py:110
  231.1 43.1 %collective-permute-start.31 = (bf16[1,2,432,768]{3,2,1,0:T(8,128)(2,1)S(1)}, bf16[1,2,432,768]{3,2,1,0:T(8,128)(2,1)}, u32[]{:S(2)}, u32[]{:S(2)}) collective-permute-start(bf16[1,2,432,768]{3,2,1,0:T(8,128)(2,1)S(1)} %get-tuple-element.199), channel_id=1, source_target_pairs={{0,16},{4,20},{8,24},{12,28},{16,0},{20,4},{24,8},{28,12},{1,17},{... | collective-permute-start | bytes 3981320 | tf_op jit(solution)/shard_map/ppermute | solution.py:110
  290.6 18.1 %collective-permute-start.36 = (bf16[432,768]{1,0:T(8,128)(2,1)}, bf16[432,768]{1,0:T(8,128)(2,1)}, u32[]{:S(2)}, u32[]{:S(2)}) collective-permute-start(bf16[432,768]{1,0:T(8,128)(2,1)} %get-tuple-element.212), channel_id=1, source_target_pairs={{0,8},{4,12},{8,0},{12,4},{16,24},{20,28},{24,16},{28,20},{1,9},{5... | collective-permute-start | bytes 1990664 | tf_op jit(solution)/shard_map/ppermute | solution.py:110
  292.6 19.2 %collective-permute-start.34 = (bf16[512,768]{1,0:T(8,128)(2,1)}, bf16[512,768]{1,0:T(8,128)(2,1)}, u32[]{:S(2)}, u32[]{:S(2)}) collective-permute-start(bf16[512,768]{1,0:T(8,128)(2,1)} %get-tuple-element.241), channel_id=1, source_target_pairs={{0,0},{1,1},{4,2},{5,3},{2,4},{3,5},{6,6},{7,7},{8,8},{9,9},{12,10... | collective-permute-start | bytes 2359304 | tf_op jit(solution)/shard_map/ppermute | solution.py:67
  300.0 31.1 %collective-permute-start.33 = (bf16[512,768]{1,0:T(8,128)(2,1)S(1)}, bf16[512,768]{1,0:T(8,128)(2,1)}, u32[]{:S(2)}, u32[]{:S(2)}) collective-permute-start(bf16[512,768]{1,0:T(8,128)(2,1)S(1)} %get-tuple-element.240), channel_id=1, source_target_pairs={{1,0},{0,1},{5,2},{4,3},{3,4},{2,5},{7,6},{6,7},{9,8},{8,9},{13,10... | collective-permute-start | bytes 2359304 | tf_op jit(solution)/shard_map/ppermute | solution.py:67
  301.4 31.2 %collective-permute-start.38 = (bf16[1,2,4,32,1152]{4,3,1,2,0:T(8,128)(2,1)}, bf16[1,2,4,32,1152]{4,3,1,2,0:T(8,128)(2,1)}, u32[]{:S(2)}, u32[]{:S(2)}) collective-permute-start(bf16[1,2,4,32,1152]{4,3,1,2,0:T(8,128)(2,1)} %get-tuple-element.233), channel_id=1, source_target_pairs={{0,8},{4,12},{8,0},{12,4},{16,24},{20,28},{24,16},{28,20},{1,9},{5... | collective-permute-start | bytes 1769480 | tf_op jit(solution)/shard_map/ppermute | solution.py:110
  306.4 27.4 %collective-permute-start.39 = (bf16[1,2,4,32,1152]{4,3,1,2,0:T(8,128)(2,1)}, bf16[1,2,4,32,1152]{4,3,1,2,0:T(8,128)(2,1)}, u32[]{:S(2)}, u32[]{:S(2)}) collective-permute-start(bf16[1,2,4,32,1152]{4,3,1,2,0:T(8,128)(2,1)} %get-tuple-element.234), channel_id=1, source_target_pairs={{0,16},{4,20},{8,24},{12,28},{16,0},{20,4},{24,8},{28,12},{1,17},{... | collective-permute-start | bytes 1769480 | tf_op jit(solution)/shard_map/ppermute | solution.py:110
  308.7 25.1 %collective-permute-start.40 = (bf16[1,2,4,32,1152]{4,3,1,2,0:T(8,128)(2,1)}, bf16[1,2,4,32,1152]{4,3,1,2,0:T(8,128)(2,1)}, u32[]{:S(2)}, u32[]{:S(2)}) collective-permute-start(bf16[1,2,4,32,1152]{4,3,1,2,0:T(8,128)(2,1)} %get-tuple-element.235), channel_id=1, source_target_pairs={{0,24},{4,28},{8,16},{12,20},{16,8},{20,12},{24,0},{28,4},{1,25},{... | collective-permute-start | bytes 1769480 | tf_op jit(solution)/shard_map/ppermute | solution.py:110
  314.9 27.9 %collective-permute-start.41 = (bf16[2,216,768]{2,1,0:T(8,128)(2,1)}, bf16[2,216,768]{2,1,0:T(8,128)(2,1)S(1)}, u32[]{:S(2)}, u32[]{:S(2)}) collective-permute-start(bf16[2,216,768]{2,1,0:T(8,128)(2,1)} %get-tuple-element.221), channel_id=1, source_target_pairs={{0,1},{1,0},{2,3},{3,2},{4,5},{5,4},{6,7},{7,6},{8,9},{9,8},{10,11... | collective-permute-start | bytes 1990664 | tf_op jit(solution)/shard_map/ppermute | solution.py:35
  (62 other events, 911.9 us)

commit v6 on v5

--- a/solution.py
+++ b/solution.py
@@ -1188,10 +1188,13 @@
         chip = lax.axis_index("dp") >> 1
         x, y = chip & 1, chip >> 1
         grad_other, come = join(swap(grad_down), come)
-        sums = added(grad_in, grad_other).reshape(2, 2, -1, width)
         cut = chunks * span + span // 2
-        upper, lower = sums[:, :, :cut], sums[:, :, cut:]
-        moves = [pick(upper, x, 1), pick(upper, 1 - x, 1), pick(lower, y, 0), pick(lower, 1 - y, 0)]
+        both = [p.reshape(2, 2, -1, width) for p in (grad_in, grad_other)]
+        moves = [
+            added(*(pick(p[:, :, rows], which, axis) for p in both))
+            for rows, axis, own_side in ((slice(0, cut), 1, x), (slice(cut, None), 0, y))
+            for which in (own_side, 1 - own_side)
+        ]
         mine, come, *moves = join(mine, come, *moves)
         moves[1], moves[3] = flip_chip(moves[1], 1), flip_chip(moves[3], 2)
     grad_qkv, grad_own, grad_theirs, sums = attend_back(
@@ -1210,13 +1213,15 @@
         grad_qkv, grad_own, grad_theirs, sums, *moves = join(grad_qkv, grad_own, grad_theirs, sums, *moves)
     come_rows = swap(grad_theirs)
     if direct:
-        upper, lower = added(*moves[:2]), added(*moves[2:])
-        moves = [pick(upper, y, 0), pick(upper, 1 - y, 0), pick(lower, x, 1), pick(lower, 1 - x, 1)]
+        moves = [
+            added(*(pick(p, which, axis) for p in pair))
+            for pair, axis, own_side in ((moves[:2], 0, y), (moves[2:], 1, x))
+            for which in (own_side, 1 - own_side)
+        ]
         grad_own, *moves = join(grad_own, *(move.reshape(-1, width) for move in moves))
         moves[1], moves[3] = flip_chip(moves[1], 2), flip_chip(moves[3], 1)
-    grad_tokens = added(grad_own, come_rows)
-    grad_tokens, grad_qkv = join(grad_tokens, grad_qkv)
-    grad_inputs = start_back(grad_tokens)
+    grad_inputs = [added(*pair) for pair in zip(start_back(grad_own), start_back(come_rows))]
+    grad_inputs, grad_qkv = join(grad_inputs, grad_qkv)
     first_back = finish_back(grad_inputs, 0)
     grad_w_qkv = dot(tokens, grad_qkv, TN).astype(LOW)
     vectors = in_sums[: 6 + chunks].reshape(-1)

time: 376 us -> 373 us (level)
  the two profiles are of different devices: /device:TPU:0 before, /device:TPU:8 now
where the time goes in v6:
time: 373 us; the launch traced here: 367 us
  Pallas kernels  146 us (39%)
  waiting for transfers between devices  103 us (28%)
  starting transfers between devices  48.2 us (13%)
  local copies, waits for them, and re-layouts  32.8 us (9%)
  other arithmetic  28.6 us (8%)
  matrix products  4.44 us (1%)
    pallas_call x1, Pallas kernels, attend_back(): pl.pallas_call(partial(attend_back_kernel, blocks, 2), out_shape=(jax.Sha...  42.4 us
    ppermute x8, waiting for transfers between devices, flip_seq(): return lax.ppermute(array, 'seq', [(i, i ^ k) for i in range(size)])  42.2 us
    pallas_call x1, Pallas kernels, layer_backward(): pl.pallas_call(partial(backward_kernel, TILE, chips, direct), grid=(own /...  37.2 us
    ppermute x14, waiting for transfers between devices, flip_chip(): return lax.ppermute(array, 'dp', [(i, i ^ 2 * away) for i in range(size)])  35 us
    pallas_call x1, Pallas kernels, layer_forward(): pl.pallas_call(partial(forward_kernel, chips, direct), grid=(own // TILE,...  29 us
    pallas_call x1, Pallas kernels, attend(): pl.pallas_call(partial(attend_kernel, pairs, blocks, 4), out_shape=(jax.S...  19.2 us
    ppermute x14, starting transfers between devices, flip_chip(): return lax.ppermute(array, 'dp', [(i, i ^ 2 * away) for i in range(size)])  16.7 us
    ppermute x4, waiting for transfers between devices, finish_back(): return lax.ppermute(parts[a], ('dp', 'seq'), [(t, s) for s, t in pairs])  13 us
  transfers between devices with their start and end apart: 45, of which 18 were waited for; matrix products, arithmetic and copies ran while one was open for 11% of the time, Pallas kernels for 40%

profile of v6, /device:TPU:8, one launch (start us, length us, event | category | flops | bytes accessed | tf_op | source)
XLA Modules:
  0.0 366.6 jit_solution(12343656662816001537)
XLA Ops:
  11.3 3.9 %collective-permute-start.4 = (bf16[2,32,1152]{2,1,0:T(8,128)(2,1)S(1)}, bf16[2,32,1152]{2,1,0:T(8,128)(2,1)S(1)}, u32[]{:S(2)}, u32[]{:S(2)}) collective-permute-start(bf16[2,32,1152]{2,1,0:T(8,128)(2,1)S(1)} %pad_maximum_fusion.8.shard_ref), channel_id=1, source_target_pairs={{0,3},{1,2},{2,1},{3,0},{4,7},{5,6},{6,5},{7,4},{8,11},{9,10},{10,... | collective-permute-start | bytes 442376 | tf_op jit(solution)/shard_map/ppermute | solution.py:35
  16.2 14.0 %collective-permute-done.4.mirror_ref = bf16[2,32,1152]{2,1,0:T(8,128)(2,1)S(1)} collective-permute-done((bf16[2,32,1152]{2,1,0:T(8,128)(2,1)S(1)}, bf16[2,32,1152]{2,1,0:T(8,128)(2,1)S(1)}, u32[]{:S(2)}, u32[]{:S(2)}) %collective-permute-start.4) | collective-permute-done | bytes 147488 | tf_op jit(solution)/shard_map/ppermute | solution.py:35
  57.7 11.5 %collective-permute-done.10.refs_7_ = bf16[2,112,1152]{2,1,0:T(8,128)(2,1)} collective-permute-done((bf16[2,112,1152]{2,1,0:T(8,128)(2,1)}, bf16[2,112,1152]{2,1,0:T(8,128)(2,1)}, u32[]{:S(2)}, u32[]{:S(2)}) %collective-permute-start.10) | collective-permute-done | bytes 516128 | tf_op jit(solution)/shard_map/ppermute | solution.py:110
  78.4 13.7 %collective-permute-done.12 = bf16[432,768]{1,0:T(8,128)(2,1)S(1)} collective-permute-done((bf16[432,768]{1,0:T(8,128)(2,1)}, bf16[432,768]{1,0:T(8,128)(2,1)S(1)}, u32[]{:S(2)}, u32[]{:S(2)}) %collective-permute-start.12) | collective-permute-done | bytes 663584 | tf_op jit(solution)/shard_map/ppermute | solution.py:110
  96.1 10.9 %project.1 = (bf16[2048,1152]{1,0:T(8,128)(2,1)}, bf16[2048,768]{1,0:T(8,128)(2,1)}, bf16[768,1152]{1,0:T(8,128)(2,1)}) custom-call(s32[3]{0:T(128)S(1)} %copy-done.7, bf16[512,768]{1,0:T(8,128)(2,1)S(1)} %collective-permute-done.6.refs_0_, bf16[512,768]{1,0:T(8,128)(2,1)} %collective-permute-done.14.refs_1_, ...), custom_call_target="tpu_custom_call" | custom-call | flops 1 | bytes 1 | tf_op jit(solution)/shard_map/project/pallas_call | solution.py:775
  110.0 19.2 %attend.1 = (bf16[2048,384]{1,0:T(8,128)(2,1)S(1)}, f32[32,8,128]{2,1,0:T(8,128)S(1)}) custom-call(s32[64]{0:T(128)S(1)} %pad_add_fusion.5.near_ref, s32[576]{0:T(1024)S(1)} %fusion.16.rand_ref, s32[2]{0:T(128)S(1)} %fusion.35.glob_ref, f32[32,3,8,128]{3,2,1,0:T(8,128)S(1)} %reshape.552.bias_ref, bf16[2048,1152]{1,0:T(8,128)(2,1)} %get-tuple-element.142.qkv_ref), custom_call_target="tpu_custom_call" | custom-call | flops 1 | bytes 1 | tf_op jit(solution)/shard_map/attend/pallas_call | solution.py:798
  131.4 4.1 %collective-permute-done.20.other_ref = bf16[1024,384]{1,0:T(8,128)(2,1)S(1)} collective-permute-done((bf16[1024,384]{1,0:T(8,128)(2,1)S(1)}, bf16[1024,384]{1,0:T(8,128)(2,1)S(1)}, u32[]{:S(2)}, u32[]{:S(2)}) %collective-permute-start.20) | collective-permute-done | bytes 786464 | tf_op jit(solution)/shard_map/ppermute | solution.py:30
  138.0 29.0 %layer_forward.1 = (bf16[1024,768]{1,0:T(8,128)(2,1)}, bf16[1024,3072]{1,0:T(8,128)(2,1)}, bf16[1024,3072]{1,0:T(8,128)(2,1)}, bf16[1024,768]{1,0:T(8,128)(2,1)}...) custom-call(s32[3]{0:T(128)} %pad_add_fusion.4.at_ref, bf16[2048,384]{1,0:T(8,128)(2,1)} %copy-done.2, ...), custom_call_target="tpu_custom_call" | custom-call | flops 1 | bytes 1 | tf_op jit(solution)/shard_map/layer_forward/pallas_call | solution.py:892
  170.8 37.2 %layer_backward.1 = (bf16[1024,768]{1,0:T(8,128)(2,1)}, bf16[1024,384]{1,0:T(8,128)(2,1)}, bf16[1024,384]{1,0:T(8,128)(2,1)}, f32[16,768]{1,0:T(8,128)}, bf16[4,...) custom-call(s32[3]{0:T(128)} %pad_add_fusion.4.at_ref, bf16[2048,384]{1,0:T(8,128)(2,1)} %copy-done.2, ...), custom_call_target="tpu_custom_call" | custom-call | flops 1 | bytes 1 | tf_op jit(solution)/shard_map/layer_backward/pallas_call | solution.py:924
  209.0 2.8 collective-permute-start.28
  212.1 2.9 fusion.45
  215.0 5.0 %collective-permute-done.29.come_ref = bf16[1024,384]{1,0:T(8,128)(2,1)S(1)} collective-permute-done((bf16[1024,384]{1,0:T(8,128)(2,1)}, bf16[1024,384]{1,0:T(8,128)(2,1)S(1)}, u32[]{:S(2)}, u32[]{:S(2)}) %collective-permute-start.29) | collective-permute-done | bytes 786464 | tf_op jit(solution)/shard_map/ppermute | solution.py:30
  221.7 2.9 fusion.46
  228.3 42.4 %attend_back.1 = (bf16[2048,1152]{1,0:T(8,128)(2,1)}, bf16[1024,768]{1,0:T(8,128)(2,1)}, bf16[1024,768]{1,0:T(8,128)(2,1)}, f32[1,1152]{1,0:T(1,128)}) custom-call(s32[64]{0:T(128)} %copy-done.9, s32[576]{0:T(1024)} %copy-done.6, s32[2]{0:T(128)} %copy-done.8, f32[32,3,8,128]{3,2,1,0:T(8,128)} %copy-done.3, f32[32,8,128]{2,1,0:T(8,128)} %copy-done.5, ...), custom_call_target="tpu_custom_call" | custom-call | flops 1 | bytes 1 | tf_op jit(solution)/shard_map/attend_back/pallas_call | solution.py:816
  271.8 2.9 fusion.6
  279.2 4.4 %convolution_convert_fusion = bf16[768,1152]{1,0:T(8,128)(2,1)S(1)} fusion(bf16[2048,768]{1,0:T(8,128)(2,1)S(1)} %copy-done.18, bf16[2048,1152]{1,0:T(8,128)(2,1)S(1)} %copy-done.42), kind=kOutput, calls=%fused_computation | convolution fusion | flops 3624763392 | bytes 9633792 | tf_op jit(solution)/shard_map/dot_general | solution.py:25
  287.4 7.4 %collective-permute-start.34 = (bf16[512,768]{1,0:T(8,128)(2,1)}, bf16[512,768]{1,0:T(8,128)(2,1)}, u32[]{:S(2)}, u32[]{:S(2)}) collective-permute-start(bf16[512,768]{1,0:T(8,128)(2,1)} %get-tuple-element.210), channel_id=1, source_target_pairs={{0,0},{1,1},{4,2},{5,3},{2,4},{3,5},{6,6},{7,7},{8,8},{9,9},{12,10... | collective-permute-start | bytes 2359304 | tf_op jit(solution)/shard_map/ppermute | solution.py:67
  299.0 3.5 collective-permute-done.35.refs_1_
  307.8 3.1 unpack.1
  311.4 13.0 %collective-permute-done.33 = bf16[512,768]{1,0:T(8,128)(2,1)} collective-permute-done((bf16[512,768]{1,0:T(8,128)(2,1)S(1)}, bf16[512,768]{1,0:T(8,128)(2,1)}, u32[]{:S(2)}, u32[]{:S(2)}) %collective-permute-start.33) | collective-permute-done | bytes 786464 | tf_op jit(solution)/shard_map/ppermute | solution.py:67
  325.8 4.1 %collective-permute-done.39 = bf16[1,2,4,32,1152]{4,3,1,2,0:T(8,128)(2,1)} collective-permute-done((bf16[1,2,4,32,1152]{4,3,1,2,0:T(8,128)(2,1)}, bf16[1,2,4,32,1152]{4,3,1,2,0:T(8,128)(2,1)}, u32[]{:S(2)}, u32[]{:S(2)}) %collective-permute-start.39) | collective-permute-done | bytes 589856 | tf_op jit(solution)/shard_map/ppermute | solution.py:110
  331.6 5.3 %collective-permute-done.41 = bf16[2,216,768]{2,1,0:T(8,128)(2,1)S(1)} collective-permute-done((bf16[2,216,768]{2,1,0:T(8,128)(2,1)}, bf16[2,216,768]{2,1,0:T(8,128)(2,1)S(1)}, u32[]{:S(2)}, u32[]{:S(2)}) %collective-permute-start.41) | collective-permute-done | bytes 663584 | tf_op jit(solution)/shard_map/ppermute | solution.py:35
  340.9 6.5 %collective-permute-done.42 = bf16[2,2,32,1152]{3,2,1,0:T(8,128)(2,1)S(1)} collective-permute-done((bf16[2,2,32,1152]{3,2,1,0:T(8,128)(2,1)S(1)}, bf16[2,2,32,1152]{3,2,1,0:T(8,128)(2,1)S(1)}, u32[]{:S(2)}, u32[]{:S(2)}) %collective-permute-start.42) | collective-permute-done | bytes 294944 | tf_op jit(solution)/shard_map/ppermute | solution.py:35
  348.0 12.5 %collective-permute-done.44 = bf16[216,768]{1,0:T(8,128)(2,1)S(1)} collective-permute-done((bf16[216,768]{1,0:T(8,128)(2,1)S(1)}, bf16[216,768]{1,0:T(8,128)(2,1)S(1)}, u32[]{:S(2)}, u32[]{:S(2)}) %collective-permute-start.44) | collective-permute-done | bytes 331808 | tf_op jit(solution)/shard_map/ppermute | solution.py:35
  (317 shorter events, 101.0 us)
Async XLA Ops:
  16.2 21.6 %collective-permute-start.1 = (bf16[232,768]{1,0:T(8,128)(2,1)S(1)}, bf16[232,768]{1,0:T(8,128)(2,1)S(1)}, u32[]{:S(2)}, u32[]{:S(2)}) collective-permute-start(bf16[232,768]{1,0:T(8,128)(2,1)S(1)} %concatenate.104.shard_ref), channel_id=1, source_target_pairs={{0,3},{1,2},{2,1},{3,0},{4,7},{5,6},{6,5},{7,4},{8,11},{9,10},{10,... | collective-permute-start | bytes 1069064 | tf_op jit(solution)/shard_map/ppermute | solution.py:35
  38.8 31.6 %collective-permute-start.5 = (bf16[2,232,768]{2,1,0:T(8,128)(2,1)}, bf16[2,232,768]{2,1,0:T(8,128)(2,1)}, u32[]{:S(2)}, u32[]{:S(2)}) collective-permute-start(bf16[2,232,768]{2,1,0:T(8,128)(2,1)} %pad_maximum_fusion.4), channel_id=1, source_target_pairs={{0,1},{1,0},{2,3},{3,2},{4,5},{5,4},{6,7},{7,6},{8,9},{9,8},{10,11... | collective-permute-start | bytes 2138120 | tf_op jit(solution)/shard_map/ppermute | solution.py:35
  43.8 25.4 %collective-permute-start.10 = (bf16[2,112,1152]{2,1,0:T(8,128)(2,1)}, bf16[2,112,1152]{2,1,0:T(8,128)(2,1)}, u32[]{:S(2)}, u32[]{:S(2)}) collective-permute-start(bf16[2,112,1152]{2,1,0:T(8,128)(2,1)} %pack_columns.1.refs_5_), channel_id=1, source_target_pairs={{0,16},{4,20},{8,24},{12,28},{16,0},{20,4},{24,8},{28,12},{1,17},{... | collective-permute-start | bytes 1548296 | tf_op jit(solution)/shard_map/ppermute | solution.py:110
  45.3 23.9 %collective-permute-start.11 = (bf16[2,112,1152]{2,1,0:T(8,128)(2,1)}, bf16[2,112,1152]{2,1,0:T(8,128)(2,1)}, u32[]{:S(2)}, u32[]{:S(2)}) collective-permute-start(bf16[2,112,1152]{2,1,0:T(8,128)(2,1)} %pack_columns.1.refs_5_), channel_id=1, source_target_pairs={{0,24},{4,28},{8,16},{12,20},{16,8},{20,12},{24,0},{28,4},{1,25},{... | collective-permute-start | bytes 1548296 | tf_op jit(solution)/shard_map/ppermute | solution.py:110
  49.6 20.9 %collective-permute-start.9 = (bf16[2,112,1152]{2,1,0:T(8,128)(2,1)}, bf16[2,112,1152]{2,1,0:T(8,128)(2,1)}, u32[]{:S(2)}, u32[]{:S(2)}) collective-permute-start(bf16[2,112,1152]{2,1,0:T(8,128)(2,1)} %pack_columns.1.refs_5_), channel_id=1, source_target_pairs={{0,8},{4,12},{8,0},{12,4},{16,24},{20,28},{24,16},{28,20},{1,9},{5... | collective-permute-start | bytes 1548296 | tf_op jit(solution)/shard_map/ppermute | solution.py:110
  52.4 26.0 %collective-permute-start.14 = (bf16[512,768]{1,0:T(8,128)(2,1)}, bf16[512,768]{1,0:T(8,128)(2,1)}, u32[]{:S(2)}, u32[]{:S(2)}) collective-permute-start(bf16[512,768]{1,0:T(8,128)(2,1)} %get-tuple-element.254), channel_id=1, source_target_pairs={{0,1},{1,0},{2,5},{3,4},{4,3},{5,2},{6,7},{7,6},{8,9},{9,8},{10,13... | collective-permute-start | bytes 2359304 | tf_op jit(solution)/shard_map/ppermute | solution.py:53
  73.0 19.1 %collective-permute-start.13 = (bf16[448,768]{1,0:T(8,128)(2,1)}, bf16[448,768]{1,0:T(8,128)(2,1)S(1)}, u32[]{:S(2)}, u32[]{:S(2)}) collective-permute-start(bf16[448,768]{1,0:T(8,128)(2,1)} %get-tuple-element.148), channel_id=1, source_target_pairs={{0,16},{4,20},{8,24},{12,28},{16,0},{20,4},{24,8},{28,12},{1,17},{... | collective-permute-start | bytes 2064392 | tf_op jit(solution)/shard_map/ppermute | solution.py:110
  93.9 35.3 %collective-permute-start.19 = (bf16[2,448,768]{2,1,0:T(8,128)(2,1)S(1)}, bf16[2,448,768]{2,1,0:T(8,128)(2,1)S(1)}, u32[]{:S(2)}, u32[]{:S(2)}) collective-permute-start(bf16[2,448,768]{2,1,0:T(8,128)(2,1)S(1)} %pad_maximum_fusion.2.refs_2_), channel_id=1, source_target_pairs={{0,8},{4,12},{8,0},{12,4},{16,24},{20,28},{24,16},{28,20},{1,9},{5... | collective-permute-start | bytes 4128776 | tf_op jit(solution)/shard_map/ppermute | solution.py:110
  95.5 33.6 %collective-permute-start.18 = (bf16[2,432,768]{2,1,0:T(8,128)(2,1)S(1)}, bf16[2,432,768]{2,1,0:T(8,128)(2,1)}, u32[]{:S(2)}, u32[]{:S(2)}) collective-permute-start(bf16[2,432,768]{2,1,0:T(8,128)(2,1)S(1)} %pad_maximum_fusion.3.refs_0_), channel_id=1, source_target_pairs={{0,16},{4,20},{8,24},{12,28},{16,0},{20,4},{24,8},{28,12},{1,17},{... | collective-permute-start | bytes 3981320 | tf_op jit(solution)/shard_map/ppermute | solution.py:110
  107.1 22.1 %collective-permute-start.17 = (bf16[512,768]{1,0:T(8,128)(2,1)S(1)}, bf16[512,768]{1,0:T(8,128)(2,1)S(1)}, u32[]{:S(2)}, u32[]{:S(2)}) collective-permute-start(bf16[512,768]{1,0:T(8,128)(2,1)S(1)} %dynamic-slice_bitcast_fusion.1), channel_id=1, source_target_pairs={{0,0},{1,1},{2,4},{3,5},{4,2},{5,3},{6,6},{7,7},{8,8},{9,9},{10,12... | collective-permute-start | bytes 2359304 | tf_op jit(solution)/shard_map/ppermute | solution.py:53
  108.3 22.5 %collective-permute-start.21 = (bf16[2,432,768]{2,1,0:T(8,128)(2,1)S(1)}, bf16[2,432,768]{2,1,0:T(8,128)(2,1)S(1)}, u32[]{:S(2)}, u32[]{:S(2)}) collective-permute-start(bf16[2,432,768]{2,1,0:T(8,128)(2,1)S(1)} %pad_maximum_fusion.3.refs_0_), channel_id=1, source_target_pairs={{0,4},{4,0},{8,12},{12,8},{16,20},{20,16},{24,28},{28,24},{1,5},{5... | collective-permute-start | bytes 3981320 | tf_op jit(solution)/shard_map/ppermute | solution.py:30
  109.9 21.5 %collective-permute-start.23 = (bf16[2,448,768]{2,1,0:T(8,128)(2,1)S(1)}, bf16[2,448,768]{2,1,0:T(8,128)(2,1)S(1)}, u32[]{:S(2)}, u32[]{:S(2)}) collective-permute-start(bf16[2,448,768]{2,1,0:T(8,128)(2,1)S(1)} %pad_maximum_fusion.2.refs_2_), channel_id=1, source_target_pairs={{0,4},{4,0},{8,12},{12,8},{16,20},{20,16},{24,28},{28,24},{1,5},{5... | collective-permute-start | bytes 4128776 | tf_op jit(solution)/shard_map/ppermute | solution.py:30
  130.8 36.2 %collective-permute-start.25 = (bf16[512,768]{1,0:T(8,128)(2,1)S(1)}, bf16[512,768]{1,0:T(8,128)(2,1)S(1)}, u32[]{:S(2)}, u32[]{:S(2)}) collective-permute-start(bf16[512,768]{1,0:T(8,128)(2,1)S(1)} %dynamic-slice_bitcast_fusion), channel_id=1, source_target_pairs={{0,1},{1,0},{2,5},{3,4},{4,3},{5,2},{6,7},{7,6},{8,9},{9,8},{10,13... | collective-permute-start | bytes 2359304 | tf_op jit(solution)/shard_map/ppermute | solution.py:53
  169.4 38.7 %collective-permute-start.26 = (bf16[512,768]{1,0:T(8,128)(2,1)S(1)}, bf16[512,768]{1,0:T(8,128)(2,1)S(1)}, u32[]{:S(2)}, u32[]{:S(2)}) collective-permute-start(bf16[512,768]{1,0:T(8,128)(2,1)S(1)} %get-tuple-element.253), channel_id=1, source_target_pairs={{0,0},{1,1},{4,2},{5,3},{2,4},{3,5},{6,6},{7,7},{8,8},{9,9},{12,10... | collective-permute-start | bytes 2359304 | tf_op jit(solution)/shard_map/ppermute | solution.py:67
  170.1 38.0 %collective-permute-start.27 = (bf16[512,768]{1,0:T(8,128)(2,1)S(1)}, bf16[512,768]{1,0:T(8,128)(2,1)S(1)}, u32[]{:S(2)}, u32[]{:S(2)}) collective-permute-start(bf16[512,768]{1,0:T(8,128)(2,1)S(1)} %get-tuple-element.252), channel_id=1, source_target_pairs={{1,0},{0,1},{5,2},{4,3},{3,4},{2,5},{7,6},{6,7},{9,8},{8,9},{13,10... | collective-permute-start | bytes 2359304 | tf_op jit(solution)/shard_map/ppermute | solution.py:67
  226.1 44.5 %collective-permute-start.30 = (bf16[2,1,432,768]{3,2,1,0:T(8,128)(2,1)S(1)}, bf16[2,1,432,768]{3,2,1,0:T(8,128)(2,1)S(1)}, u32[]{:S(2)}, u32[]{:S(2)}) collective-permute-start(bf16[2,1,432,768]{3,2,1,0:T(8,128)(2,1)S(1)} %get-tuple-element.198), channel_id=1, source_target_pairs={{0,8},{4,12},{8,0},{12,4},{16,24},{20,28},{24,16},{28,20},{1,9},{5... | collective-permute-start | bytes 3981320 | tf_op jit(solution)/shard_map/ppermute | solution.py:110
  227.7 42.9 %collective-permute-start.31 = (bf16[1,2,432,768]{3,2,1,0:T(8,128)(2,1)S(1)}, bf16[1,2,432,768]{3,2,1,0:T(8,128)(2,1)}, u32[]{:S(2)}, u32[]{:S(2)}) collective-permute-start(bf16[1,2,432,768]{3,2,1,0:T(8,128)(2,1)S(1)} %get-tuple-element.200), channel_id=1, source_target_pairs={{0,16},{4,20},{8,24},{12,28},{16,0},{20,4},{24,8},{28,12},{1,17},{... | collective-permute-start | bytes 3981320 | tf_op jit(solution)/shard_map/ppermute | solution.py:110
  287.4 20.4 %collective-permute-start.34 = (bf16[512,768]{1,0:T(8,128)(2,1)}, bf16[512,768]{1,0:T(8,128)(2,1)}, u32[]{:S(2)}, u32[]{:S(2)}) collective-permute-start(bf16[512,768]{1,0:T(8,128)(2,1)} %get-tuple-element.210), channel_id=1, source_target_pairs={{0,0},{1,1},{4,2},{5,3},{2,4},{3,5},{6,6},{7,7},{8,8},{9,9},{12,10... | collective-permute-start | bytes 2359304 | tf_op jit(solution)/shard_map/ppermute | solution.py:67
  294.8 29.5 %collective-permute-start.33 = (bf16[512,768]{1,0:T(8,128)(2,1)S(1)}, bf16[512,768]{1,0:T(8,128)(2,1)}, u32[]{:S(2)}, u32[]{:S(2)}) collective-permute-start(bf16[512,768]{1,0:T(8,128)(2,1)S(1)} %get-tuple-element.209), channel_id=1, source_target_pairs={{1,0},{0,1},{5,2},{4,3},{3,4},{2,5},{7,6},{6,7},{9,8},{8,9},{13,10... | collective-permute-start | bytes 2359304 | tf_op jit(solution)/shard_map/ppermute | solution.py:67
  298.0 27.8 %collective-permute-start.38 = (bf16[1,2,4,32,1152]{4,3,1,2,0:T(8,128)(2,1)}, bf16[1,2,4,32,1152]{4,3,1,2,0:T(8,128)(2,1)}, u32[]{:S(2)}, u32[]{:S(2)}) collective-permute-start(bf16[1,2,4,32,1152]{4,3,1,2,0:T(8,128)(2,1)} %get-tuple-element.243), channel_id=1, source_target_pairs={{0,8},{4,12},{8,0},{12,4},{16,24},{20,28},{24,16},{28,20},{1,9},{5... | collective-permute-start | bytes 1769480 | tf_op jit(solution)/shard_map/ppermute | solution.py:110
  302.6 27.3 %collective-permute-start.39 = (bf16[1,2,4,32,1152]{4,3,1,2,0:T(8,128)(2,1)}, bf16[1,2,4,32,1152]{4,3,1,2,0:T(8,128)(2,1)}, u32[]{:S(2)}, u32[]{:S(2)}) collective-permute-start(bf16[1,2,4,32,1152]{4,3,1,2,0:T(8,128)(2,1)} %get-tuple-element.244), channel_id=1, source_target_pairs={{0,16},{4,20},{8,24},{12,28},{16,0},{20,4},{24,8},{28,12},{1,17},{... | collective-permute-start | bytes 1769480 | tf_op jit(solution)/shard_map/ppermute | solution.py:110
  305.0 24.9 %collective-permute-start.40 = (bf16[1,2,4,32,1152]{4,3,1,2,0:T(8,128)(2,1)}, bf16[1,2,4,32,1152]{4,3,1,2,0:T(8,128)(2,1)}, u32[]{:S(2)}, u32[]{:S(2)}) collective-permute-start(bf16[1,2,4,32,1152]{4,3,1,2,0:T(8,128)(2,1)} %get-tuple-element.245), channel_id=1, source_target_pairs={{0,24},{4,28},{8,16},{12,20},{16,8},{20,12},{24,0},{28,4},{1,25},{... | collective-permute-start | bytes 1769480 | tf_op jit(solution)/shard_map/ppermute | solution.py:110
  310.9 26.0 %collective-permute-start.41 = (bf16[2,216,768]{2,1,0:T(8,128)(2,1)}, bf16[2,216,768]{2,1,0:T(8,128)(2,1)S(1)}, u32[]{:S(2)}, u32[]{:S(2)}) collective-permute-start(bf16[2,216,768]{2,1,0:T(8,128)(2,1)} %get-tuple-element.223), channel_id=1, source_target_pairs={{0,1},{1,0},{2,3},{3,2},{4,5},{5,4},{6,7},{7,6},{8,9},{9,8},{10,11... | collective-permute-start | bytes 1990664 | tf_op jit(solution)/shard_map/ppermute | solution.py:35
  340.8 19.7 %collective-permute-start.44 = (bf16[216,768]{1,0:T(8,128)(2,1)S(1)}, bf16[216,768]{1,0:T(8,128)(2,1)S(1)}, u32[]{:S(2)}, u32[]{:S(2)}) collective-permute-start(bf16[216,768]{1,0:T(8,128)(2,1)S(1)} %fusion.12), channel_id=1, source_target_pairs={{0,3},{1,2},{2,1},{3,0},{4,7},{5,6},{6,5},{7,4},{8,11},{9,10},{10,... | collective-permute-start | bytes 995336 | tf_op jit(solution)/shard_map/ppermute | solution.py:35
  (64 other events, 897.7 us)

commit v7 on v6

--- a/solution.py
+++ b/solution.py
@@ -354,10 +354,12 @@
     come_ref,
     w_ref,
     grad_first_ref,
-    out_ref,
+    tokens_ref,
+    weights_ref,
     rows_own_ref,
     rows_other_ref,
     sums_ref,
+    out_ref,
     grad_ref,
     acc_ref,
 ):
@@ -485,6 +487,9 @@
             return carry
 
         lax.fori_loop(0, half // tile, token_rows, 0)
+    for pair in range(pairs):
+        lanes = slice(384 * pair, 384 * pair + 384)
+        weights_ref[:, lanes] = dot(tokens_ref[...], out_ref[:, lanes], TN).astype(LOW)
 
 
 def pack_kernel(seq, chunks, cut, at_ref, shard_ref, near_ref, mirror_ref, upper_ref, lower_ref):
@@ -809,28 +814,29 @@
     )(near, rand, globs, bias, qkv)
 
 
-def attend_back(near, rand, globs, bias, log_total, qkv, mine, come, w_qkv, grad_first):
+def attend_back(near, rand, globs, bias, log_total, qkv, mine, come, w_qkv, grad_first, tokens):
     length, (wide, width) = qkv.shape[0], w_qkv.shape
     pairs, blocks = width // 384, length // BLOCK
     rows = jax.ShapeDtypeStruct((length // 2, wide), LOW)
     return pl.pallas_call(
         partial(attend_back_kernel, blocks, 2),
         out_shape=(
-            jax.ShapeDtypeStruct((length, width), LOW),
+            jax.ShapeDtypeStruct((wide, width), LOW),
             rows,
             rows,
             jax.ShapeDtypeStruct((1, width), WIDE),
         ),
-        in_specs=[IN_SMEM] * 3 + [IN_VMEM] * 7,
+        in_specs=[IN_SMEM] * 3 + [IN_VMEM] * 8,
         out_specs=(IN_VMEM,) * 4,
         scratch_shapes=[
+            pltpu.VMEM((length, width), LOW),
             pltpu.VMEM((length, 128 * pairs), LOW),
             pltpu.VMEM((length, 256 * pairs), WIDE),
         ],
         compiler_params=pltpu.CompilerParams(vmem_limit_bytes=56 << 20),
         cost_estimate=pl.CostEstimate(flops=1, bytes_accessed=1, transcendentals=0),
         name="attend_back",
-    )(near, rand, globs, bias, log_total, qkv, mine, come, w_qkv, grad_first)
+    )(near, rand, globs, bias, log_total, qkv, mine, come, w_qkv, grad_first, tokens)
 
 
 def pack_columns(at, shard, near, mirror, rows_in):
@@ -1197,7 +1203,7 @@
         ]
         mine, come, *moves = join(mine, come, *moves)
         moves[1], moves[3] = flip_chip(moves[1], 1), flip_chip(moves[3], 2)
-    grad_qkv, grad_own, grad_theirs, sums = attend_back(
+    grad_w_qkv, grad_own, grad_theirs, sums = attend_back(
         sides,
         rand,
         glob_at,
@@ -1208,9 +1214,12 @@
         come,
         w_qkv,
         grad_first,
+        tokens,
     )
     if direct:
-        grad_qkv, grad_own, grad_theirs, sums, *moves = join(grad_qkv, grad_own, grad_theirs, sums, *moves)
+        grad_w_qkv, grad_own, grad_theirs, sums, *moves = join(
+            grad_w_qkv, grad_own, grad_theirs, sums, *moves
+        )
     come_rows = swap(grad_theirs)
     if direct:
         moves = [
@@ -1221,9 +1230,7 @@
         grad_own, *moves = join(grad_own, *(move.reshape(-1, width) for move in moves))
         moves[1], moves[3] = flip_chip(moves[1], 2), flip_chip(moves[3], 1)
     grad_inputs = [added(*pair) for pair in zip(start_back(grad_own), start_back(come_rows))]
-    grad_inputs, grad_qkv = join(grad_inputs, grad_qkv)
     first_back = finish_back(grad_inputs, 0)
-    grad_w_qkv = dot(tokens, grad_qkv, TN).astype(LOW)
     vectors = in_sums[: 6 + chunks].reshape(-1)
     vectors = jnp.pad(vectors, (0, -vectors.shape[0] % (3 * half_width))).reshape(-1, 3 * half_width)
     lines = jnp.concatenate([sums, vectors], 0).astype(LOW)

time: 373 us -> 383 us (1.027)
  the two profiles are of different devices: /device:TPU:8 before, /device:TPU:0 now
where the time goes in v7:
time: 383 us; the launch traced here: 376 us
  Pallas kernels  152 us (40%)
  waiting for transfers between devices  88.3 us (23%)
  starting transfers between devices  66.1 us (17%)
  other arithmetic  35.3 us (9%)
  local copies, waits for them, and re-layouts  31.1 us (8%)
    pallas_call x1, Pallas kernels, attend_back(): pl.pallas_call(partial(attend_back_kernel, blocks, 2), out_shape=(jax.Sha...  47.7 us
    ppermute x14, waiting for transfers between devices, flip_chip(): return lax.ppermute(array, 'dp', [(i, i ^ 2 * away) for i in range(size)])  43.3 us
    pallas_call x1, Pallas kernels, layer_backward(): pl.pallas_call(partial(backward_kernel, TILE, chips, direct), grid=(own /...  37.4 us
    ppermute x8, waiting for transfers between devices, flip_seq(): return lax.ppermute(array, 'seq', [(i, i ^ k) for i in range(size)])  30.6 us
    pallas_call x1, Pallas kernels, layer_forward(): pl.pallas_call(partial(forward_kernel, chips, direct), grid=(own // TILE,...  29 us
    ppermute x8, starting transfers between devices, flip_seq(): return lax.ppermute(array, 'seq', [(i, i ^ k) for i in range(size)])  22 us
    pallas_call x1, Pallas kernels, attend(): pl.pallas_call(partial(attend_kernel, pairs, blocks, 4), out_shape=(jax.S...  19.2 us
    ppermute x14, starting transfers between devices, flip_chip(): return lax.ppermute(array, 'dp', [(i, i ^ 2 * away) for i in range(size)])  16.5 us
  transfers between devices with their start and end apart: 45, of which 15 were waited for; matrix products, arithmetic and copies ran while one was open for 13% of the time, Pallas kernels for 40%

profile of v7, /device:TPU:0, one launch (start us, length us, event | category | flops | bytes accessed | tf_op | source)
XLA Modules:
  0.0 375.7 jit_solution(3494620409848517720)
XLA Ops:
  12.6 6.7 %collective-permute-start.4 = (bf16[2,32,1152]{2,1,0:T(8,128)(2,1)S(1)}, bf16[2,32,1152]{2,1,0:T(8,128)(2,1)S(1)}, u32[]{:S(2)}, u32[]{:S(2)}) collective-permute-start(bf16[2,32,1152]{2,1,0:T(8,128)(2,1)S(1)} %pad_maximum_fusion.8.shard_ref), channel_id=1, source_target_pairs={{0,3},{1,2},{2,1},{3,0},{4,7},{5,6},{6,5},{7,4},{8,11},{9,10},{10,... | collective-permute-start | bytes 442376 | tf_op jit(solution)/shard_map/ppermute | solution.py:35
  22.6 10.8 %collective-permute-start.7 = (bf16[2,2,32,1152]{3,2,1,0:T(8,128)(2,1)S(1)}, bf16[2,2,32,1152]{3,2,1,0:T(8,128)(2,1)}, u32[]{:S(2)}, u32[]{:S(2)}) collective-permute-start(bf16[2,2,32,1152]{3,2,1,0:T(8,128)(2,1)S(1)} %pad_maximum_fusion.5), channel_id=1, source_target_pairs={{0,1},{1,0},{2,3},{3,2},{4,5},{5,4},{6,7},{7,6},{8,9},{9,8},{10,11... | collective-permute-start | bytes 884744 | tf_op jit(solution)/shard_map/ppermute | solution.py:35
  58.3 12.5 %collective-permute-done.10.refs_7_ = bf16[2,112,1152]{2,1,0:T(8,128)(2,1)} collective-permute-done((bf16[2,112,1152]{2,1,0:T(8,128)(2,1)}, bf16[2,112,1152]{2,1,0:T(8,128)(2,1)}, u32[]{:S(2)}, u32[]{:S(2)}) %collective-permute-start.10) | collective-permute-done | bytes 516128 | tf_op jit(solution)/shard_map/ppermute | solution.py:110
  80.0 12.1 %collective-permute-done.12 = bf16[432,768]{1,0:T(8,128)(2,1)S(1)} collective-permute-done((bf16[432,768]{1,0:T(8,128)(2,1)}, bf16[432,768]{1,0:T(8,128)(2,1)S(1)}, u32[]{:S(2)}, u32[]{:S(2)}) %collective-permute-start.12) | collective-permute-done | bytes 663584 | tf_op jit(solution)/shard_map/ppermute | solution.py:110
  96.5 10.8 %project.1 = (bf16[2048,1152]{1,0:T(8,128)(2,1)}, bf16[2048,768]{1,0:T(8,128)(2,1)}, bf16[768,1152]{1,0:T(8,128)(2,1)}) custom-call(s32[3]{0:T(128)S(1)} %copy-done.7, bf16[512,768]{1,0:T(8,128)(2,1)S(1)} %collective-permute-done.6.refs_0_, bf16[512,768]{1,0:T(8,128)(2,1)} %collective-permute-done.14.refs_1_, ...), custom_call_target="tpu_custom_call" | custom-call | flops 1 | bytes 1 | tf_op jit(solution)/shard_map/project/pallas_call | solution.py:780
  110.6 19.2 %attend.1 = (bf16[2048,384]{1,0:T(8,128)(2,1)S(1)}, f32[32,8,128]{2,1,0:T(8,128)S(1)}) custom-call(s32[64]{0:T(128)S(1)} %pad_add_fusion.5.near_ref, s32[576]{0:T(1024)S(1)} %fusion.16.rand_ref, s32[2]{0:T(128)S(1)} %fusion.35.glob_ref, f32[32,3,8,128]{3,2,1,0:T(8,128)S(1)} %reshape.552.bias_ref, bf16[2048,1152]{1,0:T(8,128)(2,1)} %get-tuple-element.139.qkv_ref), custom_call_target="tpu_custom_call" | custom-call | flops 1 | bytes 1 | tf_op jit(solution)/shard_map/attend/pallas_call | solution.py:803
  132.8 3.3 collective-permute-done.20.other_ref
  138.6 29.0 %layer_forward.1 = (bf16[1024,768]{1,0:T(8,128)(2,1)}, bf16[1024,3072]{1,0:T(8,128)(2,1)}, bf16[1024,3072]{1,0:T(8,128)(2,1)}, bf16[1024,768]{1,0:T(8,128)(2,1)}...) custom-call(s32[3]{0:T(128)} %pad_add_fusion.4.at_ref, bf16[2048,384]{1,0:T(8,128)(2,1)} %copy-done.2, ...), custom_call_target="tpu_custom_call" | custom-call | flops 1 | bytes 1 | tf_op jit(solution)/shard_map/layer_forward/pallas_call | solution.py:898
  171.6 37.4 %layer_backward.1 = (bf16[1024,768]{1,0:T(8,128)(2,1)}, bf16[1024,384]{1,0:T(8,128)(2,1)}, bf16[1024,384]{1,0:T(8,128)(2,1)}, f32[16,768]{1,0:T(8,128)}, bf16[4,...) custom-call(s32[3]{0:T(128)} %pad_add_fusion.4.at_ref, bf16[2048,384]{1,0:T(8,128)(2,1)} %copy-done.2, ...), custom_call_target="tpu_custom_call" | custom-call | flops 1 | bytes 1 | tf_op jit(solution)/shard_map/layer_backward/pallas_call | solution.py:930
  209.9 3.4 collective-permute-start.28
  213.6 2.9 fusion.45
  216.5 5.0 %collective-permute-done.29.come_ref = bf16[1024,384]{1,0:T(8,128)(2,1)S(1)} collective-permute-done((bf16[1024,384]{1,0:T(8,128)(2,1)}, bf16[1024,384]{1,0:T(8,128)(2,1)S(1)}, u32[]{:S(2)}, u32[]{:S(2)}) %collective-permute-start.29) | collective-permute-done | bytes 786464 | tf_op jit(solution)/shard_map/ppermute | solution.py:30
  223.2 2.9 fusion.46
  231.1 47.7 %attend_back.1 = (bf16[768,1152]{1,0:T(8,128)(2,1)}, bf16[1024,768]{1,0:T(8,128)(2,1)}, bf16[1024,768]{1,0:T(8,128)(2,1)}, f32[1,1152]{1,0:T(1,128)}) custom-call(s32[64]{0:T(128)} %copy-done.9, s32[576]{0:T(1024)} %copy-done.6, s32[2]{0:T(128)} %copy-done.8, f32[32,3,8,128]{3,2,1,0:T(8,128)} %copy-done.3, f32[32,8,128]{2,1,0:T(8,128)} %copy-done.5, ...), custom_call_target="tpu_custom_call" | custom-call | flops 1 | bytes 1 | tf_op jit(solution)/shard_map/attend_back/pallas_call | solution.py:821
  285.7 2.9 fusion.4
  290.8 2.9 add_convert_fusion.5
  293.7 7.4 %collective-permute-start.34 = (bf16[512,768]{1,0:T(8,128)(2,1)}, bf16[512,768]{1,0:T(8,128)(2,1)}, u32[]{:S(2)}, u32[]{:S(2)}) collective-permute-start(bf16[512,768]{1,0:T(8,128)(2,1)} %get-tuple-element.232), channel_id=1, source_target_pairs={{0,0},{1,1},{4,2},{5,3},{2,4},{3,5},{6,6},{7,7},{8,8},{9,9},{12,10... | collective-permute-start | bytes 2359304 | tf_op jit(solution)/shard_map/ppermute | solution.py:67
  311.1 3.1 unpack.1
  316.0 4.6 %collective-permute-done.38 = bf16[1,2,4,32,1152]{4,3,1,2,0:T(8,128)(2,1)} collective-permute-done((bf16[1,2,4,32,1152]{4,3,1,2,0:T(8,128)(2,1)}, bf16[1,2,4,32,1152]{4,3,1,2,0:T(8,128)(2,1)}, u32[]{:S(2)}, u32[]{:S(2)}) %collective-permute-start.38) | collective-permute-done | bytes 589856 | tf_op jit(solution)/shard_map/ppermute | solution.py:110
  320.6 11.6 %collective-permute-done.40 = bf16[1,2,4,32,1152]{4,3,1,2,0:T(8,128)(2,1)} collective-permute-done((bf16[1,2,4,32,1152]{4,3,1,2,0:T(8,128)(2,1)}, bf16[1,2,4,32,1152]{4,3,1,2,0:T(8,128)(2,1)}, u32[]{:S(2)}, u32[]{:S(2)}) %collective-permute-start.40) | collective-permute-done | bytes 589856 | tf_op jit(solution)/shard_map/ppermute | solution.py:110
  334.0 4.2 %collective-permute-done.33 = bf16[512,768]{1,0:T(8,128)(2,1)} collective-permute-done((bf16[512,768]{1,0:T(8,128)(2,1)S(1)}, bf16[512,768]{1,0:T(8,128)(2,1)}, u32[]{:S(2)}, u32[]{:S(2)}) %collective-permute-start.33) | collective-permute-done | bytes 786464 | tf_op jit(solution)/shard_map/ppermute | solution.py:67
  339.7 9.7 %collective-permute-done.41 = bf16[2,216,768]{2,1,0:T(8,128)(2,1)S(1)} collective-permute-done((bf16[2,216,768]{2,1,0:T(8,128)(2,1)}, bf16[2,216,768]{2,1,0:T(8,128)(2,1)S(1)}, u32[]{:S(2)}, u32[]{:S(2)}) %collective-permute-start.41) | collective-permute-done | bytes 663584 | tf_op jit(solution)/shard_map/ppermute | solution.py:35
  351.0 13.9 %collective-permute-done.42 = bf16[2,2,32,1152]{3,2,1,0:T(8,128)(2,1)S(1)} collective-permute-done((bf16[2,2,32,1152]{3,2,1,0:T(8,128)(2,1)S(1)}, bf16[2,2,32,1152]{3,2,1,0:T(8,128)(2,1)S(1)}, u32[]{:S(2)}, u32[]{:S(2)}) %collective-permute-start.42) | collective-permute-done | bytes 294944 | tf_op jit(solution)/shard_map/ppermute | solution.py:35
  367.3 4.8 %collective-permute-done.43 = bf16[2,32,1152]{2,1,0:T(8,128)(2,1)S(1)} collective-permute-done((bf16[2,32,1152]{2,1,0:T(8,128)(2,1)S(1)}, bf16[2,32,1152]{2,1,0:T(8,128)(2,1)S(1)}, u32[]{:S(2)}, u32[]{:S(2)}) %collective-permute-start.43) | collective-permute-done | bytes 147488 | tf_op jit(solution)/shard_map/ppermute | solution.py:35
  (308 shorter events, 103.4 us)
Async XLA Ops:
  20.3 18.1 %collective-permute-start.1 = (bf16[232,768]{1,0:T(8,128)(2,1)S(1)}, bf16[232,768]{1,0:T(8,128)(2,1)S(1)}, u32[]{:S(2)}, u32[]{:S(2)}) collective-permute-start(bf16[232,768]{1,0:T(8,128)(2,1)S(1)} %concatenate.104.shard_ref), channel_id=1, source_target_pairs={{0,3},{1,2},{2,1},{3,0},{4,7},{5,6},{6,5},{7,4},{8,11},{9,10},{10,... | collective-permute-start | bytes 1069064 | tf_op jit(solution)/shard_map/ppermute | solution.py:35
  22.6 19.3 %collective-permute-start.7 = (bf16[2,2,32,1152]{3,2,1,0:T(8,128)(2,1)S(1)}, bf16[2,2,32,1152]{3,2,1,0:T(8,128)(2,1)}, u32[]{:S(2)}, u32[]{:S(2)}) collective-permute-start(bf16[2,2,32,1152]{3,2,1,0:T(8,128)(2,1)S(1)} %pad_maximum_fusion.5), channel_id=1, source_target_pairs={{0,1},{1,0},{2,3},{3,2},{4,5},{5,4},{6,7},{7,6},{8,9},{9,8},{10,11... | collective-permute-start | bytes 884744 | tf_op jit(solution)/shard_map/ppermute | solution.py:35
  36.6 17.8 %collective-permute-start.6 = (bf16[512,768]{1,0:T(8,128)(2,1)}, bf16[512,768]{1,0:T(8,128)(2,1)S(1)}, u32[]{:S(2)}, u32[]{:S(2)}) collective-permute-start(bf16[512,768]{1,0:T(8,128)(2,1)} %get-tuple-element.249), channel_id=1, source_target_pairs={{0,0},{1,1},{2,4},{3,5},{4,2},{5,3},{6,6},{7,7},{8,8},{9,9},{10,12... | collective-permute-start | bytes 2359304 | tf_op jit(solution)/shard_map/ppermute | solution.py:53
  39.3 32.7 %collective-permute-start.5 = (bf16[2,232,768]{2,1,0:T(8,128)(2,1)}, bf16[2,232,768]{2,1,0:T(8,128)(2,1)}, u32[]{:S(2)}, u32[]{:S(2)}) collective-permute-start(bf16[2,232,768]{2,1,0:T(8,128)(2,1)} %pad_maximum_fusion.4), channel_id=1, source_target_pairs={{0,1},{1,0},{2,3},{3,2},{4,5},{5,4},{6,7},{7,6},{8,9},{9,8},{10,11... | collective-permute-start | bytes 2138120 | tf_op jit(solution)/shard_map/ppermute | solution.py:35
  45.8 25.0 %collective-permute-start.10 = (bf16[2,112,1152]{2,1,0:T(8,128)(2,1)}, bf16[2,112,1152]{2,1,0:T(8,128)(2,1)}, u32[]{:S(2)}, u32[]{:S(2)}) collective-permute-start(bf16[2,112,1152]{2,1,0:T(8,128)(2,1)} %pack_columns.1.refs_5_), channel_id=1, source_target_pairs={{0,16},{4,20},{8,24},{12,28},{16,0},{20,4},{24,8},{28,12},{1,17},{... | collective-permute-start | bytes 1548296 | tf_op jit(solution)/shard_map/ppermute | solution.py:110
  47.3 23.5 %collective-permute-start.11 = (bf16[2,112,1152]{2,1,0:T(8,128)(2,1)}, bf16[2,112,1152]{2,1,0:T(8,128)(2,1)}, u32[]{:S(2)}, u32[]{:S(2)}) collective-permute-start(bf16[2,112,1152]{2,1,0:T(8,128)(2,1)} %pack_columns.1.refs_5_), channel_id=1, source_target_pairs={{0,24},{4,28},{8,16},{12,20},{16,8},{20,12},{24,0},{28,4},{1,25},{... | collective-permute-start | bytes 1548296 | tf_op jit(solution)/shard_map/ppermute | solution.py:110
  51.5 20.5 %collective-permute-start.9 = (bf16[2,112,1152]{2,1,0:T(8,128)(2,1)}, bf16[2,112,1152]{2,1,0:T(8,128)(2,1)}, u32[]{:S(2)}, u32[]{:S(2)}) collective-permute-start(bf16[2,112,1152]{2,1,0:T(8,128)(2,1)} %pack_columns.1.refs_5_), channel_id=1, source_target_pairs={{0,8},{4,12},{8,0},{12,4},{16,24},{20,28},{24,16},{28,20},{1,9},{5... | collective-permute-start | bytes 1548296 | tf_op jit(solution)/shard_map/ppermute | solution.py:110
  54.3 25.7 %collective-permute-start.14 = (bf16[512,768]{1,0:T(8,128)(2,1)}, bf16[512,768]{1,0:T(8,128)(2,1)}, u32[]{:S(2)}, u32[]{:S(2)}) collective-permute-start(bf16[512,768]{1,0:T(8,128)(2,1)} %get-tuple-element.248), channel_id=1, source_target_pairs={{0,1},{1,0},{2,5},{3,4},{4,3},{5,2},{6,7},{7,6},{8,9},{9,8},{10,13... | collective-permute-start | bytes 2359304 | tf_op jit(solution)/shard_map/ppermute | solution.py:53
  93.9 35.9 %collective-permute-start.19 = (bf16[2,448,768]{2,1,0:T(8,128)(2,1)S(1)}, bf16[2,448,768]{2,1,0:T(8,128)(2,1)S(1)}, u32[]{:S(2)}, u32[]{:S(2)}) collective-permute-start(bf16[2,448,768]{2,1,0:T(8,128)(2,1)S(1)} %pad_maximum_fusion.2.refs_2_), channel_id=1, source_target_pairs={{0,8},{4,12},{8,0},{12,4},{16,24},{20,28},{24,16},{28,20},{1,9},{5... | collective-permute-start | bytes 4128776 | tf_op jit(solution)/shard_map/ppermute | solution.py:110
  95.6 34.2 %collective-permute-start.18 = (bf16[2,432,768]{2,1,0:T(8,128)(2,1)S(1)}, bf16[2,432,768]{2,1,0:T(8,128)(2,1)}, u32[]{:S(2)}, u32[]{:S(2)}) collective-permute-start(bf16[2,432,768]{2,1,0:T(8,128)(2,1)S(1)} %pad_maximum_fusion.3.refs_0_), channel_id=1, source_target_pairs={{0,16},{4,20},{8,24},{12,28},{16,0},{20,4},{24,8},{28,12},{1,17},{... | collective-permute-start | bytes 3981320 | tf_op jit(solution)/shard_map/ppermute | solution.py:110
  107.4 22.4 %collective-permute-start.17 = (bf16[512,768]{1,0:T(8,128)(2,1)S(1)}, bf16[512,768]{1,0:T(8,128)(2,1)S(1)}, u32[]{:S(2)}, u32[]{:S(2)}) collective-permute-start(bf16[512,768]{1,0:T(8,128)(2,1)S(1)} %dynamic-slice_bitcast_fusion.1), channel_id=1, source_target_pairs={{0,0},{1,1},{2,4},{3,5},{4,2},{5,3},{6,6},{7,7},{8,8},{9,9},{10,12... | collective-permute-start | bytes 2359304 | tf_op jit(solution)/shard_map/ppermute | solution.py:53
  108.4 23.0 %collective-permute-start.21 = (bf16[2,432,768]{2,1,0:T(8,128)(2,1)S(1)}, bf16[2,432,768]{2,1,0:T(8,128)(2,1)S(1)}, u32[]{:S(2)}, u32[]{:S(2)}) collective-permute-start(bf16[2,432,768]{2,1,0:T(8,128)(2,1)S(1)} %pad_maximum_fusion.3.refs_0_), channel_id=1, source_target_pairs={{0,4},{4,0},{8,12},{12,8},{16,20},{20,16},{24,28},{28,24},{1,5},{5... | collective-permute-start | bytes 3981320 | tf_op jit(solution)/shard_map/ppermute | solution.py:30
  110.5 22.3 %collective-permute-start.23 = (bf16[2,448,768]{2,1,0:T(8,128)(2,1)S(1)}, bf16[2,448,768]{2,1,0:T(8,128)(2,1)S(1)}, u32[]{:S(2)}, u32[]{:S(2)}) collective-permute-start(bf16[2,448,768]{2,1,0:T(8,128)(2,1)S(1)} %pad_maximum_fusion.2.refs_2_), channel_id=1, source_target_pairs={{0,4},{4,0},{8,12},{12,8},{16,20},{20,16},{24,28},{28,24},{1,5},{5... | collective-permute-start | bytes 4128776 | tf_op jit(solution)/shard_map/ppermute | solution.py:30
  131.4 36.2 %collective-permute-start.25 = (bf16[512,768]{1,0:T(8,128)(2,1)S(1)}, bf16[512,768]{1,0:T(8,128)(2,1)S(1)}, u32[]{:S(2)}, u32[]{:S(2)}) collective-permute-start(bf16[512,768]{1,0:T(8,128)(2,1)S(1)} %dynamic-slice_bitcast_fusion), channel_id=1, source_target_pairs={{0,1},{1,0},{2,5},{3,4},{4,3},{5,2},{6,7},{7,6},{8,9},{9,8},{10,13... | collective-permute-start | bytes 2359304 | tf_op jit(solution)/shard_map/ppermute | solution.py:53
  169.4 39.6 %collective-permute-start.26 = (bf16[512,768]{1,0:T(8,128)(2,1)S(1)}, bf16[512,768]{1,0:T(8,128)(2,1)S(1)}, u32[]{:S(2)}, u32[]{:S(2)}) collective-permute-start(bf16[512,768]{1,0:T(8,128)(2,1)S(1)} %get-tuple-element.247), channel_id=1, source_target_pairs={{0,0},{1,1},{4,2},{5,3},{2,4},{3,5},{6,6},{7,7},{8,8},{9,9},{12,10... | collective-permute-start | bytes 2359304 | tf_op jit(solution)/shard_map/ppermute | solution.py:67
  170.1 38.9 %collective-permute-start.27 = (bf16[512,768]{1,0:T(8,128)(2,1)S(1)}, bf16[512,768]{1,0:T(8,128)(2,1)S(1)}, u32[]{:S(2)}, u32[]{:S(2)}) collective-permute-start(bf16[512,768]{1,0:T(8,128)(2,1)S(1)} %get-tuple-element.246), channel_id=1, source_target_pairs={{1,0},{0,1},{5,2},{4,3},{3,4},{2,5},{7,6},{6,7},{9,8},{8,9},{13,10... | collective-permute-start | bytes 2359304 | tf_op jit(solution)/shard_map/ppermute | solution.py:67
  229.2 49.6 %collective-permute-start.30 = (bf16[2,1,432,768]{3,2,1,0:T(8,128)(2,1)}, bf16[2,1,432,768]{3,2,1,0:T(8,128)(2,1)}, u32[]{:S(2)}, u32[]{:S(2)}) collective-permute-start(bf16[2,1,432,768]{3,2,1,0:T(8,128)(2,1)} %get-tuple-element.195), channel_id=1, source_target_pairs={{0,8},{4,12},{8,0},{12,4},{16,24},{20,28},{24,16},{28,20},{1,9},{5... | collective-permute-start | bytes 3981320 | tf_op jit(solution)/shard_map/ppermute | solution.py:110
  230.2 48.6 %collective-permute-start.31 = (bf16[1,2,432,768]{3,2,1,0:T(8,128)(2,1)S(1)}, bf16[1,2,432,768]{3,2,1,0:T(8,128)(2,1)}, u32[]{:S(2)}, u32[]{:S(2)}) collective-permute-start(bf16[1,2,432,768]{3,2,1,0:T(8,128)(2,1)S(1)} %get-tuple-element.197), channel_id=1, source_target_pairs={{0,16},{4,20},{8,24},{12,28},{16,0},{20,4},{24,8},{28,12},{1,17},{... | collective-permute-start | bytes 3981320 | tf_op jit(solution)/shard_map/ppermute | solution.py:110
  282.4 18.7 %collective-permute-start.37 = (bf16[4,4,32,1152]{3,2,1,0:T(8,128)(2,1)}, bf16[4,4,32,1152]{3,2,1,0:T(8,128)(2,1)}, u32[]{:S(2)}, u32[]{:S(2)}) collective-permute-start(bf16[4,4,32,1152]{3,2,1,0:T(8,128)(2,1)} %get-tuple-element.240), channel_id=1, source_target_pairs={{0,4},{4,0},{8,12},{12,8},{16,20},{20,16},{24,28},{28,24},{1,5},{5... | collective-permute-start | bytes 3538952 | tf_op jit(solution)/shard_map/ppermute | solution.py:30
  288.5 18.1 %collective-permute-start.35 = (bf16[432,768]{1,0:T(8,128)(2,1)}, bf16[432,768]{1,0:T(8,128)(2,1)}, u32[]{:S(2)}, u32[]{:S(2)}) collective-permute-start(bf16[432,768]{1,0:T(8,128)(2,1)} %get-tuple-element.206), channel_id=1, source_target_pairs={{0,16},{4,20},{8,24},{12,28},{16,0},{20,4},{24,8},{28,12},{1,17},{... | collective-permute-start | bytes 1990664 | tf_op jit(solution)/shard_map/ppermute | solution.py:110
  289.8 18.5 %collective-permute-start.36 = (bf16[432,768]{1,0:T(8,128)(2,1)}, bf16[432,768]{1,0:T(8,128)(2,1)}, u32[]{:S(2)}, u32[]{:S(2)}) collective-permute-start(bf16[432,768]{1,0:T(8,128)(2,1)} %get-tuple-element.208), channel_id=1, source_target_pairs={{0,8},{4,12},{8,0},{12,4},{16,24},{20,28},{24,16},{28,20},{1,9},{5... | collective-permute-start | bytes 1990664 | tf_op jit(solution)/shard_map/ppermute | solution.py:110
  306.6 25.6 %collective-permute-start.40 = (bf16[1,2,4,32,1152]{4,3,1,2,0:T(8,128)(2,1)}, bf16[1,2,4,32,1152]{4,3,1,2,0:T(8,128)(2,1)}, u32[]{:S(2)}, u32[]{:S(2)}) collective-permute-start(bf16[1,2,4,32,1152]{4,3,1,2,0:T(8,128)(2,1)} %get-tuple-element.239), channel_id=1, source_target_pairs={{0,24},{4,28},{8,16},{12,20},{16,8},{20,12},{24,0},{28,4},{1,25},{... | collective-permute-start | bytes 1769480 | tf_op jit(solution)/shard_map/ppermute | solution.py:110
  308.3 29.9 %collective-permute-start.33 = (bf16[512,768]{1,0:T(8,128)(2,1)S(1)}, bf16[512,768]{1,0:T(8,128)(2,1)}, u32[]{:S(2)}, u32[]{:S(2)}) collective-permute-start(bf16[512,768]{1,0:T(8,128)(2,1)S(1)} %copy-done.23), channel_id=1, source_target_pairs={{1,0},{0,1},{5,2},{4,3},{3,4},{2,5},{7,6},{6,7},{9,8},{8,9},{13,10... | collective-permute-start | bytes 2359304 | tf_op jit(solution)/shard_map/ppermute | solution.py:67
  314.2 35.2 %collective-permute-start.41 = (bf16[2,216,768]{2,1,0:T(8,128)(2,1)}, bf16[2,216,768]{2,1,0:T(8,128)(2,1)S(1)}, u32[]{:S(2)}, u32[]{:S(2)}) collective-permute-start(bf16[2,216,768]{2,1,0:T(8,128)(2,1)} %get-tuple-element.217), channel_id=1, source_target_pairs={{0,1},{1,0},{2,3},{3,2},{4,5},{5,4},{6,7},{7,6},{8,9},{9,8},{10,11... | collective-permute-start | bytes 1990664 | tf_op jit(solution)/shard_map/ppermute | solution.py:35
  (60 other events, 870.9 us)
